TPU v7x, 128 devices: a whole 4x4x4 slice. The times are simulated.
128 devices in a mesh: row: 16 (over z, y), col: 8 (over x, core).
Axes of the slice: x: 4, y: 4, z: 4, core: 2. Of those that a mesh axis runs over, the one named last changes fastest.
Arguments:
- image: bfloat16 [64, 64, 6144], P('row', None, 'col'), may hold values from -8 to 8
- filter_bank: float32 [2, 64, 64, 6144], P(None, None, 'row', 'col'), may hold values from -6 to 6
- gain_first: float32 [6144], P('col'), may hold values from 0.1 to 1.9
- gain_second: float32 [6144], P('col'), may hold values from 0.1 to 1.9
- w_in: bfloat16 [6144, 24576], P('col', 'row'), may hold values from -0.078125 to 0.078125
- b_in: float32 [24576], P('row'), may hold values from -4 to 4
- w_out: bfloat16 [24576, 6144], P('row', 'col'), may hold values from -0.0390625 to 0.0390625
- b_out: float32 [6144], P('col'), may hold values from -3 to 3
Outputs:
- block_out: bfloat16 [64, 64, 6144], P('row', None, 'col')
All inputs are finite; a program needn't handle non-finite values.
Results may differ from a plain program's by a relative error of at most 0.017.
Values may be sent and summed in bfloat16 or wider, within the bound.
No kernel may reach another device: no remote copies, remote signals or barrier semaphores. Data moves between devices by JAX's collectives and lax.ppermute only.
A program may use at most 128 MiB of HBM per device.

v0:
```python
import math

import jax
import jax.numpy as jnp
from jax import lax
from jax.sharding import PartitionSpec as P


def tables(count):
    index = jnp.arange(count, dtype=jnp.int32)
    angle = (index[:, None] * index[None, :] % count).astype(jnp.float32) * (2.0 * math.pi / count)
    return (jnp.cos(angle), jnp.sin(angle))


def finish_norm(values, totals, width_all):
    mean = totals[0][..., None] / width_all
    square = totals[1][..., None] / width_all
    return (values - mean) / jnp.sqrt(square - mean * mean + 1e-05)


def on_device(image, filter_bank, gain_first, gain_second, w_in, b_in, w_out, b_out):
    high = lax.Precision.HIGHEST
    rows_here, width, chans = image.shape
    height = rows_here * lax.axis_size("row")
    width_all = chans * lax.axis_size("col")
    source = image.astype(jnp.float32)
    totals = lax.psum((jnp.sum(source, axis=-1), jnp.sum(source * source, axis=-1)), "col")
    normed = finish_norm(source, totals, width_all) * gain_first
    cos_w, sin_w = tables(width)
    cos_h, sin_h = tables(height)
    col_re = jnp.einsum("rcd,ck->rkd", normed, cos_w, precision=high)
    col_im = -jnp.einsum("rcd,ck->rkd", normed, sin_w, precision=high)
    col_re, col_im = (
        lax.all_to_all(
            col_re.astype(jnp.bfloat16), "row", split_axis=1, concat_axis=0, tiled=True
        ).astype(col_re.dtype),
        lax.all_to_all(
            col_im.astype(jnp.bfloat16), "row", split_axis=1, concat_axis=0, tiled=True
        ).astype(col_im.dtype),
    )
    spec_re = jnp.einsum("rn,rkd->nkd", cos_h, col_re, precision=high) + jnp.einsum(
        "rn,rkd->nkd", sin_h, col_im, precision=high
    )
    spec_im = jnp.einsum("rn,rkd->nkd", cos_h, col_im, precision=high) - jnp.einsum(
        "rn,rkd->nkd", sin_h, col_re, precision=high
    )
    filt_re = filter_bank[0] * spec_re - filter_bank[1] * spec_im
    filt_im = filter_bank[0] * spec_im + filter_bank[1] * spec_re
    back_re = jnp.einsum("nr,nkd->rkd", cos_h, filt_re, precision=high) - jnp.einsum(
        "nr,nkd->rkd", sin_h, filt_im, precision=high
    )
    back_im = jnp.einsum("nr,nkd->rkd", sin_h, filt_re, precision=high) + jnp.einsum(
        "nr,nkd->rkd", cos_h, filt_im, precision=high
    )
    back_re, back_im = (
        lax.all_to_all(
            back_re.astype(jnp.bfloat16), "row", split_axis=0, concat_axis=1, tiled=True
        ).astype(back_re.dtype),
        lax.all_to_all(
            back_im.astype(jnp.bfloat16), "row", split_axis=0, concat_axis=1, tiled=True
        ).astype(back_im.dtype),
    )
    mixed = (
        jnp.einsum("rkd,kc->rcd", back_re, cos_w, precision=high)
        - jnp.einsum("rkd,kc->rcd", back_im, sin_w, precision=high)
    ) / (height * width)
    resid = (source + mixed).reshape(rows_here * width, chans)
    totals_two = lax.psum((jnp.sum(resid, axis=-1), jnp.sum(resid * resid, axis=-1)), "col")
    act = (finish_norm(resid, totals_two, width_all) * gain_second).astype(jnp.bfloat16)
    partial_pre = jnp.dot(
        lax.all_gather(act, "row", axis=0, tiled=True), w_in, preferred_element_type=jnp.float32
    )
    summed = lax.psum_scatter(
        partial_pre.astype(jnp.bfloat16), "col", scatter_dimension=0, tiled=True
    ).astype(jnp.float32)
    hidden = jax.nn.gelu(summed + b_in, approximate=False).astype(jnp.bfloat16)
    partial_out = jnp.dot(
        lax.all_gather(hidden, "col", axis=0, tiled=True), w_out, preferred_element_type=jnp.float32
    )
    proj = lax.psum_scatter(
        partial_out.astype(jnp.bfloat16), "row", scatter_dimension=0, tiled=True
    ).astype(jnp.float32)
    result = (resid + proj + b_out).astype(jnp.bfloat16)
    return result.reshape(rows_here, width, chans)


def solution(mesh):
    placed = (
        P("row", None, "col"),
        P(None, None, "row", "col"),
        P("col"),
        P("col"),
        P("col", "row"),
        P("row"),
        P("row", "col"),
        P("col"),
    )
    return jax.shard_map(
        on_device, mesh=mesh, in_specs=placed, out_specs=P("row", None, "col"), check_vma=False
    )
```

profile of v0, /device:TPU:1, one launch (start us, length us, event | category | flops | bytes accessed | tf_op | source)
XLA Modules:
  0.0 432.7 jit_solution(3554515615974507233)
XLA Ops:
  6.5 0.0 copy-start
  6.5 1.3 convert_reduce_fusion
  7.9 13.2 %all-reduce.1 = (f32[4,64]{1,0:T(4,128)S(1)}, f32[4,64]{1,0:T(4,128)S(1)}) all-reduce(f32[4,64]{1,0:T(4,128)S(1)} %get-tuple-element.8, f32[4,64]{1,0:T(4,128)S(1)} %get-tuple-element.7), channel_id=1, replica_groups=mesh['row'=16,'col'=8] {'col'}, use_global_device_ids=true, to_apply=%region_3.0 | all-reduce | flops 512 | bytes 4096 | tf_op jit(solution)/shard_map/psum | solution.py:27
  21.1 2.0 fusion.19
  23.1 1.1 copy.18
  24.1 7.8 %all-to-all-start.1 = ((bf16[4,64,768]{2,0,1:T(4,128)(2,1)}), bf16[4,64,768]{2,0,1:T(4,128)(2,1)S(1)}, u32[]{:S(2)}, u32[]{:S(2)}) async-start(bf16[4,64,768]{2,0,1:T(4,128)(2,1)} %copy.18), calls=%async_computation.1 | async-start | bytes 786432 | tf_op jit(solution)/shard_map/all_to_all | solution.py:37
  32.0 0.0 copy-done.4
  32.0 1.0 fusion.18
  33.0 1.1 copy.16
  34.0 6.3 %all-to-all-done.1 = bf16[4,64,768]{2,0,1:T(4,128)(2,1)S(1)} async-done(((bf16[4,64,768]{2,0,1:T(4,128)(2,1)}), bf16[4,64,768]{2,0,1:T(4,128)(2,1)S(1)}, u32[]{:S(2)}, u32[]{:S(2)}) %all-to-all-start.1) | async-done | bytes 393248 | tf_op jit(solution)/shard_map/all_to_all | solution.py:37
  40.4 3.6 all-to-all-start
  43.9 2.6 fusion.122
  46.6 0.9 copy.43
  47.5 1.1 all_to_all.59
  48.5 3.6 all-to-all-done
  52.1 0.9 copy.44
  53.0 1.1 all_to_all.55
  54.1 0.6 fusion.53
  54.7 0.6 fusion.51
  55.3 0.6 convolution_subtract_fusion.2
  55.9 0.0 copy-done.2
  55.9 0.0 copy-done.3
  55.9 0.9 multiply_add_fusion
  56.8 0.0 copy-start.1
  56.8 0.9 fusion.49
  57.7 0.0 copy-done.1
  57.7 0.9 fusion.15
  58.7 1.1 copy.21
  59.7 3.6 all-to-all-start.2
  63.3 0.9 fusion.40
  64.2 2.0 fusion.16
  66.3 0.0 copy-start.5
  66.3 1.1 copy.23
  67.4 4.1 all-to-all-done.2
  71.5 3.6 all-to-all-start.3
  75.1 0.2 all-gather.3.cloned.1.call-start
  75.3 0.9 copy.42
  76.2 1.8 all_to_all.63
  78.0 5.2 %all-to-all-done.3 = bf16[64,4,768]{2,1,0:T(4,128)(2,1)S(1)} async-done(((bf16[64,4,768]{2,1,0:T(4,128)(2,1)}), bf16[64,4,768]{2,1,0:T(4,128)(2,1)S(1)}, u32[]{:S(2)}, u32[]{:S(2)}) %all-to-all-start.3) | async-done | bytes 393248 | tf_op jit(solution)/shard_map/all_to_all | solution.py:59
  83.3 0.1 copy.41
  83.4 0.8 all_to_all.67
  84.3 1.6 fusion.47
  85.8 1.8 fusion.121
  87.7 0.1 reduce_sum.43
  87.7 0.1 reduce_sum.45
  87.8 19.3 %all-reduce = (f32[256]{0:T(256)S(1)}, f32[256]{0:T(256)S(1)}) all-reduce(f32[256]{0:T(256)S(1)} %reduce_sum.45, f32[256]{0:T(256)S(1)} %reduce_sum.43), channel_id=1, replica_groups=mesh['row'=16,'col'=8] {'col'}, use_global_device_ids=true, to_apply=%region_7.8 | all-reduce | flops 512 | bytes 4096 | tf_op jit(solution)/shard_map/psum | solution.py:68
  107.2 0.0 copy-done.7
  107.2 0.9 fusion.25
  108.1 0.0 all-gather.3.cloned.1.call-update
  108.1 0.0 reduce-scatter.3.cloned.1.call-start
  108.2 56.5 %all-gather.3.cloned.1.call-done = bf16[4096,768]{1,0:T(8,128)(2,1)} async-done(((bf16[256,768]{1,0:T(8,128)(2,1)}), bf16[4096,768]{1,0:T(8,128)(2,1)}) %all-gather.3.cloned.1.call-update) | async-done | bytes 6291472 | tf_op jit(solution)/shard_map/all_gather | solution.py:71
  164.6 15.2 %convolution_convert_fusion = bf16[4096,1536]{1,0:T(8,128)(2,1)} fusion(bf16[4096,768]{1,0:T(8,128)(2,1)} %all-gather.3.cloned.1.call-done, bf16[768,1536]{1,0:T(8,128)(2,1)S(1)} %copy-done), kind=kOutput, calls=%fused_computation | convolution fusion | flops 9669967872 | bytes 21233664 | tf_op jit(solution)/shard_map/dot_general | solution.py:70
  179.8 0.0 reduce-scatter.3.cloned.1.call-update
  179.8 0.0 all-gather.5.cloned.1.call-start
  179.9 71.5 %reduce-scatter.3.cloned.1.call-done = bf16[512,1536]{1,0:T(8,128)(2,1)} async-done(((bf16[4096,1536]{1,0:T(8,128)(2,1)}), bf16[512,1536]{1,0:T(8,128)(2,1)}) %reduce-scatter.3.cloned.1.call-update) | async-done | bytes 1572880 | tf_op jit(solution)/shard_map/reduce_scatter | solution.py:73
  251.4 8.9 %fusion.2 = bf16[512,1536]{1,0:T(8,128)(2,1)} fusion(bf16[512,1536]{1,0:T(8,128)(2,1)} %reduce-scatter.3.cloned.1.call-done, f32[1536]{0:T(1024)S(1)} %copy-done.6), kind=kLoop, calls=%fused_computation.5 | loop fusion | flops 52690944 | bytes 3151872 | tf_op jit(solution)/shard_map/convert_element_type | solution.py:76
  260.2 0.0 all-gather.5.cloned.1.call-update
  260.3 0.0 reduce-scatter.5.cloned.1.call-start
  260.3 68.0 %all-gather.5.cloned.1.call-done = bf16[4096,1536]{1,0:T(8,128)(2,1)} async-done(((bf16[512,1536]{1,0:T(8,128)(2,1)}), bf16[4096,1536]{1,0:T(8,128)(2,1)}) %all-gather.5.cloned.1.call-update) | async-done | bytes 12582928 | tf_op jit(solution)/shard_map/all_gather | solution.py:78
  328.3 15.3 %convolution_convert_fusion.1 = bf16[4096,768]{1,0:T(8,128)(2,1)} fusion(bf16[4096,1536]{1,0:T(8,128)(2,1)} %all-gather.5.cloned.1.call-done, bf16[1536,768]{1,0:T(8,128)(2,1)} %param.14), kind=kOutput, calls=%fused_computation.1 | convolution fusion | flops 9666822144 | bytes 21233664 | tf_op jit(solution)/shard_map/dot_general | solution.py:77
  343.6 0.0 reduce-scatter.5.cloned.1.call-update
  343.6 80.6 %reduce-scatter.5.cloned.1.call-done = bf16[256,768]{1,0:T(8,128)(2,1)} async-done(((bf16[4096,768]{1,0:T(8,128)(2,1)}), bf16[256,768]{1,0:T(8,128)(2,1)}) %reduce-scatter.5.cloned.1.call-update) | async-done | bytes 393232 | tf_op jit(solution)/shard_map/reduce_scatter | solution.py:80
  424.2 0.0 copy-done.8
  424.2 1.9 fusion.27
  (13 shorter events, 0.0 us)
Async XLA Ops:
  6.5 158.1 %copy-start = (bf16[768,1536]{1,0:T(8,128)(2,1)S(1)}, bf16[768,1536]{1,0:T(8,128)(2,1)}, u32[]{:S(2)}) copy-start(bf16[768,1536]{1,0:T(8,128)(2,1)} %param.12) | copy-start | bytes 7077892
  6.5 25.4 %copy-start.4 = (bf16[4,64,768]{2,1,0:T(8,128)(2,1)S(1)}, bf16[4,64,768]{2,1,0:T(8,128)(2,1)}, u32[]{:S(2)}) copy-start(bf16[4,64,768]{2,1,0:T(8,128)(2,1)} %param.8) | copy-start | bytes 1179652
  6.5 25.5 %copy-start.9 = (f32[768]{0:T(1024)S(1)}, f32[768]{0:T(1024)}, u32[]{:S(2)}) copy-start(f32[768]{0:T(1024)} %param.10) | copy-start | bytes 9220
  24.1 16.2 %all-to-all-start.1 = ((bf16[4,64,768]{2,0,1:T(4,128)(2,1)}), bf16[4,64,768]{2,0,1:T(4,128)(2,1)S(1)}, u32[]{:S(2)}, u32[]{:S(2)}) async-start(bf16[4,64,768]{2,0,1:T(4,128)(2,1)} %copy.18), calls=%async_computation.1 | async-start | bytes 786432 | tf_op jit(solution)/shard_map/all_to_all | solution.py:37
  40.4 11.8 %all-to-all-start = ((bf16[4,64,768]{2,0,1:T(4,128)(2,1)}), bf16[4,64,768]{2,0,1:T(4,128)(2,1)S(1)}, u32[]{:S(2)}, u32[]{:S(2)}) async-start(bf16[4,64,768]{2,0,1:T(4,128)(2,1)} %copy.16), calls=%async_computation | async-start | bytes 786432 | tf_op jit(solution)/shard_map/all_to_all | solution.py:34
  54.1 1.8 copy-start.2
  54.1 1.8 copy-start.3
  56.8 0.9 copy-start.1
  59.7 11.8 %all-to-all-start.2 = ((bf16[64,4,768]{2,1,0:T(4,128)(2,1)}), bf16[64,4,768]{2,1,0:T(4,128)(2,1)S(1)}, u32[]{:S(2)}, u32[]{:S(2)}) async-start(bf16[64,4,768]{2,1,0:T(4,128)(2,1)} %copy.21), calls=%async_computation.2 | async-start | bytes 786432 | tf_op jit(solution)/shard_map/all_to_all | solution.py:56
  66.3 19.5 %copy-start.5 = (bf16[4,64,768]{2,1,0:T(8,128)(2,1)S(1)}, bf16[4,64,768]{2,1,0:T(8,128)(2,1)}, u32[]{:S(2)}) copy-start(bf16[4,64,768]{2,1,0:T(8,128)(2,1)} %param.8) | copy-start | bytes 1179652
  71.5 11.8 %all-to-all-start.3 = ((bf16[64,4,768]{2,1,0:T(4,128)(2,1)}), bf16[64,4,768]{2,1,0:T(4,128)(2,1)S(1)}, u32[]{:S(2)}, u32[]{:S(2)}) async-start(bf16[64,4,768]{2,1,0:T(4,128)(2,1)} %copy.23), calls=%async_computation.3 | async-start | bytes 786432 | tf_op jit(solution)/shard_map/all_to_all | solution.py:59
  75.1 89.6 %all-gather.3.cloned.1.call-start = ((), (), s32[]{:S(2)}) async-start(), calls=%async_computation.6 | async-start | bytes 6684672 | tf_op jit(solution)/shard_map/all_gather | solution.py:71
  76.2 31.0 %copy-start.7 = (f32[768]{0:T(1024)S(1)}, f32[768]{0:T(1024)}, u32[]{:S(2)}) copy-start(f32[768]{0:T(1024)} %param.11) | copy-start | bytes 9220
  108.1 143.2 %reduce-scatter.3.cloned.1.call-start = ((), (), s32[]{:S(2)}) async-start(), calls=%async_computation.7 | async-start | bytes 14155776 | tf_op jit(solution)/shard_map/reduce_scatter | solution.py:73
  179.8 71.5 %copy-start.6 = (f32[1536]{0:T(1024)S(1)}, f32[1536]{0:T(1024)}, u32[]{:S(2)}) copy-start(f32[1536]{0:T(1024)} %param.13) | copy-start | bytes 18436
  179.8 148.5 %all-gather.5.cloned.1.call-start = ((), (), s32[]{:S(2)}) async-start(), calls=%async_computation.8 | async-start | bytes 14155776 | tf_op jit(solution)/shard_map/all_gather | solution.py:78
  260.3 164.0 %reduce-scatter.5.cloned.1.call-start = ((), (), s32[]{:S(2)}) async-start(), calls=%async_computation.9 | async-start | bytes 6684672 | tf_op jit(solution)/shard_map/reduce_scatter | solution.py:80
  343.6 80.6 %copy-start.8 = (f32[768]{0:T(1024)S(1)}, f32[768]{0:T(1024)}, u32[]{:S(2)}) copy-start(f32[768]{0:T(1024)} %param.15) | copy-start | bytes 9220
Sparse Core Ops, SparseCore 0:
  108.2 56.3 all-gather.2
  180.0 71.3 reduce-scatter.2
  260.4 67.8 all-gather.4
  343.8 80.4 reduce-scatter.4
where the time goes:
time: 434 us; the launch traced here: 433 us
  waiting for transfers between devices  296 us (68%)
  matrix products  44.3 us (10%)
  blocking collectives  32.5 us (7%)
  starting transfers between devices  18.9 us (4%)
  local copies, waits for them, and re-layouts  14.7 us (3%)
  between operations  13.4 us (3%)
  other arithmetic  13 us (3%)
    reduce_scatter x1, waiting for transfers between devices, on_device(): lax.psum_scatter(partial_out.astype(jnp.bfloat16), 'row', scatter_dimensi...  80.6 us
    reduce_scatter x1, waiting for transfers between devices, on_device(): lax.psum_scatter(partial_pre.astype(jnp.bfloat16), 'col', scatter_dimensi...  71.5 us
    all_gather x1, waiting for transfers between devices, on_device(): lax.all_gather(hidden, 'col', axis=0, tiled=True)  68 us
    all_gather x1, waiting for transfers between devices, on_device(): lax.all_gather(act, 'row', axis=0, tiled=True)  56.5 us
    psum x1, blocking collectives, on_device(): lax.psum((jnp.sum(resid, axis=-1), jnp.sum(resid * resid, axis=-1)), 'col')  19.3 us
    dot_general x1, matrix products, on_device(): jnp.dot(lax.all_gather(hidden, 'col', axis=0, tiled=True), w_out, preferr...  15.3 us
    dot_general x1, matrix products, on_device(): jnp.dot(lax.all_gather(act, 'row', axis=0, tiled=True), w_in, preferred_e...  15.2 us
    psum x1, blocking collectives, on_device(): lax.psum((jnp.sum(source, axis=-1), jnp.sum(source * source, axis=-1)), '...  13.2 us
  transfers between devices with their start and end apart: 8, of which 8 were waited for; matrix products, arithmetic and copies ran while one was open for 2% of the time, Pallas kernels for 0%

commit v1 on v0

v1 whole, which is shorter than its diff:
```python
import functools
import math

import jax
import jax.numpy as jnp
import numpy as np
from jax import lax
from jax.experimental import pallas as pl
from jax.experimental.pallas import tpu as pltpu
from jax.sharding import PartitionSpec as P

SIDE = 4
BF = jnp.bfloat16
F32 = jnp.float32
MB = 1 << 20


def angles(count):
    index = np.arange(count)
    turn = (index[:, None] * index[None, :]) % count * (2.0 * math.pi / count)
    return np.cos(turn), np.sin(turn)


def spectral_tables(here, width, height):
    groups = height // here
    per = width // groups
    cos_w, sin_w = angles(width)
    cos_h, sin_h = angles(height)
    eye_r, eye_k = np.eye(here), np.eye(per)
    out = np.stack([cos_w, -sin_w]).reshape(2, width, groups, per)
    one = np.einsum("scqk,rt->qrsktc", out, eye_r).reshape(2 * here * width, here * width)
    turn = np.stack([np.stack([cos_h, sin_h]), np.stack([-sin_h, cos_h])])
    turn = turn.reshape(2, 2, groups, here, height)
    two = np.einsum("uvqrn,kl->unkqrvl", turn, eye_k).reshape(2 * height * per, 2 * height * per)
    back = np.stack([np.stack([cos_h, -sin_h]), np.stack([sin_h, cos_h])])
    back = back.reshape(2, 2, height, groups, here)
    three = np.einsum("uvnqr,kl->qrukvnl", back, eye_k).reshape(2 * height * per, 2 * height * per)
    four = np.einsum("sqkc,rt->rcqtsk", out.transpose(0, 2, 3, 1), eye_r)
    four = four.reshape(here * width, 2 * here * width) / (width * height)
    return [t.astype(np.float32) for t in (one, two, three, four)]


def shift_row(a, dz, dy):
    pairs = []
    for z in range(SIDE):
        for y in range(SIDE):
            pairs.append((z * SIDE + y, (z + dz) % SIDE * SIDE + (y + dy) % SIDE))
    return lax.ppermute(a, "row", pairs)


def along(a, axis, step):
    return shift_row(a, step, 0) if axis == "z" else shift_row(a, 0, step)


def params(mb):
    return pltpu.CompilerParams(vmem_limit_bytes=mb * MB)


def act_kernel(moved_ref, first_ref, second_ref):
    cols, rows, chans = moved_ref.shape
    half = first_ref.shape[0]
    values = moved_ref[:, : 2 * half, :].astype(F32)
    gains = jnp.sum(moved_ref[:, 2 * half :, :].astype(F32)[:, :3], axis=1)
    mean = jnp.sum(jnp.sum(values, axis=0), axis=-1, keepdims=True) / (cols * chans)
    square = jnp.sum(jnp.sum(values * values, axis=0), axis=-1, keepdims=True) / (cols * chans)
    scale = 1.0 / jnp.sqrt(square - mean * mean + 1e-05)
    for j in range(cols):
        part = ((values[j] - mean) * scale * gains[j][None, :]).astype(BF)
        first_ref[:, j * chans : (j + 1) * chans] = part[:half]
        second_ref[:, j * chans : (j + 1) * chans] = part[half:]


def normalize(moved, half):
    cols, _, chans = moved.shape
    shape = jax.ShapeDtypeStruct((half, cols * chans), BF)
    return pl.pallas_call(act_kernel, out_shape=(shape, shape), compiler_params=params(16))(moved)


def mm1_kernel(block, *refs):
    pieces, (w_ref, b_ref, o_ref) = refs[:-3], refs[-3:]
    depth = w_ref.shape[0]
    total = None
    for at in range(0, depth, block):
        left = jnp.concatenate(
            [p[:, :, at : at + block].reshape(-1, block) for p in pieces], axis=0
        )
        term = jnp.dot(left, w_ref[at : at + block, :], preferred_element_type=F32)
        total = term if total is None else total + term
    pre = total + b_ref[...]
    o_ref[...] = (0.5 * pre * (1.0 + lax.erf(pre * math.sqrt(0.5)))).astype(BF)


def matmul_in(pieces, w, b):
    depth, width = w.shape
    shape = pieces[0].shape
    tokens = len(pieces) * shape[0] * shape[1]
    tile = 256
    return pl.pallas_call(
        functools.partial(mm1_kernel, 768),
        grid=(width // tile,),
        in_specs=[pl.BlockSpec(shape, lambda i: (0, 0, 0)) for _ in pieces]
        + [
            pl.BlockSpec((depth, tile), lambda i: (0, i)),
            pl.BlockSpec((1, tile), lambda i: (0, i)),
        ],
        out_specs=pl.BlockSpec((tokens, tile), lambda i: (0, i)),
        out_shape=jax.ShapeDtypeStruct((tokens, width), BF),
        compiler_params=params(40),
        cost_estimate=pl.CostEstimate(
            flops=2 * tokens * depth * width,
            bytes_accessed=2 * (tokens * depth + depth * width),
            transcendentals=0,
        ),
    )(*pieces, w, b[None])


def mm2_kernel(h_ref, w_ref, *outs):
    out = jnp.dot(h_ref[...], w_ref[0], preferred_element_type=F32)
    shape = outs[0].shape
    rows = shape[0] * shape[1]
    for i, o_ref in enumerate(outs):
        o_ref[...] = out[i * rows : (i + 1) * rows].astype(BF).reshape(shape)


def matmul_out(hidden, w, half):
    cols, depth, chans = w.shape
    tokens = hidden.shape[0]
    count = tokens // (SIDE * half)
    return pl.pallas_call(
        mm2_kernel,
        grid=(cols,),
        in_specs=[
            pl.BlockSpec((tokens, depth), lambda j: (0, 0)),
            pl.BlockSpec((1, depth, chans), lambda j: (j, 0, 0)),
        ],
        out_specs=[pl.BlockSpec((SIDE, half, chans), lambda j: (0, 0, j))] * count,
        out_shape=[jax.ShapeDtypeStruct((SIDE, half, cols * chans), BF)] * count,
        compiler_params=params(40),
        cost_estimate=pl.CostEstimate(
            flops=2 * tokens * depth * cols * chans,
            bytes_accessed=2 * (tokens * depth + depth * cols * chans + tokens * cols * chans),
            transcendentals=0,
        ),
    )(hidden, w)


def add_kernel(a, b, c, d, *outs):
    total = (a[...].astype(F32) + b[...].astype(F32)) + (c[...].astype(F32) + d[...].astype(F32))
    for i, o_ref in enumerate(outs):
        o_ref[...] = total[i].astype(BF)


def add_pieces(parts):
    count, half, width = parts[0].shape
    tile = width // 4
    return pl.pallas_call(
        add_kernel,
        grid=(width // tile,),
        in_specs=[pl.BlockSpec((count, half, tile), lambda j: (0, 0, j))] * len(parts),
        out_specs=[pl.BlockSpec((half, tile), lambda j: (0, j))] * count,
        out_shape=[jax.ShapeDtypeStruct((half, width), BF)] * count,
        compiler_params=params(16),
    )(*parts)


def last_kernel(a, b, c, d, e, f, g, h, o_ref):
    half = a.shape[0]
    top = (a[...].astype(F32) + b[...].astype(F32)) + (c[...].astype(F32) + d[...].astype(F32))
    low = (e[...].astype(F32) + f[...].astype(F32)) + (g[...].astype(F32) + h[...].astype(F32))
    o_ref[0, :half, :] = top.astype(BF)
    o_ref[0, half:, :] = low.astype(BF)


def add_last(first, second, cols):
    half, width = first[0].shape
    chans = width // cols
    return pl.pallas_call(
        last_kernel,
        grid=(cols,),
        in_specs=[pl.BlockSpec((half, chans), lambda j: (0, j))] * 8,
        out_specs=pl.BlockSpec((1, 2 * half, chans), lambda j: (j, 0, 0)),
        out_shape=jax.ShapeDtypeStruct((cols, 2 * half, chans), BF),
        compiler_params=params(16),
    )(*first, *second)


def exchange(a, axis):
    return lax.all_to_all(a, axis, split_axis=0, concat_axis=0, tiled=True)


def spectral(image, filter_bank, gain_first):
    rows_here, width, chans = image.shape
    groups = lax.axis_size("row")
    width_all = chans * lax.axis_size("col")
    tokens = rows_here * width
    one, two, three, four = spectral_tables(rows_here, width, rows_here * groups)
    high = lax.Precision.HIGH
    source = image.astype(F32).reshape(tokens, chans)
    sums, squares = lax.psum(
        (jnp.sum(source, axis=-1), jnp.sum(source * source, axis=-1)), "col"
    )
    mean = sums[:, None] / width_all
    square = squares[:, None] / width_all
    normed = (source - mean) / jnp.sqrt(square - mean * mean + 1e-05) * gain_first
    col = jnp.dot(one, normed, precision=high).astype(BF)
    col = exchange(col.reshape(groups, -1, chans), "row").reshape(-1, chans)
    spec = jnp.dot(two, col.astype(F32), precision=high)
    split = spec.shape[0] // 2
    spec_re, spec_im = spec[:split], spec[split:]
    f_re, f_im = filter_bank[0].reshape(-1, chans), filter_bank[1].reshape(-1, chans)
    filt = jnp.concatenate(
        [f_re * spec_re - f_im * spec_im, f_re * spec_im + f_im * spec_re], axis=0
    )
    back = jnp.dot(three, filt, precision=high).astype(BF)
    back = exchange(back.reshape(groups, -1, chans), "row").reshape(-1, chans)
    return source + jnp.dot(four, back.astype(F32), precision=high)


def three_parts(gain):
    top = lax.reduce_precision(gain, 8, 7)
    mid = lax.reduce_precision(gain - top, 8, 7)
    return jnp.stack([top, mid, gain - top - mid]).astype(BF)


def gather_two(a, axis_one, axis_two):
    got = jnp.stack([a] + [along(a, axis_one, s) for s in (1, -1, 2)])
    return [got] + [along(got, axis_two, s) for s in (1, -1, 2)]


def send_back(parts, axis):
    return [parts[0]] + [along(p, axis, s) for p, s in zip(parts[1:], (-1, 1, 2))]


def on_device(image, filter_bank, gain_first, gain_second, w_in, b_in, w_out, b_out):
    rows_here, width, chans = image.shape
    cols = lax.axis_size("col")
    w_in_all = lax.all_gather(w_in, "col", axis=0, tiled=True)
    w_out_all = lax.all_gather(w_out, "col", axis=0, tiled=False)
    resid = spectral(image, filter_bank, gain_first)
    tokens = rows_here * width
    own = tokens // cols
    half = own // 2
    extra = jnp.pad(three_parts(gain_second), ((0, half - 3), (0, 0)))
    message = jnp.concatenate(
        [
            resid.astype(BF).reshape(cols, own, chans),
            jnp.broadcast_to(extra[None], (cols, half, chans)),
        ],
        axis=1,
    )
    first, second = normalize(exchange(message, "col"), half)
    pieces = gather_two(first, "z", "y") + gather_two(second, "y", "z")
    hidden = matmul_in(pieces, w_in_all, b_in)
    outs = matmul_out(hidden, w_out_all, half)
    count = len(outs) // 2
    first = send_back(add_pieces(send_back(outs[:count], "y")), "z")
    second = send_back(add_pieces(send_back(outs[count:], "z")), "y")
    proj = exchange(add_last(first, second, cols), "col")
    result = (resid + proj.reshape(tokens, chans).astype(F32) + b_out).astype(BF)
    return result.reshape(rows_here, width, chans)


def solution(mesh):
    placed = (
        P("row", None, "col"),
        P(None, None, "row", "col"),
        P("col"),
        P("col"),
        P("col", "row"),
        P("row"),
        P("row", "col"),
        P("col"),
    )
    return jax.shard_map(
        on_device, mesh=mesh, in_specs=placed, out_specs=P("row", None, "col"), check_vma=False
    )
```

time: 434 us -> 319 us (0.74)
  waiting for transfers between devices: 296 us -> 153 us
  matrix products: 44.3 us -> 8.24 us
  Pallas kernels: 0 us -> 30 us
  blocking collectives: 32.5 us -> 58.4 us
  starting transfers between devices: 18.9 us -> 39.7 us
  other arithmetic: 13 us -> 1.52 us
    reduce_scatter x2 -> x0, waiting for transfers between devices: 152 us -> none  [the longest x1 80.6 us: on_device(): lax.psum_scatter(partial_out.astype(jnp.bfloat16), 'row', scatter_dimensi...]
    ppermute x0 -> x24, waiting for transfers between devices: none -> 106 us  [shift_row(): return lax.ppermute(a, 'row', pairs)]
    all_gather x2, waiting for transfers between devices: 124 us -> 25.7 us  [the longest x1 25.7 us: on_device(): w_out_all = lax.all_gather(w_out, 'col', axis=0, tiled=False)]
    all_to_all x0 -> x2, blocking collectives: none -> 45.2 us  [exchange(): return lax.all_to_all(a, axis, split_axis=0, concat_axis=0, tiled=True)]
    dot_general x14 -> x5, matrix products: 44.3 us -> 8.24 us  [the longest x2 2.8 us: spectral(): back = jnp.dot(three, filt, precision=high).astype(BF)]
    pallas_call x0 -> x6, Pallas kernels: none -> 30 us  [the longest x1 14.1 us: matmul_out(): pl.pallas_call(mm2_kernel, grid=(cols,), in_specs=[pl.BlockSpec((tokens,...]
    ppermute x0 -> x24, starting transfers between devices: none -> 28.1 us  [shift_row(): return lax.ppermute(a, 'row', pairs)]
    psum x2 -> x1, blocking collectives: 32.5 us -> 13.2 us  [spectral(): lax.psum((jnp.sum(source, axis=-1), jnp.sum(source * source, axis=-1)), '...]
  transfers between devices with their start and end apart: 8 -> 28, of which waited for: 8 -> 15; matrix products, arithmetic and copies ran while one was open for 2% -> 3% of each run, Pallas kernels for 0% -> 5%
where the time goes in v1:
time: 319 us; the launch traced here: 318 us
  waiting for transfers between devices  153 us (48%)
  blocking collectives  58.4 us (18%)
  starting transfers between devices  39.7 us (12%)
  Pallas kernels  30 us (9%)
  between operations  13.7 us (4%)
  local copies, waits for them, and re-layouts  13.2 us (4%)
  matrix products  8.24 us (3%)
    ppermute x24, waiting for transfers between devices, shift_row(): return lax.ppermute(a, 'row', pairs)  106 us
    all_to_all x2, blocking collectives, exchange(): return lax.all_to_all(a, axis, split_axis=0, concat_axis=0, tiled=True)  45.2 us
    ppermute x24, starting transfers between devices, shift_row(): return lax.ppermute(a, 'row', pairs)  28.1 us
    all_gather x1, waiting for transfers between devices, on_device(): w_out_all = lax.all_gather(w_out, 'col', axis=0, tiled=False)  25.7 us
    all_to_all x2, waiting for transfers between devices, exchange(): return lax.all_to_all(a, axis, split_axis=0, concat_axis=0, tiled=True)  20.1 us
    pallas_call x1, Pallas kernels, matmul_out(): pl.pallas_call(mm2_kernel, grid=(cols,), in_specs=[pl.BlockSpec((tokens,...  14.1 us
    pallas_call x1, Pallas kernels, matmul_in(): pl.pallas_call(functools.partial(mm1_kernel, 768), grid=(width // tile,),...  13.4 us
    psum x1, blocking collectives, spectral(): lax.psum((jnp.sum(source, axis=-1), jnp.sum(source * source, axis=-1)), '...  13.2 us
  transfers between devices with their start and end apart: 28, of which 15 were waited for; matrix products, arithmetic and copies ran while one was open for 3% of the time, Pallas kernels for 5%

profile of v1, /device:TPU:1, one launch (start us, length us, event | category | flops | bytes accessed | tf_op | source)
XLA Modules:
  0.0 317.6 jit_solution(4327590818729846921)
XLA Ops:
  6.5 0.7 all-gather.4.cloned.1.call-update
  7.3 0.7 all-gather.6.cloned.1.call-update
  8.0 0.2 copy-done.10
  8.6 13.2 %all-reduce.1 = (f32[256]{0:T(256)S(1)}, f32[256]{0:T(256)S(1)}) all-reduce(f32[256]{0:T(256)S(1)} %reduce_sum.25, f32[256]{0:T(256)S(1)} %reduce_sum.23), channel_id=1, replica_groups=mesh['row'=16,'col'=8] {'col'}, use_global_device_ids=true, to_apply=%region_3.0 | all-reduce | flops 512 | bytes 4096 | tf_op jit(solution)/shard_map/psum | solution.py:199
  22.0 1.7 convolution_convert_fusion
  23.7 7.8 %all-to-all-start = ((bf16[16,32,768]{2,1,0:T(8,128)(2,1)}), bf16[16,32,768]{2,1,0:T(8,128)(2,1)S(1)}, u32[]{:S(2)}, u32[]{:S(2)}) async-start(bf16[16,32,768]{2,1,0:T(8,128)(2,1)} %bitcast.2), calls=%async_computation | async-start | bytes 1572864 | tf_op jit(solution)/shard_map/all_to_all | solution.py:188
  31.5 1.5 fusion.21
  33.0 0.3 reshape_squeeze.7
  33.3 0.3 reshape_squeeze.6
  33.6 9.7 %all-to-all-done = bf16[16,32,768]{2,1,0:T(8,128)(2,1)S(1)} async-done(((bf16[16,32,768]{2,1,0:T(8,128)(2,1)}), bf16[16,32,768]{2,1,0:T(8,128)(2,1)S(1)}, u32[]{:S(2)}, u32[]{:S(2)}) %all-to-all-start) | async-done | bytes 786464 | tf_op jit(solution)/shard_map/all_to_all | solution.py:188
  43.2 2.3 fusion.23
  45.6 0.9 fusion.7
  46.6 1.8 add_convert_fusion
  48.5 3.7 %all-to-all-start.1 = ((bf16[16,32,768]{2,1,0:T(8,128)(2,1)}), bf16[16,32,768]{2,1,0:T(8,128)(2,1)S(1)}, u32[]{:S(2)}, u32[]{:S(2)}) async-start(bf16[16,32,768]{2,1,0:T(8,128)(2,1)} %bitcast.5), calls=%async_computation.1 | async-start | bytes 1572864 | tf_op jit(solution)/shard_map/all_to_all | solution.py:188
  52.3 10.5 %all-to-all-done.1 = bf16[16,32,768]{2,1,0:T(8,128)(2,1)S(1)} async-done(((bf16[16,32,768]{2,1,0:T(8,128)(2,1)}), bf16[16,32,768]{2,1,0:T(8,128)(2,1)S(1)}, u32[]{:S(2)}, u32[]{:S(2)}) %all-to-all-start.1) | async-done | bytes 786464 | tf_op jit(solution)/shard_map/all_to_all | solution.py:188
  62.8 1.5 fusion.22
  64.3 29.3 %all_to_all.20.moved_ref = bf16[8,48,768]{2,1,0:T(8,128)(2,1)S(1)} all-to-all(bf16[8,48,768]{2,1,0:T(8,128)(2,1)S(1)} %pad_maximum_fusion.2), channel_id=1, replica_groups=mesh['row'=16,'col'=8] {'col'}, dimensions={0} | all-to-all | bytes 1179648 | tf_op jit(solution)/shard_map/all_to_all | solution.py:188
  93.6 0.3 shard_map.118
  93.9 0.6 collective-permute-start.2
  94.5 0.9 collective-permute-start.1
  95.4 0.6 collective-permute-start
  96.0 1.5 collective-permute-start.8
  97.5 1.2 collective-permute-start.7
  98.7 2.3 collective-permute-done.2
  101.0 0.3 collective-permute-start.6
  101.4 2.3 collective-permute-done.1
  103.7 2.9 collective-permute-done
  106.7 0.4 collective-permute-start.3
  107.2 2.3 collective-permute-start.4
  109.7 2.7 collective-permute-start.10
  112.4 31.4 %collective-permute-done.3.refs_1_ = bf16[4,16,6144]{2,1,0:T(8,128)(2,1)S(1)} collective-permute-done((bf16[4,16,6144]{2,1,0:T(8,128)(2,1)S(1)}, bf16[4,16,6144]{2,1,0:T(8,128)(2,1)S(1)}, u32[]{:S(2)}, u32[]{:S(2)}) %collective-permute-start.3) | collective-permute-done | bytes 786464 | tf_op jit(solution)/shard_map/ppermute | solution.py:48
  143.8 0.9 copy-done
  144.7 0.9 copy-done.2
  145.6 0.9 copy-done.4
  146.5 16.7 %collective-permute-done.11.refs_7_ = bf16[4,16,6144]{2,1,0:T(8,128)(2,1)S(1)} collective-permute-done((bf16[4,16,6144]{2,1,0:T(8,128)(2,1)S(1)}, bf16[4,16,6144]{2,1,0:T(8,128)(2,1)S(1)}, u32[]{:S(2)}, u32[]{:S(2)}) %collective-permute-start.11) | collective-permute-done | bytes 786464 | tf_op jit(solution)/shard_map/ppermute | solution.py:48
  163.2 0.9 copy-done.6
  164.1 1.1 copy-done.1
  165.3 1.1 copy-done.3
  166.4 1.1 copy-done.5
  167.5 1.1 copy-done.7
  168.7 13.4 %shard_map.119.h_ref = bf16[512,1536]{1,0:T(8,128)(2,1)S(1)} custom-call(bf16[4,16,6144]{2,1,0:T(8,128)(2,1)S(1)} %pad_maximum_fusion.refs_0_, bf16[4,16,6144]{2,1,0:T(8,128)(2,1)S(1)} %collective-permute-done.3.refs_1_, bf16[4,16,6144]{2,1,0:T(8,128)(2,1)S(1)} %collective-permute-done.4.refs_2_, bf16[4,16,6144]{2,1,0:T(8,128)(2,1)S(1)} %copy-done.1, ...), custom_call_target="tpu_custom_call" | custom-call | flops 9663676416 | bytes 25165824 | tf_op jit(solution)/shard_map/pallas_call | solution.py:98
  182.1 1.1 copy-done.8
  183.3 25.7 %all-gather.6.cloned.1.call-done = bf16[12288,768]{1,0:T(8,128)(2,1)} async-done(((bf16[1536,768]{1,0:T(8,128)(2,1)}), bf16[12288,768]{1,0:T(8,128)(2,1)}) %all-gather.6.cloned.1.call-update) | async-done | bytes 18874384 | tf_op jit(solution)/shard_map/all_gather | solution.py:238
  208.9 1.4 copy-done.9
  210.3 14.1 %shard_map.120 = (bf16[4,16,6144]{2,1,0:T(8,128)(2,1)S(1)}, bf16[4,16,6144]{2,1,0:T(8,128)(2,1)S(1)}, bf16[4,16,6144]{2,1,0:T(8,128)(2,1)S(1)}, bf16[4,16,6144]{...) custom-call(bf16[512,1536]{1,0:T(8,128)(2,1)S(1)} %copy-done.9, ...), custom_call_target="tpu_custom_call" | custom-call | flops 9663676416 | bytes 26738688 | tf_op jit(solution)/shard_map/pallas_call | solution.py:129
  224.4 2.5 collective-permute-start.12
  227.0 1.7 collective-permute-start.14
  228.7 2.7 collective-permute-start.18
  231.4 29.0 %collective-permute-done.12.b = bf16[4,16,6144]{2,1,0:T(8,128)(2,1)S(1)} collective-permute-done((bf16[4,16,6144]{2,1,0:T(8,128)(2,1)S(1)}, bf16[4,16,6144]{2,1,0:T(8,128)(2,1)S(1)}, u32[]{:S(2)}, u32[]{:S(2)}) %collective-permute-start.12) | collective-permute-done | bytes 786464 | tf_op jit(solution)/shard_map/ppermute | solution.py:48
  260.4 2.9 collective-permute-start.20
  263.2 0.8 shard_map.121
  264.0 2.2 collective-permute-start.15
  266.2 1.7 collective-permute-start.17
  267.9 11.8 %collective-permute-done.20.d = bf16[4,16,6144]{2,1,0:T(8,128)(2,1)S(1)} collective-permute-done((bf16[4,16,6144]{2,1,0:T(8,128)(2,1)S(1)}, bf16[4,16,6144]{2,1,0:T(8,128)(2,1)S(1)}, u32[]{:S(2)}, u32[]{:S(2)}) %collective-permute-start.20) | collective-permute-done | bytes 786464 | tf_op jit(solution)/shard_map/ppermute | solution.py:48
  279.7 0.8 shard_map.122
  280.5 3.8 %collective-permute-start.21 = (bf16[16,6144]{1,0:T(8,128)(2,1)S(1)}, bf16[16,6144]{1,0:T(8,128)(2,1)S(1)}, u32[]{:S(2)}, u32[]{:S(2)}) collective-permute-start(bf16[16,6144]{1,0:T(8,128)(2,1)S(1)} %get-tuple-element.38), channel_id=1, source_target_pairs={{0,24},{8,0},{16,8},{24,16},{32,56},{40,32},{48,40},{56,48},{64,88... | collective-permute-start | bytes 589832 | tf_op jit(solution)/shard_map/ppermute | solution.py:48
  284.3 1.6 collective-permute-done.15.b
  285.9 1.2 collective-permute-done.16.c
  287.2 1.0 collective-permute-done.17.d
  288.1 2.8 collective-permute-done.22.g
  290.9 2.4 collective-permute-done.23.h
  293.4 0.6 shard_map.123
  294.0 16.0 %all_to_all.21 = bf16[8,32,768]{2,1,0:T(8,128)(2,1)S(1)} all-to-all(bf16[8,32,768]{2,1,0:T(8,128)(2,1)S(1)} %shard_map.123), channel_id=1, replica_groups=mesh['row'=16,'col'=8] {'col'}, dimensions={0} | all-to-all | bytes 786432 | tf_op jit(solution)/shard_map/all_to_all | solution.py:188
  309.9 0.9 fusion.1
  (67 shorter events, 1.2 us)
Async XLA Ops:
  6.5 157.6 %all-gather.4.cloned.1.call-start = ((), (), s32[]{:S(2)}) async-start(), calls=%async_computation.4 | async-start | bytes 21233664 | tf_op jit(solution)/shard_map/all_gather | solution.py:237
  7.3 1.0 copy-start.10
  7.3 14.5 %copy-start.17 = (f32[768]{0:T(1024)S(1)}, f32[768]{0:T(1024)}, u32[]{:S(2)}) copy-start(f32[768]{0:T(1024)} %param.14) | copy-start | bytes 9220
  7.3 14.7 %copy-start.15 = (f32[512,256]{1,0:T(8,128)S(1)}, f32[512,256]{1,0:T(8,128)}, u32[]{:S(2)}) copy-start(f32[512,256]{1,0:T(8,128)} %constant.19.clone) | copy-start | bytes 1572868
  7.3 201.6 %all-gather.6.cloned.1.call-start = ((), (), s32[]{:S(2)}) async-start(), calls=%async_computation.5 | async-start | bytes 21233664 | tf_op jit(solution)/shard_map/all_gather | solution.py:238
  23.7 19.6 %all-to-all-start = ((bf16[16,32,768]{2,1,0:T(8,128)(2,1)}), bf16[16,32,768]{2,1,0:T(8,128)(2,1)S(1)}, u32[]{:S(2)}, u32[]{:S(2)}) async-start(bf16[16,32,768]{2,1,0:T(8,128)(2,1)} %bitcast.2), calls=%async_computation | async-start | bytes 1572864 | tf_op jit(solution)/shard_map/all_to_all | solution.py:188
  43.2 2.3 copy-start.13
  45.6 1.0 copy-start.12
  48.4 3.8 %copy-start.19 = (f32[768]{0:T(1024)S(1)}, f32[768]{0:T(1024)}, u32[]{:S(2)}) copy-start(f32[768]{0:T(1024)} %param.15) | copy-start | bytes 9220
  48.5 14.3 %copy-start.14 = (f32[256,512]{1,0:T(8,128)S(1)}, f32[256,512]{1,0:T(8,128)}, u32[]{:S(2)}) copy-start(f32[256,512]{1,0:T(8,128)} %constant.22.clone) | copy-start | bytes 1572868
  48.5 14.3 %all-to-all-start.1 = ((bf16[16,32,768]{2,1,0:T(8,128)(2,1)}), bf16[16,32,768]{2,1,0:T(8,128)(2,1)S(1)}, u32[]{:S(2)}, u32[]{:S(2)}) async-start(bf16[16,32,768]{2,1,0:T(8,128)(2,1)} %bitcast.5), calls=%async_computation.1 | async-start | bytes 1572864 | tf_op jit(solution)/shard_map/all_to_all | solution.py:188
  93.9 7.1 %collective-permute-start.2 = (bf16[16,6144]{1,0:T(8,128)(2,1)S(1)}, bf16[16,6144]{1,0:T(8,128)(2,1)S(1)}, u32[]{:S(2)}, u32[]{:S(2)}) collective-permute-start(bf16[16,6144]{1,0:T(8,128)(2,1)S(1)} %get-tuple-element.23), channel_id=1, source_target_pairs={{0,64},{8,72},{16,80},{24,88},{32,96},{40,104},{48,112},{56,120},{... | collective-permute-start | bytes 589832 | tf_op jit(solution)/shard_map/ppermute | solution.py:48
  94.5 9.2 %collective-permute-start.1 = (bf16[16,6144]{1,0:T(8,128)(2,1)S(1)}, bf16[16,6144]{1,0:T(8,128)(2,1)S(1)}, u32[]{:S(2)}, u32[]{:S(2)}) collective-permute-start(bf16[16,6144]{1,0:T(8,128)(2,1)S(1)} %get-tuple-element.23), channel_id=1, source_target_pairs={{0,96},{8,104},{16,112},{24,120},{32,0},{40,8},{48,16},{56,24},{64... | collective-permute-start | bytes 589832 | tf_op jit(solution)/shard_map/ppermute | solution.py:48
  95.4 11.2 %collective-permute-start = (bf16[16,6144]{1,0:T(8,128)(2,1)S(1)}, bf16[16,6144]{1,0:T(8,128)(2,1)S(1)}, u32[]{:S(2)}, u32[]{:S(2)}) collective-permute-start(bf16[16,6144]{1,0:T(8,128)(2,1)S(1)} %get-tuple-element.23), channel_id=1, source_target_pairs={{0,32},{8,40},{16,48},{24,56},{32,64},{40,72},{48,80},{56,88},{64,... | collective-permute-start | bytes 589832 | tf_op jit(solution)/shard_map/ppermute | solution.py:48
  96.0 13.5 %collective-permute-start.8 = (bf16[16,6144]{1,0:T(8,128)(2,1)S(1)}, bf16[16,6144]{1,0:T(8,128)(2,1)S(1)}, u32[]{:S(2)}, u32[]{:S(2)}) collective-permute-start(bf16[16,6144]{1,0:T(8,128)(2,1)S(1)} %get-tuple-element.24), channel_id=1, source_target_pairs={{0,16},{8,24},{16,0},{24,8},{32,48},{40,56},{48,32},{56,40},{64,80... | collective-permute-start | bytes 589832 | tf_op jit(solution)/shard_map/ppermute | solution.py:48
  97.5 12.0 %collective-permute-start.7 = (bf16[16,6144]{1,0:T(8,128)(2,1)S(1)}, bf16[16,6144]{1,0:T(8,128)(2,1)S(1)}, u32[]{:S(2)}, u32[]{:S(2)}) collective-permute-start(bf16[16,6144]{1,0:T(8,128)(2,1)S(1)} %get-tuple-element.24), channel_id=1, source_target_pairs={{0,24},{8,0},{16,8},{24,16},{32,56},{40,32},{48,40},{56,48},{64,88... | collective-permute-start | bytes 589832 | tf_op jit(solution)/shard_map/ppermute | solution.py:48
  101.0 8.5 %collective-permute-start.6 = (bf16[16,6144]{1,0:T(8,128)(2,1)S(1)}, bf16[16,6144]{1,0:T(8,128)(2,1)S(1)}, u32[]{:S(2)}, u32[]{:S(2)}) collective-permute-start(bf16[16,6144]{1,0:T(8,128)(2,1)S(1)} %get-tuple-element.24), channel_id=1, source_target_pairs={{0,8},{8,16},{16,24},{24,0},{32,40},{40,48},{48,56},{56,32},{64,72... | collective-permute-start | bytes 589832 | tf_op jit(solution)/shard_map/ppermute | solution.py:48
  106.6 37.1 %copy-start.16 = (f32[1536]{0:T(1024)S(1)}, f32[1536]{0:T(1024)}, u32[]{:S(2)}) copy-start(f32[1536]{0:T(1024)} %param.17) | copy-start | bytes 18436
  106.7 37.0 %collective-permute-start.3 = (bf16[4,16,6144]{2,1,0:T(8,128)(2,1)S(1)}, bf16[4,16,6144]{2,1,0:T(8,128)(2,1)S(1)}, u32[]{:S(2)}, u32[]{:S(2)}) collective-permute-start(bf16[4,16,6144]{2,1,0:T(8,128)(2,1)S(1)} %pad_maximum_fusion.refs_0_), channel_id=1, source_target_pairs={{0,8},{8,16},{16,24},{24,0},{32,40},{40,48},{48,56},{56,32},{64,72... | collective-permute-start | bytes 2359304 | tf_op jit(solution)/shard_map/ppermute | solution.py:48
  107.2 36.6 %collective-permute-start.4 = (bf16[4,16,6144]{2,1,0:T(8,128)(2,1)S(1)}, bf16[4,16,6144]{2,1,0:T(8,128)(2,1)S(1)}, u32[]{:S(2)}, u32[]{:S(2)}) collective-permute-start(bf16[4,16,6144]{2,1,0:T(8,128)(2,1)S(1)} %pad_maximum_fusion.refs_0_), channel_id=1, source_target_pairs={{0,24},{8,0},{16,8},{24,16},{32,56},{40,32},{48,40},{56,48},{64,88... | collective-permute-start | bytes 2359304 | tf_op jit(solution)/shard_map/ppermute | solution.py:48
  109.5 34.3 %collective-permute-start.5 = (bf16[4,16,6144]{2,1,0:T(8,128)(2,1)S(1)}, bf16[4,16,6144]{2,1,0:T(8,128)(2,1)S(1)}, u32[]{:S(2)}, u32[]{:S(2)}) collective-permute-start(bf16[4,16,6144]{2,1,0:T(8,128)(2,1)S(1)} %pad_maximum_fusion.refs_0_), channel_id=1, source_target_pairs={{0,16},{8,24},{16,0},{24,8},{32,48},{40,56},{48,32},{56,40},{64,80... | collective-permute-start | bytes 2359304 | tf_op jit(solution)/shard_map/ppermute | solution.py:48
  109.6 35.1 %collective-permute-start.9 = (bf16[4,16,6144]{2,1,0:T(8,128)(2,1)S(1)}, bf16[4,16,6144]{2,1,0:T(8,128)(2,1)S(1)}, u32[]{:S(2)}, u32[]{:S(2)}) collective-permute-start(bf16[4,16,6144]{2,1,0:T(8,128)(2,1)S(1)} %pad_maximum_fusion.1.refs_4_), channel_id=1, source_target_pairs={{0,32},{8,40},{16,48},{24,56},{32,64},{40,72},{48,80},{56,88},{64,... | collective-permute-start | bytes 2359304 | tf_op jit(solution)/shard_map/ppermute | solution.py:48
  109.7 35.9 %collective-permute-start.10 = (bf16[4,16,6144]{2,1,0:T(8,128)(2,1)S(1)}, bf16[4,16,6144]{2,1,0:T(8,128)(2,1)S(1)}, u32[]{:S(2)}, u32[]{:S(2)}) collective-permute-start(bf16[4,16,6144]{2,1,0:T(8,128)(2,1)S(1)} %pad_maximum_fusion.1.refs_4_), channel_id=1, source_target_pairs={{0,96},{8,104},{16,112},{24,120},{32,0},{40,8},{48,16},{56,24},{64... | collective-permute-start | bytes 2359304 | tf_op jit(solution)/shard_map/ppermute | solution.py:48
  143.8 19.4 %collective-permute-start.11 = (bf16[4,16,6144]{2,1,0:T(8,128)(2,1)S(1)}, bf16[4,16,6144]{2,1,0:T(8,128)(2,1)S(1)}, u32[]{:S(2)}, u32[]{:S(2)}) collective-permute-start(bf16[4,16,6144]{2,1,0:T(8,128)(2,1)S(1)} %pad_maximum_fusion.1.refs_4_), channel_id=1, source_target_pairs={{0,64},{8,72},{16,80},{24,88},{32,96},{40,104},{48,112},{56,120},{... | collective-permute-start | bytes 2359304 | tf_op jit(solution)/shard_map/ppermute | solution.py:48
  143.8 0.9 copy-start
  144.7 0.9 copy-start.2
  145.6 0.9 copy-start.4
  163.2 0.9 copy-start.6
  164.1 1.1 copy-start.1
  165.3 1.1 copy-start.3
  166.4 1.1 copy-start.5
  167.5 1.1 copy-start.7
  182.1 1.1 copy-start.8
  208.9 1.4 copy-start.9
  224.4 35.9 %collective-permute-start.12 = (bf16[4,16,6144]{2,1,0:T(8,128)(2,1)S(1)}, bf16[4,16,6144]{2,1,0:T(8,128)(2,1)S(1)}, u32[]{:S(2)}, u32[]{:S(2)}) collective-permute-start(bf16[4,16,6144]{2,1,0:T(8,128)(2,1)S(1)} %get-tuple-element.26), channel_id=1, source_target_pairs={{0,24},{8,0},{16,8},{24,16},{32,56},{40,32},{48,40},{56,48},{64,88... | collective-permute-start | bytes 2359304 | tf_op jit(solution)/shard_map/ppermute | solution.py:48
  227.0 36.3 %collective-permute-start.13 = (bf16[4,16,6144]{2,1,0:T(8,128)(2,1)S(1)}, bf16[4,16,6144]{2,1,0:T(8,128)(2,1)S(1)}, u32[]{:S(2)}, u32[]{:S(2)}) collective-permute-start(bf16[4,16,6144]{2,1,0:T(8,128)(2,1)S(1)} %get-tuple-element.27), channel_id=1, source_target_pairs={{0,8},{8,16},{16,24},{24,0},{32,40},{40,48},{48,56},{56,32},{64,72... | collective-permute-start | bytes 2359304 | tf_op jit(solution)/shard_map/ppermute | solution.py:48
  227.0 36.3 %collective-permute-start.14 = (bf16[4,16,6144]{2,1,0:T(8,128)(2,1)S(1)}, bf16[4,16,6144]{2,1,0:T(8,128)(2,1)S(1)}, u32[]{:S(2)}, u32[]{:S(2)}) collective-permute-start(bf16[4,16,6144]{2,1,0:T(8,128)(2,1)S(1)} %get-tuple-element.28), channel_id=1, source_target_pairs={{0,16},{8,24},{16,0},{24,8},{32,48},{40,56},{48,32},{56,40},{64,80... | collective-permute-start | bytes 2359304 | tf_op jit(solution)/shard_map/ppermute | solution.py:48
  228.7 37.5 %collective-permute-start.18 = (bf16[4,16,6144]{2,1,0:T(8,128)(2,1)S(1)}, bf16[4,16,6144]{2,1,0:T(8,128)(2,1)S(1)}, u32[]{:S(2)}, u32[]{:S(2)}) collective-permute-start(bf16[4,16,6144]{2,1,0:T(8,128)(2,1)S(1)} %get-tuple-element.34), channel_id=1, source_target_pairs={{0,96},{8,104},{16,112},{24,120},{32,0},{40,8},{48,16},{56,24},{64... | collective-permute-start | bytes 2359304 | tf_op jit(solution)/shard_map/ppermute | solution.py:48
  231.4 36.5 %collective-permute-start.19 = (bf16[4,16,6144]{2,1,0:T(8,128)(2,1)S(1)}, bf16[4,16,6144]{2,1,0:T(8,128)(2,1)S(1)}, u32[]{:S(2)}, u32[]{:S(2)}) collective-permute-start(bf16[4,16,6144]{2,1,0:T(8,128)(2,1)S(1)} %get-tuple-element.35), channel_id=1, source_target_pairs={{0,32},{8,40},{16,48},{24,56},{32,64},{40,72},{48,80},{56,88},{64,... | collective-permute-start | bytes 2359304 | tf_op jit(solution)/shard_map/ppermute | solution.py:48
  260.4 19.3 %collective-permute-start.20 = (bf16[4,16,6144]{2,1,0:T(8,128)(2,1)S(1)}, bf16[4,16,6144]{2,1,0:T(8,128)(2,1)S(1)}, u32[]{:S(2)}, u32[]{:S(2)}) collective-permute-start(bf16[4,16,6144]{2,1,0:T(8,128)(2,1)S(1)} %get-tuple-element.36), channel_id=1, source_target_pairs={{0,64},{8,72},{16,80},{24,88},{32,96},{40,104},{48,112},{56,120},{... | collective-permute-start | bytes 2359304 | tf_op jit(solution)/shard_map/ppermute | solution.py:48
  264.0 21.9 %collective-permute-start.15 = (bf16[16,6144]{1,0:T(8,128)(2,1)S(1)}, bf16[16,6144]{1,0:T(8,128)(2,1)S(1)}, u32[]{:S(2)}, u32[]{:S(2)}) collective-permute-start(bf16[16,6144]{1,0:T(8,128)(2,1)S(1)} %get-tuple-element.30), channel_id=1, source_target_pairs={{0,96},{8,104},{16,112},{24,120},{32,0},{40,8},{48,16},{56,24},{64... | collective-permute-start | bytes 589832 | tf_op jit(solution)/shard_map/ppermute | solution.py:48
  266.2 20.9 %collective-permute-start.16 = (bf16[16,6144]{1,0:T(8,128)(2,1)S(1)}, bf16[16,6144]{1,0:T(8,128)(2,1)S(1)}, u32[]{:S(2)}, u32[]{:S(2)}) collective-permute-start(bf16[16,6144]{1,0:T(8,128)(2,1)S(1)} %get-tuple-element.31), channel_id=1, source_target_pairs={{0,32},{8,40},{16,48},{24,56},{32,64},{40,72},{48,80},{56,88},{64,... | collective-permute-start | bytes 589832 | tf_op jit(solution)/shard_map/ppermute | solution.py:48
  266.2 21.9 %collective-permute-start.17 = (bf16[16,6144]{1,0:T(8,128)(2,1)S(1)}, bf16[16,6144]{1,0:T(8,128)(2,1)S(1)}, u32[]{:S(2)}, u32[]{:S(2)}) collective-permute-start(bf16[16,6144]{1,0:T(8,128)(2,1)S(1)} %get-tuple-element.32), channel_id=1, source_target_pairs={{0,64},{8,72},{16,80},{24,88},{32,96},{40,104},{48,112},{56,120},{... | collective-permute-start | bytes 589832 | tf_op jit(solution)/shard_map/ppermute | solution.py:48
  280.5 29.4 %copy-start.11 = (f32[256,768]{1,0:T(8,128)S(1)}, f32[256,768]{1,0:T(8,128)}, u32[]{:S(2)}) copy-start(f32[256,768]{1,0:T(8,128)} %get-tuple-element.53) | copy-start | bytes 2359300
  280.5 29.4 %copy-start.18 = (f32[768]{0:T(1024)S(1)}, f32[768]{0:T(1024)}, u32[]{:S(2)}) copy-start(f32[768]{0:T(1024)} %param.19) | copy-start | bytes 9220
  280.5 7.6 %collective-permute-start.21 = (bf16[16,6144]{1,0:T(8,128)(2,1)S(1)}, bf16[16,6144]{1,0:T(8,128)(2,1)S(1)}, u32[]{:S(2)}, u32[]{:S(2)}) collective-permute-start(bf16[16,6144]{1,0:T(8,128)(2,1)S(1)} %get-tuple-element.38), channel_id=1, source_target_pairs={{0,24},{8,0},{16,8},{24,16},{32,56},{40,32},{48,40},{56,48},{64,88... | collective-permute-start | bytes 589832 | tf_op jit(solution)/shard_map/ppermute | solution.py:48
  284.3 6.6 %collective-permute-start.22 = (bf16[16,6144]{1,0:T(8,128)(2,1)S(1)}, bf16[16,6144]{1,0:T(8,128)(2,1)S(1)}, u32[]{:S(2)}, u32[]{:S(2)}) collective-permute-start(bf16[16,6144]{1,0:T(8,128)(2,1)S(1)} %get-tuple-element.39), channel_id=1, source_target_pairs={{0,8},{8,16},{16,24},{24,0},{32,40},{40,48},{48,56},{56,32},{64,72... | collective-permute-start | bytes 589832 | tf_op jit(solution)/shard_map/ppermute | solution.py:48
  285.9 7.4 %collective-permute-start.23 = (bf16[16,6144]{1,0:T(8,128)(2,1)S(1)}, bf16[16,6144]{1,0:T(8,128)(2,1)S(1)}, u32[]{:S(2)}, u32[]{:S(2)}) collective-permute-start(bf16[16,6144]{1,0:T(8,128)(2,1)S(1)} %get-tuple-element.40), channel_id=1, source_target_pairs={{0,16},{8,24},{16,0},{24,8},{32,48},{40,56},{48,32},{56,40},{64,80... | collective-permute-start | bytes 589832 | tf_op jit(solution)/shard_map/ppermute | solution.py:48
Sparse Core Ops, SparseCore 0:
  9.0 103.6 all-gather.3
  114.4 94.4 all-gather.5

commit v2 on v1

--- a/solution.py
+++ b/solution.py
@@ -48,6 +48,14 @@
     return lax.ppermute(a, "row", pairs)
 
 
+def shift_col(a, dx, dc):
+    pairs = []
+    for x in range(SIDE):
+        for core in range(2):
+            pairs.append((x * 2 + core, (x + dx) % SIDE * 2 + (core ^ dc)))
+    return lax.ppermute(a, "col", pairs)
+
+
 def along(a, axis, step):
     return shift_row(a, step, 0) if axis == "z" else shift_row(a, 0, step)
 
@@ -56,76 +64,80 @@
     return pltpu.CompilerParams(vmem_limit_bytes=mb * MB)
 
 
-def act_kernel(moved_ref, first_ref, second_ref):
-    cols, rows, chans = moved_ref.shape
+def act_kernel(order_ref, moved_ref, gain_ref, first_ref, second_ref):
+    cols, _, chans = moved_ref.shape
     half = first_ref.shape[0]
-    values = moved_ref[:, : 2 * half, :].astype(F32)
-    gains = jnp.sum(moved_ref[:, 2 * half :, :].astype(F32)[:, :3], axis=1)
+    values = moved_ref[...].astype(F32)
     mean = jnp.sum(jnp.sum(values, axis=0), axis=-1, keepdims=True) / (cols * chans)
     square = jnp.sum(jnp.sum(values * values, axis=0), axis=-1, keepdims=True) / (cols * chans)
     scale = 1.0 / jnp.sqrt(square - mean * mean + 1e-05)
     for j in range(cols):
-        part = ((values[j] - mean) * scale * gains[j][None, :]).astype(BF)
+        at = order_ref[j]
+        part = (moved_ref[at].astype(F32) - mean) * scale * gain_ref[at, :1, :]
+        part = part.astype(BF)
         first_ref[:, j * chans : (j + 1) * chans] = part[:half]
         second_ref[:, j * chans : (j + 1) * chans] = part[half:]
 
 
-def normalize(moved, half):
+def normalize(order, moved, gains, half):
     cols, _, chans = moved.shape
     shape = jax.ShapeDtypeStruct((half, cols * chans), BF)
-    return pl.pallas_call(act_kernel, out_shape=(shape, shape), compiler_params=params(16))(moved)
-
-
-def mm1_kernel(block, *refs):
-    pieces, (w_ref, b_ref, o_ref) = refs[:-3], refs[-3:]
-    depth = w_ref.shape[0]
+    return pl.pallas_call(
+        act_kernel,
+        in_specs=[pl.BlockSpec(memory_space=pltpu.SMEM)] + [pl.BlockSpec(memory_space=pltpu.VMEM)] * 2,
+        out_shape=(shape, shape),
+        compiler_params=params(16),
+    )(order, moved, gains)
+
+
+def mm1_kernel(count, block, *refs):
+    pieces, weights, (b_ref, o_ref) = refs[:count], refs[count:-2], refs[-2:]
     total = None
-    for at in range(0, depth, block):
-        left = jnp.concatenate(
-            [p[:, :, at : at + block].reshape(-1, block) for p in pieces], axis=0
-        )
-        term = jnp.dot(left, w_ref[at : at + block, :], preferred_element_type=F32)
+    at = 0
+    for w_ref in weights:
+        size = w_ref.shape[0]
+        left = jnp.concatenate([p[:, :, at : at + size].reshape(-1, size) for p in pieces], axis=0)
+        term = jnp.dot(left, w_ref[...], preferred_element_type=F32)
         total = term if total is None else total + term
+        at += size
     pre = total + b_ref[...]
     o_ref[...] = (0.5 * pre * (1.0 + lax.erf(pre * math.sqrt(0.5)))).astype(BF)
 
 
-def matmul_in(pieces, w, b):
-    depth, width = w.shape
-    shape = pieces[0].shape
-    tokens = len(pieces) * shape[0] * shape[1]
+def matmul_in(pieces, weights, b):
+    width = weights[0].shape[1]
+    depth = pieces[0].shape[2]
+    tokens = sum(p.shape[0] * p.shape[1] for p in pieces)
     tile = 256
     return pl.pallas_call(
-        functools.partial(mm1_kernel, 768),
+        functools.partial(mm1_kernel, len(pieces), 768),
         grid=(width // tile,),
-        in_specs=[pl.BlockSpec(shape, lambda i: (0, 0, 0)) for _ in pieces]
-        + [
-            pl.BlockSpec((depth, tile), lambda i: (0, i)),
-            pl.BlockSpec((1, tile), lambda i: (0, i)),
-        ],
+        in_specs=[pl.BlockSpec(p.shape, lambda i: (0, 0, 0)) for p in pieces]
+        + [pl.BlockSpec((w.shape[0], tile), lambda i: (0, i)) for w in weights]
+        + [pl.BlockSpec((1, tile), lambda i: (0, i))],
         out_specs=pl.BlockSpec((tokens, tile), lambda i: (0, i)),
         out_shape=jax.ShapeDtypeStruct((tokens, width), BF),
-        compiler_params=params(40),
+        compiler_params=params(62),
         cost_estimate=pl.CostEstimate(
             flops=2 * tokens * depth * width,
             bytes_accessed=2 * (tokens * depth + depth * width),
             transcendentals=0,
         ),
-    )(*pieces, w, b[None])
+    )(*pieces, *weights, b[None])
 
 
 def mm2_kernel(h_ref, w_ref, *outs):
     out = jnp.dot(h_ref[...], w_ref[0], preferred_element_type=F32)
-    shape = outs[0].shape
-    rows = shape[0] * shape[1]
-    for i, o_ref in enumerate(outs):
-        o_ref[...] = out[i * rows : (i + 1) * rows].astype(BF).reshape(shape)
-
-
-def matmul_out(hidden, w, half):
+    at = 0
+    for o_ref in outs:
+        rows = o_ref.shape[0] * o_ref.shape[1]
+        o_ref[...] = out[at : at + rows].astype(BF).reshape(o_ref.shape)
+        at += rows
+
+
+def matmul_out(hidden, w, shapes):
     cols, depth, chans = w.shape
     tokens = hidden.shape[0]
-    count = tokens // (SIDE * half)
     return pl.pallas_call(
         mm2_kernel,
         grid=(cols,),
@@ -133,9 +145,9 @@
             pl.BlockSpec((tokens, depth), lambda j: (0, 0)),
             pl.BlockSpec((1, depth, chans), lambda j: (j, 0, 0)),
         ],
-        out_specs=[pl.BlockSpec((SIDE, half, chans), lambda j: (0, 0, j))] * count,
-        out_shape=[jax.ShapeDtypeStruct((SIDE, half, cols * chans), BF)] * count,
-        compiler_params=params(40),
+        out_specs=[pl.BlockSpec(s[:2] + (chans,), lambda j: (0, 0, j)) for s in shapes],
+        out_shape=[jax.ShapeDtypeStruct(s, BF) for s in shapes],
+        compiler_params=params(62),
         cost_estimate=pl.CostEstimate(
             flops=2 * tokens * depth * cols * chans,
             bytes_accessed=2 * (tokens * depth + depth * cols * chans + tokens * cols * chans),
@@ -144,8 +156,30 @@
     )(hidden, w)
 
 
-def add_kernel(a, b, c, d, *outs):
-    total = (a[...].astype(F32) + b[...].astype(F32)) + (c[...].astype(F32) + d[...].astype(F32))
+def merge_kernel(l1, r1, l2, r2, low1, top1, low2, top2, ol1, or1, ol2, or2):
+    for a, b, o in ((l1, low1, ol1), (r1, top1, or1), (l2, low2, ol2), (r2, top2, or2)):
+        o[...] = (a[...].astype(F32) + b[...].astype(F32)).astype(BF)
+
+
+def merge(left1, right1, left2, right2, low1, top1, low2, top2):
+    count, half, width = left1.shape
+    tile = width // 4
+    block = (count // 2, half, tile)
+    low = pl.BlockSpec(block, lambda j: (1, 0, j))
+    top = pl.BlockSpec(block, lambda j: (0, 0, j))
+    return pl.pallas_call(
+        merge_kernel,
+        grid=(width // tile,),
+        in_specs=[low, top, low, top, top, top, top, top],
+        out_specs=[low, top, low, top],
+        out_shape=[jax.ShapeDtypeStruct(left1.shape, BF)] * 4,
+        input_output_aliases={0: 0, 1: 1, 2: 2, 3: 3},
+        compiler_params=params(16),
+    )(left1, right1, left2, right2, low1, top1, low2, top2)
+
+
+def add_kernel(a, b, c, *outs):
+    total = a[...].astype(F32) + (b[...].astype(F32) + c[...].astype(F32))
     for i, o_ref in enumerate(outs):
         o_ref[...] = total[i].astype(BF)
 
@@ -188,7 +222,24 @@
     return lax.all_to_all(a, axis, split_axis=0, concat_axis=0, tiled=True)
 
 
-def spectral(image, filter_bank, gain_first):
+def tie_kernel(*refs):
+    pass
+
+
+def tie(values, others):
+    count = len(values)
+    anywhere = pl.BlockSpec(memory_space=pl.ANY)
+    return pl.pallas_call(
+        tie_kernel,
+        in_specs=[anywhere] * (count + len(others)),
+        out_specs=[anywhere] * count,
+        out_shape=[jax.ShapeDtypeStruct(v.shape, v.dtype) for v in values],
+        input_output_aliases={i: i for i in range(count)},
+        compiler_params=params(62),
+    )(*values, *others)
+
+
+def spectral(image, filter_bank, gain_first, early, late):
     rows_here, width, chans = image.shape
     groups = lax.axis_size("row")
     width_all = chans * lax.axis_size("col")
@@ -204,6 +255,7 @@
     normed = (source - mean) / jnp.sqrt(square - mean * mean + 1e-05) * gain_first
     col = jnp.dot(one, normed, precision=high).astype(BF)
     col = exchange(col.reshape(groups, -1, chans), "row").reshape(-1, chans)
+    col, *early = tie([col, *early], [])
     spec = jnp.dot(two, col.astype(F32), precision=high)
     split = spec.shape[0] // 2
     spec_re, spec_im = spec[:split], spec[split:]
@@ -213,18 +265,28 @@
     )
     back = jnp.dot(three, filt, precision=high).astype(BF)
     back = exchange(back.reshape(groups, -1, chans), "row").reshape(-1, chans)
-    return source + jnp.dot(four, back.astype(F32), precision=high)
-
-
-def three_parts(gain):
-    top = lax.reduce_precision(gain, 8, 7)
-    mid = lax.reduce_precision(gain - top, 8, 7)
-    return jnp.stack([top, mid, gain - top - mid]).astype(BF)
-
-
-def gather_two(a, axis_one, axis_two):
-    got = jnp.stack([a] + [along(a, axis_one, s) for s in (1, -1, 2)])
-    return [got] + [along(got, axis_two, s) for s in (1, -1, 2)]
+    back, *late = tie([back, *late], [])
+    return source + jnp.dot(four, back.astype(F32), precision=high), early, late
+
+
+def weight_order():
+    table = []
+    for x in range(SIDE):
+        for core in range(2):
+            steps = [((x + dx) % SIDE, core ^ other) for dx in (0, -1, 1, 2) for other in (0, 1)]
+            table.append([2 * at + c for at, c in steps])
+    return jnp.asarray(np.array(table, np.int32))[lax.axis_index("col")]
+
+
+def gather_near(a, axis):
+    return jnp.stack([a] + [along(a, axis, s) for s in (1, -1, 2)])
+
+
+def gather_far(a, axis, waits):
+    half = a.shape[0] // 2
+    left, right = along(a, axis, 1), along(a, axis, -1)
+    left, right = tie([left, right], waits)
+    return [a, left, right, along(left[:half], axis, 1), along(right[half:], axis, -1)]
 
 
 def send_back(parts, axis):
@@ -234,28 +296,47 @@
 def on_device(image, filter_bank, gain_first, gain_second, w_in, b_in, w_out, b_out):
     rows_here, width, chans = image.shape
     cols = lax.axis_size("col")
-    w_in_all = lax.all_gather(w_in, "col", axis=0, tiled=True)
+    padded = jnp.pad(gain_second[None], ((0, 63), (0, 0)))
+    gains = lax.all_gather(padded, "col", axis=0, tiled=False)
+    swap = functools.partial(shift_col, dx=0, dc=1)
+    w_half = w_in.shape[0] // 2
+    sibling = swap(w_in)
+    ends = [w_in[:w_half], w_in[w_half:]]
+    early, late = [[shift_col(end, 1, 0), shift_col(end, -1, 0)] for end in ends]
     w_out_all = lax.all_gather(w_out, "col", axis=0, tiled=False)
-    resid = spectral(image, filter_bank, gain_first)
+    resid, (up0, down0, sibling), (up1, down1) = spectral(
+        image, filter_bank, gain_first, early + [sibling], late
+    )
+    near = [up0, up1, down0, down1]
+    near_swap = [swap(part) for part in near]
+    far = [shift_col(up0, 1, 0), shift_col(down1, -1, 0)]
+    far_swap = [swap(part) for part in far]
+    weights = [w_in, sibling] + near[:2] + near_swap[:2] + near[2:] + near_swap[2:] + far + far_swap
     tokens = rows_here * width
     own = tokens // cols
     half = own // 2
-    extra = jnp.pad(three_parts(gain_second), ((0, half - 3), (0, 0)))
-    message = jnp.concatenate(
-        [
-            resid.astype(BF).reshape(cols, own, chans),
-            jnp.broadcast_to(extra[None], (cols, half, chans)),
-        ],
-        axis=1,
-    )
-    first, second = normalize(exchange(message, "col"), half)
-    pieces = gather_two(first, "z", "y") + gather_two(second, "y", "z")
-    hidden = matmul_in(pieces, w_in_all, b_in)
-    outs = matmul_out(hidden, w_out_all, half)
-    count = len(outs) // 2
-    first = send_back(add_pieces(send_back(outs[:count], "y")), "z")
-    second = send_back(add_pieces(send_back(outs[count:], "z")), "y")
-    proj = exchange(add_last(first, second, cols), "col")
+    moved = exchange(resid.astype(BF).reshape(cols, own, chans), "col")
+    (moved,) = tie([moved], near_swap)
+    first, second = normalize(weight_order(), moved, gains, half)
+    first, second = gather_near(first, "z"), gather_near(second, "y")
+    first, second = tie([first, second], far)
+    pieces = gather_far(first, "y", far_swap) + gather_far(second, "z", far_swap)
+    hidden = matmul_in(pieces, weights, b_in)
+    outs = matmul_out(hidden, w_out_all, [p.shape for p in pieces])
+    own1, left1, right1, top1, low1, own2, left2, right2, top2, low2 = outs
+    left1, right1, left2, right2 = merge(
+        left1,
+        right1,
+        left2,
+        right2,
+        along(low1, "y", -1),
+        along(top1, "y", 1),
+        along(low2, "z", -1),
+        along(top2, "z", 1),
+    )
+    first = add_pieces([own1, along(right1, "y", 1), along(left1, "y", -1)])
+    second = add_pieces([own2, along(right2, "z", 1), along(left2, "z", -1)])
+    proj = exchange(add_last(send_back(first, "z"), send_back(second, "y"), cols), "col")
     result = (resid + proj.reshape(tokens, chans).astype(F32) + b_out).astype(BF)
     return result.reshape(rows_here, width, chans)
 

time: 319 us -> 362 us (1.13)
  starting transfers between devices: 39.7 us -> 77.2 us
  waiting for transfers between devices: 153 us -> 136 us
  Pallas kernels: 30 us -> 40.2 us
  local copies, waits for them, and re-layouts: 13.2 us -> 20.7 us
    ppermute x24 -> x28, waiting for transfers between devices: 106 us -> 48.2 us  [shift_row(): return lax.ppermute(a, 'row', pairs)]
    all_to_all x2 -> x3, waiting for transfers between devices: 20.1 us -> 58.4 us  [exchange(): return lax.all_to_all(a, axis, split_axis=0, concat_axis=0, tiled=True)]
    ppermute x0 -> x13, waiting for transfers between devices: none -> 28.6 us  [shift_col(): return lax.ppermute(a, 'col', pairs)]
    psum x1, blocking collectives: 13.2 us -> 39 us  [spectral(): lax.psum((jnp.sum(source, axis=-1), jnp.sum(source * source, axis=-1)), '...]
    all_gather x1, waiting for transfers between devices: 25.7 us -> 0.02 us  [on_device(): w_out_all = lax.all_gather(w_out, 'col', axis=0, tiled=False)]
    all_to_all x2 -> x1, blocking collectives: 45.2 us -> 20.7 us  [exchange(): return lax.all_to_all(a, axis, split_axis=0, concat_axis=0, tiled=True)]
    ppermute x0 -> x13, starting transfers between devices: none -> 23.7 us  [shift_col(): return lax.ppermute(a, 'col', pairs)]
    ppermute x24 -> x28, starting transfers between devices: 28.1 us -> 37.9 us  [shift_row(): return lax.ppermute(a, 'row', pairs)]
  transfers between devices with their start and end apart: 28 -> 46, of which waited for: 15 -> 19; matrix products, arithmetic and copies ran while one was open for 3% -> 6% of each run, Pallas kernels for 5% -> 6%
where the time goes in v2:
time: 362 us; the launch traced here: 361 us
  waiting for transfers between devices  136 us (38%)
  starting transfers between devices  77.2 us (21%)
  blocking collectives  59.7 us (16%)
  Pallas kernels  40.2 us (11%)
  local copies, waits for them, and re-layouts  20.7 us (6%)
  between operations  13.7 us (4%)
  matrix products  10.1 us (3%)
    all_to_all x3, waiting for transfers between devices, exchange(): return lax.all_to_all(a, axis, split_axis=0, concat_axis=0, tiled=True)  58.4 us
    ppermute x28, waiting for transfers between devices, shift_row(): return lax.ppermute(a, 'row', pairs)  48.2 us
    psum x1, blocking collectives, spectral(): lax.psum((jnp.sum(source, axis=-1), jnp.sum(source * source, axis=-1)), '...  39 us
    ppermute x28, starting transfers between devices, shift_row(): return lax.ppermute(a, 'row', pairs)  37.9 us
    ppermute x13, waiting for transfers between devices, shift_col(): return lax.ppermute(a, 'col', pairs)  28.6 us
    ppermute x13, starting transfers between devices, shift_col(): return lax.ppermute(a, 'col', pairs)  23.7 us
    all_to_all x1, blocking collectives, exchange(): return lax.all_to_all(a, axis, split_axis=0, concat_axis=0, tiled=True)  20.7 us
    pallas_call x1, Pallas kernels, matmul_in(): pl.pallas_call(functools.partial(mm1_kernel, len(pieces), 768), grid=(wid...  18.2 us
  transfers between devices with their start and end apart: 46, of which 19 were waited for; matrix products, arithmetic and copies ran while one was open for 6% of the time, Pallas kernels for 6%

profile of v2, /device:TPU:1, one launch (start us, length us, event | category | flops | bytes accessed | tf_op | source)
XLA Modules:
  0.0 360.7 jit_solution(11983782743136010998)
XLA Ops:
  8.7 1.5 collective-permute-start.2
  10.2 3.2 fusion.15
  13.5 1.3 collective-permute-start
  14.8 1.4 collective-permute-start.1
  16.5 39.0 %all-reduce.1 = (f32[256]{0:T(256)S(1)}, f32[256]{0:T(256)S(1)}) all-reduce(f32[256]{0:T(256)S(1)} %reduce_sum.25, f32[256]{0:T(256)S(1)} %reduce_sum.23), channel_id=1, replica_groups=mesh['row'=16,'col'=8] {'col'}, use_global_device_ids=true, to_apply=%region_3.4 | all-reduce | flops 512 | bytes 4096 | tf_op jit(solution)/shard_map/psum | solution.py:250
  55.7 1.7 convolution_convert_fusion
  57.4 7.9 %all-to-all-start = ((bf16[16,32,768]{2,1,0:T(8,128)(2,1)}), bf16[16,32,768]{2,1,0:T(8,128)(2,1)}, u32[]{:S(2)}, u32[]{:S(2)}) async-start(bf16[16,32,768]{2,1,0:T(8,128)(2,1)} %bitcast.2), calls=%async_computation | async-start | bytes 1572864 | tf_op jit(solution)/shard_map/all_to_all | solution.py:222
  65.5 2.8 collective-permute-start.4
  68.3 1.5 fusion.16
  70.3 5.5 %all-to-all-done = bf16[16,32,768]{2,1,0:T(8,128)(2,1)} async-done(((bf16[16,32,768]{2,1,0:T(8,128)(2,1)}), bf16[16,32,768]{2,1,0:T(8,128)(2,1)}, u32[]{:S(2)}, u32[]{:S(2)}) %all-to-all-start) | async-done | bytes 786464 | tf_op jit(solution)/shard_map/all_to_all | solution.py:222
  75.8 5.2 %collective-permute-start.5 = (bf16[384,1536]{1,0:T(8,128)(2,1)}, bf16[384,1536]{1,0:T(8,128)(2,1)}, u32[]{:S(2)}, u32[]{:S(2)}) collective-permute-start(bf16[384,1536]{1,0:T(8,128)(2,1)} %get-tuple-element.44.refs_12_), channel_id=1, source_target_pairs={{0,1},{1,0},{2,3},{3,2},{4,5},{5,4},{6,7},{7,6},{8,9},{9,8},{10,11... | collective-permute-start | bytes 3538952 | tf_op jit(solution)/shard_map/ppermute | solution.py:56
  81.1 2.5 fusion.18
  84.6 1.9 add_convert_fusion
  86.5 3.6 %all-to-all-start.1 = ((bf16[16,32,768]{2,1,0:T(8,128)(2,1)}), bf16[16,32,768]{2,1,0:T(8,128)(2,1)S(1)}, u32[]{:S(2)}, u32[]{:S(2)}) async-start(bf16[16,32,768]{2,1,0:T(8,128)(2,1)} %bitcast.5), calls=%async_computation.1 | async-start | bytes 1572864 | tf_op jit(solution)/shard_map/all_to_all | solution.py:222
  90.3 28.6 %collective-permute-done.3.refs_1_ = bf16[384,1536]{1,0:T(8,128)(2,1)} collective-permute-done((bf16[384,1536]{1,0:T(8,128)(2,1)}, bf16[384,1536]{1,0:T(8,128)(2,1)}, u32[]{:S(2)}, u32[]{:S(2)}) %collective-permute-start.3) | collective-permute-done | bytes 1179680 | tf_op jit(solution)/shard_map/ppermute | solution.py:56
  119.7 4.8 %collective-permute-start.6 = (bf16[384,1536]{1,0:T(8,128)(2,1)}, bf16[384,1536]{1,0:T(8,128)(2,1)S(1)}, u32[]{:S(2)}, u32[]{:S(2)}) collective-permute-start(bf16[384,1536]{1,0:T(8,128)(2,1)} %get-tuple-element.45.refs_13_), channel_id=1, source_target_pairs={{0,1},{1,0},{2,3},{3,2},{4,5},{5,4},{6,7},{7,6},{8,9},{9,8},{10,11... | collective-permute-start | bytes 3538952 | tf_op jit(solution)/shard_map/ppermute | solution.py:56
  124.5 3.0 collective-permute-start.16
  127.5 3.1 fusion.17
  130.6 4.1 %all-to-all-start.2 = ((bf16[8,32,768]{2,1,0:T(8,128)(2,1)}), bf16[8,32,768]{2,1,0:T(8,128)(2,1)S(1)}, u32[]{:S(2)}, u32[]{:S(2)}) async-start(bf16[8,32,768]{2,1,0:T(8,128)(2,1)} %bitcast.8), calls=%async_computation.2 | async-start | bytes 786432 | tf_op jit(solution)/shard_map/all_to_all | solution.py:222
  135.4 52.9 %all-to-all-done.2.refs_0_ = bf16[8,32,768]{2,1,0:T(8,128)(2,1)S(1)} async-done(((bf16[8,32,768]{2,1,0:T(8,128)(2,1)}), bf16[8,32,768]{2,1,0:T(8,128)(2,1)S(1)}, u32[]{:S(2)}, u32[]{:S(2)}) %all-to-all-start.2) | async-done | bytes 393248 | tf_op jit(solution)/shard_map/all_to_all | solution.py:222
  189.5 1.0 copy-done.1
  190.5 1.4 copy-done.2
  192.7 3.0 collective-permute-start.11
  197.2 1.6 collective-permute-start.19
  198.7 2.7 collective-permute-start.14
  201.5 1.0 collective-permute-start.13
  202.5 2.2 collective-permute-done.10
  204.6 1.2 collective-permute-start.12
  205.8 1.8 collective-permute-start.20
  207.7 1.0 pad_maximum_fusion.refs_0_
  208.7 2.1 collective-permute-done.13
  211.8 1.7 collective-permute-start.17
  213.5 1.0 collective-permute-start.18
  214.5 3.0 collective-permute-start.23
  217.5 1.5 collective-permute-start.24
  219.0 11.0 %collective-permute-done.17.refs_0_ = bf16[4,16,6144]{2,1,0:T(8,128)(2,1)} collective-permute-done((bf16[4,16,6144]{2,1,0:T(8,128)(2,1)}, bf16[4,16,6144]{2,1,0:T(8,128)(2,1)}, u32[]{:S(2)}, u32[]{:S(2)}) %collective-permute-start.17) | collective-permute-done | bytes 786464 | tf_op jit(solution)/shard_map/ppermute | solution.py:48
  230.0 1.9 collective-permute-done.18.refs_1_
  231.9 1.0 slice.36
  233.3 1.0 slice.37
  234.3 2.4 collective-permute-start.22
  237.7 1.0 slice.38
  238.7 2.2 collective-permute-start.25
  240.9 1.0 slice.39
  241.9 1.5 collective-permute-start.26
  244.1 4.9 %collective-permute-done.25.refs_8_ = bf16[2,16,6144]{2,1,0:T(8,128)(2,1)S(1)} collective-permute-done((bf16[2,16,6144]{2,1,0:T(8,128)(2,1)S(1)}, bf16[2,16,6144]{2,1,0:T(8,128)(2,1)S(1)}, u32[]{:S(2)}, u32[]{:S(2)}) %collective-permute-start.25) | collective-permute-done | bytes 393248 | tf_op jit(solution)/shard_map/ppermute | solution.py:48
  250.3 18.2 %shard_map.134.h_ref = bf16[512,1536]{1,0:T(8,128)(2,1)} custom-call(bf16[4,16,6144]{2,1,0:T(8,128)(2,1)} %get-tuple-element.50.refs_0_, bf16[4,16,6144]{2,1,0:T(8,128)(2,1)} %get-tuple-element.51.refs_1_, bf16[4,16,6144]{2,1,0:T(8,128)(2,1)} %get-tuple-element.52.refs_2_, bf16[2,16,6144]{2,1,0:T(8,128)(2,1)} %copy-done.19, ...), custom_call_target="tpu_custom_call" | custom-call | flops 9663676416 | bytes 25165824 | tf_op jit(solution)/shard_map/pallas_call | solution.py:112
  268.5 15.7 %shard_map.135 = (bf16[4,16,6144]{2,1,0:T(8,128)(2,1)}, bf16[4,16,6144]{2,1,0:T(8,128)(2,1)}, bf16[4,16,6144]{2,1,0:T(8,128)(2,1)}, bf16[2,16,6144]{2,1,0:T(8,12...) custom-call(bf16[512,1536]{1,0:T(8,128)(2,1)} %shard_map.134.h_ref, ...), custom_call_target="tpu_custom_call" | custom-call | flops 9663676416 | bytes 26738688 | tf_op jit(solution)/shard_map/pallas_call | solution.py:141
  285.7 2.9 collective-permute-start.29
  288.7 2.4 collective-permute-done.27.low1
  291.1 2.1 collective-permute-done.28.top1
  293.7 3.3 collective-permute-done.30.top2
  297.0 1.1 copy-done.3
  298.1 1.1 copy-done.4
  299.3 3.6 shard_map.136
  302.8 2.7 collective-permute-start.32
  305.5 2.7 collective-permute-start.37
  308.2 9.5 %collective-permute-done.31.b = bf16[4,16,6144]{2,1,0:T(8,128)(2,1)S(1)} collective-permute-done((bf16[4,16,6144]{2,1,0:T(8,128)(2,1)S(1)}, bf16[4,16,6144]{2,1,0:T(8,128)(2,1)S(1)}, u32[]{:S(2)}, u32[]{:S(2)}) %collective-permute-start.31) | collective-permute-done | bytes 786464 | tf_op jit(solution)/shard_map/ppermute | solution.py:48
  318.6 1.2 collective-permute-start.34
  320.6 2.4 collective-permute-start.38
  323.1 2.3 collective-permute-done.33.b
  326.3 2.0 collective-permute-done.34.c
  328.2 1.1 collective-permute-done.35.d
  329.4 2.3 collective-permute-done.40.h
  332.3 20.7 %all_to_all.20 = bf16[8,32,768]{2,1,0:T(8,128)(2,1)S(1)} all-to-all(bf16[8,32,768]{2,1,0:T(8,128)(2,1)S(1)} %shard_map.139), channel_id=1, replica_groups=mesh['row'=16,'col'=8] {'col'}, dimensions={0} | all-to-all | bytes 786432 | tf_op jit(solution)/shard_map/all_to_all | solution.py:222
  (114 shorter events, 20.2 us)
Async XLA Ops:
  6.5 182.9 %all-gather.5.cloned.1.call-start = ((), (), s32[]{:S(2)}) async-start(), calls=%async_computation.4 | async-start | bytes 1769472 | tf_op jit(solution)/shard_map/all_gather | solution.py:300
  8.0 260.5 %all-gather.7.cloned.1.call-start = ((), (), s32[]{:S(2)}) async-start(), calls=%async_computation.5 | async-start | bytes 21233664 | tf_op jit(solution)/shard_map/all_gather | solution.py:306
  8.7 7.4 %copy-start.9 = (bf16[4,64,768]{2,1,0:T(8,128)(2,1)S(1)}, bf16[4,64,768]{2,1,0:T(8,128)(2,1)}, u32[]{:S(2)}) copy-start(bf16[4,64,768]{2,1,0:T(8,128)(2,1)} %param.13) | copy-start | bytes 1179652
  8.7 46.8 %copy-start.17 = (f32[768]{0:T(1024)S(1)}, f32[768]{0:T(1024)}, u32[]{:S(2)}) copy-start(f32[768]{0:T(1024)} %param.15) | copy-start | bytes 9220
  8.7 67.1 %collective-permute-start.2 = (bf16[768,1536]{1,0:T(8,128)(2,1)}, bf16[768,1536]{1,0:T(8,128)(2,1)}, u32[]{:S(2)}, u32[]{:S(2)}) collective-permute-start(bf16[768,1536]{1,0:T(8,128)(2,1)} %refs_10_.1), channel_id=1, source_target_pairs={{0,1},{1,0},{2,3},{3,2},{4,5},{5,4},{6,7},{7,6},{8,9},{9,8},{10,11... | collective-permute-start | bytes 7077896 | tf_op jit(solution)/shard_map/ppermute | solution.py:56
  13.5 42.3 %copy-start.15 = (f32[512,256]{1,0:T(8,128)S(1)}, f32[512,256]{1,0:T(8,128)}, u32[]{:S(2)}) copy-start(f32[512,256]{1,0:T(8,128)} %constant.27.clone) | copy-start | bytes 1572868
  13.5 62.3 %collective-permute-start = (bf16[384,1536]{1,0:T(8,128)(2,1)}, bf16[384,1536]{1,0:T(8,128)(2,1)}, u32[]{:S(2)}, u32[]{:S(2)}) collective-permute-start(bf16[384,1536]{1,0:T(8,128)(2,1)} %get-tuple-element.84), channel_id=1, source_target_pairs={{0,2},{1,3},{2,4},{3,5},{4,6},{5,7},{6,0},{7,1},{8,10},{9,11},{10,... | collective-permute-start | bytes 3538952 | tf_op jit(solution)/shard_map/ppermute | solution.py:56
  14.8 61.0 %collective-permute-start.1 = (bf16[384,1536]{1,0:T(8,128)(2,1)}, bf16[384,1536]{1,0:T(8,128)(2,1)}, u32[]{:S(2)}, u32[]{:S(2)}) collective-permute-start(bf16[384,1536]{1,0:T(8,128)(2,1)} %get-tuple-element.84), channel_id=1, source_target_pairs={{0,6},{1,7},{2,0},{3,1},{4,2},{5,3},{6,4},{7,5},{8,14},{9,15},{10,... | collective-permute-start | bytes 3538952 | tf_op jit(solution)/shard_map/ppermute | solution.py:56
  57.4 18.4 %all-to-all-start = ((bf16[16,32,768]{2,1,0:T(8,128)(2,1)}), bf16[16,32,768]{2,1,0:T(8,128)(2,1)}, u32[]{:S(2)}, u32[]{:S(2)}) async-start(bf16[16,32,768]{2,1,0:T(8,128)(2,1)} %bitcast.2), calls=%async_computation | async-start | bytes 1572864 | tf_op jit(solution)/shard_map/all_to_all | solution.py:222
  65.3 53.5 %collective-permute-start.3 = (bf16[384,1536]{1,0:T(8,128)(2,1)}, bf16[384,1536]{1,0:T(8,128)(2,1)}, u32[]{:S(2)}, u32[]{:S(2)}) collective-permute-start(bf16[384,1536]{1,0:T(8,128)(2,1)} %get-tuple-element.83), channel_id=1, source_target_pairs={{0,2},{1,3},{2,4},{3,5},{4,6},{5,7},{6,0},{7,1},{8,10},{9,11},{10,... | collective-permute-start | bytes 3538952 | tf_op jit(solution)/shard_map/ppermute | solution.py:56
  65.5 53.3 %collective-permute-start.4 = (bf16[384,1536]{1,0:T(8,128)(2,1)}, bf16[384,1536]{1,0:T(8,128)(2,1)}, u32[]{:S(2)}, u32[]{:S(2)}) collective-permute-start(bf16[384,1536]{1,0:T(8,128)(2,1)} %get-tuple-element.83), channel_id=1, source_target_pairs={{0,6},{1,7},{2,0},{3,1},{4,2},{5,3},{6,4},{7,5},{8,14},{9,15},{10,... | collective-permute-start | bytes 3538952 | tf_op jit(solution)/shard_map/ppermute | solution.py:56
  75.8 48.7 %collective-permute-start.5 = (bf16[384,1536]{1,0:T(8,128)(2,1)}, bf16[384,1536]{1,0:T(8,128)(2,1)}, u32[]{:S(2)}, u32[]{:S(2)}) collective-permute-start(bf16[384,1536]{1,0:T(8,128)(2,1)} %get-tuple-element.44.refs_12_), channel_id=1, source_target_pairs={{0,1},{1,0},{2,3},{3,2},{4,5},{5,4},{6,7},{7,6},{8,9},{9,8},{10,11... | collective-permute-start | bytes 3538952 | tf_op jit(solution)/shard_map/ppermute | solution.py:56
  81.1 2.5 copy-start.14
  83.6 1.1 copy-start.13
  86.5 32.3 %all-to-all-start.1 = ((bf16[16,32,768]{2,1,0:T(8,128)(2,1)}), bf16[16,32,768]{2,1,0:T(8,128)(2,1)S(1)}, u32[]{:S(2)}, u32[]{:S(2)}) async-start(bf16[16,32,768]{2,1,0:T(8,128)(2,1)} %bitcast.5), calls=%async_computation.1 | async-start | bytes 1572864 | tf_op jit(solution)/shard_map/all_to_all | solution.py:222
  90.1 98.2 %collective-permute-start.7 = (bf16[384,1536]{1,0:T(8,128)(2,1)}, bf16[384,1536]{1,0:T(8,128)(2,1)}, u32[]{:S(2)}, u32[]{:S(2)}) collective-permute-start(bf16[384,1536]{1,0:T(8,128)(2,1)} %get-tuple-element.46.refs_16_), channel_id=1, source_target_pairs={{0,1},{1,0},{2,3},{3,2},{4,5},{5,4},{6,7},{7,6},{8,9},{9,8},{10,11... | collective-permute-start | bytes 3538952 | tf_op jit(solution)/shard_map/ppermute | solution.py:56
  119.7 68.6 %collective-permute-start.6 = (bf16[384,1536]{1,0:T(8,128)(2,1)}, bf16[384,1536]{1,0:T(8,128)(2,1)S(1)}, u32[]{:S(2)}, u32[]{:S(2)}) collective-permute-start(bf16[384,1536]{1,0:T(8,128)(2,1)} %get-tuple-element.45.refs_13_), channel_id=1, source_target_pairs={{0,1},{1,0},{2,3},{3,2},{4,5},{5,4},{6,7},{7,6},{8,9},{9,8},{10,11... | collective-permute-start | bytes 3538952 | tf_op jit(solution)/shard_map/ppermute | solution.py:56
  124.5 63.8 %collective-permute-start.8 = (bf16[384,1536]{1,0:T(8,128)(2,1)}, bf16[384,1536]{1,0:T(8,128)(2,1)}, u32[]{:S(2)}, u32[]{:S(2)}) collective-permute-start(bf16[384,1536]{1,0:T(8,128)(2,1)} %get-tuple-element.47.refs_17_), channel_id=1, source_target_pairs={{0,1},{1,0},{2,3},{3,2},{4,5},{5,4},{6,7},{7,6},{8,9},{9,8},{10,11... | collective-permute-start | bytes 3538952 | tf_op jit(solution)/shard_map/ppermute | solution.py:56
  124.5 72.6 %collective-permute-start.15 = (bf16[384,1536]{1,0:T(8,128)(2,1)}, bf16[384,1536]{1,0:T(8,128)(2,1)}, u32[]{:S(2)}, u32[]{:S(2)}) collective-permute-start(bf16[384,1536]{1,0:T(8,128)(2,1)} %get-tuple-element.44.refs_12_), channel_id=1, source_target_pairs={{0,2},{1,3},{2,4},{3,5},{4,6},{5,7},{6,0},{7,1},{8,10},{9,11},{10,... | collective-permute-start | bytes 3538952 | tf_op jit(solution)/shard_map/ppermute | solution.py:56
  124.5 74.2 %collective-permute-start.16 = (bf16[384,1536]{1,0:T(8,128)(2,1)}, bf16[384,1536]{1,0:T(8,128)(2,1)}, u32[]{:S(2)}, u32[]{:S(2)}) collective-permute-start(bf16[384,1536]{1,0:T(8,128)(2,1)} %get-tuple-element.47.refs_17_), channel_id=1, source_target_pairs={{0,6},{1,7},{2,0},{3,1},{4,2},{5,3},{6,4},{7,5},{8,14},{9,15},{10,... | collective-permute-start | bytes 3538952 | tf_op jit(solution)/shard_map/ppermute | solution.py:56
  130.6 57.7 %all-to-all-start.2 = ((bf16[8,32,768]{2,1,0:T(8,128)(2,1)}), bf16[8,32,768]{2,1,0:T(8,128)(2,1)S(1)}, u32[]{:S(2)}, u32[]{:S(2)}) async-start(bf16[8,32,768]{2,1,0:T(8,128)(2,1)} %bitcast.8), calls=%async_computation.2 | async-start | bytes 786432 | tf_op jit(solution)/shard_map/all_to_all | solution.py:222
  188.3 1.1 copy-start.12
  189.5 1.0 copy-start.1
  190.4 1.4 copy-start.2
  192.7 8.8 %collective-permute-start.11 = (bf16[16,6144]{1,0:T(8,128)(2,1)S(1)}, bf16[16,6144]{1,0:T(8,128)(2,1)S(1)}, u32[]{:S(2)}, u32[]{:S(2)}) collective-permute-start(bf16[16,6144]{1,0:T(8,128)(2,1)S(1)} %get-tuple-element.48), channel_id=1, source_target_pairs={{0,64},{8,72},{16,80},{24,88},{32,96},{40,104},{48,112},{56,120},{... | collective-permute-start | bytes 589832 | tf_op jit(solution)/shard_map/ppermute | solution.py:48
  195.7 8.9 %collective-permute-start.10 = (bf16[16,6144]{1,0:T(8,128)(2,1)S(1)}, bf16[16,6144]{1,0:T(8,128)(2,1)S(1)}, u32[]{:S(2)}, u32[]{:S(2)}) collective-permute-start(bf16[16,6144]{1,0:T(8,128)(2,1)S(1)} %get-tuple-element.48), channel_id=1, source_target_pairs={{0,96},{8,104},{16,112},{24,120},{32,0},{40,8},{48,16},{56,24},{64... | collective-permute-start | bytes 589832 | tf_op jit(solution)/shard_map/ppermute | solution.py:48
  196.5 9.4 %collective-permute-start.9 = (bf16[16,6144]{1,0:T(8,128)(2,1)S(1)}, bf16[16,6144]{1,0:T(8,128)(2,1)S(1)}, u32[]{:S(2)}, u32[]{:S(2)}) collective-permute-start(bf16[16,6144]{1,0:T(8,128)(2,1)S(1)} %get-tuple-element.48), channel_id=1, source_target_pairs={{0,32},{8,40},{16,48},{24,56},{32,64},{40,72},{48,80},{56,88},{64,... | collective-permute-start | bytes 589832 | tf_op jit(solution)/shard_map/ppermute | solution.py:48
  197.2 20.3 %collective-permute-start.19 = (bf16[384,1536]{1,0:T(8,128)(2,1)}, bf16[384,1536]{1,0:T(8,128)(2,1)S(1)}, u32[]{:S(2)}, u32[]{:S(2)}) collective-permute-start(bf16[384,1536]{1,0:T(8,128)(2,1)} %collective-permute-done.15.refs_2_.refs_20_), channel_id=1, source_target_pairs={{0,1},{1,0},{2,3},{3,2},{4,5},{5,4},{6,7},{7,6},{8,9},{9,8},{10,11... | collective-permute-start | bytes 3538952 | tf_op jit(solution)/shard_map/ppermute | solution.py:56
  198.7 10.0 %collective-permute-start.14 = (bf16[16,6144]{1,0:T(8,128)(2,1)S(1)}, bf16[16,6144]{1,0:T(8,128)(2,1)S(1)}, u32[]{:S(2)}, u32[]{:S(2)}) collective-permute-start(bf16[16,6144]{1,0:T(8,128)(2,1)S(1)} %get-tuple-element.49), channel_id=1, source_target_pairs={{0,16},{8,24},{16,0},{24,8},{32,48},{40,56},{48,32},{56,40},{64,80... | collective-permute-start | bytes 589832 | tf_op jit(solution)/shard_map/ppermute | solution.py:48
  201.5 9.3 %collective-permute-start.13 = (bf16[16,6144]{1,0:T(8,128)(2,1)S(1)}, bf16[16,6144]{1,0:T(8,128)(2,1)S(1)}, u32[]{:S(2)}, u32[]{:S(2)}) collective-permute-start(bf16[16,6144]{1,0:T(8,128)(2,1)S(1)} %get-tuple-element.49), channel_id=1, source_target_pairs={{0,24},{8,0},{16,8},{24,16},{32,56},{40,32},{48,40},{56,48},{64,88... | collective-permute-start | bytes 589832 | tf_op jit(solution)/shard_map/ppermute | solution.py:48
  204.6 6.2 %collective-permute-start.12 = (bf16[16,6144]{1,0:T(8,128)(2,1)S(1)}, bf16[16,6144]{1,0:T(8,128)(2,1)S(1)}, u32[]{:S(2)}, u32[]{:S(2)}) collective-permute-start(bf16[16,6144]{1,0:T(8,128)(2,1)S(1)} %get-tuple-element.49), channel_id=1, source_target_pairs={{0,8},{8,16},{16,24},{24,0},{32,40},{40,48},{48,56},{56,32},{64,72... | collective-permute-start | bytes 589832 | tf_op jit(solution)/shard_map/ppermute | solution.py:48
  205.8 26.0 %collective-permute-start.20 = (bf16[384,1536]{1,0:T(8,128)(2,1)}, bf16[384,1536]{1,0:T(8,128)(2,1)}, u32[]{:S(2)}, u32[]{:S(2)}) collective-permute-start(bf16[384,1536]{1,0:T(8,128)(2,1)} %collective-permute-done.16.refs_3_.refs_21_), channel_id=1, source_target_pairs={{0,1},{1,0},{2,3},{3,2},{4,5},{5,4},{6,7},{7,6},{8,9},{9,8},{10,11... | collective-permute-start | bytes 3538952 | tf_op jit(solution)/shard_map/ppermute | solution.py:56
  211.8 18.2 %collective-permute-start.17 = (bf16[4,16,6144]{2,1,0:T(8,128)(2,1)}, bf16[4,16,6144]{2,1,0:T(8,128)(2,1)}, u32[]{:S(2)}, u32[]{:S(2)}) collective-permute-start(bf16[4,16,6144]{2,1,0:T(8,128)(2,1)} %get-tuple-element.50.refs_0_), channel_id=1, source_target_pairs={{0,8},{8,16},{16,24},{24,0},{32,40},{40,48},{48,56},{56,32},{64,72... | collective-permute-start | bytes 2359304 | tf_op jit(solution)/shard_map/ppermute | solution.py:48
  213.5 18.4 %collective-permute-start.18 = (bf16[4,16,6144]{2,1,0:T(8,128)(2,1)}, bf16[4,16,6144]{2,1,0:T(8,128)(2,1)}, u32[]{:S(2)}, u32[]{:S(2)}) collective-permute-start(bf16[4,16,6144]{2,1,0:T(8,128)(2,1)} %get-tuple-element.50.refs_0_), channel_id=1, source_target_pairs={{0,24},{8,0},{16,8},{24,16},{32,56},{40,32},{48,40},{56,48},{64,88... | collective-permute-start | bytes 2359304 | tf_op jit(solution)/shard_map/ppermute | solution.py:48
  214.5 22.3 %collective-permute-start.23 = (bf16[4,16,6144]{2,1,0:T(8,128)(2,1)}, bf16[4,16,6144]{2,1,0:T(8,128)(2,1)S(1)}, u32[]{:S(2)}, u32[]{:S(2)}) collective-permute-start(bf16[4,16,6144]{2,1,0:T(8,128)(2,1)} %get-tuple-element.53.refs_5_), channel_id=1, source_target_pairs={{0,32},{8,40},{16,48},{24,56},{32,64},{40,72},{48,80},{56,88},{64,... | collective-permute-start | bytes 2359304 | tf_op jit(solution)/shard_map/ppermute | solution.py:48
  217.4 14.4 %copy-start.8 = (bf16[384,1536]{1,0:T(8,128)(2,1)}, bf16[384,1536]{1,0:T(8,128)(2,1)S(1)}, u32[]{:S(2)}) copy-start(bf16[384,1536]{1,0:T(8,128)(2,1)S(1)} %collective-permute-done.19.refs_2_.refs_22_) | copy-start | bytes 3538948
  217.5 19.3 %collective-permute-start.24 = (bf16[4,16,6144]{2,1,0:T(8,128)(2,1)}, bf16[4,16,6144]{2,1,0:T(8,128)(2,1)}, u32[]{:S(2)}, u32[]{:S(2)}) collective-permute-start(bf16[4,16,6144]{2,1,0:T(8,128)(2,1)} %get-tuple-element.53.refs_5_), channel_id=1, source_target_pairs={{0,96},{8,104},{16,112},{24,120},{32,0},{40,8},{48,16},{56,24},{64... | collective-permute-start | bytes 2359304 | tf_op jit(solution)/shard_map/ppermute | solution.py:48
  232.9 11.1 %collective-permute-start.21 = (bf16[2,16,6144]{2,1,0:T(8,128)(2,1)S(1)}, bf16[2,16,6144]{2,1,0:T(8,128)(2,1)S(1)}, u32[]{:S(2)}, u32[]{:S(2)}) collective-permute-start(bf16[2,16,6144]{2,1,0:T(8,128)(2,1)S(1)} %slice.36), channel_id=1, source_target_pairs={{0,8},{8,16},{16,24},{24,0},{32,40},{40,48},{48,56},{56,32},{64,72... | collective-permute-start | bytes 1179656 | tf_op jit(solution)/shard_map/ppermute | solution.py:48
  234.3 9.7 %collective-permute-start.22 = (bf16[2,16,6144]{2,1,0:T(8,128)(2,1)S(1)}, bf16[2,16,6144]{2,1,0:T(8,128)(2,1)}, u32[]{:S(2)}, u32[]{:S(2)}) collective-permute-start(bf16[2,16,6144]{2,1,0:T(8,128)(2,1)S(1)} %slice.37), channel_id=1, source_target_pairs={{0,24},{8,0},{16,8},{24,16},{32,56},{40,32},{48,40},{56,48},{64,88... | collective-permute-start | bytes 1179656 | tf_op jit(solution)/shard_map/ppermute | solution.py:48
  236.8 0.9 copy-start.11
  237.7 5.8 %copy-start.16 = (f32[1536]{0:T(1024)S(1)}, f32[1536]{0:T(1024)}, u32[]{:S(2)}) copy-start(f32[1536]{0:T(1024)} %param.18) | copy-start | bytes 18436
  238.7 10.2 %collective-permute-start.25 = (bf16[2,16,6144]{2,1,0:T(8,128)(2,1)S(1)}, bf16[2,16,6144]{2,1,0:T(8,128)(2,1)S(1)}, u32[]{:S(2)}, u32[]{:S(2)}) collective-permute-start(bf16[2,16,6144]{2,1,0:T(8,128)(2,1)S(1)} %slice.38), channel_id=1, source_target_pairs={{0,32},{8,40},{16,48},{24,56},{32,64},{40,72},{48,80},{56,88},{64,... | collective-permute-start | bytes 1179656 | tf_op jit(solution)/shard_map/ppermute | solution.py:48
  241.9 7.6 %collective-permute-start.26 = (bf16[2,16,6144]{2,1,0:T(8,128)(2,1)S(1)}, bf16[2,16,6144]{2,1,0:T(8,128)(2,1)S(1)}, u32[]{:S(2)}, u32[]{:S(2)}) collective-permute-start(bf16[2,16,6144]{2,1,0:T(8,128)(2,1)S(1)} %slice.39), channel_id=1, source_target_pairs={{0,96},{8,104},{16,112},{24,120},{32,0},{40,8},{48,16},{56,24},{64... | collective-permute-start | bytes 1179656 | tf_op jit(solution)/shard_map/ppermute | solution.py:48
  244.1 5.5 %copy-start.19 = (bf16[2,16,6144]{2,1,0:T(8,128)(2,1)}, bf16[2,16,6144]{2,1,0:T(8,128)(2,1)S(1)}, u32[]{:S(2)}) copy-start(bf16[2,16,6144]{2,1,0:T(8,128)(2,1)S(1)} %collective-permute-done.21.refs_3_) | copy-start | bytes 1179652
  284.2 6.9 %collective-permute-start.27 = (bf16[2,16,6144]{2,1,0:T(8,128)(2,1)}, bf16[2,16,6144]{2,1,0:T(8,128)(2,1)S(1)}, u32[]{:S(2)}, u32[]{:S(2)}) collective-permute-start(bf16[2,16,6144]{2,1,0:T(8,128)(2,1)} %get-tuple-element.62), channel_id=1, source_target_pairs={{0,24},{8,0},{16,8},{24,16},{32,56},{40,32},{48,40},{56,48},{64,88... | collective-permute-start | bytes 1179656 | tf_op jit(solution)/shard_map/ppermute | solution.py:48
  285.1 8.0 %collective-permute-start.28 = (bf16[2,16,6144]{2,1,0:T(8,128)(2,1)}, bf16[2,16,6144]{2,1,0:T(8,128)(2,1)S(1)}, u32[]{:S(2)}, u32[]{:S(2)}) collective-permute-start(bf16[2,16,6144]{2,1,0:T(8,128)(2,1)} %get-tuple-element.63), channel_id=1, source_target_pairs={{0,8},{8,16},{16,24},{24,0},{32,40},{40,48},{48,56},{56,32},{64,72... | collective-permute-start | bytes 1179656 | tf_op jit(solution)/shard_map/ppermute | solution.py:48
  285.7 8.0 %collective-permute-start.29 = (bf16[2,16,6144]{2,1,0:T(8,128)(2,1)}, bf16[2,16,6144]{2,1,0:T(8,128)(2,1)S(1)}, u32[]{:S(2)}, u32[]{:S(2)}) collective-permute-start(bf16[2,16,6144]{2,1,0:T(8,128)(2,1)} %get-tuple-element.64), channel_id=1, source_target_pairs={{0,96},{8,104},{16,112},{24,120},{32,0},{40,8},{48,16},{56,24},{64... | collective-permute-start | bytes 1179656 | tf_op jit(solution)/shard_map/ppermute | solution.py:48
  288.7 8.3 %collective-permute-start.30 = (bf16[2,16,6144]{2,1,0:T(8,128)(2,1)}, bf16[2,16,6144]{2,1,0:T(8,128)(2,1)S(1)}, u32[]{:S(2)}, u32[]{:S(2)}) collective-permute-start(bf16[2,16,6144]{2,1,0:T(8,128)(2,1)} %get-tuple-element.65), channel_id=1, source_target_pairs={{0,32},{8,40},{16,48},{24,56},{32,64},{40,72},{48,80},{56,88},{64,... | collective-permute-start | bytes 1179656 | tf_op jit(solution)/shard_map/ppermute | solution.py:48
  297.0 1.1 copy-start.3
  298.1 1.1 copy-start.4
  299.3 18.4 %copy-start.6 = (bf16[4,16,6144]{2,1,0:T(8,128)(2,1)S(1)}, bf16[4,16,6144]{2,1,0:T(8,128)(2,1)}, u32[]{:S(2)}) copy-start(bf16[4,16,6144]{2,1,0:T(8,128)(2,1)} %get-tuple-element.57.a) | copy-start | bytes 2359300
  302.8 17.1 %copy-start.5 = (bf16[4,16,6144]{2,1,0:T(8,128)(2,1)S(1)}, bf16[4,16,6144]{2,1,0:T(8,128)(2,1)}, u32[]{:S(2)}) copy-start(bf16[4,16,6144]{2,1,0:T(8,128)(2,1)} %get-tuple-element.72.a) | copy-start | bytes 2359300
  302.8 14.8 %collective-permute-start.31 = (bf16[4,16,6144]{2,1,0:T(8,128)(2,1)S(1)}, bf16[4,16,6144]{2,1,0:T(8,128)(2,1)S(1)}, u32[]{:S(2)}, u32[]{:S(2)}) collective-permute-start(bf16[4,16,6144]{2,1,0:T(8,128)(2,1)S(1)} %get-tuple-element.66), channel_id=1, source_target_pairs={{0,8},{8,16},{16,24},{24,0},{32,40},{40,48},{48,56},{56,32},{64,72... | collective-permute-start | bytes 2359304 | tf_op jit(solution)/shard_map/ppermute | solution.py:48
  302.8 14.8 %collective-permute-start.32 = (bf16[4,16,6144]{2,1,0:T(8,128)(2,1)S(1)}, bf16[4,16,6144]{2,1,0:T(8,128)(2,1)S(1)}, u32[]{:S(2)}, u32[]{:S(2)}) collective-permute-start(bf16[4,16,6144]{2,1,0:T(8,128)(2,1)S(1)} %get-tuple-element.67), channel_id=1, source_target_pairs={{0,24},{8,0},{16,8},{24,16},{32,56},{40,32},{48,40},{56,48},{64,88... | collective-permute-start | bytes 2359304 | tf_op jit(solution)/shard_map/ppermute | solution.py:48
  305.5 14.5 %collective-permute-start.36 = (bf16[4,16,6144]{2,1,0:T(8,128)(2,1)}, bf16[4,16,6144]{2,1,0:T(8,128)(2,1)S(1)}, u32[]{:S(2)}, u32[]{:S(2)}) collective-permute-start(bf16[4,16,6144]{2,1,0:T(8,128)(2,1)} %get-tuple-element.73), channel_id=1, source_target_pairs={{0,32},{8,40},{16,48},{24,56},{32,64},{40,72},{48,80},{56,88},{64,... | collective-permute-start | bytes 2359304 | tf_op jit(solution)/shard_map/ppermute | solution.py:48
  305.5 14.5 %collective-permute-start.37 = (bf16[4,16,6144]{2,1,0:T(8,128)(2,1)}, bf16[4,16,6144]{2,1,0:T(8,128)(2,1)S(1)}, u32[]{:S(2)}, u32[]{:S(2)}) collective-permute-start(bf16[4,16,6144]{2,1,0:T(8,128)(2,1)} %get-tuple-element.74), channel_id=1, source_target_pairs={{0,96},{8,104},{16,112},{24,120},{32,0},{40,8},{48,16},{56,24},{64... | collective-permute-start | bytes 2359304 | tf_op jit(solution)/shard_map/ppermute | solution.py:48
  318.3 7.1 %collective-permute-start.33 = (bf16[16,6144]{1,0:T(8,128)(2,1)S(1)}, bf16[16,6144]{1,0:T(8,128)(2,1)S(1)}, u32[]{:S(2)}, u32[]{:S(2)}) collective-permute-start(bf16[16,6144]{1,0:T(8,128)(2,1)S(1)} %get-tuple-element.69), channel_id=1, source_target_pairs={{0,96},{8,104},{16,112},{24,120},{32,0},{40,8},{48,16},{56,24},{64... | collective-permute-start | bytes 589832 | tf_op jit(solution)/shard_map/ppermute | solution.py:48
  318.6 9.6 %collective-permute-start.34 = (bf16[16,6144]{1,0:T(8,128)(2,1)S(1)}, bf16[16,6144]{1,0:T(8,128)(2,1)S(1)}, u32[]{:S(2)}, u32[]{:S(2)}) collective-permute-start(bf16[16,6144]{1,0:T(8,128)(2,1)S(1)} %get-tuple-element.70), channel_id=1, source_target_pairs={{0,32},{8,40},{16,48},{24,56},{32,64},{40,72},{48,80},{56,88},{64,... | collective-permute-start | bytes 589832 | tf_op jit(solution)/shard_map/ppermute | solution.py:48
  319.8 9.5 %collective-permute-start.35 = (bf16[16,6144]{1,0:T(8,128)(2,1)S(1)}, bf16[16,6144]{1,0:T(8,128)(2,1)S(1)}, u32[]{:S(2)}, u32[]{:S(2)}) collective-permute-start(bf16[16,6144]{1,0:T(8,128)(2,1)S(1)} %get-tuple-element.71), channel_id=1, source_target_pairs={{0,64},{8,72},{16,80},{24,88},{32,96},{40,104},{48,112},{56,120},{... | collective-permute-start | bytes 589832 | tf_op jit(solution)/shard_map/ppermute | solution.py:48
  320.6 32.4 %copy-start.10 = (f32[256,768]{1,0:T(8,128)S(1)}, f32[256,768]{1,0:T(8,128)}, u32[]{:S(2)}) copy-start(f32[256,768]{1,0:T(8,128)} %get-tuple-element.90) | copy-start | bytes 2359300
  320.6 32.4 %copy-start.18 = (f32[768]{0:T(1024)S(1)}, f32[768]{0:T(1024)}, u32[]{:S(2)}) copy-start(f32[768]{0:T(1024)} %param.20) | copy-start | bytes 9220
  320.6 8.7 %collective-permute-start.38 = (bf16[16,6144]{1,0:T(8,128)(2,1)S(1)}, bf16[16,6144]{1,0:T(8,128)(2,1)S(1)}, u32[]{:S(2)}, u32[]{:S(2)}) collective-permute-start(bf16[16,6144]{1,0:T(8,128)(2,1)S(1)} %get-tuple-element.76), channel_id=1, source_target_pairs={{0,24},{8,0},{16,8},{24,16},{32,56},{40,32},{48,40},{56,48},{64,88... | collective-permute-start | bytes 589832 | tf_op jit(solution)/shard_map/ppermute | solution.py:48
  323.0 6.3 %collective-permute-start.39 = (bf16[16,6144]{1,0:T(8,128)(2,1)S(1)}, bf16[16,6144]{1,0:T(8,128)(2,1)S(1)}, u32[]{:S(2)}, u32[]{:S(2)}) collective-permute-start(bf16[16,6144]{1,0:T(8,128)(2,1)S(1)} %get-tuple-element.77), channel_id=1, source_target_pairs={{0,8},{8,16},{16,24},{24,0},{32,40},{40,48},{48,56},{56,32},{64,72... | collective-permute-start | bytes 589832 | tf_op jit(solution)/shard_map/ppermute | solution.py:48
  325.3 6.3 %collective-permute-start.40 = (bf16[16,6144]{1,0:T(8,128)(2,1)S(1)}, bf16[16,6144]{1,0:T(8,128)(2,1)S(1)}, u32[]{:S(2)}, u32[]{:S(2)}) collective-permute-start(bf16[16,6144]{1,0:T(8,128)(2,1)S(1)} %get-tuple-element.78), channel_id=1, source_target_pairs={{0,16},{8,24},{16,0},{24,8},{32,48},{40,56},{48,32},{56,40},{64,80... | collective-permute-start | bytes 589832 | tf_op jit(solution)/shard_map/ppermute | solution.py:48
  (4 other events, 3.1 us)
Sparse Core Ops, SparseCore 0:
  9.0 31.2 all-gather.4
  42.0 148.4 all-gather.6

commit v3 on v1

v3 whole, which is shorter than its diff:
```python
import functools
import math

import jax
import jax.numpy as jnp
import numpy as np
from jax import lax
from jax.experimental import pallas as pl
from jax.experimental.pallas import tpu as pltpu
from jax.sharding import PartitionSpec as P

SIDE = 4
BF = jnp.bfloat16
F32 = jnp.float32
MB = 1 << 20


def angles(count):
    index = np.arange(count)
    turn = (index[:, None] * index[None, :]) % count * (2.0 * math.pi / count)
    return np.cos(turn), np.sin(turn)


def spectral_tables(here, width, height):
    groups = height // here
    per = width // groups
    cos_w, sin_w = angles(width)
    cos_h, sin_h = angles(height)
    eye_r, eye_k = np.eye(here), np.eye(per)
    out = np.stack([cos_w, -sin_w]).reshape(2, width, groups, per)
    one = np.einsum("scqk,rt->qrsktc", out, eye_r).reshape(2 * here * width, here * width)
    turn = np.stack([np.stack([cos_h, sin_h]), np.stack([-sin_h, cos_h])])
    turn = turn.reshape(2, 2, groups, here, height)
    two = np.einsum("uvqrn,kl->unkqrvl", turn, eye_k).reshape(2 * height * per, 2 * height * per)
    back = np.stack([np.stack([cos_h, -sin_h]), np.stack([sin_h, cos_h])])
    back = back.reshape(2, 2, height, groups, here)
    three = np.einsum("uvnqr,kl->qrukvnl", back, eye_k).reshape(2 * height * per, 2 * height * per)
    four = np.einsum("sqkc,rt->rcqtsk", out.transpose(0, 2, 3, 1), eye_r)
    four = four.reshape(here * width, 2 * here * width) / (width * height)
    return [t.astype(np.float32) for t in (one, two, three, four)]


def hop(a, axis, steps):
    pairs = []
    for z in range(SIDE):
        for y in range(SIDE):
            for x in range(SIDE):
                for core, step in enumerate(steps):
                    to = {"z": z, "y": y, "x": x}
                    to[axis] = (to[axis] + step) % SIDE
                    source = ((z * SIDE + y) * SIDE + x) * 2 + core
                    pairs.append((source, ((to["z"] * SIDE + to["y"]) * SIDE + to["x"]) * 2 + core))
    return lax.ppermute(a, ("row", "col"), pairs)


APART = (1, -1)
OTHER = (-1, 1)


def swap_cores(a):
    pairs = [(x * 2 + core, x * 2 + 1 - core) for x in range(SIDE) for core in range(2)]
    return lax.ppermute(a, "col", pairs)


def params(mb):
    return pltpu.CompilerParams(vmem_limit_bytes=mb * MB)


def act_kernel(moved_ref, gain_ref, first_ref, second_ref):
    cols, _, chans = moved_ref.shape
    half = first_ref.shape[0]
    values = moved_ref[...].astype(F32)
    mean = jnp.sum(jnp.sum(values, axis=0), axis=-1, keepdims=True) / (cols * chans)
    square = jnp.sum(jnp.sum(values * values, axis=0), axis=-1, keepdims=True) / (cols * chans)
    scale = 1.0 / jnp.sqrt(square - mean * mean + 1e-05)
    for j in range(cols):
        part = (values[j] - mean) * scale * gain_ref[j, :1, :]
        part = part.astype(BF)
        first_ref[:, j * chans : (j + 1) * chans] = part[:half]
        second_ref[:, j * chans : (j + 1) * chans] = part[half:]


def normalize(moved, gains, half):
    cols, _, chans = moved.shape
    shape = jax.ShapeDtypeStruct((half, cols * chans), BF)
    return pl.pallas_call(
        act_kernel,
        out_shape=(shape, shape),
        compiler_params=params(63),
    )(moved, gains)


def mm1_kernel(*refs):
    pieces, (w_ref, b_ref, o_ref, left, sems) = refs[:-5], refs[-5:]
    rows = left.shape[0] // len(pieces)
    copies = [
        pltpu.make_async_copy(p, left.at[pl.ds(i * rows, rows)], sems.at[i])
        for i, p in enumerate(pieces)
    ]

    @pl.when(pl.program_id(0) == 0)
    def _():
        for copy in copies:
            copy.start()
        for copy in copies:
            copy.wait()

    pre = jnp.dot(left[...], w_ref[...], preferred_element_type=F32) + b_ref[...]
    o_ref[...] = (0.5 * pre * (1.0 + lax.erf(pre * math.sqrt(0.5)))).astype(BF)


def matmul_in(pieces, w, b):
    depth, width = w.shape
    tokens = len(pieces) * pieces[0].shape[0]
    tile = 256
    return pl.pallas_call(
        mm1_kernel,
        grid=(width // tile,),
        in_specs=[pl.BlockSpec(memory_space=pl.ANY) for _ in pieces]
        + [
            pl.BlockSpec((depth, tile), lambda i: (0, i)),
            pl.BlockSpec((1, tile), lambda i: (0, i)),
        ],
        out_specs=pl.BlockSpec((tokens, tile), lambda i: (0, i)),
        out_shape=jax.ShapeDtypeStruct((tokens, width), BF),
        scratch_shapes=[pltpu.VMEM((tokens, depth), BF), pltpu.SemaphoreType.DMA((len(pieces),))],
        compiler_params=params(63),
        cost_estimate=pl.CostEstimate(
            flops=2 * tokens * depth * width,
            bytes_accessed=2 * (tokens * depth + depth * width),
            transcendentals=0,
        ),
    )(*pieces, w, b[None])


def mm2_kernel(count, *refs):
    h_ref, weights, outs, (held, sems) = refs[0], refs[1 : 1 + count], refs[1 + count : -2], refs[-2:]
    step = pl.program_id(0)
    copies = [pltpu.make_async_copy(w, held.at[j % 2], sems.at[j % 2]) for j, w in enumerate(weights)]
    for j in range(count):

        @pl.when(step == j)
        def _(j=j):
            if j == 0:
                copies[0].start()
            if j + 1 < count:
                copies[j + 1].start()
            copies[j].wait()

    out = jnp.dot(h_ref[...], held[lax.rem(step, 2)], preferred_element_type=F32)
    rows = outs[0].shape[0]
    for i, o_ref in enumerate(outs):
        o_ref[...] = out[i * rows : (i + 1) * rows].astype(BF)


def matmul_out(hidden, weights, count):
    depth, chans = weights[0].shape
    tokens = hidden.shape[0]
    cols = len(weights)
    rows = tokens // count
    return pl.pallas_call(
        functools.partial(mm2_kernel, cols),
        grid=(cols,),
        in_specs=[pl.BlockSpec((tokens, depth), lambda j: (0, 0))]
        + [pl.BlockSpec(memory_space=pl.ANY) for _ in weights],
        out_specs=[pl.BlockSpec((rows, chans), lambda j: (0, j))] * count,
        out_shape=[jax.ShapeDtypeStruct((rows, cols * chans), BF)] * count,
        scratch_shapes=[pltpu.VMEM((2, depth, chans), BF), pltpu.SemaphoreType.DMA((2,))],
        compiler_params=params(63),
        cost_estimate=pl.CostEstimate(
            flops=2 * tokens * depth * cols * chans,
            bytes_accessed=2 * (tokens * depth + depth * cols * chans + tokens * cols * chans),
            transcendentals=0,
        ),
    )(hidden, *weights)


def pair_kernel(a1, b1, a2, b2, o1, o2):
    o1[...] = (a1[...].astype(F32) + b1[...].astype(F32)).astype(BF)
    o2[...] = (a2[...].astype(F32) + b2[...].astype(F32)).astype(BF)


def add_pairs(*parts):
    rows, width = parts[0].shape
    tile = width // 4
    block = pl.BlockSpec((rows, tile), lambda j: (0, j))
    return pl.pallas_call(
        pair_kernel,
        grid=(width // tile,),
        in_specs=[block] * 4,
        out_specs=[block] * 2,
        out_shape=[jax.ShapeDtypeStruct((rows, width), BF)] * 2,
        compiler_params=params(63),
    )(*parts)


def add_kernel(a, b, c, *outs):
    total = a[...].astype(F32) + (b[...].astype(F32) + c[...].astype(F32))
    rows = outs[0].shape[0]
    for i, o_ref in enumerate(outs):
        o_ref[...] = total[i * rows : (i + 1) * rows].astype(BF)


def add_pieces(*parts):
    rows, width = parts[0].shape
    tile = width // 4
    return pl.pallas_call(
        add_kernel,
        grid=(width // tile,),
        in_specs=[pl.BlockSpec((rows, tile), lambda j: (0, j))] * len(parts),
        out_specs=[pl.BlockSpec((rows // SIDE, tile), lambda j: (0, j))] * SIDE,
        out_shape=[jax.ShapeDtypeStruct((rows // SIDE, width), BF)] * SIDE,
        compiler_params=params(63),
    )(*parts)


def last_kernel(place_ref, a, b, c, d, e, f, g, h, o_ref):
    half = a.shape[0]
    top = (a[...].astype(F32) + b[...].astype(F32)) + (c[...].astype(F32) + d[...].astype(F32))
    low = (e[...].astype(F32) + f[...].astype(F32)) + (g[...].astype(F32) + h[...].astype(F32))
    o_ref[0, :half, :] = top.astype(BF)
    o_ref[0, half:, :] = low.astype(BF)


def add_last(place, first, second, cols):
    half, width = first[0].shape
    chans = width // cols
    return pl.pallas_call(
        last_kernel,
        grid_spec=pltpu.PrefetchScalarGridSpec(
            num_scalar_prefetch=1,
            grid=(cols,),
            in_specs=[pl.BlockSpec((half, chans), lambda j, place: (0, j))] * 8,
            out_specs=pl.BlockSpec((1, 2 * half, chans), lambda j, place: (place[j], 0, 0)),
        ),
        out_shape=jax.ShapeDtypeStruct((cols, 2 * half, chans), BF),
        compiler_params=params(63),
    )(place, *first, *second)


def exchange(a, axis):
    return lax.all_to_all(a, axis, split_axis=0, concat_axis=0, tiled=True)


def tie_kernel(*refs):
    pass


def tie(values, others):
    count = len(values)
    anywhere = pl.BlockSpec(memory_space=pl.ANY)
    return pl.pallas_call(
        tie_kernel,
        in_specs=[anywhere] * (count + len(others)),
        out_specs=[anywhere] * count,
        out_shape=[jax.ShapeDtypeStruct(v.shape, v.dtype) for v in values],
        input_output_aliases={i: i for i in range(count)},
        compiler_params=params(62),
    )(*values, *others)


def spectral(image, filter_bank, gain_first, late):
    rows_here, width, chans = image.shape
    groups = lax.axis_size("row")
    width_all = chans * lax.axis_size("col")
    tokens = rows_here * width
    one, two, three, four = spectral_tables(rows_here, width, rows_here * groups)
    high = lax.Precision.HIGH
    source = image.astype(F32).reshape(tokens, chans)
    sums, squares = lax.psum(
        (jnp.sum(source, axis=-1), jnp.sum(source * source, axis=-1)), "col"
    )
    mean = sums[:, None] / width_all
    square = squares[:, None] / width_all
    normed = (source - mean) / jnp.sqrt(square - mean * mean + 1e-05) * gain_first
    col = jnp.dot(one, normed, precision=high).astype(BF)
    col = exchange(col.reshape(groups, -1, chans), "row").reshape(-1, chans)
    spec = jnp.dot(two, col.astype(F32), precision=high)
    split = spec.shape[0] // 2
    spec_re, spec_im = spec[:split], spec[split:]
    f_re, f_im = filter_bank[0].reshape(-1, chans), filter_bank[1].reshape(-1, chans)
    filt = jnp.concatenate(
        [f_re * spec_re - f_im * spec_im, f_re * spec_im + f_im * spec_re], axis=0
    )
    back = jnp.dot(three, filt, precision=high).astype(BF)
    back = exchange(back.reshape(groups, -1, chans), "row").reshape(-1, chans)
    back, *late = tie([back, *late], [])
    return source + jnp.dot(four, back.astype(F32), precision=high), late


def block_places():
    table = []
    for x in range(SIDE):
        for core in range(2):
            row = []
            for far in (False, True):
                at = core ^ far
                for step in (0, APART[at], OTHER[at], 2):
                    row.append((x + (step if step == 0 else -step)) % SIDE * 2 + at)
            table.append(row)
    return jnp.asarray(np.array(table, np.int32))[lax.axis_index("col")]


def gather_near(a, axis):
    far, *near = [hop(a, axis, (s, s)) for s in (2, 1, -1)]
    return jnp.stack([a, *near, far]).reshape(-1, a.shape[1])


def send_back(parts, axis):
    far, *near = [hop(parts[i], axis, (s, s)) for i, s in ((3, 2), (1, -1), (2, 1))]
    return [parts[0], *near, far]


def on_device(image, filter_bank, gain_first, gain_second, w_in, b_in, w_out, b_out):
    rows_here, width, chans = image.shape
    cols = lax.axis_size("col")
    padded = jnp.pad(gain_second[None], ((0, 63), (0, 0)))
    w_in_all = lax.all_gather(w_in, "col", axis=0, tiled=True)
    gains = lax.all_gather(padded, "col", axis=0, tiled=False)
    one = hop(w_out, "x", APART)
    own_swap = swap_cores(w_out)
    resid, (one, own_swap) = spectral(image, filter_bank, gain_first, [one, own_swap])
    one_swap = swap_cores(one)
    tokens = rows_here * width
    own = tokens // cols
    half = own // 2
    moved = exchange(resid.astype(BF).reshape(cols, own, chans), "col")
    moved, one, one_swap, later = tie([moved, one, one_swap, w_out], [])
    first, second = normalize(moved, gains, half)
    first, second = gather_near(first, "z"), gather_near(second, "y")
    first, second, later = tie([first, second, later], [])
    two = hop(later, "x", OTHER)
    first = [first, hop(first, "y", APART), hop(first, "y", OTHER)]
    second = [second, hop(second, "z", APART), hop(second, "z", OTHER)]
    first[1], second[1], one = tie([first[1], second[1], one], [])
    three = hop(one, "x", APART)
    first.append(hop(first[1], "y", APART))
    second.append(hop(second[1], "z", APART))
    *pieces, two = tie(first + second + [two], [])
    two_swap = swap_cores(two)
    hidden = matmul_in(pieces, w_in_all, b_in)
    hidden, three = tie([hidden, three], [])
    blocks = [later, one, two, three, own_swap, one_swap, two_swap, swap_cores(three)]
    own1, fore1, back1, far1, own2, fore2, back2, far2 = matmul_out(hidden, blocks, len(pieces))
    back1, back2 = hop(back1, "y", APART), hop(back2, "z", APART)
    fore1, fore2 = add_pairs(fore1, hop(far1, "y", OTHER), fore2, hop(far2, "z", OTHER))
    first = add_pieces(own1, back1, hop(fore1, "y", OTHER))
    second = add_pieces(own2, back2, hop(fore2, "z", OTHER))
    first, second = send_back(first, "z"), send_back(second, "y")
    proj = exchange(add_last(block_places(), first, second, cols), "col")
    result = (resid + proj.reshape(tokens, chans).astype(F32) + b_out).astype(BF)
    return result.reshape(rows_here, width, chans)


def solution(mesh):
    placed = (
        P("row", None, "col"),
        P(None, None, "row", "col"),
        P("col"),
        P("col"),
        P("col", "row"),
        P("row"),
        P("row", "col"),
        P("col"),
    )
    return jax.shard_map(
        on_device, mesh=mesh, in_specs=placed, out_specs=P("row", None, "col"), check_vma=False
    )
```

time: 319 us -> 322 us (level)
  waiting for transfers between devices: 153 us -> 91.5 us
  starting transfers between devices: 39.7 us -> 69 us
  Pallas kernels: 30 us -> 53.4 us
  blocking collectives: 58.4 us -> 64.3 us
  other arithmetic: 1.52 us -> 5.8 us
    ppermute x24 -> x31, starting transfers between devices: 28.1 us -> 61 us  [the longest x27 47.3 us: hop(): return lax.ppermute(a, ('row', 'col'), pairs)]
    all_gather x1, waiting for transfers between devices: 25.7 us -> 0.01 us  [on_device(): gains = lax.all_gather(padded, 'col', axis=0, tiled=False)]
    all_to_all x2 -> x1, waiting for transfers between devices: 20.1 us -> 1.99 us  [exchange(): return lax.all_to_all(a, axis, split_axis=0, concat_axis=0, tiled=True)]
    ppermute x24 -> x31, waiting for transfers between devices: 106 us -> 88.8 us  [the longest x27 84.3 us: hop(): return lax.ppermute(a, ('row', 'col'), pairs)]
    pallas_call x3 -> x10, Pallas kernels: 28.1 us -> 43.5 us  [the longest x1 17.1 us: matmul_in(): pl.pallas_call(mm1_kernel, grid=(width // tile,), in_specs=[pl.BlockSpec(...]
    unnamed x40 -> x33, local copies, waits for them, and re-layouts: 11 us -> 3.61 us
    all_to_all x2 -> x3, blocking collectives: 45.2 us -> 51.1 us  [exchange(): return lax.all_to_all(a, axis, split_axis=0, concat_axis=0, tiled=True)]
    pallas_call x2, Pallas kernels: 1.57 us -> 7.3 us  [add_pieces(): pl.pallas_call(add_kernel, grid=(width // tile,), in_specs=[pl.BlockSpec(...]
  transfers between devices with their start and end apart: 28 -> 34, of which waited for: 15 -> 14; matrix products, arithmetic and copies ran while one was open for 3% -> 7% of each run, Pallas kernels for 5% -> 10%
where the time goes in v3:
time: 322 us; the launch traced here: 320 us
  waiting for transfers between devices  91.5 us (28%)
  starting transfers between devices  69 us (21%)
  blocking collectives  64.3 us (20%)
  Pallas kernels  53.4 us (17%)
  between operations  13.6 us (4%)
  local copies, waits for them, and re-layouts  12.8 us (4%)
  matrix products  9.79 us (3%)
  other arithmetic  5.8 us (2%)
    ppermute x27, waiting for transfers between devices, hop(): return lax.ppermute(a, ('row', 'col'), pairs)  84.3 us
    all_to_all x3, blocking collectives, exchange(): return lax.all_to_all(a, axis, split_axis=0, concat_axis=0, tiled=True)  51.1 us
    ppermute x27, starting transfers between devices, hop(): return lax.ppermute(a, ('row', 'col'), pairs)  47.3 us
    pallas_call x1, Pallas kernels, matmul_in(): pl.pallas_call(mm1_kernel, grid=(width // tile,), in_specs=[pl.BlockSpec(...  17.1 us
    pallas_call x1, Pallas kernels, matmul_out(): pl.pallas_call(functools.partial(mm2_kernel, cols), grid=(cols,), in_spec...  16.7 us
    ppermute x4, starting transfers between devices, swap_cores(): return lax.ppermute(a, 'col', pairs)  13.7 us
    psum x1, blocking collectives, spectral(): lax.psum((jnp.sum(source, axis=-1), jnp.sum(source * source, axis=-1)), '...  13.2 us
    all_to_all x1, starting transfers between devices, exchange(): return lax.all_to_all(a, axis, split_axis=0, concat_axis=0, tiled=True)  7.89 us
  transfers between devices with their start and end apart: 34, of which 14 were waited for; matrix products, arithmetic and copies ran while one was open for 7% of the time, Pallas kernels for 10%

profile of v3, /device:TPU:1, one launch (start us, length us, event | category | flops | bytes accessed | tf_op | source)
XLA Modules:
  0.0 320.2 jit_solution(6859532210806774986)
XLA Ops:
  6.5 1.7 copy.63.refs_3_
  10.1 13.2 %all-reduce.1 = (f32[256]{0:T(256)S(1)}, f32[256]{0:T(256)S(1)}) all-reduce(f32[256]{0:T(256)S(1)} %reduce_sum.25, f32[256]{0:T(256)S(1)} %reduce_sum.23), channel_id=1, replica_groups=mesh['row'=16,'col'=8] {'col'}, use_global_device_ids=true, to_apply=%region_3.4 | all-reduce | flops 512 | bytes 4096 | tf_op jit(solution)/shard_map/psum | solution.py:270
  23.5 2.8 convolution_convert_fusion
  26.2 7.9 %all-to-all-start = ((bf16[16,32,768]{2,1,0:T(8,128)(2,1)}), bf16[16,32,768]{2,1,0:T(8,128)(2,1)}, u32[]{:S(2)}, u32[]{:S(2)}) async-start(bf16[16,32,768]{2,1,0:T(8,128)(2,1)} %bitcast.2), calls=%async_computation | async-start | bytes 1572864 | tf_op jit(solution)/shard_map/all_to_all | solution.py:242
  34.1 2.0 collective-permute-start
  36.1 1.3 collective-permute-start.1
  37.4 2.7 fusion.15
  40.1 1.4 reshape_squeeze.6
  41.5 2.4 reshape_squeeze.7
  43.9 2.0 all-to-all-done
  45.9 2.5 fusion.17
  48.5 0.9 fusion.7
  49.5 1.0 add_convert_fusion
  50.5 16.6 %all_to_all.20 = bf16[16,32,768]{2,1,0:T(8,128)(2,1)} all-to-all(bf16[16,32,768]{2,1,0:T(8,128)(2,1)S(1)} %bitcast.45), channel_id=1, replica_groups=mesh['row'=16,'col'=8] {'row'}, dimensions={0} | all-to-all | bytes 1572864 | tf_op jit(solution)/shard_map/all_to_all | solution.py:242
  67.1 7.7 %collective-permute-done.refs_1_ = bf16[1536,768]{1,0:T(8,128)(2,1)} collective-permute-done((bf16[1536,768]{1,0:T(8,128)(2,1)S(1)}, bf16[1536,768]{1,0:T(8,128)(2,1)}, u32[]{:S(2)}, u32[]{:S(2)}) %collective-permute-start) | collective-permute-done | bytes 2359328 | tf_op jit(solution)/shard_map/ppermute | solution.py:53
  74.8 11.8 %collective-permute-start.2 = (bf16[1536,768]{1,0:T(8,128)(2,1)}, bf16[1536,768]{1,0:T(8,128)(2,1)}, u32[]{:S(2)}, u32[]{:S(2)}) collective-permute-start(bf16[1536,768]{1,0:T(8,128)(2,1)} %get-tuple-element.50.refs_1_), channel_id=1, source_target_pairs={{0,1},{1,0},{2,3},{3,2},{4,5},{5,4},{6,7},{7,6},{8,9},{9,8},{10,11... | collective-permute-start | bytes 7077896 | tf_op jit(solution)/shard_map/ppermute | solution.py:62
  86.7 2.6 fusion.16
  89.2 16.5 %all_to_all.21.refs_0_ = bf16[8,32,768]{2,1,0:T(8,128)(2,1)} all-to-all(bf16[8,32,768]{2,1,0:T(8,128)(2,1)S(1)} %bitcast.47), channel_id=1, replica_groups=mesh['row'=16,'col'=8] {'col'}, dimensions={0} | all-to-all | bytes 786432 | tf_op jit(solution)/shard_map/all_to_all | solution.py:242
  105.8 2.6 shard_map.129
  108.4 2.1 collective-permute-start.6
  110.4 1.1 collective-permute-start.7
  111.6 1.8 collective-permute-start.8
  113.4 1.0 collective-permute-start.3
  114.4 1.7 collective-permute-start.4
  116.0 2.3 collective-permute-start.5
  118.3 2.5 collective-permute-done.8
  120.9 1.9 pad_maximum_fusion.1
  122.8 1.6 collective-permute-done.5
  124.4 2.0 pad_maximum_fusion
  126.6 1.7 collective-permute-start.10
  128.3 1.4 collective-permute-start.9
  129.8 8.2 %collective-permute-done.10.refs_1_ = bf16[64,6144]{1,0:T(8,128)(2,1)} collective-permute-done((bf16[64,6144]{1,0:T(8,128)(2,1)}, bf16[64,6144]{1,0:T(8,128)(2,1)}, u32[]{:S(2)}, u32[]{:S(2)}) %collective-permute-start.10) | collective-permute-done | bytes 786464 | tf_op jit(solution)/shard_map/ppermute | solution.py:53
  138.0 5.9 %collective-permute-done.9.refs_0_ = bf16[64,6144]{1,0:T(8,128)(2,1)S(1)} collective-permute-done((bf16[64,6144]{1,0:T(8,128)(2,1)}, bf16[64,6144]{1,0:T(8,128)(2,1)S(1)}, u32[]{:S(2)}, u32[]{:S(2)}) %collective-permute-start.9) | collective-permute-done | bytes 786464 | tf_op jit(solution)/shard_map/ppermute | solution.py:53
  144.9 5.4 %collective-permute-start.16 = (bf16[1536,768]{1,0:T(8,128)(2,1)}, bf16[1536,768]{1,0:T(8,128)(2,1)}, u32[]{:S(2)}, u32[]{:S(2)}) collective-permute-start(bf16[1536,768]{1,0:T(8,128)(2,1)} %get-tuple-element.69.refs_2_), channel_id=1, source_target_pairs={{0,2},{1,7},{2,4},{3,1},{4,6},{5,3},{6,0},{7,5},{8,10},{9,15},{10,... | collective-permute-start | bytes 7077896 | tf_op jit(solution)/shard_map/ppermute | solution.py:53
  150.2 1.1 collective-permute-start.12
  151.3 2.7 collective-permute-start.14
  154.6 13.3 %collective-permute-done.13.refs_6_ = bf16[64,6144]{1,0:T(8,128)(2,1)S(1)} collective-permute-done((bf16[64,6144]{1,0:T(8,128)(2,1)S(1)}, bf16[64,6144]{1,0:T(8,128)(2,1)S(1)}, u32[]{:S(2)}, u32[]{:S(2)}) %collective-permute-start.13) | collective-permute-done | bytes 786464 | tf_op jit(solution)/shard_map/ppermute | solution.py:53
  167.9 2.5 collective-permute-done.14.refs_7_
  170.3 17.7 %collective-permute-done.15.refs_8_ = bf16[1536,768]{1,0:T(8,128)(2,1)} collective-permute-done((bf16[1536,768]{1,0:T(8,128)(2,1)}, bf16[1536,768]{1,0:T(8,128)(2,1)}, u32[]{:S(2)}, u32[]{:S(2)}) %collective-permute-start.15) | collective-permute-done | bytes 2359328 | tf_op jit(solution)/shard_map/ppermute | solution.py:53
  188.1 17.1 %shard_map.133.refs_0_ = bf16[512,1536]{1,0:T(8,128)(2,1)} custom-call(bf16[64,6144]{1,0:T(8,128)(2,1)} %get-tuple-element.61.refs_0_, bf16[64,6144]{1,0:T(8,128)(2,1)} %get-tuple-element.62.refs_1_, bf16[64,6144]{1,0:T(8,128)(2,1)} %get-tuple-element.63.refs_2_, bf16[64,6144]{1,0:T(8,128)(2,1)} %get-tuple-element.64.refs_3_, ...), custom_call_target="tpu_custom_call" | custom-call | flops 9663676416 | bytes 25165824 | tf_op jit(solution)/shard_map/pallas_call | solution.py:116
  205.7 4.5 %collective-permute-done.18.refs_8_ = bf16[1536,768]{1,0:T(8,128)(2,1)} collective-permute-done((bf16[1536,768]{1,0:T(8,128)(2,1)}, bf16[1536,768]{1,0:T(8,128)(2,1)}, u32[]{:S(2)}, u32[]{:S(2)}) %collective-permute-start.18) | collective-permute-done | bytes 2359328 | tf_op jit(solution)/shard_map/ppermute | solution.py:62
  210.2 16.7 %shard_map.135 = (bf16[64,6144]{1,0:T(8,128)(2,1)}, bf16[64,6144]{1,0:T(8,128)(2,1)}, bf16[64,6144]{1,0:T(8,128)(2,1)}, bf16[64,6144]{1,0:T(8,128)(2,1)}, bf16[6...) custom-call(bf16[512,1536]{1,0:T(8,128)(2,1)} %get-tuple-element.70.refs_0_,, ...), custom_call_target="tpu_custom_call" | custom-call | flops 9663676416 | bytes 26738688 | tf_op jit(solution)/shard_map/pallas_call | solution.py:161
  227.0 3.0 collective-permute-start.20
  230.0 1.5 collective-permute-start.21
  231.4 1.4 collective-permute-start.26
  232.8 8.4 %collective-permute-done.20.b1 = bf16[64,6144]{1,0:T(8,128)(2,1)S(1)} collective-permute-done((bf16[64,6144]{1,0:T(8,128)(2,1)}, bf16[64,6144]{1,0:T(8,128)(2,1)S(1)}, u32[]{:S(2)}, u32[]{:S(2)}) %collective-permute-start.20) | collective-permute-done | bytes 786464 | tf_op jit(solution)/shard_map/ppermute | solution.py:53
  241.3 4.3 %collective-permute-done.21.b2 = bf16[64,6144]{1,0:T(8,128)(2,1)} collective-permute-done((bf16[64,6144]{1,0:T(8,128)(2,1)}, bf16[64,6144]{1,0:T(8,128)(2,1)}, u32[]{:S(2)}, u32[]{:S(2)}) %collective-permute-start.21) | collective-permute-done | bytes 786464 | tf_op jit(solution)/shard_map/ppermute | solution.py:53
  245.6 4.1 %shard_map.136 = (bf16[64,6144]{1,0:T(8,128)(2,1)}, bf16[64,6144]{1,0:T(8,128)(2,1)}) custom-call(bf16[64,6144]{1,0:T(8,128)(2,1)} %get-tuple-element.77.a1, bf16[64,6144]{1,0:T(8,128)(2,1)} %copy-done.8, bf16[64,6144]{1,0:T(8,128)(2,1)} %get-tuple-element.79.a2, bf16[64,6144]{1,0:T(8,128)(2,1)} %collective-permute-done.21.b2), custom_call_target="tpu_custom_call" | custom-call | tf_op jit(solution)/shard_map/pallas_call | solution.py:187
  249.6 1.6 collective-permute-start.27
  251.3 2.8 collective-permute-start.19
  254.1 1.9 collective-permute-start.22
  256.0 7.7 %collective-permute-done.27.c = bf16[64,6144]{1,0:T(8,128)(2,1)} collective-permute-done((bf16[64,6144]{1,0:T(8,128)(2,1)}, bf16[64,6144]{1,0:T(8,128)(2,1)}, u32[]{:S(2)}, u32[]{:S(2)}) %collective-permute-start.27) | collective-permute-done | bytes 786464 | tf_op jit(solution)/shard_map/ppermute | solution.py:53
  263.7 3.6 %shard_map.138 = (bf16[16,6144]{1,0:T(8,128)(2,1)}, bf16[16,6144]{1,0:T(8,128)(2,1)}, bf16[16,6144]{1,0:T(8,128)(2,1)}, bf16[16,6144]{1,0:T(8,128)(2,1)}) custom-call(bf16[64,6144]{1,0:T(8,128)(2,1)} %get-tuple-element.86.a, bf16[64,6144]{1,0:T(8,128)(2,1)} %collective-permute-done.26.b, bf16[64,6144]{1,0:T(8,128)(2,1)} %collective-permute-done.27.c), custom_call_target="tpu_custom_call" | custom-call | tf_op jit(solution)/shard_map/pallas_call | solution.py:207
  267.3 2.3 collective-permute-start.28
  269.6 2.1 collective-permute-start.29
  271.7 2.0 collective-permute-start.30
  274.6 3.7 %shard_map.137 = (bf16[16,6144]{1,0:T(8,128)(2,1)}, bf16[16,6144]{1,0:T(8,128)(2,1)}, bf16[16,6144]{1,0:T(8,128)(2,1)}, bf16[16,6144]{1,0:T(8,128)(2,1)}) custom-call(bf16[64,6144]{1,0:T(8,128)(2,1)} %get-tuple-element.75.a, bf16[64,6144]{1,0:T(8,128)(2,1)} %copy-done.7, bf16[64,6144]{1,0:T(8,128)(2,1)} %collective-permute-done.22.c), custom_call_target="tpu_custom_call" | custom-call | tf_op jit(solution)/shard_map/pallas_call | solution.py:207
  278.3 1.8 collective-permute-start.23
  280.1 2.5 collective-permute-start.25
  282.6 1.3 dynamic-slice_bitcast_fusion.place_ref
  283.8 4.4 %collective-permute-done.24.c = bf16[16,6144]{1,0:T(8,128)(2,1)} collective-permute-done((bf16[16,6144]{1,0:T(8,128)(2,1)}, bf16[16,6144]{1,0:T(8,128)(2,1)}, u32[]{:S(2)}, u32[]{:S(2)}) %collective-permute-start.24) | collective-permute-done | bytes 196640 | tf_op jit(solution)/shard_map/ppermute | solution.py:53
  288.2 5.6 %shard_map.139 = bf16[8,32,768]{2,1,0:T(8,128)(2,1)} custom-call(s32[8]{0:T(128)} %dynamic-slice_bitcast_fusion.place_ref, bf16[16,6144]{1,0:T(8,128)(2,1)} %get-tuple-element.82.a, bf16[16,6144]{1,0:T(8,128)(2,1)} %collective-permute-done.23.b, bf16[16,6144]{1,0:T(8,128)(2,1)} %collective-permute-done.24.c, bf16[16,6144]{1,0:T(8,128)(2,1)} %collective-permute-done.25.d, ...), custom_call_target="tpu_custom_call" | custom-call | tf_op jit(solution)/shard_map/pallas_call | solution.py:228
  293.8 18.0 %all_to_all.22 = bf16[8,32,768]{2,1,0:T(8,128)(2,1)S(1)} all-to-all(bf16[8,32,768]{2,1,0:T(8,128)(2,1)} %shard_map.139), channel_id=1, replica_groups=mesh['row'=16,'col'=8] {'col'}, dimensions={0} | all-to-all | bytes 786432 | tf_op jit(solution)/shard_map/all_to_all | solution.py:242
  311.8 1.5 fusion.1
  (76 shorter events, 5.5 us)
Async XLA Ops:
  6.5 1.7 copy-start.15
  6.5 99.2 %all-gather.6.cloned.1.call-start = ((), (), s32[]{:S(2)}) async-start(), calls=%async_computation.5 | async-start | bytes 1769472 | tf_op jit(solution)/shard_map/all_gather | solution.py:319
  8.2 27.9 %copy-start = (bf16[1536,768]{1,0:T(8,128)(2,1)}, bf16[1536,768]{1,0:T(8,128)(2,1)S(1)}, u32[]{:S(2)}) copy-start(bf16[1536,768]{1,0:T(8,128)(2,1)S(1)} %copy.63.refs_3_) | copy-start | bytes 7077892
  8.2 1.5 copy-start.3
  8.2 15.0 %copy-start.14 = (f32[768]{0:T(1024)S(1)}, f32[768]{0:T(1024)}, u32[]{:S(2)}) copy-start(f32[768]{0:T(1024)} %param.15) | copy-start | bytes 9220
  9.0 179.1 %all-gather.4.cloned.1.call-start = ((), (), s32[]{:S(2)}) async-start(), calls=%async_computation.4 | async-start | bytes 21233664 | tf_op jit(solution)/shard_map/all_gather | solution.py:318
  26.2 19.7 %all-to-all-start = ((bf16[16,32,768]{2,1,0:T(8,128)(2,1)}), bf16[16,32,768]{2,1,0:T(8,128)(2,1)}, u32[]{:S(2)}, u32[]{:S(2)}) async-start(bf16[16,32,768]{2,1,0:T(8,128)(2,1)} %bitcast.2), calls=%async_computation | async-start | bytes 1572864 | tf_op jit(solution)/shard_map/all_to_all | solution.py:242
  34.1 40.7 %collective-permute-start = (bf16[1536,768]{1,0:T(8,128)(2,1)S(1)}, bf16[1536,768]{1,0:T(8,128)(2,1)}, u32[]{:S(2)}, u32[]{:S(2)}) collective-permute-start(bf16[1536,768]{1,0:T(8,128)(2,1)S(1)} %copy.63.refs_3_), channel_id=1, source_target_pairs={{0,2},{1,7},{2,4},{3,1},{4,6},{5,3},{6,0},{7,5},{8,10},{9,15},{10,... | collective-permute-start | bytes 7077896 | tf_op jit(solution)/shard_map/ppermute | solution.py:53
  36.1 38.7 %collective-permute-start.1 = (bf16[1536,768]{1,0:T(8,128)(2,1)S(1)}, bf16[1536,768]{1,0:T(8,128)(2,1)}, u32[]{:S(2)}, u32[]{:S(2)}) collective-permute-start(bf16[1536,768]{1,0:T(8,128)(2,1)S(1)} %copy.63.refs_3_), channel_id=1, source_target_pairs={{0,1},{1,0},{2,3},{3,2},{4,5},{5,4},{6,7},{7,6},{8,9},{9,8},{10,11... | collective-permute-start | bytes 7077896 | tf_op jit(solution)/shard_map/ppermute | solution.py:62
  45.9 2.6 copy-start.2
  45.9 2.6 copy-start.10
  48.4 1.0 copy-start.9
  74.8 11.9 %copy-start.11 = (f32[256,512]{1,0:T(8,128)S(1)}, f32[256,512]{1,0:T(8,128)}, u32[]{:S(2)}) copy-start(f32[256,512]{1,0:T(8,128)} %constant.30.clone) | copy-start | bytes 1572868
  74.8 31.0 %collective-permute-start.2 = (bf16[1536,768]{1,0:T(8,128)(2,1)}, bf16[1536,768]{1,0:T(8,128)(2,1)}, u32[]{:S(2)}, u32[]{:S(2)}) collective-permute-start(bf16[1536,768]{1,0:T(8,128)(2,1)} %get-tuple-element.50.refs_1_), channel_id=1, source_target_pairs={{0,1},{1,0},{2,3},{3,2},{4,5},{5,4},{6,7},{7,6},{8,9},{9,8},{10,11... | collective-permute-start | bytes 7077896 | tf_op jit(solution)/shard_map/ppermute | solution.py:62
  108.4 7.7 %collective-permute-start.6 = (bf16[16,6144]{1,0:T(8,128)(2,1)}, bf16[16,6144]{1,0:T(8,128)(2,1)S(1)}, u32[]{:S(2)}, u32[]{:S(2)}) collective-permute-start(bf16[16,6144]{1,0:T(8,128)(2,1)} %get-tuple-element.53), channel_id=1, source_target_pairs={{0,8},{1,9},{2,10},{3,11},{4,12},{5,13},{6,14},{7,15},{8,16},{9,17... | collective-permute-start | bytes 589832 | tf_op jit(solution)/shard_map/ppermute | solution.py:53
  110.4 7.9 %collective-permute-start.7 = (bf16[16,6144]{1,0:T(8,128)(2,1)}, bf16[16,6144]{1,0:T(8,128)(2,1)S(1)}, u32[]{:S(2)}, u32[]{:S(2)}) collective-permute-start(bf16[16,6144]{1,0:T(8,128)(2,1)} %get-tuple-element.53), channel_id=1, source_target_pairs={{0,24},{1,25},{2,26},{3,27},{4,28},{5,29},{6,30},{7,31},{8,0},{9,1... | collective-permute-start | bytes 589832 | tf_op jit(solution)/shard_map/ppermute | solution.py:53
  111.6 9.3 %collective-permute-start.8 = (bf16[16,6144]{1,0:T(8,128)(2,1)}, bf16[16,6144]{1,0:T(8,128)(2,1)S(1)}, u32[]{:S(2)}, u32[]{:S(2)}) collective-permute-start(bf16[16,6144]{1,0:T(8,128)(2,1)} %get-tuple-element.53), channel_id=1, source_target_pairs={{0,16},{1,17},{2,18},{3,19},{4,20},{5,21},{6,22},{7,23},{8,24},{9,... | collective-permute-start | bytes 589832 | tf_op jit(solution)/shard_map/ppermute | solution.py:53
  113.4 9.4 %collective-permute-start.3 = (bf16[16,6144]{1,0:T(8,128)(2,1)}, bf16[16,6144]{1,0:T(8,128)(2,1)S(1)}, u32[]{:S(2)}, u32[]{:S(2)}) collective-permute-start(bf16[16,6144]{1,0:T(8,128)(2,1)} %get-tuple-element.52), channel_id=1, source_target_pairs={{0,32},{1,33},{2,34},{3,35},{4,36},{5,37},{6,38},{7,39},{8,40},{9,... | collective-permute-start | bytes 589832 | tf_op jit(solution)/shard_map/ppermute | solution.py:53
  114.4 8.4 %collective-permute-start.4 = (bf16[16,6144]{1,0:T(8,128)(2,1)}, bf16[16,6144]{1,0:T(8,128)(2,1)S(1)}, u32[]{:S(2)}, u32[]{:S(2)}) collective-permute-start(bf16[16,6144]{1,0:T(8,128)(2,1)} %get-tuple-element.52), channel_id=1, source_target_pairs={{0,96},{1,97},{2,98},{3,99},{4,100},{5,101},{6,102},{7,103},{8,104... | collective-permute-start | bytes 589832 | tf_op jit(solution)/shard_map/ppermute | solution.py:53
  116.0 8.3 %collective-permute-start.5 = (bf16[16,6144]{1,0:T(8,128)(2,1)}, bf16[16,6144]{1,0:T(8,128)(2,1)S(1)}, u32[]{:S(2)}, u32[]{:S(2)}) collective-permute-start(bf16[16,6144]{1,0:T(8,128)(2,1)} %get-tuple-element.52), channel_id=1, source_target_pairs={{0,64},{1,65},{2,66},{3,67},{4,68},{5,69},{6,70},{7,71},{8,72},{9,... | collective-permute-start | bytes 589832 | tf_op jit(solution)/shard_map/ppermute | solution.py:53
  126.3 23.9 %copy-start.1 = (bf16[64,6144]{1,0:T(8,128)(2,1)S(1)}, bf16[64,6144]{1,0:T(8,128)(2,1)}, u32[]{:S(2)}) copy-start(bf16[64,6144]{1,0:T(8,128)(2,1)} %get-tuple-element.56.refs_4_) | copy-start | bytes 2359300
  126.3 27.6 %copy-start.13 = (f32[1536]{0:T(1024)S(1)}, f32[1536]{0:T(1024)}, u32[]{:S(2)}) copy-start(f32[1536]{0:T(1024)} %param.18) | copy-start | bytes 18436
  126.3 61.7 %collective-permute-start.15 = (bf16[1536,768]{1,0:T(8,128)(2,1)}, bf16[1536,768]{1,0:T(8,128)(2,1)}, u32[]{:S(2)}, u32[]{:S(2)}) collective-permute-start(bf16[1536,768]{1,0:T(8,128)(2,1)} %get-tuple-element.60.refs_1_), channel_id=1, source_target_pairs={{0,6},{1,3},{2,0},{3,5},{4,2},{5,7},{6,4},{7,1},{8,14},{9,11},{10,... | collective-permute-start | bytes 7077896 | tf_op jit(solution)/shard_map/ppermute | solution.py:53
  126.6 11.5 %collective-permute-start.10 = (bf16[64,6144]{1,0:T(8,128)(2,1)}, bf16[64,6144]{1,0:T(8,128)(2,1)}, u32[]{:S(2)}, u32[]{:S(2)}) collective-permute-start(bf16[64,6144]{1,0:T(8,128)(2,1)} %get-tuple-element.56.refs_4_), channel_id=1, source_target_pairs={{0,32},{1,97},{2,34},{3,99},{4,36},{5,101},{6,38},{7,103},{8,40},{... | collective-permute-start | bytes 2359304 | tf_op jit(solution)/shard_map/ppermute | solution.py:53
  128.3 15.6 %collective-permute-start.9 = (bf16[64,6144]{1,0:T(8,128)(2,1)}, bf16[64,6144]{1,0:T(8,128)(2,1)S(1)}, u32[]{:S(2)}, u32[]{:S(2)}) collective-permute-start(bf16[64,6144]{1,0:T(8,128)(2,1)} %get-tuple-element.55.refs_0_), channel_id=1, source_target_pairs={{0,8},{1,25},{2,10},{3,27},{4,12},{5,29},{6,14},{7,31},{8,16},{9,1... | collective-permute-start | bytes 2359304 | tf_op jit(solution)/shard_map/ppermute | solution.py:53
  129.7 21.6 %collective-permute-start.11 = (bf16[64,6144]{1,0:T(8,128)(2,1)}, bf16[64,6144]{1,0:T(8,128)(2,1)}, u32[]{:S(2)}, u32[]{:S(2)}) collective-permute-start(bf16[64,6144]{1,0:T(8,128)(2,1)} %get-tuple-element.55.refs_0_), channel_id=1, source_target_pairs={{0,24},{1,9},{2,26},{3,11},{4,28},{5,13},{6,30},{7,15},{8,0},{9,17... | collective-permute-start | bytes 2359304 | tf_op jit(solution)/shard_map/ppermute | solution.py:53
  144.0 0.9 copy-start.5
  144.9 60.3 %collective-permute-start.16 = (bf16[1536,768]{1,0:T(8,128)(2,1)}, bf16[1536,768]{1,0:T(8,128)(2,1)}, u32[]{:S(2)}, u32[]{:S(2)}) collective-permute-start(bf16[1536,768]{1,0:T(8,128)(2,1)} %get-tuple-element.69.refs_2_), channel_id=1, source_target_pairs={{0,2},{1,7},{2,4},{3,1},{4,6},{5,3},{6,0},{7,5},{8,10},{9,15},{10,... | collective-permute-start | bytes 7077896 | tf_op jit(solution)/shard_map/ppermute | solution.py:53
  150.2 17.6 %collective-permute-start.13 = (bf16[64,6144]{1,0:T(8,128)(2,1)S(1)}, bf16[64,6144]{1,0:T(8,128)(2,1)S(1)}, u32[]{:S(2)}, u32[]{:S(2)}) collective-permute-start(bf16[64,6144]{1,0:T(8,128)(2,1)S(1)} %copy-done.1), channel_id=1, source_target_pairs={{0,96},{1,33},{2,98},{3,35},{4,100},{5,37},{6,102},{7,39},{8,104},... | collective-permute-start | bytes 2359304 | tf_op jit(solution)/shard_map/ppermute | solution.py:53
  150.2 17.6 %collective-permute-start.12 = (bf16[64,6144]{1,0:T(8,128)(2,1)}, bf16[64,6144]{1,0:T(8,128)(2,1)}, u32[]{:S(2)}, u32[]{:S(2)}) collective-permute-start(bf16[64,6144]{1,0:T(8,128)(2,1)} %get-tuple-element.58.refs_1_), channel_id=1, source_target_pairs={{0,8},{1,25},{2,10},{3,27},{4,12},{5,29},{6,14},{7,31},{8,16},{9,1... | collective-permute-start | bytes 2359304 | tf_op jit(solution)/shard_map/ppermute | solution.py:53
  151.3 19.0 %collective-permute-start.14 = (bf16[64,6144]{1,0:T(8,128)(2,1)}, bf16[64,6144]{1,0:T(8,128)(2,1)}, u32[]{:S(2)}, u32[]{:S(2)}) collective-permute-start(bf16[64,6144]{1,0:T(8,128)(2,1)} %get-tuple-element.59.refs_5_), channel_id=1, source_target_pairs={{0,32},{1,97},{2,34},{3,99},{4,36},{5,101},{6,38},{7,103},{8,40},{... | collective-permute-start | bytes 2359304 | tf_op jit(solution)/shard_map/ppermute | solution.py:53
  167.9 20.2 %copy-start.6 = (bf16[64,6144]{1,0:T(8,128)(2,1)}, bf16[64,6144]{1,0:T(8,128)(2,1)S(1)}, u32[]{:S(2)}) copy-start(bf16[64,6144]{1,0:T(8,128)(2,1)S(1)} %collective-permute-done.13.refs_6_) | copy-start | bytes 2359300
  188.1 17.7 %collective-permute-start.17 = (bf16[1536,768]{1,0:T(8,128)(2,1)}, bf16[1536,768]{1,0:T(8,128)(2,1)}, u32[]{:S(2)}, u32[]{:S(2)}) collective-permute-start(bf16[1536,768]{1,0:T(8,128)(2,1)} %get-tuple-element.71.refs_3_), channel_id=1, source_target_pairs={{0,1},{1,0},{2,3},{3,2},{4,5},{5,4},{6,7},{7,6},{8,9},{9,8},{10,11... | collective-permute-start | bytes 7077896 | tf_op jit(solution)/shard_map/ppermute | solution.py:62
  205.2 5.1 %collective-permute-start.18 = (bf16[1536,768]{1,0:T(8,128)(2,1)}, bf16[1536,768]{1,0:T(8,128)(2,1)}, u32[]{:S(2)}, u32[]{:S(2)}) collective-permute-start(bf16[1536,768]{1,0:T(8,128)(2,1)} %get-tuple-element.72.refs_4_), channel_id=1, source_target_pairs={{0,1},{1,0},{2,3},{3,2},{4,5},{5,4},{6,7},{7,6},{8,9},{9,8},{10,11... | collective-permute-start | bytes 7077896 | tf_op jit(solution)/shard_map/ppermute | solution.py:62
  227.0 14.3 %collective-permute-start.20 = (bf16[64,6144]{1,0:T(8,128)(2,1)}, bf16[64,6144]{1,0:T(8,128)(2,1)S(1)}, u32[]{:S(2)}, u32[]{:S(2)}) collective-permute-start(bf16[64,6144]{1,0:T(8,128)(2,1)} %get-tuple-element.78), channel_id=1, source_target_pairs={{0,24},{1,9},{2,26},{3,11},{4,28},{5,13},{6,30},{7,15},{8,0},{9,17... | collective-permute-start | bytes 2359304 | tf_op jit(solution)/shard_map/ppermute | solution.py:53
  230.0 15.6 %collective-permute-start.21 = (bf16[64,6144]{1,0:T(8,128)(2,1)}, bf16[64,6144]{1,0:T(8,128)(2,1)}, u32[]{:S(2)}, u32[]{:S(2)}) collective-permute-start(bf16[64,6144]{1,0:T(8,128)(2,1)} %get-tuple-element.80), channel_id=1, source_target_pairs={{0,96},{1,33},{2,98},{3,35},{4,100},{5,37},{6,102},{7,39},{8,104},... | collective-permute-start | bytes 2359304 | tf_op jit(solution)/shard_map/ppermute | solution.py:53
  231.4 24.6 %collective-permute-start.26 = (bf16[64,6144]{1,0:T(8,128)(2,1)}, bf16[64,6144]{1,0:T(8,128)(2,1)}, u32[]{:S(2)}, u32[]{:S(2)}) collective-permute-start(bf16[64,6144]{1,0:T(8,128)(2,1)} %get-tuple-element.87), channel_id=1, source_target_pairs={{0,32},{1,97},{2,34},{3,99},{4,36},{5,101},{6,38},{7,103},{8,40},{... | collective-permute-start | bytes 2359304 | tf_op jit(solution)/shard_map/ppermute | solution.py:53
  241.3 4.3 %copy-start.8 = (bf16[64,6144]{1,0:T(8,128)(2,1)}, bf16[64,6144]{1,0:T(8,128)(2,1)S(1)}, u32[]{:S(2)}) copy-start(bf16[64,6144]{1,0:T(8,128)(2,1)S(1)} %collective-permute-done.20.b1) | copy-start | bytes 2359300
  249.6 14.0 %collective-permute-start.27 = (bf16[64,6144]{1,0:T(8,128)(2,1)}, bf16[64,6144]{1,0:T(8,128)(2,1)}, u32[]{:S(2)}, u32[]{:S(2)}) collective-permute-start(bf16[64,6144]{1,0:T(8,128)(2,1)} %get-tuple-element.88), channel_id=1, source_target_pairs={{0,96},{1,33},{2,98},{3,35},{4,100},{5,37},{6,102},{7,39},{8,104},... | collective-permute-start | bytes 2359304 | tf_op jit(solution)/shard_map/ppermute | solution.py:53
  251.3 22.4 %collective-permute-start.19 = (bf16[64,6144]{1,0:T(8,128)(2,1)}, bf16[64,6144]{1,0:T(8,128)(2,1)S(1)}, u32[]{:S(2)}, u32[]{:S(2)}) collective-permute-start(bf16[64,6144]{1,0:T(8,128)(2,1)} %get-tuple-element.76), channel_id=1, source_target_pairs={{0,8},{1,25},{2,10},{3,27},{4,12},{5,29},{6,14},{7,31},{8,16},{9,1... | collective-permute-start | bytes 2359304 | tf_op jit(solution)/shard_map/ppermute | solution.py:53
  254.1 19.6 %collective-permute-start.22 = (bf16[64,6144]{1,0:T(8,128)(2,1)}, bf16[64,6144]{1,0:T(8,128)(2,1)}, u32[]{:S(2)}, u32[]{:S(2)}) collective-permute-start(bf16[64,6144]{1,0:T(8,128)(2,1)} %get-tuple-element.81), channel_id=1, source_target_pairs={{0,24},{1,9},{2,26},{3,11},{4,28},{5,13},{6,30},{7,15},{8,0},{9,17... | collective-permute-start | bytes 2359304 | tf_op jit(solution)/shard_map/ppermute | solution.py:53
  267.3 12.8 %collective-permute-start.28 = (bf16[16,6144]{1,0:T(8,128)(2,1)}, bf16[16,6144]{1,0:T(8,128)(2,1)S(1)}, u32[]{:S(2)}, u32[]{:S(2)}) collective-permute-start(bf16[16,6144]{1,0:T(8,128)(2,1)} %get-tuple-element.90), channel_id=1, source_target_pairs={{0,24},{1,25},{2,26},{3,27},{4,28},{5,29},{6,30},{7,31},{8,0},{9,1... | collective-permute-start | bytes 589832 | tf_op jit(solution)/shard_map/ppermute | solution.py:53
  269.6 14.2 %collective-permute-start.29 = (bf16[16,6144]{1,0:T(8,128)(2,1)}, bf16[16,6144]{1,0:T(8,128)(2,1)}, u32[]{:S(2)}, u32[]{:S(2)}) collective-permute-start(bf16[16,6144]{1,0:T(8,128)(2,1)} %get-tuple-element.91), channel_id=1, source_target_pairs={{0,8},{1,9},{2,10},{3,11},{4,12},{5,13},{6,14},{7,15},{8,16},{9,17... | collective-permute-start | bytes 589832 | tf_op jit(solution)/shard_map/ppermute | solution.py:53
  271.7 12.1 %collective-permute-start.30 = (bf16[16,6144]{1,0:T(8,128)(2,1)}, bf16[16,6144]{1,0:T(8,128)(2,1)}, u32[]{:S(2)}, u32[]{:S(2)}) collective-permute-start(bf16[16,6144]{1,0:T(8,128)(2,1)} %get-tuple-element.92), channel_id=1, source_target_pairs={{0,16},{1,17},{2,18},{3,19},{4,20},{5,21},{6,22},{7,23},{8,24},{9,... | collective-permute-start | bytes 589832 | tf_op jit(solution)/shard_map/ppermute | solution.py:53
  273.7 0.9 copy-start.7
  274.6 37.2 %copy-start.4 = (f32[256,768]{1,0:T(8,128)S(1)}, f32[256,768]{1,0:T(8,128)}, u32[]{:S(2)}) copy-start(f32[256,768]{1,0:T(8,128)} %get-tuple-element.102) | copy-start | bytes 2359300
  278.3 5.6 %collective-permute-start.23 = (bf16[16,6144]{1,0:T(8,128)(2,1)}, bf16[16,6144]{1,0:T(8,128)(2,1)}, u32[]{:S(2)}, u32[]{:S(2)}) collective-permute-start(bf16[16,6144]{1,0:T(8,128)(2,1)} %get-tuple-element.83), channel_id=1, source_target_pairs={{0,96},{1,97},{2,98},{3,99},{4,100},{5,101},{6,102},{7,103},{8,104... | collective-permute-start | bytes 589832 | tf_op jit(solution)/shard_map/ppermute | solution.py:53
  280.1 8.2 %collective-permute-start.24 = (bf16[16,6144]{1,0:T(8,128)(2,1)}, bf16[16,6144]{1,0:T(8,128)(2,1)}, u32[]{:S(2)}, u32[]{:S(2)}) collective-permute-start(bf16[16,6144]{1,0:T(8,128)(2,1)} %get-tuple-element.84), channel_id=1, source_target_pairs={{0,32},{1,33},{2,34},{3,35},{4,36},{5,37},{6,38},{7,39},{8,40},{9,... | collective-permute-start | bytes 589832 | tf_op jit(solution)/shard_map/ppermute | solution.py:53
  280.1 8.2 %copy-start.12 = (bf16[16,6144]{1,0:T(8,128)(2,1)}, bf16[16,6144]{1,0:T(8,128)(2,1)S(1)}, u32[]{:S(2)}) copy-start(bf16[16,6144]{1,0:T(8,128)(2,1)S(1)} %collective-permute-done.28.f) | copy-start | bytes 589828
  280.1 8.1 %collective-permute-start.25 = (bf16[16,6144]{1,0:T(8,128)(2,1)}, bf16[16,6144]{1,0:T(8,128)(2,1)}, u32[]{:S(2)}, u32[]{:S(2)}) collective-permute-start(bf16[16,6144]{1,0:T(8,128)(2,1)} %get-tuple-element.85), channel_id=1, source_target_pairs={{0,64},{1,65},{2,66},{3,67},{4,68},{5,69},{6,70},{7,71},{8,72},{9,... | collective-permute-start | bytes 589832 | tf_op jit(solution)/shard_map/ppermute | solution.py:53
Sparse Core Ops, SparseCore 0:
  9.1 28.0 all-gather.5
  38.9 118.8 all-gather.3

commit v4 on v3

--- a/solution.py
+++ b/solution.py
@@ -66,28 +66,24 @@
     return pltpu.CompilerParams(vmem_limit_bytes=mb * MB)
 
 
-def act_kernel(moved_ref, gain_ref, first_ref, second_ref):
+def act_kernel(moved_ref, first_ref, second_ref):
     cols, _, chans = moved_ref.shape
     half = first_ref.shape[0]
-    values = moved_ref[...].astype(F32)
+    values = moved_ref[:, : 2 * half, :].astype(F32)
+    gains = jnp.sum(moved_ref[:, 2 * half :, :].astype(F32)[:, :3], axis=1)
     mean = jnp.sum(jnp.sum(values, axis=0), axis=-1, keepdims=True) / (cols * chans)
     square = jnp.sum(jnp.sum(values * values, axis=0), axis=-1, keepdims=True) / (cols * chans)
     scale = 1.0 / jnp.sqrt(square - mean * mean + 1e-05)
     for j in range(cols):
-        part = (values[j] - mean) * scale * gain_ref[j, :1, :]
-        part = part.astype(BF)
+        part = ((values[j] - mean) * scale * gains[j][None, :]).astype(BF)
         first_ref[:, j * chans : (j + 1) * chans] = part[:half]
         second_ref[:, j * chans : (j + 1) * chans] = part[half:]
 
 
-def normalize(moved, gains, half):
+def normalize(moved, half):
     cols, _, chans = moved.shape
     shape = jax.ShapeDtypeStruct((half, cols * chans), BF)
-    return pl.pallas_call(
-        act_kernel,
-        out_shape=(shape, shape),
-        compiler_params=params(63),
-    )(moved, gains)
+    return pl.pallas_call(act_kernel, out_shape=(shape, shape), compiler_params=params(16))(moved)
 
 
 def mm1_kernel(*refs):
@@ -124,7 +120,7 @@
         out_specs=pl.BlockSpec((tokens, tile), lambda i: (0, i)),
         out_shape=jax.ShapeDtypeStruct((tokens, width), BF),
         scratch_shapes=[pltpu.VMEM((tokens, depth), BF), pltpu.SemaphoreType.DMA((len(pieces),))],
-        compiler_params=params(63),
+        compiler_params=params(40),
         cost_estimate=pl.CostEstimate(
             flops=2 * tokens * depth * width,
             bytes_accessed=2 * (tokens * depth + depth * width),
@@ -166,7 +162,7 @@
         out_specs=[pl.BlockSpec((rows, chans), lambda j: (0, j))] * count,
         out_shape=[jax.ShapeDtypeStruct((rows, cols * chans), BF)] * count,
         scratch_shapes=[pltpu.VMEM((2, depth, chans), BF), pltpu.SemaphoreType.DMA((2,))],
-        compiler_params=params(63),
+        compiler_params=params(40),
         cost_estimate=pl.CostEstimate(
             flops=2 * tokens * depth * cols * chans,
             bytes_accessed=2 * (tokens * depth + depth * cols * chans + tokens * cols * chans),
@@ -182,7 +178,7 @@
 
 def add_pairs(*parts):
     rows, width = parts[0].shape
-    tile = width // 4
+    tile = width // 2
     block = pl.BlockSpec((rows, tile), lambda j: (0, j))
     return pl.pallas_call(
         pair_kernel,
@@ -190,7 +186,7 @@
         in_specs=[block] * 4,
         out_specs=[block] * 2,
         out_shape=[jax.ShapeDtypeStruct((rows, width), BF)] * 2,
-        compiler_params=params(63),
+        compiler_params=params(24),
     )(*parts)
 
 
@@ -203,38 +199,37 @@
 
 def add_pieces(*parts):
     rows, width = parts[0].shape
-    tile = width // 4
+    tile = width // 2
     return pl.pallas_call(
         add_kernel,
         grid=(width // tile,),
         in_specs=[pl.BlockSpec((rows, tile), lambda j: (0, j))] * len(parts),
         out_specs=[pl.BlockSpec((rows // SIDE, tile), lambda j: (0, j))] * SIDE,
         out_shape=[jax.ShapeDtypeStruct((rows // SIDE, width), BF)] * SIDE,
-        compiler_params=params(63),
+        compiler_params=params(24),
     )(*parts)
 
 
 def last_kernel(place_ref, a, b, c, d, e, f, g, h, o_ref):
     half = a.shape[0]
-    top = (a[...].astype(F32) + b[...].astype(F32)) + (c[...].astype(F32) + d[...].astype(F32))
-    low = (e[...].astype(F32) + f[...].astype(F32)) + (g[...].astype(F32) + h[...].astype(F32))
-    o_ref[0, :half, :] = top.astype(BF)
-    o_ref[0, half:, :] = low.astype(BF)
+    cols, _, chans = o_ref.shape
+    for j in range(cols):
+        at = pl.ds(j * chans, chans)
+        top, low = [
+            sum(p[:, at].astype(F32) for p in parts).astype(BF)
+            for parts in ((a, b, c, d), (e, f, g, h))
+        ]
+        o_ref[place_ref[j], :half, :] = top
+        o_ref[place_ref[j], half:, :] = low
 
 
 def add_last(place, first, second, cols):
     half, width = first[0].shape
-    chans = width // cols
     return pl.pallas_call(
         last_kernel,
-        grid_spec=pltpu.PrefetchScalarGridSpec(
-            num_scalar_prefetch=1,
-            grid=(cols,),
-            in_specs=[pl.BlockSpec((half, chans), lambda j, place: (0, j))] * 8,
-            out_specs=pl.BlockSpec((1, 2 * half, chans), lambda j, place: (place[j], 0, 0)),
-        ),
-        out_shape=jax.ShapeDtypeStruct((cols, 2 * half, chans), BF),
-        compiler_params=params(63),
+        in_specs=[pl.BlockSpec(memory_space=pltpu.SMEM)] + [pl.BlockSpec(memory_space=pltpu.VMEM)] * 8,
+        out_shape=jax.ShapeDtypeStruct((cols, 2 * half, width // cols), BF),
+        compiler_params=params(16),
     )(place, *first, *second)
 
 
@@ -255,11 +250,11 @@
         out_specs=[anywhere] * count,
         out_shape=[jax.ShapeDtypeStruct(v.shape, v.dtype) for v in values],
         input_output_aliases={i: i for i in range(count)},
-        compiler_params=params(62),
+        compiler_params=params(1),
     )(*values, *others)
 
 
-def spectral(image, filter_bank, gain_first, late):
+def spectral(image, filter_bank, gain_first):
     rows_here, width, chans = image.shape
     groups = lax.axis_size("row")
     width_all = chans * lax.axis_size("col")
@@ -284,8 +279,13 @@
     )
     back = jnp.dot(three, filt, precision=high).astype(BF)
     back = exchange(back.reshape(groups, -1, chans), "row").reshape(-1, chans)
-    back, *late = tie([back, *late], [])
-    return source + jnp.dot(four, back.astype(F32), precision=high), late
+    return source + jnp.dot(four, back.astype(F32), precision=high)
+
+
+def three_parts(gain):
+    top = lax.reduce_precision(gain, 8, 7)
+    mid = lax.reduce_precision(gain - top, 8, 7)
+    return jnp.stack([top, mid, gain - top - mid]).astype(BF)
 
 
 def block_places():
@@ -314,19 +314,23 @@
 def on_device(image, filter_bank, gain_first, gain_second, w_in, b_in, w_out, b_out):
     rows_here, width, chans = image.shape
     cols = lax.axis_size("col")
-    padded = jnp.pad(gain_second[None], ((0, 63), (0, 0)))
     w_in_all = lax.all_gather(w_in, "col", axis=0, tiled=True)
-    gains = lax.all_gather(padded, "col", axis=0, tiled=False)
-    one = hop(w_out, "x", APART)
-    own_swap = swap_cores(w_out)
-    resid, (one, own_swap) = spectral(image, filter_bank, gain_first, [one, own_swap])
-    one_swap = swap_cores(one)
+    resid = spectral(image, filter_bank, gain_first)
     tokens = rows_here * width
     own = tokens // cols
     half = own // 2
-    moved = exchange(resid.astype(BF).reshape(cols, own, chans), "col")
-    moved, one, one_swap, later = tie([moved, one, one_swap, w_out], [])
-    first, second = normalize(moved, gains, half)
+    extra = jnp.pad(three_parts(gain_second), ((0, half - 3), (0, 0)))
+    message = jnp.concatenate(
+        [
+            resid.astype(BF).reshape(cols, own, chans),
+            jnp.broadcast_to(extra[None], (cols, half, chans)),
+        ],
+        axis=1,
+    )
+    moved = exchange(message, "col")
+    moved, later = tie([moved, w_out], [])
+    one = hop(later, "x", APART)
+    first, second = normalize(moved, half)
     first, second = gather_near(first, "z"), gather_near(second, "y")
     first, second, later = tie([first, second, later], [])
     two = hop(later, "x", OTHER)
@@ -336,8 +340,8 @@
     three = hop(one, "x", APART)
     first.append(hop(first[1], "y", APART))
     second.append(hop(second[1], "z", APART))
-    *pieces, two = tie(first + second + [two], [])
-    two_swap = swap_cores(two)
+    *pieces, later, one, two = tie(first + second + [later, one, two], [])
+    own_swap, one_swap, two_swap = swap_cores(later), swap_cores(one), swap_cores(two)
     hidden = matmul_in(pieces, w_in_all, b_in)
     hidden, three = tie([hidden, three], [])
     blocks = [later, one, two, three, own_swap, one_swap, two_swap, swap_cores(three)]

time: 322 us -> 326 us (1.012)
  waiting for transfers between devices: 91.5 us -> 138 us
  Pallas kernels: 53.4 us -> 29.4 us
  starting transfers between devices: 69 us -> 46.4 us
  local copies, waits for them, and re-layouts: 12.8 us -> 27.2 us
  blocking collectives: 64.3 us -> 58.2 us
  other arithmetic: 5.8 us -> 2.13 us
    ppermute x27, waiting for transfers between devices: 84.3 us -> 119 us  [hop(): return lax.ppermute(a, ('row', 'col'), pairs)]
    unnamed x33 -> x59, local copies, waits for them, and re-layouts: 3.61 us -> 19.9 us
    ppermute x27, starting transfers between devices: 47.3 us -> 31.3 us  [hop(): return lax.ppermute(a, ('row', 'col'), pairs)]
    all_to_all x1 -> x2, waiting for transfers between devices: 1.99 us -> 15.1 us  [exchange(): return lax.all_to_all(a, axis, split_axis=0, concat_axis=0, tiled=True)]
    ppermute x4, starting transfers between devices: 13.7 us -> 3.44 us  [swap_cores(): return lax.ppermute(a, 'col', pairs)]
    pallas_call x2, Pallas kernels: 7.3 us -> 1.12 us  [add_pieces(): pl.pallas_call(add_kernel, grid=(width // tile,), in_specs=[pl.BlockSpec(...]
    all_to_all x3 -> x2, blocking collectives: 51.1 us -> 45 us  [exchange(): return lax.all_to_all(a, axis, split_axis=0, concat_axis=0, tiled=True)]
    pallas_call x1, Pallas kernels: 5.57 us -> 0.73 us  [add_last(): pl.pallas_call(last_kernel, in_specs=[pl.BlockSpec(memory_space=pltpu.SME...]
  transfers between devices with their start and end apart: 34 -> 34, of which waited for: 14 -> 23; matrix products, arithmetic and copies ran while one was open for 7% -> 6% of each run, Pallas kernels for 10% -> 5%
where the time goes in v4:
time: 326 us; the launch traced here: 325 us
  waiting for transfers between devices  138 us (42%)
  blocking collectives  58.2 us (18%)
  starting transfers between devices  46.4 us (14%)
  Pallas kernels  29.4 us (9%)
  local copies, waits for them, and re-layouts  27.2 us (8%)
  between operations  13.8 us (4%)
  matrix products  9.54 us (3%)
    ppermute x27, waiting for transfers between devices, hop(): return lax.ppermute(a, ('row', 'col'), pairs)  119 us
    all_to_all x2, blocking collectives, exchange(): return lax.all_to_all(a, axis, split_axis=0, concat_axis=0, tiled=True)  45 us
    ppermute x27, starting transfers between devices, hop(): return lax.ppermute(a, ('row', 'col'), pairs)  31.3 us
    unnamed x59, local copies, waits for them, and re-layouts  19.9 us
    all_to_all x2, waiting for transfers between devices, exchange(): return lax.all_to_all(a, axis, split_axis=0, concat_axis=0, tiled=True)  15.1 us
    pallas_call x1, Pallas kernels, matmul_in(): pl.pallas_call(mm1_kernel, grid=(width // tile,), in_specs=[pl.BlockSpec(...  13.7 us
    psum x1, blocking collectives, spectral(): lax.psum((jnp.sum(source, axis=-1), jnp.sum(source * source, axis=-1)), '...  13.2 us
    pallas_call x1, Pallas kernels, matmul_out(): pl.pallas_call(functools.partial(mm2_kernel, cols), grid=(cols,), in_spec...  12.8 us
  transfers between devices with their start and end apart: 34, of which 23 were waited for; matrix products, arithmetic and copies ran while one was open for 6% of the time, Pallas kernels for 5%

profile of v4, /device:TPU:1, one launch (start us, length us, event | category | flops | bytes accessed | tf_op | source)
XLA Modules:
  0.0 324.9 jit_solution(10619704820841808478)
XLA Ops:
  6.5 1.7 copy.57.refs_1_
  8.2 1.0 copy-done.18
  9.5 13.2 %all-reduce.1 = (f32[256]{0:T(256)S(1)}, f32[256]{0:T(256)S(1)}) all-reduce(f32[256]{0:T(256)S(1)} %reduce_sum.25, f32[256]{0:T(256)S(1)} %reduce_sum.23), channel_id=1, replica_groups=mesh['row'=16,'col'=8] {'col'}, use_global_device_ids=true, to_apply=%region_3.0 | all-reduce | flops 512 | bytes 4096 | tf_op jit(solution)/shard_map/psum | solution.py:265
  22.9 1.7 convolution_convert_fusion
  24.6 7.9 %all-to-all-start = ((bf16[16,32,768]{2,1,0:T(8,128)(2,1)}), bf16[16,32,768]{2,1,0:T(8,128)(2,1)}, u32[]{:S(2)}, u32[]{:S(2)}) async-start(bf16[16,32,768]{2,1,0:T(8,128)(2,1)} %bitcast.2), calls=%async_computation | async-start | bytes 1572864 | tf_op jit(solution)/shard_map/all_to_all | solution.py:237
  32.5 2.6 fusion.21
  35.2 1.4 reshape_squeeze.6
  36.6 2.3 reshape_squeeze.7
  38.9 5.4 %all-to-all-done = bf16[16,32,768]{2,1,0:T(8,128)(2,1)} async-done(((bf16[16,32,768]{2,1,0:T(8,128)(2,1)}), bf16[16,32,768]{2,1,0:T(8,128)(2,1)}, u32[]{:S(2)}, u32[]{:S(2)}) %all-to-all-start) | async-done | bytes 786464 | tf_op jit(solution)/shard_map/all_to_all | solution.py:237
  44.3 2.5 fusion.23
  46.9 0.9 fusion.7
  47.9 1.8 add_convert_fusion
  49.8 3.7 %all-to-all-start.1 = ((bf16[16,32,768]{2,1,0:T(8,128)(2,1)}), bf16[16,32,768]{2,1,0:T(8,128)(2,1)S(1)}, u32[]{:S(2)}, u32[]{:S(2)}) async-start(bf16[16,32,768]{2,1,0:T(8,128)(2,1)} %bitcast.45), calls=%async_computation.1 | async-start | bytes 1572864 | tf_op jit(solution)/shard_map/all_to_all | solution.py:237
  54.2 9.7 %all-to-all-done.1 = bf16[16,32,768]{2,1,0:T(8,128)(2,1)S(1)} async-done(((bf16[16,32,768]{2,1,0:T(8,128)(2,1)}), bf16[16,32,768]{2,1,0:T(8,128)(2,1)S(1)}, u32[]{:S(2)}, u32[]{:S(2)}) %all-to-all-start.1) | async-done | bytes 786464 | tf_op jit(solution)/shard_map/all_to_all | solution.py:237
  63.9 2.6 fusion.22
  66.6 29.5 %all_to_all.21.refs_0_ = bf16[8,48,768]{2,1,0:T(8,128)(2,1)S(1)} all-to-all(bf16[8,48,768]{2,1,0:T(8,128)(2,1)S(1)} %pad_maximum_fusion.2), channel_id=1, replica_groups=mesh['row'=16,'col'=8] {'col'}, dimensions={0} | all-to-all | bytes 1179648 | tf_op jit(solution)/shard_map/all_to_all | solution.py:237
  97.7 2.4 collective-permute-start.4
  100.0 8.7 %collective-permute-done.3 = bf16[16,6144]{1,0:T(8,128)(2,1)S(1)} collective-permute-done((bf16[16,6144]{1,0:T(8,128)(2,1)S(1)}, bf16[16,6144]{1,0:T(8,128)(2,1)S(1)}, u32[]{:S(2)}, u32[]{:S(2)}) %collective-permute-start.3) | collective-permute-done | bytes 196640 | tf_op jit(solution)/shard_map/ppermute | solution.py:53
  108.9 5.0 %collective-permute-done.1 = bf16[16,6144]{1,0:T(8,128)(2,1)S(1)} collective-permute-done((bf16[16,6144]{1,0:T(8,128)(2,1)S(1)}, bf16[16,6144]{1,0:T(8,128)(2,1)S(1)}, u32[]{:S(2)}, u32[]{:S(2)}) %collective-permute-start.1) | collective-permute-done | bytes 196640 | tf_op jit(solution)/shard_map/ppermute | solution.py:53
  113.9 0.9 collective-permute-done.2
  114.9 20.8 %collective-permute-done.8.refs_2_ = bf16[1536,768]{1,0:T(8,128)(2,1)} collective-permute-done((bf16[1536,768]{1,0:T(8,128)(2,1)S(1)}, bf16[1536,768]{1,0:T(8,128)(2,1)}, u32[]{:S(2)}, u32[]{:S(2)}) %collective-permute-start.8) | collective-permute-done | bytes 2359328 | tf_op jit(solution)/shard_map/ppermute | solution.py:53
  135.7 2.5 collective-permute-start.6
  138.2 2.7 collective-permute-start.7
  140.8 1.1 collective-permute-start.13
  141.9 5.2 %collective-permute-done.6.refs_0_ = bf16[64,6144]{1,0:T(8,128)(2,1)S(1)} collective-permute-done((bf16[64,6144]{1,0:T(8,128)(2,1)S(1)}, bf16[64,6144]{1,0:T(8,128)(2,1)S(1)}, u32[]{:S(2)}, u32[]{:S(2)}) %collective-permute-start.6) | collective-permute-done | bytes 786464 | tf_op jit(solution)/shard_map/ppermute | solution.py:53
  147.1 2.7 collective-permute-done.7.refs_1_
  149.8 1.4 collective-permute-start.14
  151.1 0.9 collective-permute-start.11
  152.0 2.7 collective-permute-start.10
  154.7 9.6 %collective-permute-done.11.refs_6_ = bf16[64,6144]{1,0:T(8,128)(2,1)S(1)} collective-permute-done((bf16[64,6144]{1,0:T(8,128)(2,1)S(1)}, bf16[64,6144]{1,0:T(8,128)(2,1)S(1)}, u32[]{:S(2)}, u32[]{:S(2)}) %collective-permute-start.11) | collective-permute-done | bytes 786464 | tf_op jit(solution)/shard_map/ppermute | solution.py:53
  164.3 1.6 collective-permute-start.12
  165.9 4.2 %collective-permute-done.9.refs_2_ = bf16[64,6144]{1,0:T(8,128)(2,1)S(1)} collective-permute-done((bf16[64,6144]{1,0:T(8,128)(2,1)S(1)}, bf16[64,6144]{1,0:T(8,128)(2,1)S(1)}, u32[]{:S(2)}, u32[]{:S(2)}) %collective-permute-start.9) | collective-permute-done | bytes 786464 | tf_op jit(solution)/shard_map/ppermute | solution.py:53
  170.1 1.8 collective-permute-done.10.refs_3_
  171.8 3.7 %collective-permute-done.12.refs_7_ = bf16[64,6144]{1,0:T(8,128)(2,1)S(1)} collective-permute-done((bf16[64,6144]{1,0:T(8,128)(2,1)S(1)}, bf16[64,6144]{1,0:T(8,128)(2,1)S(1)}, u32[]{:S(2)}, u32[]{:S(2)}) %collective-permute-start.12) | collective-permute-done | bytes 786464 | tf_op jit(solution)/shard_map/ppermute | solution.py:53
  175.6 9.1 %collective-permute-done.13.refs_10_ = bf16[1536,768]{1,0:T(8,128)(2,1)} collective-permute-done((bf16[1536,768]{1,0:T(8,128)(2,1)S(1)}, bf16[1536,768]{1,0:T(8,128)(2,1)}, u32[]{:S(2)}, u32[]{:S(2)}) %collective-permute-start.13) | collective-permute-done | bytes 2359328 | tf_op jit(solution)/shard_map/ppermute | solution.py:53
  184.6 8.2 %collective-permute-done.14.refs_1_ = bf16[1536,768]{1,0:T(8,128)(2,1)S(1)} collective-permute-done((bf16[1536,768]{1,0:T(8,128)(2,1)}, bf16[1536,768]{1,0:T(8,128)(2,1)S(1)}, u32[]{:S(2)}, u32[]{:S(2)}) %collective-permute-start.14) | collective-permute-done | bytes 2359328 | tf_op jit(solution)/shard_map/ppermute | solution.py:53
  192.9 1.5 copy-done.6
  194.3 0.9 copy-done
  199.7 0.9 copy-done.15
  200.6 2.8 collective-permute-start.15
  204.0 1.1 copy-done.1
  205.1 1.1 copy-done.3
  206.3 1.1 copy-done.5
  207.4 1.1 copy-done.10
  208.5 1.1 copy-done.12
  209.7 1.1 copy-done.14
  210.8 1.1 copy-done.16
  211.9 13.7 %shard_map.132.refs_0_ = bf16[512,1536]{1,0:T(8,128)(2,1)S(1)} custom-call(bf16[64,6144]{1,0:T(8,128)(2,1)S(1)} %copy-done.1, bf16[64,6144]{1,0:T(8,128)(2,1)S(1)} %copy-done.3, bf16[64,6144]{1,0:T(8,128)(2,1)S(1)} %copy-done.12, bf16[64,6144]{1,0:T(8,128)(2,1)S(1)} %copy-done.14, bf16[64,6144]{1,0:T(8,128)(2,1)S(1)} %get-tuple-element.60.refs_4_, ...), custom_call_target="tpu_custom_call" | custom-call | flops 9663676416 | bytes 25165824 | tf_op jit(solution)/shard_map/pallas_call | solution.py:112
  225.7 4.5 %collective-permute-done.18.refs_8_ = bf16[1536,768]{1,0:T(8,128)(2,1)S(1)} collective-permute-done((bf16[1536,768]{1,0:T(8,128)(2,1)S(1)}, bf16[1536,768]{1,0:T(8,128)(2,1)S(1)}, u32[]{:S(2)}, u32[]{:S(2)}) %collective-permute-start.18) | collective-permute-done | bytes 2359328 | tf_op jit(solution)/shard_map/ppermute | solution.py:62
  230.2 1.4 copy-done.28
  231.7 12.8 %shard_map.134 = (bf16[64,6144]{1,0:T(8,128)(2,1)S(1)}, bf16[64,6144]{1,0:T(8,128)(2,1)S(1)}, bf16[64,6144]{1,0:T(8,128)(2,1)S(1)}, bf16[64,6144]{1,0:T(8,128)(2...) custom-call(bf16[512,1536]{1,0:T(8,128)(2,1)S(1)} %get-tuple-element, ...), custom_call_target="tpu_custom_call" | custom-call | flops 9663676416 | bytes 26738688 | tf_op jit(solution)/shard_map/pallas_call | solution.py:157
  244.6 2.7 collective-permute-start.26
  247.3 9.6 %collective-permute-done.20.b1 = bf16[64,6144]{1,0:T(8,128)(2,1)S(1)} collective-permute-done((bf16[64,6144]{1,0:T(8,128)(2,1)S(1)}, bf16[64,6144]{1,0:T(8,128)(2,1)S(1)}, u32[]{:S(2)}, u32[]{:S(2)}) %collective-permute-start.20) | collective-permute-done | bytes 786464 | tf_op jit(solution)/shard_map/ppermute | solution.py:53
  256.9 6.3 %collective-permute-done.21.b2 = bf16[64,6144]{1,0:T(8,128)(2,1)S(1)} collective-permute-done((bf16[64,6144]{1,0:T(8,128)(2,1)S(1)}, bf16[64,6144]{1,0:T(8,128)(2,1)S(1)}, u32[]{:S(2)}, u32[]{:S(2)}) %collective-permute-start.21) | collective-permute-done | bytes 786464 | tf_op jit(solution)/shard_map/ppermute | solution.py:53
  264.0 4.5 %collective-permute-start.19 = (bf16[64,6144]{1,0:T(8,128)(2,1)S(1)}, bf16[64,6144]{1,0:T(8,128)(2,1)S(1)}, u32[]{:S(2)}, u32[]{:S(2)}) collective-permute-start(bf16[64,6144]{1,0:T(8,128)(2,1)S(1)} %get-tuple-element.70), channel_id=1, source_target_pairs={{0,8},{1,25},{2,10},{3,27},{4,12},{5,29},{6,14},{7,31},{8,16},{9,1... | collective-permute-start | bytes 2359304 | tf_op jit(solution)/shard_map/ppermute | solution.py:53
  268.6 7.8 %collective-permute-done.27.c = bf16[64,6144]{1,0:T(8,128)(2,1)S(1)} collective-permute-done((bf16[64,6144]{1,0:T(8,128)(2,1)S(1)}, bf16[64,6144]{1,0:T(8,128)(2,1)S(1)}, u32[]{:S(2)}, u32[]{:S(2)}) %collective-permute-start.27) | collective-permute-done | bytes 786464 | tf_op jit(solution)/shard_map/ppermute | solution.py:53
  276.9 4.5 %collective-permute-start.28 = (bf16[16,6144]{1,0:T(8,128)(2,1)S(1)}, bf16[16,6144]{1,0:T(8,128)(2,1)S(1)}, u32[]{:S(2)}, u32[]{:S(2)}) collective-permute-start(bf16[16,6144]{1,0:T(8,128)(2,1)S(1)} %get-tuple-element.84), channel_id=1, source_target_pairs={{0,24},{1,25},{2,26},{3,27},{4,28},{5,29},{6,30},{7,31},{8,0},{9,1... | collective-permute-start | bytes 589832 | tf_op jit(solution)/shard_map/ppermute | solution.py:53
  281.5 1.3 collective-permute-start.30
  283.1 7.7 %collective-permute-done.22.c = bf16[64,6144]{1,0:T(8,128)(2,1)S(1)} collective-permute-done((bf16[64,6144]{1,0:T(8,128)(2,1)S(1)}, bf16[64,6144]{1,0:T(8,128)(2,1)S(1)}, u32[]{:S(2)}, u32[]{:S(2)}) %collective-permute-start.22) | collective-permute-done | bytes 786464 | tf_op jit(solution)/shard_map/ppermute | solution.py:53
  291.9 1.0 collective-permute-start.24
  293.8 3.5 %collective-permute-done.29.g = bf16[16,6144]{1,0:T(8,128)(2,1)S(1)} collective-permute-done((bf16[16,6144]{1,0:T(8,128)(2,1)S(1)}, bf16[16,6144]{1,0:T(8,128)(2,1)S(1)}, u32[]{:S(2)}, u32[]{:S(2)}) %collective-permute-start.29) | collective-permute-done | bytes 196640 | tf_op jit(solution)/shard_map/ppermute | solution.py:53
  297.3 2.3 collective-permute-done.24.c
  299.6 1.3 collective-permute-done.25.d
  301.6 15.5 %all_to_all.20 = bf16[8,32,768]{2,1,0:T(8,128)(2,1)S(1)} all-to-all(bf16[8,32,768]{2,1,0:T(8,128)(2,1)S(1)} %shard_map.138), channel_id=1, replica_groups=mesh['row'=16,'col'=8] {'col'}, dimensions={0} | all-to-all | bytes 786432 | tf_op jit(solution)/shard_map/all_to_all | solution.py:237
  (104 shorter events, 13.8 us)
Async XLA Ops:
  6.5 197.5 %all-gather.2.cloned.1.call-start = ((), (), s32[]{:S(2)}) async-start(), calls=%async_computation.4 | async-start | bytes 21233664 | tf_op jit(solution)/shard_map/all_gather | solution.py:317
  8.2 1.0 copy-start.18
  8.2 14.5 %copy-start.25 = (f32[768]{0:T(1024)S(1)}, f32[768]{0:T(1024)}, u32[]{:S(2)}) copy-start(f32[768]{0:T(1024)} %param.15) | copy-start | bytes 9220
  8.2 14.7 %copy-start.22 = (f32[512,256]{1,0:T(8,128)S(1)}, f32[512,256]{1,0:T(8,128)}, u32[]{:S(2)}) copy-start(f32[512,256]{1,0:T(8,128)} %constant.28.clone) | copy-start | bytes 1572868
  24.6 19.7 %all-to-all-start = ((bf16[16,32,768]{2,1,0:T(8,128)(2,1)}), bf16[16,32,768]{2,1,0:T(8,128)(2,1)}, u32[]{:S(2)}, u32[]{:S(2)}) async-start(bf16[16,32,768]{2,1,0:T(8,128)(2,1)} %bitcast.2), calls=%async_computation | async-start | bytes 1572864 | tf_op jit(solution)/shard_map/all_to_all | solution.py:237
  44.3 2.6 copy-start.17
  44.3 2.6 copy-start.21
  46.9 1.0 copy-start.20
  49.8 3.8 %copy-start.27 = (f32[768]{0:T(1024)S(1)}, f32[768]{0:T(1024)}, u32[]{:S(2)}) copy-start(f32[768]{0:T(1024)} %param.16) | copy-start | bytes 9220
  49.8 14.2 %all-to-all-start.1 = ((bf16[16,32,768]{2,1,0:T(8,128)(2,1)}), bf16[16,32,768]{2,1,0:T(8,128)(2,1)S(1)}, u32[]{:S(2)}, u32[]{:S(2)}) async-start(bf16[16,32,768]{2,1,0:T(8,128)(2,1)} %bitcast.45), calls=%async_computation.1 | async-start | bytes 1572864 | tf_op jit(solution)/shard_map/all_to_all | solution.py:237
  63.9 2.6 copy-start.23
  96.1 39.6 %collective-permute-start.8 = (bf16[1536,768]{1,0:T(8,128)(2,1)S(1)}, bf16[1536,768]{1,0:T(8,128)(2,1)}, u32[]{:S(2)}, u32[]{:S(2)}) collective-permute-start(bf16[1536,768]{1,0:T(8,128)(2,1)S(1)} %get-tuple-element.49.refs_2_), channel_id=1, source_target_pairs={{0,2},{1,7},{2,4},{3,1},{4,6},{5,3},{6,0},{7,5},{8,10},{9,15},{10,... | collective-permute-start | bytes 7077896 | tf_op jit(solution)/shard_map/ppermute | solution.py:53
  97.3 11.5 %collective-permute-start.3 = (bf16[16,6144]{1,0:T(8,128)(2,1)S(1)}, bf16[16,6144]{1,0:T(8,128)(2,1)S(1)}, u32[]{:S(2)}, u32[]{:S(2)}) collective-permute-start(bf16[16,6144]{1,0:T(8,128)(2,1)S(1)} %get-tuple-element.48), channel_id=1, source_target_pairs={{0,8},{1,9},{2,10},{3,11},{4,12},{5,13},{6,14},{7,15},{8,16},{9,17... | collective-permute-start | bytes 589832 | tf_op jit(solution)/shard_map/ppermute | solution.py:53
  97.7 11.1 %collective-permute-start.4 = (bf16[16,6144]{1,0:T(8,128)(2,1)S(1)}, bf16[16,6144]{1,0:T(8,128)(2,1)S(1)}, u32[]{:S(2)}, u32[]{:S(2)}) collective-permute-start(bf16[16,6144]{1,0:T(8,128)(2,1)S(1)} %get-tuple-element.48), channel_id=1, source_target_pairs={{0,24},{1,25},{2,26},{3,27},{4,28},{5,29},{6,30},{7,31},{8,0},{9,1... | collective-permute-start | bytes 589832 | tf_op jit(solution)/shard_map/ppermute | solution.py:53
  100.0 8.7 %collective-permute-start.5 = (bf16[16,6144]{1,0:T(8,128)(2,1)S(1)}, bf16[16,6144]{1,0:T(8,128)(2,1)S(1)}, u32[]{:S(2)}, u32[]{:S(2)}) collective-permute-start(bf16[16,6144]{1,0:T(8,128)(2,1)S(1)} %get-tuple-element.48), channel_id=1, source_target_pairs={{0,16},{1,17},{2,18},{3,19},{4,20},{5,21},{6,22},{7,23},{8,24},{9,... | collective-permute-start | bytes 589832 | tf_op jit(solution)/shard_map/ppermute | solution.py:53
  100.0 8.9 %collective-permute-start = (bf16[16,6144]{1,0:T(8,128)(2,1)S(1)}, bf16[16,6144]{1,0:T(8,128)(2,1)S(1)}, u32[]{:S(2)}, u32[]{:S(2)}) collective-permute-start(bf16[16,6144]{1,0:T(8,128)(2,1)S(1)} %get-tuple-element.47), channel_id=1, source_target_pairs={{0,32},{1,33},{2,34},{3,35},{4,36},{5,37},{6,38},{7,39},{8,40},{9,... | collective-permute-start | bytes 589832 | tf_op jit(solution)/shard_map/ppermute | solution.py:53
  108.7 5.2 %collective-permute-start.1 = (bf16[16,6144]{1,0:T(8,128)(2,1)S(1)}, bf16[16,6144]{1,0:T(8,128)(2,1)S(1)}, u32[]{:S(2)}, u32[]{:S(2)}) collective-permute-start(bf16[16,6144]{1,0:T(8,128)(2,1)S(1)} %get-tuple-element.47), channel_id=1, source_target_pairs={{0,96},{1,97},{2,98},{3,99},{4,100},{5,101},{6,102},{7,103},{8,104... | collective-permute-start | bytes 589832 | tf_op jit(solution)/shard_map/ppermute | solution.py:53
  108.8 6.1 %collective-permute-start.2 = (bf16[16,6144]{1,0:T(8,128)(2,1)S(1)}, bf16[16,6144]{1,0:T(8,128)(2,1)S(1)}, u32[]{:S(2)}, u32[]{:S(2)}) collective-permute-start(bf16[16,6144]{1,0:T(8,128)(2,1)S(1)} %get-tuple-element.47), channel_id=1, source_target_pairs={{0,64},{1,65},{2,66},{3,67},{4,68},{5,69},{6,70},{7,71},{8,72},{9,... | collective-permute-start | bytes 589832 | tf_op jit(solution)/shard_map/ppermute | solution.py:53
  135.7 11.4 %collective-permute-start.6 = (bf16[64,6144]{1,0:T(8,128)(2,1)S(1)}, bf16[64,6144]{1,0:T(8,128)(2,1)S(1)}, u32[]{:S(2)}, u32[]{:S(2)}) collective-permute-start(bf16[64,6144]{1,0:T(8,128)(2,1)S(1)} %get-tuple-element.50.refs_0_), channel_id=1, source_target_pairs={{0,8},{1,25},{2,10},{3,27},{4,12},{5,29},{6,14},{7,31},{8,16},{9,1... | collective-permute-start | bytes 2359304 | tf_op jit(solution)/shard_map/ppermute | solution.py:53
  138.2 11.6 %collective-permute-start.7 = (bf16[64,6144]{1,0:T(8,128)(2,1)S(1)}, bf16[64,6144]{1,0:T(8,128)(2,1)S(1)}, u32[]{:S(2)}, u32[]{:S(2)}) collective-permute-start(bf16[64,6144]{1,0:T(8,128)(2,1)S(1)} %get-tuple-element.51.refs_4_), channel_id=1, source_target_pairs={{0,32},{1,97},{2,34},{3,99},{4,36},{5,101},{6,38},{7,103},{8,40},{... | collective-permute-start | bytes 2359304 | tf_op jit(solution)/shard_map/ppermute | solution.py:53
  140.8 25.1 %copy-start.24 = (f32[1536]{0:T(1024)S(1)}, f32[1536]{0:T(1024)}, u32[]{:S(2)}) copy-start(f32[1536]{0:T(1024)} %param.18) | copy-start | bytes 18436
  140.8 43.8 %collective-permute-start.13 = (bf16[1536,768]{1,0:T(8,128)(2,1)S(1)}, bf16[1536,768]{1,0:T(8,128)(2,1)}, u32[]{:S(2)}, u32[]{:S(2)}) collective-permute-start(bf16[1536,768]{1,0:T(8,128)(2,1)S(1)} %get-tuple-element.54.refs_8_), channel_id=1, source_target_pairs={{0,6},{1,3},{2,0},{3,5},{4,2},{5,7},{6,4},{7,1},{8,14},{9,11},{10,... | collective-permute-start | bytes 7077896 | tf_op jit(solution)/shard_map/ppermute | solution.py:53
  149.8 43.1 %collective-permute-start.14 = (bf16[1536,768]{1,0:T(8,128)(2,1)}, bf16[1536,768]{1,0:T(8,128)(2,1)S(1)}, u32[]{:S(2)}, u32[]{:S(2)}) collective-permute-start(bf16[1536,768]{1,0:T(8,128)(2,1)} %get-tuple-element.55.refs_9_), channel_id=1, source_target_pairs={{0,2},{1,7},{2,4},{3,1},{4,6},{5,3},{6,0},{7,5},{8,10},{9,15},{10,... | collective-permute-start | bytes 7077896 | tf_op jit(solution)/shard_map/ppermute | solution.py:53
  151.1 13.2 %collective-permute-start.11 = (bf16[64,6144]{1,0:T(8,128)(2,1)S(1)}, bf16[64,6144]{1,0:T(8,128)(2,1)S(1)}, u32[]{:S(2)}, u32[]{:S(2)}) collective-permute-start(bf16[64,6144]{1,0:T(8,128)(2,1)S(1)} %get-tuple-element.51.refs_4_), channel_id=1, source_target_pairs={{0,96},{1,33},{2,98},{3,35},{4,100},{5,37},{6,102},{7,39},{8,104},... | collective-permute-start | bytes 2359304 | tf_op jit(solution)/shard_map/ppermute | solution.py:53
  152.0 18.0 %collective-permute-start.9 = (bf16[64,6144]{1,0:T(8,128)(2,1)S(1)}, bf16[64,6144]{1,0:T(8,128)(2,1)S(1)}, u32[]{:S(2)}, u32[]{:S(2)}) collective-permute-start(bf16[64,6144]{1,0:T(8,128)(2,1)S(1)} %get-tuple-element.50.refs_0_), channel_id=1, source_target_pairs={{0,24},{1,9},{2,26},{3,11},{4,28},{5,13},{6,30},{7,15},{8,0},{9,17... | collective-permute-start | bytes 2359304 | tf_op jit(solution)/shard_map/ppermute | solution.py:53
  152.0 19.8 %collective-permute-start.10 = (bf16[64,6144]{1,0:T(8,128)(2,1)S(1)}, bf16[64,6144]{1,0:T(8,128)(2,1)S(1)}, u32[]{:S(2)}, u32[]{:S(2)}) collective-permute-start(bf16[64,6144]{1,0:T(8,128)(2,1)S(1)} %get-tuple-element.52.refs_1_), channel_id=1, source_target_pairs={{0,8},{1,25},{2,10},{3,27},{4,12},{5,29},{6,14},{7,31},{8,16},{9,1... | collective-permute-start | bytes 2359304 | tf_op jit(solution)/shard_map/ppermute | solution.py:53
  164.3 11.2 %collective-permute-start.12 = (bf16[64,6144]{1,0:T(8,128)(2,1)S(1)}, bf16[64,6144]{1,0:T(8,128)(2,1)S(1)}, u32[]{:S(2)}, u32[]{:S(2)}) collective-permute-start(bf16[64,6144]{1,0:T(8,128)(2,1)S(1)} %get-tuple-element.53.refs_5_), channel_id=1, source_target_pairs={{0,32},{1,97},{2,34},{3,99},{4,36},{5,101},{6,38},{7,103},{8,40},{... | collective-permute-start | bytes 2359304 | tf_op jit(solution)/shard_map/ppermute | solution.py:53
  192.9 1.5 copy-start.6
  194.3 0.9 copy-start
  195.3 0.9 copy-start.2
  196.2 0.9 copy-start.4
  197.1 0.9 copy-start.9
  197.9 0.9 copy-start.11
  198.8 0.9 copy-start.13
  199.7 0.9 copy-start.15
  200.6 25.1 %collective-permute-start.15 = (bf16[1536,768]{1,0:T(8,128)(2,1)S(1)}, bf16[1536,768]{1,0:T(8,128)(2,1)}, u32[]{:S(2)}, u32[]{:S(2)}) collective-permute-start(bf16[1536,768]{1,0:T(8,128)(2,1)S(1)} %get-tuple-element.65.refs_1_), channel_id=1, source_target_pairs={{0,1},{1,0},{2,3},{3,2},{4,5},{5,4},{6,7},{7,6},{8,9},{9,8},{10,11... | collective-permute-start | bytes 7077896 | tf_op jit(solution)/shard_map/ppermute | solution.py:62
  203.5 22.2 %collective-permute-start.16 = (bf16[1536,768]{1,0:T(8,128)(2,1)}, bf16[1536,768]{1,0:T(8,128)(2,1)}, u32[]{:S(2)}, u32[]{:S(2)}) collective-permute-start(bf16[1536,768]{1,0:T(8,128)(2,1)} %get-tuple-element.66.refs_2_), channel_id=1, source_target_pairs={{0,1},{1,0},{2,3},{3,2},{4,5},{5,4},{6,7},{7,6},{8,9},{9,8},{10,11... | collective-permute-start | bytes 7077896 | tf_op jit(solution)/shard_map/ppermute | solution.py:62
  203.5 22.3 %collective-permute-start.17 = (bf16[1536,768]{1,0:T(8,128)(2,1)}, bf16[1536,768]{1,0:T(8,128)(2,1)}, u32[]{:S(2)}, u32[]{:S(2)}) collective-permute-start(bf16[1536,768]{1,0:T(8,128)(2,1)} %get-tuple-element.67.refs_3_), channel_id=1, source_target_pairs={{0,1},{1,0},{2,3},{3,2},{4,5},{5,4},{6,7},{7,6},{8,9},{9,8},{10,11... | collective-permute-start | bytes 7077896 | tf_op jit(solution)/shard_map/ppermute | solution.py:62
  204.0 1.1 copy-start.1
  205.1 1.1 copy-start.3
  206.3 1.1 copy-start.5
  207.4 1.1 copy-start.10
  208.5 1.1 copy-start.12
  209.7 1.1 copy-start.14
  210.8 1.1 copy-start.16
  211.9 13.7 %copy-start.7 = (bf16[1536,768]{1,0:T(8,128)(2,1)S(1)}, bf16[1536,768]{1,0:T(8,128)(2,1)}, u32[]{:S(2)}) copy-start(bf16[1536,768]{1,0:T(8,128)(2,1)} %copy-done.6) | copy-start | bytes 7077892
  225.6 4.6 %copy-start.8 = (bf16[1536,768]{1,0:T(8,128)(2,1)}, bf16[1536,768]{1,0:T(8,128)(2,1)S(1)}, u32[]{:S(2)}) copy-start(bf16[1536,768]{1,0:T(8,128)(2,1)S(1)} %get-tuple-element.68.refs_4_) | copy-start | bytes 7077892
  225.6 4.6 %collective-permute-start.18 = (bf16[1536,768]{1,0:T(8,128)(2,1)S(1)}, bf16[1536,768]{1,0:T(8,128)(2,1)S(1)}, u32[]{:S(2)}, u32[]{:S(2)}) collective-permute-start(bf16[1536,768]{1,0:T(8,128)(2,1)S(1)} %get-tuple-element.68.refs_4_), channel_id=1, source_target_pairs={{0,1},{1,0},{2,3},{3,2},{4,5},{5,4},{6,7},{7,6},{8,9},{9,8},{10,11... | collective-permute-start | bytes 7077896 | tf_op jit(solution)/shard_map/ppermute | solution.py:62
  230.2 1.4 copy-start.28
  244.5 12.4 %collective-permute-start.20 = (bf16[64,6144]{1,0:T(8,128)(2,1)S(1)}, bf16[64,6144]{1,0:T(8,128)(2,1)S(1)}, u32[]{:S(2)}, u32[]{:S(2)}) collective-permute-start(bf16[64,6144]{1,0:T(8,128)(2,1)S(1)} %get-tuple-element.72), channel_id=1, source_target_pairs={{0,24},{1,9},{2,26},{3,11},{4,28},{5,13},{6,30},{7,15},{8,0},{9,17... | collective-permute-start | bytes 2359304 | tf_op jit(solution)/shard_map/ppermute | solution.py:53
  244.5 18.7 %collective-permute-start.21 = (bf16[64,6144]{1,0:T(8,128)(2,1)S(1)}, bf16[64,6144]{1,0:T(8,128)(2,1)S(1)}, u32[]{:S(2)}, u32[]{:S(2)}) collective-permute-start(bf16[64,6144]{1,0:T(8,128)(2,1)S(1)} %get-tuple-element.74), channel_id=1, source_target_pairs={{0,96},{1,33},{2,98},{3,35},{4,100},{5,37},{6,102},{7,39},{8,104},... | collective-permute-start | bytes 2359304 | tf_op jit(solution)/shard_map/ppermute | solution.py:53
  244.6 23.9 %collective-permute-start.26 = (bf16[64,6144]{1,0:T(8,128)(2,1)S(1)}, bf16[64,6144]{1,0:T(8,128)(2,1)S(1)}, u32[]{:S(2)}, u32[]{:S(2)}) collective-permute-start(bf16[64,6144]{1,0:T(8,128)(2,1)S(1)} %get-tuple-element.81), channel_id=1, source_target_pairs={{0,32},{1,97},{2,34},{3,99},{4,36},{5,101},{6,38},{7,103},{8,40},{... | collective-permute-start | bytes 2359304 | tf_op jit(solution)/shard_map/ppermute | solution.py:53
  263.9 12.4 %collective-permute-start.27 = (bf16[64,6144]{1,0:T(8,128)(2,1)S(1)}, bf16[64,6144]{1,0:T(8,128)(2,1)S(1)}, u32[]{:S(2)}, u32[]{:S(2)}) collective-permute-start(bf16[64,6144]{1,0:T(8,128)(2,1)S(1)} %get-tuple-element.82), channel_id=1, source_target_pairs={{0,96},{1,33},{2,98},{3,35},{4,100},{5,37},{6,102},{7,39},{8,104},... | collective-permute-start | bytes 2359304 | tf_op jit(solution)/shard_map/ppermute | solution.py:53
  264.0 19.1 %collective-permute-start.19 = (bf16[64,6144]{1,0:T(8,128)(2,1)S(1)}, bf16[64,6144]{1,0:T(8,128)(2,1)S(1)}, u32[]{:S(2)}, u32[]{:S(2)}) collective-permute-start(bf16[64,6144]{1,0:T(8,128)(2,1)S(1)} %get-tuple-element.70), channel_id=1, source_target_pairs={{0,8},{1,25},{2,10},{3,27},{4,12},{5,29},{6,14},{7,31},{8,16},{9,1... | collective-permute-start | bytes 2359304 | tf_op jit(solution)/shard_map/ppermute | solution.py:53
  268.6 22.2 %collective-permute-start.22 = (bf16[64,6144]{1,0:T(8,128)(2,1)S(1)}, bf16[64,6144]{1,0:T(8,128)(2,1)S(1)}, u32[]{:S(2)}, u32[]{:S(2)}) collective-permute-start(bf16[64,6144]{1,0:T(8,128)(2,1)S(1)} %get-tuple-element.75), channel_id=1, source_target_pairs={{0,24},{1,9},{2,26},{3,11},{4,28},{5,13},{6,30},{7,15},{8,0},{9,17... | collective-permute-start | bytes 2359304 | tf_op jit(solution)/shard_map/ppermute | solution.py:53
  276.9 16.0 %collective-permute-start.28 = (bf16[16,6144]{1,0:T(8,128)(2,1)S(1)}, bf16[16,6144]{1,0:T(8,128)(2,1)S(1)}, u32[]{:S(2)}, u32[]{:S(2)}) collective-permute-start(bf16[16,6144]{1,0:T(8,128)(2,1)S(1)} %get-tuple-element.84), channel_id=1, source_target_pairs={{0,24},{1,25},{2,26},{3,27},{4,28},{5,29},{6,30},{7,31},{8,0},{9,1... | collective-permute-start | bytes 589832 | tf_op jit(solution)/shard_map/ppermute | solution.py:53
  281.4 15.9 %collective-permute-start.29 = (bf16[16,6144]{1,0:T(8,128)(2,1)S(1)}, bf16[16,6144]{1,0:T(8,128)(2,1)S(1)}, u32[]{:S(2)}, u32[]{:S(2)}) collective-permute-start(bf16[16,6144]{1,0:T(8,128)(2,1)S(1)} %get-tuple-element.85), channel_id=1, source_target_pairs={{0,8},{1,9},{2,10},{3,11},{4,12},{5,13},{6,14},{7,15},{8,16},{9,17... | collective-permute-start | bytes 589832 | tf_op jit(solution)/shard_map/ppermute | solution.py:53
  281.5 15.9 %collective-permute-start.30 = (bf16[16,6144]{1,0:T(8,128)(2,1)S(1)}, bf16[16,6144]{1,0:T(8,128)(2,1)S(1)}, u32[]{:S(2)}, u32[]{:S(2)}) collective-permute-start(bf16[16,6144]{1,0:T(8,128)(2,1)S(1)} %get-tuple-element.86), channel_id=1, source_target_pairs={{0,16},{1,17},{2,18},{3,19},{4,20},{5,21},{6,22},{7,23},{8,24},{9,... | collective-permute-start | bytes 589832 | tf_op jit(solution)/shard_map/ppermute | solution.py:53
  291.3 25.8 %copy-start.19 = (f32[256,768]{1,0:T(8,128)S(1)}, f32[256,768]{1,0:T(8,128)}, u32[]{:S(2)}) copy-start(f32[256,768]{1,0:T(8,128)} %get-tuple-element.99) | copy-start | bytes 2359300
  291.3 25.8 %copy-start.26 = (f32[768]{0:T(1024)S(1)}, f32[768]{0:T(1024)}, u32[]{:S(2)}) copy-start(f32[768]{0:T(1024)} %param.20) | copy-start | bytes 9220
  291.4 6.0 %collective-permute-start.23 = (bf16[16,6144]{1,0:T(8,128)(2,1)S(1)}, bf16[16,6144]{1,0:T(8,128)(2,1)S(1)}, u32[]{:S(2)}, u32[]{:S(2)}) collective-permute-start(bf16[16,6144]{1,0:T(8,128)(2,1)S(1)} %get-tuple-element.77), channel_id=1, source_target_pairs={{0,96},{1,97},{2,98},{3,99},{4,100},{5,101},{6,102},{7,103},{8,104... | collective-permute-start | bytes 589832 | tf_op jit(solution)/shard_map/ppermute | solution.py:53
  291.9 7.8 %collective-permute-start.24 = (bf16[16,6144]{1,0:T(8,128)(2,1)S(1)}, bf16[16,6144]{1,0:T(8,128)(2,1)S(1)}, u32[]{:S(2)}, u32[]{:S(2)}) collective-permute-start(bf16[16,6144]{1,0:T(8,128)(2,1)S(1)} %get-tuple-element.78), channel_id=1, source_target_pairs={{0,32},{1,33},{2,34},{3,35},{4,36},{5,37},{6,38},{7,39},{8,40},{9,... | collective-permute-start | bytes 589832 | tf_op jit(solution)/shard_map/ppermute | solution.py:53
  292.9 8.0 %collective-permute-start.25 = (bf16[16,6144]{1,0:T(8,128)(2,1)S(1)}, bf16[16,6144]{1,0:T(8,128)(2,1)S(1)}, u32[]{:S(2)}, u32[]{:S(2)}) collective-permute-start(bf16[16,6144]{1,0:T(8,128)(2,1)S(1)} %get-tuple-element.79), channel_id=1, source_target_pairs={{0,64},{1,65},{2,66},{3,67},{4,68},{5,69},{6,70},{7,71},{8,72},{9,... | collective-permute-start | bytes 589832 | tf_op jit(solution)/shard_map/ppermute | solution.py:53
Sparse Core Ops, SparseCore 0:
  9.0 109.3 all-gather.1

commit v5 on v4

--- a/solution.py
+++ b/solution.py
@@ -87,40 +87,28 @@
 
 
 def mm1_kernel(*refs):
-    pieces, (w_ref, b_ref, o_ref, left, sems) = refs[:-5], refs[-5:]
-    rows = left.shape[0] // len(pieces)
-    copies = [
-        pltpu.make_async_copy(p, left.at[pl.ds(i * rows, rows)], sems.at[i])
-        for i, p in enumerate(pieces)
-    ]
-
-    @pl.when(pl.program_id(0) == 0)
-    def _():
-        for copy in copies:
-            copy.start()
-        for copy in copies:
-            copy.wait()
-
-    pre = jnp.dot(left[...], w_ref[...], preferred_element_type=F32) + b_ref[...]
+    pieces, (w_ref, b_ref, o_ref) = refs[:-3], refs[-3:]
+    left = jnp.concatenate([p[...] for p in pieces], axis=0)
+    pre = jnp.dot(left, w_ref[...], preferred_element_type=F32) + b_ref[...]
     o_ref[...] = (0.5 * pre * (1.0 + lax.erf(pre * math.sqrt(0.5)))).astype(BF)
 
 
 def matmul_in(pieces, w, b):
     depth, width = w.shape
-    tokens = len(pieces) * pieces[0].shape[0]
+    rows = pieces[0].shape[0]
+    tokens = len(pieces) * rows
     tile = 256
     return pl.pallas_call(
         mm1_kernel,
         grid=(width // tile,),
-        in_specs=[pl.BlockSpec(memory_space=pl.ANY) for _ in pieces]
+        in_specs=[pl.BlockSpec((rows, depth), lambda i: (0, 0)) for _ in pieces]
         + [
             pl.BlockSpec((depth, tile), lambda i: (0, i)),
             pl.BlockSpec((1, tile), lambda i: (0, i)),
         ],
         out_specs=pl.BlockSpec((tokens, tile), lambda i: (0, i)),
         out_shape=jax.ShapeDtypeStruct((tokens, width), BF),
-        scratch_shapes=[pltpu.VMEM((tokens, depth), BF), pltpu.SemaphoreType.DMA((len(pieces),))],
-        compiler_params=params(40),
+        compiler_params=params(58),
         cost_estimate=pl.CostEstimate(
             flops=2 * tokens * depth * width,
             bytes_accessed=2 * (tokens * depth + depth * width),
@@ -129,108 +117,114 @@
     )(*pieces, w, b[None])
 
 
-def mm2_kernel(count, *refs):
-    h_ref, weights, outs, (held, sems) = refs[0], refs[1 : 1 + count], refs[1 + count : -2], refs[-2:]
-    step = pl.program_id(0)
-    copies = [pltpu.make_async_copy(w, held.at[j % 2], sems.at[j % 2]) for j, w in enumerate(weights)]
-    for j in range(count):
-
-        @pl.when(step == j)
-        def _(j=j):
-            if j == 0:
-                copies[0].start()
-            if j + 1 < count:
-                copies[j + 1].start()
-            copies[j].wait()
-
-    out = jnp.dot(h_ref[...], held[lax.rem(step, 2)], preferred_element_type=F32)
-    rows = outs[0].shape[0]
-    for i, o_ref in enumerate(outs):
-        o_ref[...] = out[i * rows : (i + 1) * rows].astype(BF)
-
-
-def matmul_out(hidden, weights, count):
-    depth, chans = weights[0].shape
-    tokens = hidden.shape[0]
-    cols = len(weights)
+def mm2_kernel(*refs):
+    hiddens, (own_ref, other_ref), outs = refs[:SIDE], refs[SIDE : SIDE + 2], refs[SIDE + 2 :]
+    rows, width = outs[0].shape
+    chans = own_ref.shape[1]
+    for i, h_ref in enumerate(hiddens):
+
+        @pl.when(pl.program_id(0) == i)
+        def _(h_ref=h_ref):
+            for at, w_ref in ((0, own_ref), (chans, other_ref)):
+                out = jnp.dot(h_ref[...], w_ref[...], preferred_element_type=F32)
+                for p, o_ref in enumerate(outs):
+                    o_ref[:, at : at + chans] = out[p * rows : (p + 1) * rows].astype(BF)
+
+
+def matmul_out(hiddens, own, other, count):
+    depth, chans = own.shape
+    tokens = hiddens[0].shape[0]
     rows = tokens // count
-    return pl.pallas_call(
-        functools.partial(mm2_kernel, cols),
-        grid=(cols,),
-        in_specs=[pl.BlockSpec((tokens, depth), lambda j: (0, 0))]
-        + [pl.BlockSpec(memory_space=pl.ANY) for _ in weights],
-        out_specs=[pl.BlockSpec((rows, chans), lambda j: (0, j))] * count,
-        out_shape=[jax.ShapeDtypeStruct((rows, cols * chans), BF)] * count,
-        scratch_shapes=[pltpu.VMEM((2, depth, chans), BF), pltpu.SemaphoreType.DMA((2,))],
-        compiler_params=params(40),
+    steps = len(hiddens)
+    whole = pl.BlockSpec((depth, chans), lambda i: (0, 0))
+    return pl.pallas_call(
+        mm2_kernel,
+        grid=(steps,),
+        in_specs=[pl.BlockSpec((tokens, depth), lambda i: (0, 0))] * steps + [whole] * 2,
+        out_specs=[pl.BlockSpec((rows, 2 * chans), lambda i: (i, 0))] * count,
+        out_shape=[jax.ShapeDtypeStruct((steps * rows, 2 * chans), BF)] * count,
+        compiler_params=params(58),
         cost_estimate=pl.CostEstimate(
-            flops=2 * tokens * depth * cols * chans,
-            bytes_accessed=2 * (tokens * depth + depth * cols * chans + tokens * cols * chans),
+            flops=4 * steps * tokens * depth * chans,
+            bytes_accessed=2 * (steps * tokens * depth + 2 * depth * chans + 2 * steps * tokens * chans),
             transcendentals=0,
         ),
-    )(hidden, *weights)
-
-
-def pair_kernel(a1, b1, a2, b2, o1, o2):
-    o1[...] = (a1[...].astype(F32) + b1[...].astype(F32)).astype(BF)
-    o2[...] = (a2[...].astype(F32) + b2[...].astype(F32)).astype(BF)
-
-
-def add_pairs(*parts):
+    )(*hiddens, own, other)
+
+
+def pair_kernel(a, b, o):
+    o[...] = (a[...].astype(F32) + b[...].astype(F32)).astype(BF)
+
+
+def add_pair(a, b):
+    rows, width = a.shape
+    block = pl.BlockSpec((rows // 2, width), lambda j: (j, 0))
+    return pl.pallas_call(
+        pair_kernel,
+        grid=(2,),
+        in_specs=[block] * 2,
+        out_specs=block,
+        out_shape=jax.ShapeDtypeStruct((rows, width), BF),
+        compiler_params=params(16),
+    )(a, b)
+
+
+def add_kernel(half, a, b, c, *outs):
+    total = a[...].astype(F32) + (b[...].astype(F32) + c[...].astype(F32))
+    for s, o_ref in enumerate(outs):
+        for x in range(total.shape[0] // (SIDE * half)):
+            at = (x * SIDE + s) * half
+            o_ref[x * half : (x + 1) * half, :] = total[at : at + half].astype(BF)
+
+
+def add_pieces(half, *parts):
     rows, width = parts[0].shape
-    tile = width // 2
-    block = pl.BlockSpec((rows, tile), lambda j: (0, j))
-    return pl.pallas_call(
-        pair_kernel,
-        grid=(width // tile,),
-        in_specs=[block] * 4,
-        out_specs=[block] * 2,
-        out_shape=[jax.ShapeDtypeStruct((rows, width), BF)] * 2,
-        compiler_params=params(24),
-    )(*parts)
-
-
-def add_kernel(a, b, c, *outs):
-    total = a[...].astype(F32) + (b[...].astype(F32) + c[...].astype(F32))
-    rows = outs[0].shape[0]
-    for i, o_ref in enumerate(outs):
-        o_ref[...] = total[i * rows : (i + 1) * rows].astype(BF)
-
-
-def add_pieces(*parts):
-    rows, width = parts[0].shape
-    tile = width // 2
-    return pl.pallas_call(
-        add_kernel,
-        grid=(width // tile,),
-        in_specs=[pl.BlockSpec((rows, tile), lambda j: (0, j))] * len(parts),
-        out_specs=[pl.BlockSpec((rows // SIDE, tile), lambda j: (0, j))] * SIDE,
+    return pl.pallas_call(
+        functools.partial(add_kernel, half),
+        grid=(2,),
+        in_specs=[pl.BlockSpec((rows // 2, width), lambda j: (j, 0))] * len(parts),
+        out_specs=[pl.BlockSpec((rows // SIDE // 2, width), lambda j: (j, 0))] * SIDE,
         out_shape=[jax.ShapeDtypeStruct((rows // SIDE, width), BF)] * SIDE,
         compiler_params=params(24),
     )(*parts)
 
 
-def last_kernel(place_ref, a, b, c, d, e, f, g, h, o_ref):
-    half = a.shape[0]
-    cols, _, chans = o_ref.shape
-    for j in range(cols):
-        at = pl.ds(j * chans, chans)
-        top, low = [
-            sum(p[:, at].astype(F32) for p in parts).astype(BF)
-            for parts in ((a, b, c, d), (e, f, g, h))
-        ]
-        o_ref[place_ref[j], :half, :] = top
-        o_ref[place_ref[j], half:, :] = low
-
-
-def add_last(place, first, second, cols):
-    half, width = first[0].shape
-    return pl.pallas_call(
-        last_kernel,
-        in_specs=[pl.BlockSpec(memory_space=pltpu.SMEM)] + [pl.BlockSpec(memory_space=pltpu.VMEM)] * 8,
-        out_shape=jax.ShapeDtypeStruct((cols, 2 * half, width // cols), BF),
+def sum_kernel(a, b, c, d, own_ref, other_ref):
+    chans = own_ref.shape[1]
+    total = (a[...].astype(F32) + b[...].astype(F32)) + (c[...].astype(F32) + d[...].astype(F32))
+    own_ref[...] = total[:, :chans]
+    other_ref[...] = total[:, chans:].astype(BF)
+
+
+def add_last(parts):
+    rows, width = parts[0].shape
+    return pl.pallas_call(
+        sum_kernel,
+        out_shape=[
+            jax.ShapeDtypeStruct((rows, width // 2), F32),
+            jax.ShapeDtypeStruct((rows, width // 2), BF),
+        ],
         compiler_params=params(16),
-    )(place, *first, *second)
+    )(*parts)
+
+
+def finish_kernel(place_ref, own1, own2, got1, got2, resid_ref, bias_ref, o_ref):
+    half = o_ref.shape[1] // 2
+    for i in range(2 * SIDE):
+        at = pl.ds(i % SIDE * half, half)
+        for k, part in enumerate((own1, own2) if i < SIDE else (got1, got2)):
+            to = pl.ds(k * half, half)
+            value = part[at, :].astype(F32) + resid_ref[place_ref[i], to, :] + bias_ref[...]
+            o_ref[place_ref[i], to, :] = value.astype(BF)
+
+
+def finish(place, own1, own2, got1, got2, resid, bias):
+    return pl.pallas_call(
+        finish_kernel,
+        in_specs=[pl.BlockSpec(memory_space=pltpu.SMEM)] + [pl.BlockSpec(memory_space=pltpu.VMEM)] * 6,
+        out_shape=jax.ShapeDtypeStruct(resid.shape, BF),
+        compiler_params=params(16),
+    )(place, own1, own2, got1, got2, resid, bias[None])
 
 
 def exchange(a, axis):
@@ -250,7 +244,7 @@
         out_specs=[anywhere] * count,
         out_shape=[jax.ShapeDtypeStruct(v.shape, v.dtype) for v in values],
         input_output_aliases={i: i for i in range(count)},
-        compiler_params=params(1),
+        compiler_params=params(62),
     )(*values, *others)
 
 
@@ -304,6 +298,19 @@
 def gather_near(a, axis):
     far, *near = [hop(a, axis, (s, s)) for s in (2, 1, -1)]
     return jnp.stack([a, *near, far]).reshape(-1, a.shape[1])
+
+
+def gather_far(a, axis):
+    one, two = hop(a, axis, APART), hop(a, axis, OTHER)
+    return [a, one, two, hop(one, axis, APART)]
+
+
+def reduce_far(outs, large, small, half):
+    own, fore, back, far = outs
+    far = hop(far, large, OTHER)
+    back = hop(back, large, APART)
+    fore = hop(add_pair(fore, far), large, OTHER)
+    return send_back(add_pieces(half, own, back, fore), small)
 
 
 def send_back(parts, axis):
@@ -328,31 +335,19 @@
         axis=1,
     )
     moved = exchange(message, "col")
-    moved, later = tie([moved, w_out], [])
-    one = hop(later, "x", APART)
     first, second = normalize(moved, half)
     first, second = gather_near(first, "z"), gather_near(second, "y")
-    first, second, later = tie([first, second, later], [])
-    two = hop(later, "x", OTHER)
-    first = [first, hop(first, "y", APART), hop(first, "y", OTHER)]
-    second = [second, hop(second, "z", APART), hop(second, "z", OTHER)]
-    first[1], second[1], one = tie([first[1], second[1], one], [])
-    three = hop(one, "x", APART)
-    first.append(hop(first[1], "y", APART))
-    second.append(hop(second[1], "z", APART))
-    *pieces, later, one, two = tie(first + second + [later, one, two], [])
-    own_swap, one_swap, two_swap = swap_cores(later), swap_cores(one), swap_cores(two)
-    hidden = matmul_in(pieces, w_in_all, b_in)
-    hidden, three = tie([hidden, three], [])
-    blocks = [later, one, two, three, own_swap, one_swap, two_swap, swap_cores(three)]
-    own1, fore1, back1, far1, own2, fore2, back2, far2 = matmul_out(hidden, blocks, len(pieces))
-    back1, back2 = hop(back1, "y", APART), hop(back2, "z", APART)
-    fore1, fore2 = add_pairs(fore1, hop(far1, "y", OTHER), fore2, hop(far2, "z", OTHER))
-    first = add_pieces(own1, back1, hop(fore1, "y", OTHER))
-    second = add_pieces(own2, back2, hop(fore2, "z", OTHER))
-    first, second = send_back(first, "z"), send_back(second, "y")
-    proj = exchange(add_last(block_places(), first, second, cols), "col")
-    result = (resid + proj.reshape(tokens, chans).astype(F32) + b_out).astype(BF)
+    parts = [gather_far(first, "y"), gather_far(second, "z")]
+    hiddens = [gather_far(matmul_in(part, w_in_all, b_in), "x") for part in parts]
+    other = swap_cores(w_out)
+    sums = []
+    for hidden, (large, small) in zip(hiddens, (("y", "z"), ("z", "y"))):
+        outs = matmul_out(hidden, w_out, other, SIDE)
+        sums.append(add_last(reduce_far(outs, large, small, half)))
+    (own1, give1), (own2, give2) = sums
+    got1, got2 = swap_cores(give1), swap_cores(give2)
+    resid = resid.reshape(cols, own, chans)
+    result = finish(block_places(), own1, own2, got1, got2, resid, b_out)
     return result.reshape(rows_here, width, chans)
 
 

time: 326 us -> 277 us (0.85)
  waiting for transfers between devices: 138 us -> 95.6 us
  local copies, waits for them, and re-layouts: 27.2 us -> 5.84 us
  Pallas kernels: 29.4 us -> 46.6 us
  starting transfers between devices: 46.4 us -> 62.2 us
  blocking collectives: 58.2 us -> 42.6 us
    ppermute x27 -> x30, waiting for transfers between devices: 119 us -> 74.6 us  [hop(): return lax.ppermute(a, ('row', 'col'), pairs)]
    unnamed x59 -> x50, local copies, waits for them, and re-layouts: 19.9 us -> 2.34 us
    all_to_all x2 -> x1, blocking collectives: 45 us -> 29.4 us  [exchange(): return lax.all_to_all(a, axis, split_axis=0, concat_axis=0, tiled=True)]
    ppermute x4 -> x3, starting transfers between devices: 3.44 us -> 13.8 us  [swap_cores(): return lax.ppermute(a, 'col', pairs)]
    pallas_call x1 -> x2, Pallas kernels: 13.7 us -> 23.7 us  [matmul_in(): pl.pallas_call(mm1_kernel, grid=(width // tile,), in_specs=[pl.BlockSpec(...]
    pallas_call x10 -> x9, Pallas kernels: 15.4 us -> 22.5 us  [the longest x2 19.9 us: matmul_out(): pl.pallas_call(mm2_kernel, grid=(steps,), in_specs=[pl.BlockSpec((tokens,...]
    ppermute x27 -> x30, starting transfers between devices: 31.3 us -> 36.8 us  [hop(): return lax.ppermute(a, ('row', 'col'), pairs)]
    all_to_all x2, waiting for transfers between devices: 15.1 us -> 20 us  [exchange(): return lax.all_to_all(a, axis, split_axis=0, concat_axis=0, tiled=True)]
  transfers between devices with their start and end apart: 34 -> 36, of which waited for: 23 -> 19; matrix products, arithmetic and copies ran while one was open for 6% -> 4% of each run, Pallas kernels for 5% -> 16%
where the time goes in v5:
time: 277 us; the launch traced here: 274 us
  waiting for transfers between devices  95.6 us (35%)
  starting transfers between devices  62.2 us (22%)
  Pallas kernels  46.6 us (17%)
  blocking collectives  42.6 us (15%)
  between operations  13.7 us (5%)
  matrix products  7.31 us (3%)
  local copies, waits for them, and re-layouts  5.84 us (2%)
    ppermute x30, waiting for transfers between devices, hop(): return lax.ppermute(a, ('row', 'col'), pairs)  74.6 us
    ppermute x30, starting transfers between devices, hop(): return lax.ppermute(a, ('row', 'col'), pairs)  36.8 us
    all_to_all x1, blocking collectives, exchange(): return lax.all_to_all(a, axis, split_axis=0, concat_axis=0, tiled=True)  29.4 us
    pallas_call x2, Pallas kernels, matmul_in(): pl.pallas_call(mm1_kernel, grid=(width // tile,), in_specs=[pl.BlockSpec(...  23.7 us
    all_to_all x2, waiting for transfers between devices, exchange(): return lax.all_to_all(a, axis, split_axis=0, concat_axis=0, tiled=True)  20 us
    pallas_call x2, Pallas kernels, matmul_out(): pl.pallas_call(mm2_kernel, grid=(steps,), in_specs=[pl.BlockSpec((tokens,...  19.9 us
    ppermute x3, starting transfers between devices, swap_cores(): return lax.ppermute(a, 'col', pairs)  13.8 us
    psum x1, blocking collectives, spectral(): lax.psum((jnp.sum(source, axis=-1), jnp.sum(source * source, axis=-1)), '...  13.2 us
  transfers between devices with their start and end apart: 36, of which 19 were waited for; matrix products, arithmetic and copies ran while one was open for 4% of the time, Pallas kernels for 16%

profile of v5, /device:TPU:1, one launch (start us, length us, event | category | flops | bytes accessed | tf_op | source)
XLA Modules:
  0.0 274.5 jit_solution(3748601653200654204)
XLA Ops:
  6.5 0.7 all-gather.2.cloned.1.call-update
  7.3 0.3 copy-done.4
  7.9 13.2 %all-reduce.1 = (f32[256]{0:T(256)S(1)}, f32[256]{0:T(256)S(1)}) all-reduce(f32[256]{0:T(256)S(1)} %reduce_sum.25, f32[256]{0:T(256)S(1)} %reduce_sum.23), channel_id=1, replica_groups=mesh['row'=16,'col'=8] {'col'}, use_global_device_ids=true, to_apply=%region_3.0 | all-reduce | flops 512 | bytes 4096 | tf_op jit(solution)/shard_map/psum | solution.py:259
  21.3 1.6 convolution_convert_fusion
  23.0 7.8 %all-to-all-start = ((bf16[16,32,768]{2,1,0:T(8,128)(2,1)}), bf16[16,32,768]{2,1,0:T(8,128)(2,1)S(1)}, u32[]{:S(2)}, u32[]{:S(2)}) async-start(bf16[16,32,768]{2,1,0:T(8,128)(2,1)} %bitcast.3), calls=%async_computation | async-start | bytes 1572864 | tf_op jit(solution)/shard_map/all_to_all | solution.py:231
  30.8 1.5 fusion.19
  32.9 9.7 %all-to-all-done = bf16[16,32,768]{2,1,0:T(8,128)(2,1)S(1)} async-done(((bf16[16,32,768]{2,1,0:T(8,128)(2,1)}), bf16[16,32,768]{2,1,0:T(8,128)(2,1)S(1)}, u32[]{:S(2)}, u32[]{:S(2)}) %all-to-all-start) | async-done | bytes 786464 | tf_op jit(solution)/shard_map/all_to_all | solution.py:231
  42.6 2.3 fusion.21
  44.9 0.9 fusion.5
  45.9 1.8 add_convert_fusion
  47.8 3.7 %all-to-all-start.1 = ((bf16[16,32,768]{2,1,0:T(8,128)(2,1)}), bf16[16,32,768]{2,1,0:T(8,128)(2,1)S(1)}, u32[]{:S(2)}, u32[]{:S(2)}) async-start(bf16[16,32,768]{2,1,0:T(8,128)(2,1)} %bitcast.6), calls=%async_computation.1 | async-start | bytes 1572864 | tf_op jit(solution)/shard_map/all_to_all | solution.py:231
  51.6 10.4 %all-to-all-done.1 = bf16[16,32,768]{2,1,0:T(8,128)(2,1)S(1)} async-done(((bf16[16,32,768]{2,1,0:T(8,128)(2,1)}), bf16[16,32,768]{2,1,0:T(8,128)(2,1)S(1)}, u32[]{:S(2)}, u32[]{:S(2)}) %all-to-all-start.1) | async-done | bytes 786464 | tf_op jit(solution)/shard_map/all_to_all | solution.py:231
  62.0 0.6 fusion.20
  62.6 29.4 %all_to_all.15.moved_ref = bf16[8,48,768]{2,1,0:T(8,128)(2,1)S(1)} all-to-all(bf16[8,48,768]{2,1,0:T(8,128)(2,1)S(1)} %pad_maximum_fusion.2), channel_id=1, replica_groups=mesh['row'=16,'col'=8] {'col'}, dimensions={0} | all-to-all | bytes 1179648 | tf_op jit(solution)/shard_map/all_to_all | solution.py:231
  92.1 0.3 shard_map.127
  92.4 0.6 collective-permute-start.18
  92.9 2.2 collective-permute-start.17
  95.2 0.5 collective-permute-start.2
  95.7 1.7 collective-permute-start.1
  97.4 2.1 collective-permute-done.18
  99.5 2.1 collective-permute-done.17
  101.6 2.7 %collective-permute-done.16 = bf16[16,6144]{1,0:T(8,128)(2,1)S(1)} collective-permute-done((bf16[16,6144]{1,0:T(8,128)(2,1)S(1)}, bf16[16,6144]{1,0:T(8,128)(2,1)S(1)}, u32[]{:S(2)}, u32[]{:S(2)}) %collective-permute-start.16) | collective-permute-done | bytes 196640 | tf_op jit(solution)/shard_map/ppermute | solution.py:53
  104.5 0.6 collective-permute-start.19
  105.1 1.2 collective-permute-done
  106.4 2.7 collective-permute-start.3
  109.1 8.8 %collective-permute-done.19.refs_1_ = bf16[64,6144]{1,0:T(8,128)(2,1)S(1)} collective-permute-done((bf16[64,6144]{1,0:T(8,128)(2,1)S(1)}, bf16[64,6144]{1,0:T(8,128)(2,1)S(1)}, u32[]{:S(2)}, u32[]{:S(2)}) %collective-permute-start.19) | collective-permute-done | bytes 786464 | tf_op jit(solution)/shard_map/ppermute | solution.py:53
  117.8 2.6 collective-permute-start.21
  120.5 3.8 %collective-permute-start.9 = (bf16[1536,768]{1,0:T(8,128)(2,1)}, bf16[1536,768]{1,0:T(8,128)(2,1)}, u32[]{:S(2)}, u32[]{:S(2)}) collective-permute-start(bf16[1536,768]{1,0:T(8,128)(2,1)} %refs_4_.3), channel_id=1, source_target_pairs={{0,1},{1,0},{2,3},{3,2},{4,5},{5,4},{6,7},{7,6},{8,9},{9,8},{10,11... | collective-permute-start | bytes 7077896 | tf_op jit(solution)/shard_map/ppermute | solution.py:62
  124.3 0.5 collective-permute-start.4
  124.8 2.2 collective-permute-start.5
  127.0 0.6 broadcast_in_dim.7.refs_5_
  127.6 0.9 copy-done.9
  128.5 4.1 %collective-permute-done.21.refs_3_ = bf16[64,6144]{1,0:T(8,128)(2,1)} collective-permute-done((bf16[64,6144]{1,0:T(8,128)(2,1)S(1)}, bf16[64,6144]{1,0:T(8,128)(2,1)}, u32[]{:S(2)}, u32[]{:S(2)}) %collective-permute-start.21) | collective-permute-done | bytes 786464 | tf_op jit(solution)/shard_map/ppermute | solution.py:53
  132.6 11.9 %shard_map.133.refs_0_ = bf16[256,1536]{1,0:T(8,128)(2,1)} custom-call(bf16[64,6144]{1,0:T(8,128)(2,1)} %bitcast.44, bf16[64,6144]{1,0:T(8,128)(2,1)} %copy-done.8, bf16[64,6144]{1,0:T(8,128)(2,1)} %copy-done.9, bf16[64,6144]{1,0:T(8,128)(2,1)} %collective-permute-done.21.refs_3_, bf16[6144,1536]{1,0:T(8,128)(2,1)} %all-gather.2.cloned.1.call-done.refs_4_, ...), custom_call_target="tpu_custom_call" | custom-call | flops 4831838208 | bytes 22020096 | tf_op jit(solution)/shard_map/pallas_call | solution.py:101
  144.5 1.0 collective-permute-start.22
  145.5 11.8 %shard_map.128.refs_0_ = bf16[256,1536]{1,0:T(8,128)(2,1)} custom-call(bf16[64,6144]{1,0:T(8,128)(2,1)} %bitcast.47, bf16[64,6144]{1,0:T(8,128)(2,1)} %collective-permute-done.3.refs_1_, bf16[64,6144]{1,0:T(8,128)(2,1)} %collective-permute-done.4.refs_2_, bf16[64,6144]{1,0:T(8,128)(2,1)} %collective-permute-done.5.refs_3_, ...), custom_call_target="tpu_custom_call" | custom-call | flops 4831838208 | bytes 22020096 | tf_op jit(solution)/shard_map/pallas_call | solution.py:101
  157.5 1.3 collective-permute-start.23
  158.8 1.4 collective-permute-start.24
  160.3 11.7 %collective-permute-done.6.refs_1_ = bf16[256,1536]{1,0:T(8,128)(2,1)S(1)} collective-permute-done((bf16[256,1536]{1,0:T(8,128)(2,1)}, bf16[256,1536]{1,0:T(8,128)(2,1)S(1)}, u32[]{:S(2)}, u32[]{:S(2)}) %collective-permute-start.6) | collective-permute-done | bytes 786464 | tf_op jit(solution)/shard_map/ppermute | solution.py:53
  171.9 3.3 %collective-permute-done.23.refs_2_ = bf16[256,1536]{1,0:T(8,128)(2,1)S(1)} collective-permute-done((bf16[256,1536]{1,0:T(8,128)(2,1)S(1)}, bf16[256,1536]{1,0:T(8,128)(2,1)S(1)}, u32[]{:S(2)}, u32[]{:S(2)}) %collective-permute-start.23) | collective-permute-done | bytes 786464 | tf_op jit(solution)/shard_map/ppermute | solution.py:53
  175.3 13.6 %collective-permute-done.24.refs_3_ = bf16[256,1536]{1,0:T(8,128)(2,1)} collective-permute-done((bf16[256,1536]{1,0:T(8,128)(2,1)S(1)}, bf16[256,1536]{1,0:T(8,128)(2,1)}, u32[]{:S(2)}, u32[]{:S(2)}) %collective-permute-start.24) | collective-permute-done | bytes 786464 | tf_op jit(solution)/shard_map/ppermute | solution.py:53
  188.9 10.0 %shard_map.134 = (bf16[256,1536]{1,0:T(8,128)(2,1)}, bf16[256,1536]{1,0:T(8,128)(2,1)}, bf16[256,1536]{1,0:T(8,128)(2,1)}, bf16[256,1536]{1,0:T(8,128)(2,1)}) custom-call(bf16[256,1536]{1,0:T(8,128)(2,1)} %shard_map.133.refs_0_, bf16[256,1536]{1,0:T(8,128)(2,1)} %copy-done.21, bf16[256,1536]{1,0:T(8,128)(2,1)} %copy-done.24, ...), custom_call_target="tpu_custom_call" | custom-call | flops 4831838208 | bytes 11010048 | tf_op jit(solution)/shard_map/pallas_call | solution.py:140
  198.9 2.3 collective-permute-start.26
  201.2 1.2 collective-permute-done.8.refs_3_
  202.4 0.9 copy-done.23
  203.3 9.9 %shard_map.129 = (bf16[256,1536]{1,0:T(8,128)(2,1)}, bf16[256,1536]{1,0:T(8,128)(2,1)}, bf16[256,1536]{1,0:T(8,128)(2,1)}, bf16[256,1536]{1,0:T(8,128)(2,1)}) custom-call(bf16[256,1536]{1,0:T(8,128)(2,1)} %shard_map.128.refs_0_, bf16[256,1536]{1,0:T(8,128)(2,1)} %copy-done.20, bf16[256,1536]{1,0:T(8,128)(2,1)} %copy-done.22, bf16[256,1536]{1,0:T(8,128)(2,1)} %copy-done.23, ...), custom_call_target="tpu_custom_call" | custom-call | flops 4831838208 | bytes 11010048 | tf_op jit(solution)/shard_map/pallas_call | solution.py:140
  213.3 2.5 collective-permute-start.25
  216.1 3.0 %collective-permute-start.10 = (bf16[256,1536]{1,0:T(8,128)(2,1)S(1)}, bf16[256,1536]{1,0:T(8,128)(2,1)S(1)}, u32[]{:S(2)}, u32[]{:S(2)}) collective-permute-start(bf16[256,1536]{1,0:T(8,128)(2,1)S(1)} %copy-done.18), channel_id=1, source_target_pairs={{0,8},{1,25},{2,10},{3,27},{4,12},{5,29},{6,14},{7,31},{8,16},{9,1... | collective-permute-start | bytes 2359304 | tf_op jit(solution)/shard_map/ppermute | solution.py:53
  219.2 6.6 %collective-permute-done.11.b = bf16[256,1536]{1,0:T(8,128)(2,1)S(1)} collective-permute-done((bf16[256,1536]{1,0:T(8,128)(2,1)}, bf16[256,1536]{1,0:T(8,128)(2,1)S(1)}, u32[]{:S(2)}, u32[]{:S(2)}) %collective-permute-start.11) | collective-permute-done | bytes 786464 | tf_op jit(solution)/shard_map/ppermute | solution.py:53
  226.1 2.3 collective-permute-done.25.b
  228.4 1.4 collective-permute-done.27.c
  229.8 0.3 shard_map.136
  230.1 5.1 %collective-permute-start.28 = (bf16[64,1536]{1,0:T(8,128)(2,1)S(1)}, bf16[64,1536]{1,0:T(8,128)(2,1)S(1)}, u32[]{:S(2)}, u32[]{:S(2)}) collective-permute-start(bf16[64,1536]{1,0:T(8,128)(2,1)S(1)} %get-tuple-element.43), channel_id=1, source_target_pairs={{0,24},{1,25},{2,26},{3,27},{4,28},{5,29},{6,30},{7,31},{8,0},{9,1... | collective-permute-start | bytes 589832 | tf_op jit(solution)/shard_map/ppermute | solution.py:53
  235.2 4.0 %collective-permute-start.30 = (bf16[64,1536]{1,0:T(8,128)(2,1)S(1)}, bf16[64,1536]{1,0:T(8,128)(2,1)S(1)}, u32[]{:S(2)}, u32[]{:S(2)}) collective-permute-start(bf16[64,1536]{1,0:T(8,128)(2,1)S(1)} %get-tuple-element.45), channel_id=1, source_target_pairs={{0,16},{1,17},{2,18},{3,19},{4,20},{5,21},{6,22},{7,23},{8,24},{9,... | collective-permute-start | bytes 589832 | tf_op jit(solution)/shard_map/ppermute | solution.py:53
  239.2 7.0 %collective-permute-done.12.c = bf16[256,1536]{1,0:T(8,128)(2,1)S(1)} collective-permute-done((bf16[256,1536]{1,0:T(8,128)(2,1)S(1)}, bf16[256,1536]{1,0:T(8,128)(2,1)S(1)}, u32[]{:S(2)}, u32[]{:S(2)}) %collective-permute-start.12) | collective-permute-done | bytes 786464 | tf_op jit(solution)/shard_map/ppermute | solution.py:53
  246.5 0.9 collective-permute-start.13
  247.4 0.7 collective-permute-start.14
  248.1 0.6 collective-permute-start.15
  248.7 1.8 collective-permute-done.29.c
  250.4 4.7 %collective-permute-done.30.d = bf16[64,1536]{1,0:T(8,128)(2,1)S(1)} collective-permute-done((bf16[64,1536]{1,0:T(8,128)(2,1)S(1)}, bf16[64,1536]{1,0:T(8,128)(2,1)S(1)}, u32[]{:S(2)}, u32[]{:S(2)}) %collective-permute-start.30) | collective-permute-done | bytes 196640 | tf_op jit(solution)/shard_map/ppermute | solution.py:53
  255.2 6.1 %collective-permute-start.32 = (bf16[64,768]{1,0:T(8,128)(2,1)S(1)}, bf16[64,768]{1,0:T(8,128)(2,1)S(1)}, u32[]{:S(2)}, u32[]{:S(2)}) collective-permute-start(bf16[64,768]{1,0:T(8,128)(2,1)S(1)} %get-tuple-element.48), channel_id=1, source_target_pairs={{0,1},{1,0},{2,3},{3,2},{4,5},{5,4},{6,7},{7,6},{8,9},{9,8},{10,11... | collective-permute-start | bytes 294920 | tf_op jit(solution)/shard_map/ppermute | solution.py:62
  261.4 3.9 %collective-permute-start.31 = (bf16[64,768]{1,0:T(8,128)(2,1)S(1)}, bf16[64,768]{1,0:T(8,128)(2,1)S(1)}, u32[]{:S(2)}, u32[]{:S(2)}) collective-permute-start(bf16[64,768]{1,0:T(8,128)(2,1)S(1)} %get-tuple-element.47), channel_id=1, source_target_pairs={{0,1},{1,0},{2,3},{3,2},{4,5},{5,4},{6,7},{7,6},{8,9},{9,8},{10,11... | collective-permute-start | bytes 294920 | tf_op jit(solution)/shard_map/ppermute | solution.py:62
  265.3 0.7 dynamic-slice_bitcast_fusion.place_ref
  266.3 1.4 shard_map.138
  (98 shorter events, 3.3 us)
Async XLA Ops:
  6.5 14.8 %copy-start.13 = (f32[512,256]{1,0:T(8,128)S(1)}, f32[512,256]{1,0:T(8,128)}, u32[]{:S(2)}) copy-start(f32[512,256]{1,0:T(8,128)} %constant.28.clone) | copy-start | bytes 1572868
  6.5 1.1 copy-start.4
  6.5 14.6 %copy-start.15 = (f32[768]{0:T(1024)S(1)}, f32[768]{0:T(1024)}, u32[]{:S(2)}) copy-start(f32[768]{0:T(1024)} %param.15) | copy-start | bytes 9220
  6.5 126.1 %all-gather.2.cloned.1.call-start = ((), (), s32[]{:S(2)}) async-start(), calls=%async_computation.3 | async-start | bytes 21233664 | tf_op jit(solution)/shard_map/all_gather | solution.py:324
  23.0 19.6 %all-to-all-start = ((bf16[16,32,768]{2,1,0:T(8,128)(2,1)}), bf16[16,32,768]{2,1,0:T(8,128)(2,1)S(1)}, u32[]{:S(2)}, u32[]{:S(2)}) async-start(bf16[16,32,768]{2,1,0:T(8,128)(2,1)} %bitcast.3), calls=%async_computation | async-start | bytes 1572864 | tf_op jit(solution)/shard_map/all_to_all | solution.py:231
  42.5 2.3 copy-start.11
  44.9 1.0 copy-start.10
  47.8 3.8 %copy-start.17 = (f32[768]{0:T(1024)S(1)}, f32[768]{0:T(1024)}, u32[]{:S(2)}) copy-start(f32[768]{0:T(1024)} %param.16) | copy-start | bytes 9220
  47.8 14.2 %copy-start.12 = (f32[256,512]{1,0:T(8,128)S(1)}, f32[256,512]{1,0:T(8,128)}, u32[]{:S(2)}) copy-start(f32[256,512]{1,0:T(8,128)} %constant.31.clone) | copy-start | bytes 1572868
  47.8 14.2 %all-to-all-start.1 = ((bf16[16,32,768]{2,1,0:T(8,128)(2,1)}), bf16[16,32,768]{2,1,0:T(8,128)(2,1)S(1)}, u32[]{:S(2)}, u32[]{:S(2)}) async-start(bf16[16,32,768]{2,1,0:T(8,128)(2,1)} %bitcast.6), calls=%async_computation.1 | async-start | bytes 1572864 | tf_op jit(solution)/shard_map/all_to_all | solution.py:231
  92.4 7.1 %collective-permute-start.18 = (bf16[16,6144]{1,0:T(8,128)(2,1)S(1)}, bf16[16,6144]{1,0:T(8,128)(2,1)S(1)}, u32[]{:S(2)}, u32[]{:S(2)}) collective-permute-start(bf16[16,6144]{1,0:T(8,128)(2,1)S(1)} %get-tuple-element.37), channel_id=1, source_target_pairs={{0,16},{1,17},{2,18},{3,19},{4,20},{5,21},{6,22},{7,23},{8,24},{9,... | collective-permute-start | bytes 589832 | tf_op jit(solution)/shard_map/ppermute | solution.py:53
  92.9 8.7 %collective-permute-start.17 = (bf16[16,6144]{1,0:T(8,128)(2,1)S(1)}, bf16[16,6144]{1,0:T(8,128)(2,1)S(1)}, u32[]{:S(2)}, u32[]{:S(2)}) collective-permute-start(bf16[16,6144]{1,0:T(8,128)(2,1)S(1)} %get-tuple-element.37), channel_id=1, source_target_pairs={{0,24},{1,25},{2,26},{3,27},{4,28},{5,29},{6,30},{7,31},{8,0},{9,1... | collective-permute-start | bytes 589832 | tf_op jit(solution)/shard_map/ppermute | solution.py:53
  95.2 9.2 %collective-permute-start.16 = (bf16[16,6144]{1,0:T(8,128)(2,1)S(1)}, bf16[16,6144]{1,0:T(8,128)(2,1)S(1)}, u32[]{:S(2)}, u32[]{:S(2)}) collective-permute-start(bf16[16,6144]{1,0:T(8,128)(2,1)S(1)} %get-tuple-element.37), channel_id=1, source_target_pairs={{0,8},{1,9},{2,10},{3,11},{4,12},{5,13},{6,14},{7,15},{8,16},{9,17... | collective-permute-start | bytes 589832 | tf_op jit(solution)/shard_map/ppermute | solution.py:53
  95.2 9.9 %collective-permute-start.2 = (bf16[16,6144]{1,0:T(8,128)(2,1)S(1)}, bf16[16,6144]{1,0:T(8,128)(2,1)S(1)}, u32[]{:S(2)}, u32[]{:S(2)}) collective-permute-start(bf16[16,6144]{1,0:T(8,128)(2,1)S(1)} %get-tuple-element.27), channel_id=1, source_target_pairs={{0,64},{1,65},{2,66},{3,67},{4,68},{5,69},{6,70},{7,71},{8,72},{9,... | collective-permute-start | bytes 589832 | tf_op jit(solution)/shard_map/ppermute | solution.py:53
  95.7 9.4 %collective-permute-start.1 = (bf16[16,6144]{1,0:T(8,128)(2,1)S(1)}, bf16[16,6144]{1,0:T(8,128)(2,1)S(1)}, u32[]{:S(2)}, u32[]{:S(2)}) collective-permute-start(bf16[16,6144]{1,0:T(8,128)(2,1)S(1)} %get-tuple-element.27), channel_id=1, source_target_pairs={{0,96},{1,97},{2,98},{3,99},{4,100},{5,101},{6,102},{7,103},{8,104... | collective-permute-start | bytes 589832 | tf_op jit(solution)/shard_map/ppermute | solution.py:53
  99.5 6.8 %collective-permute-start = (bf16[16,6144]{1,0:T(8,128)(2,1)S(1)}, bf16[16,6144]{1,0:T(8,128)(2,1)S(1)}, u32[]{:S(2)}, u32[]{:S(2)}) collective-permute-start(bf16[16,6144]{1,0:T(8,128)(2,1)S(1)} %get-tuple-element.27), channel_id=1, source_target_pairs={{0,32},{1,33},{2,34},{3,35},{4,36},{5,37},{6,38},{7,39},{8,40},{9,... | collective-permute-start | bytes 589832 | tf_op jit(solution)/shard_map/ppermute | solution.py:53
  104.3 22.6 %copy-start.14 = (f32[1536]{0:T(1024)S(1)}, f32[1536]{0:T(1024)}, u32[]{:S(2)}) copy-start(f32[1536]{0:T(1024)} %param.18) | copy-start | bytes 18436
  104.5 28.2 %copy-start.5 = (bf16[4,16,6144]{2,1,0:T(8,128)(2,1)}, bf16[4,16,6144]{2,1,0:T(8,128)(2,1)S(1)}, u32[]{:S(2)}) copy-start(bf16[4,16,6144]{2,1,0:T(8,128)(2,1)S(1)} %pad_maximum_fusion.1) | copy-start | bytes 2359300
  104.5 13.4 %collective-permute-start.19 = (bf16[64,6144]{1,0:T(8,128)(2,1)S(1)}, bf16[64,6144]{1,0:T(8,128)(2,1)S(1)}, u32[]{:S(2)}, u32[]{:S(2)}) collective-permute-start(bf16[64,6144]{1,0:T(8,128)(2,1)S(1)} %bitcast.42), channel_id=1, source_target_pairs={{0,32},{1,97},{2,34},{3,99},{4,36},{5,101},{6,38},{7,103},{8,40},{... | collective-permute-start | bytes 2359304 | tf_op jit(solution)/shard_map/ppermute | solution.py:53
  106.4 38.1 %copy-start.6 = (bf16[4,16,6144]{2,1,0:T(8,128)(2,1)}, bf16[4,16,6144]{2,1,0:T(8,128)(2,1)S(1)}, u32[]{:S(2)}) copy-start(bf16[4,16,6144]{2,1,0:T(8,128)(2,1)S(1)} %pad_maximum_fusion) | copy-start | bytes 2359300
  106.4 18.4 %collective-permute-start.3 = (bf16[64,6144]{1,0:T(8,128)(2,1)S(1)}, bf16[64,6144]{1,0:T(8,128)(2,1)}, u32[]{:S(2)}, u32[]{:S(2)}) collective-permute-start(bf16[64,6144]{1,0:T(8,128)(2,1)S(1)} %bitcast.45), channel_id=1, source_target_pairs={{0,8},{1,25},{2,10},{3,27},{4,12},{5,29},{6,14},{7,31},{8,16},{9,1... | collective-permute-start | bytes 2359304 | tf_op jit(solution)/shard_map/ppermute | solution.py:53
  109.1 18.5 %collective-permute-start.20 = (bf16[64,6144]{1,0:T(8,128)(2,1)S(1)}, bf16[64,6144]{1,0:T(8,128)(2,1)S(1)}, u32[]{:S(2)}, u32[]{:S(2)}) collective-permute-start(bf16[64,6144]{1,0:T(8,128)(2,1)S(1)} %bitcast.43), channel_id=1, source_target_pairs={{0,96},{1,33},{2,98},{3,35},{4,100},{5,37},{6,102},{7,39},{8,104},... | collective-permute-start | bytes 2359304 | tf_op jit(solution)/shard_map/ppermute | solution.py:53
  117.8 14.8 %copy-start.8 = (bf16[64,6144]{1,0:T(8,128)(2,1)}, bf16[64,6144]{1,0:T(8,128)(2,1)S(1)}, u32[]{:S(2)}) copy-start(bf16[64,6144]{1,0:T(8,128)(2,1)S(1)} %collective-permute-done.19.refs_1_) | copy-start | bytes 2359300
  117.8 14.8 %collective-permute-start.21 = (bf16[64,6144]{1,0:T(8,128)(2,1)S(1)}, bf16[64,6144]{1,0:T(8,128)(2,1)}, u32[]{:S(2)}, u32[]{:S(2)}) collective-permute-start(bf16[64,6144]{1,0:T(8,128)(2,1)S(1)} %collective-permute-done.19.refs_1_), channel_id=1, source_target_pairs={{0,32},{1,97},{2,34},{3,99},{4,36},{5,101},{6,38},{7,103},{8,40},{... | collective-permute-start | bytes 2359304 | tf_op jit(solution)/shard_map/ppermute | solution.py:53
  120.5 51.5 %collective-permute-start.9 = (bf16[1536,768]{1,0:T(8,128)(2,1)}, bf16[1536,768]{1,0:T(8,128)(2,1)}, u32[]{:S(2)}, u32[]{:S(2)}) collective-permute-start(bf16[1536,768]{1,0:T(8,128)(2,1)} %refs_4_.3), channel_id=1, source_target_pairs={{0,1},{1,0},{2,3},{3,2},{4,5},{5,4},{6,7},{7,6},{8,9},{9,8},{10,11... | collective-permute-start | bytes 7077896 | tf_op jit(solution)/shard_map/ppermute | solution.py:62
  124.3 21.2 %collective-permute-start.4 = (bf16[64,6144]{1,0:T(8,128)(2,1)S(1)}, bf16[64,6144]{1,0:T(8,128)(2,1)}, u32[]{:S(2)}, u32[]{:S(2)}) collective-permute-start(bf16[64,6144]{1,0:T(8,128)(2,1)S(1)} %bitcast.46), channel_id=1, source_target_pairs={{0,24},{1,9},{2,26},{3,11},{4,28},{5,13},{6,30},{7,15},{8,0},{9,17... | collective-permute-start | bytes 2359304 | tf_op jit(solution)/shard_map/ppermute | solution.py:53
  124.8 20.7 %collective-permute-start.5 = (bf16[64,6144]{1,0:T(8,128)(2,1)}, bf16[64,6144]{1,0:T(8,128)(2,1)}, u32[]{:S(2)}, u32[]{:S(2)}) collective-permute-start(bf16[64,6144]{1,0:T(8,128)(2,1)} %collective-permute-done.3.refs_1_), channel_id=1, source_target_pairs={{0,8},{1,25},{2,10},{3,27},{4,12},{5,29},{6,14},{7,31},{8,16},{9,1... | collective-permute-start | bytes 2359304 | tf_op jit(solution)/shard_map/ppermute | solution.py:53
  127.6 0.9 copy-start.9
  144.5 13.0 %copy-start.7 = (bf16[256,1536]{1,0:T(8,128)(2,1)S(1)}, bf16[256,1536]{1,0:T(8,128)(2,1)}, u32[]{:S(2)}) copy-start(bf16[256,1536]{1,0:T(8,128)(2,1)} %shard_map.133.refs_0_) | copy-start | bytes 2359300
  144.5 14.3 %collective-permute-start.22 = (bf16[256,1536]{1,0:T(8,128)(2,1)}, bf16[256,1536]{1,0:T(8,128)(2,1)S(1)}, u32[]{:S(2)}, u32[]{:S(2)}) collective-permute-start(bf16[256,1536]{1,0:T(8,128)(2,1)} %shard_map.133.refs_0_), channel_id=1, source_target_pairs={{0,2},{1,7},{2,4},{3,1},{4,6},{5,3},{6,0},{7,5},{8,10},{9,15},{10,... | collective-permute-start | bytes 2359304 | tf_op jit(solution)/shard_map/ppermute | solution.py:53
  157.3 14.6 %collective-permute-start.6 = (bf16[256,1536]{1,0:T(8,128)(2,1)}, bf16[256,1536]{1,0:T(8,128)(2,1)S(1)}, u32[]{:S(2)}, u32[]{:S(2)}) collective-permute-start(bf16[256,1536]{1,0:T(8,128)(2,1)} %shard_map.128.refs_0_), channel_id=1, source_target_pairs={{0,2},{1,7},{2,4},{3,1},{4,6},{5,3},{6,0},{7,5},{8,10},{9,15},{10,... | collective-permute-start | bytes 2359304 | tf_op jit(solution)/shard_map/ppermute | solution.py:53
  157.5 17.7 %collective-permute-start.23 = (bf16[256,1536]{1,0:T(8,128)(2,1)S(1)}, bf16[256,1536]{1,0:T(8,128)(2,1)S(1)}, u32[]{:S(2)}, u32[]{:S(2)}) collective-permute-start(bf16[256,1536]{1,0:T(8,128)(2,1)S(1)} %copy-done.7), channel_id=1, source_target_pairs={{0,6},{1,3},{2,0},{3,5},{4,2},{5,7},{6,4},{7,1},{8,14},{9,11},{10,... | collective-permute-start | bytes 2359304 | tf_op jit(solution)/shard_map/ppermute | solution.py:53
  158.8 30.1 %copy-start.21 = (bf16[256,1536]{1,0:T(8,128)(2,1)}, bf16[256,1536]{1,0:T(8,128)(2,1)S(1)}, u32[]{:S(2)}) copy-start(bf16[256,1536]{1,0:T(8,128)(2,1)S(1)} %collective-permute-done.22.refs_1_) | copy-start | bytes 2359300
  158.8 30.1 %collective-permute-start.24 = (bf16[256,1536]{1,0:T(8,128)(2,1)S(1)}, bf16[256,1536]{1,0:T(8,128)(2,1)}, u32[]{:S(2)}, u32[]{:S(2)}) collective-permute-start(bf16[256,1536]{1,0:T(8,128)(2,1)S(1)} %collective-permute-done.22.refs_1_), channel_id=1, source_target_pairs={{0,2},{1,7},{2,4},{3,1},{4,6},{5,3},{6,0},{7,5},{8,10},{9,15},{10,... | collective-permute-start | bytes 2359304 | tf_op jit(solution)/shard_map/ppermute | solution.py:53
  160.2 41.0 %collective-permute-start.7 = (bf16[256,1536]{1,0:T(8,128)(2,1)}, bf16[256,1536]{1,0:T(8,128)(2,1)S(1)}, u32[]{:S(2)}, u32[]{:S(2)}) collective-permute-start(bf16[256,1536]{1,0:T(8,128)(2,1)} %shard_map.128.refs_0_), channel_id=1, source_target_pairs={{0,6},{1,3},{2,0},{3,5},{4,2},{5,7},{6,4},{7,1},{8,14},{9,11},{10,... | collective-permute-start | bytes 2359304 | tf_op jit(solution)/shard_map/ppermute | solution.py:53
  171.9 27.0 %copy-start.20 = (bf16[256,1536]{1,0:T(8,128)(2,1)}, bf16[256,1536]{1,0:T(8,128)(2,1)S(1)}, u32[]{:S(2)}) copy-start(bf16[256,1536]{1,0:T(8,128)(2,1)S(1)} %collective-permute-done.6.refs_1_) | copy-start | bytes 2359300
  171.9 30.5 %collective-permute-start.8 = (bf16[256,1536]{1,0:T(8,128)(2,1)S(1)}, bf16[256,1536]{1,0:T(8,128)(2,1)S(1)}, u32[]{:S(2)}, u32[]{:S(2)}) collective-permute-start(bf16[256,1536]{1,0:T(8,128)(2,1)S(1)} %collective-permute-done.6.refs_1_), channel_id=1, source_target_pairs={{0,2},{1,7},{2,4},{3,1},{4,6},{5,3},{6,0},{7,5},{8,10},{9,15},{10,... | collective-permute-start | bytes 2359304 | tf_op jit(solution)/shard_map/ppermute | solution.py:53
  175.3 13.6 %copy-start.24 = (bf16[256,1536]{1,0:T(8,128)(2,1)}, bf16[256,1536]{1,0:T(8,128)(2,1)S(1)}, u32[]{:S(2)}) copy-start(bf16[256,1536]{1,0:T(8,128)(2,1)S(1)} %collective-permute-done.23.refs_2_) | copy-start | bytes 2359300
  198.9 14.5 %copy-start.19 = (bf16[256,1536]{1,0:T(8,128)(2,1)S(1)}, bf16[256,1536]{1,0:T(8,128)(2,1)}, u32[]{:S(2)}) copy-start(bf16[256,1536]{1,0:T(8,128)(2,1)} %get-tuple-element.39) | copy-start | bytes 2359300
  198.9 16.9 %copy-start.2 = (bf16[256,1536]{1,0:T(8,128)(2,1)S(1)}, bf16[256,1536]{1,0:T(8,128)(2,1)}, u32[]{:S(2)}) copy-start(bf16[256,1536]{1,0:T(8,128)(2,1)} %get-tuple-element.40.a) | copy-start | bytes 2359300
  198.9 16.9 %collective-permute-start.26 = (bf16[256,1536]{1,0:T(8,128)(2,1)}, bf16[256,1536]{1,0:T(8,128)(2,1)S(1)}, u32[]{:S(2)}, u32[]{:S(2)}) collective-permute-start(bf16[256,1536]{1,0:T(8,128)(2,1)} %get-tuple-element.41), channel_id=1, source_target_pairs={{0,96},{1,33},{2,98},{3,35},{4,100},{5,37},{6,102},{7,39},{8,104},... | collective-permute-start | bytes 2359304 | tf_op jit(solution)/shard_map/ppermute | solution.py:53
  201.2 1.2 copy-start.22
  202.4 0.9 copy-start.23
  213.2 2.9 %copy-start.18 = (bf16[256,1536]{1,0:T(8,128)(2,1)S(1)}, bf16[256,1536]{1,0:T(8,128)(2,1)}, u32[]{:S(2)}) copy-start(bf16[256,1536]{1,0:T(8,128)(2,1)} %get-tuple-element.29) | copy-start | bytes 2359300
  213.2 12.5 %copy-start.3 = (bf16[256,1536]{1,0:T(8,128)(2,1)S(1)}, bf16[256,1536]{1,0:T(8,128)(2,1)}, u32[]{:S(2)}) copy-start(bf16[256,1536]{1,0:T(8,128)(2,1)} %get-tuple-element.30.a) | copy-start | bytes 2359300
  213.2 12.5 %collective-permute-start.11 = (bf16[256,1536]{1,0:T(8,128)(2,1)}, bf16[256,1536]{1,0:T(8,128)(2,1)S(1)}, u32[]{:S(2)}, u32[]{:S(2)}) collective-permute-start(bf16[256,1536]{1,0:T(8,128)(2,1)} %get-tuple-element.31), channel_id=1, source_target_pairs={{0,24},{1,9},{2,26},{3,11},{4,28},{5,13},{6,30},{7,15},{8,0},{9,17... | collective-permute-start | bytes 2359304 | tf_op jit(solution)/shard_map/ppermute | solution.py:53
  213.3 15.0 %collective-permute-start.25 = (bf16[256,1536]{1,0:T(8,128)(2,1)S(1)}, bf16[256,1536]{1,0:T(8,128)(2,1)S(1)}, u32[]{:S(2)}, u32[]{:S(2)}) collective-permute-start(bf16[256,1536]{1,0:T(8,128)(2,1)S(1)} %copy-done.19), channel_id=1, source_target_pairs={{0,32},{1,97},{2,34},{3,99},{4,36},{5,101},{6,38},{7,103},{8,40},{... | collective-permute-start | bytes 2359304 | tf_op jit(solution)/shard_map/ppermute | solution.py:53
  216.0 13.7 %copy-start.1 = (bf16[256,1536]{1,0:T(8,128)(2,1)S(1)}, bf16[256,1536]{1,0:T(8,128)(2,1)}, u32[]{:S(2)}) copy-start(bf16[256,1536]{1,0:T(8,128)(2,1)} %get-tuple-element.38.a) | copy-start | bytes 2359300
  216.0 13.7 %collective-permute-start.27 = (bf16[256,1536]{1,0:T(8,128)(2,1)S(1)}, bf16[256,1536]{1,0:T(8,128)(2,1)S(1)}, u32[]{:S(2)}, u32[]{:S(2)}) collective-permute-start(bf16[256,1536]{1,0:T(8,128)(2,1)S(1)} %shard_map.135), channel_id=1, source_target_pairs={{0,96},{1,33},{2,98},{3,35},{4,100},{5,37},{6,102},{7,39},{8,104},... | collective-permute-start | bytes 2359304 | tf_op jit(solution)/shard_map/ppermute | solution.py:53
  216.1 23.1 %collective-permute-start.10 = (bf16[256,1536]{1,0:T(8,128)(2,1)S(1)}, bf16[256,1536]{1,0:T(8,128)(2,1)S(1)}, u32[]{:S(2)}, u32[]{:S(2)}) collective-permute-start(bf16[256,1536]{1,0:T(8,128)(2,1)S(1)} %copy-done.18), channel_id=1, source_target_pairs={{0,8},{1,25},{2,10},{3,27},{4,12},{5,29},{6,14},{7,31},{8,16},{9,1... | collective-permute-start | bytes 2359304 | tf_op jit(solution)/shard_map/ppermute | solution.py:53
  226.0 20.2 %copy-start = (bf16[256,1536]{1,0:T(8,128)(2,1)S(1)}, bf16[256,1536]{1,0:T(8,128)(2,1)}, u32[]{:S(2)}) copy-start(bf16[256,1536]{1,0:T(8,128)(2,1)} %get-tuple-element.28.a) | copy-start | bytes 2359300
  226.0 20.2 %collective-permute-start.12 = (bf16[256,1536]{1,0:T(8,128)(2,1)S(1)}, bf16[256,1536]{1,0:T(8,128)(2,1)S(1)}, u32[]{:S(2)}, u32[]{:S(2)}) collective-permute-start(bf16[256,1536]{1,0:T(8,128)(2,1)S(1)} %shard_map.130), channel_id=1, source_target_pairs={{0,24},{1,9},{2,26},{3,11},{4,28},{5,13},{6,30},{7,15},{8,0},{9,17... | collective-permute-start | bytes 2359304 | tf_op jit(solution)/shard_map/ppermute | solution.py:53
  230.1 18.6 %copy-start.16 = (f32[768]{0:T(1024)S(1)}, f32[768]{0:T(1024)}, u32[]{:S(2)}) copy-start(f32[768]{0:T(1024)} %param.20) | copy-start | bytes 9220
  230.1 18.0 %collective-permute-start.28 = (bf16[64,1536]{1,0:T(8,128)(2,1)S(1)}, bf16[64,1536]{1,0:T(8,128)(2,1)S(1)}, u32[]{:S(2)}, u32[]{:S(2)}) collective-permute-start(bf16[64,1536]{1,0:T(8,128)(2,1)S(1)} %get-tuple-element.43), channel_id=1, source_target_pairs={{0,24},{1,25},{2,26},{3,27},{4,28},{5,29},{6,30},{7,31},{8,0},{9,1... | collective-permute-start | bytes 589832 | tf_op jit(solution)/shard_map/ppermute | solution.py:53
  235.2 15.2 %collective-permute-start.29 = (bf16[64,1536]{1,0:T(8,128)(2,1)S(1)}, bf16[64,1536]{1,0:T(8,128)(2,1)S(1)}, u32[]{:S(2)}, u32[]{:S(2)}) collective-permute-start(bf16[64,1536]{1,0:T(8,128)(2,1)S(1)} %get-tuple-element.44), channel_id=1, source_target_pairs={{0,8},{1,9},{2,10},{3,11},{4,12},{5,13},{6,14},{7,15},{8,16},{9,17... | collective-permute-start | bytes 589832 | tf_op jit(solution)/shard_map/ppermute | solution.py:53
  235.2 20.0 %collective-permute-start.30 = (bf16[64,1536]{1,0:T(8,128)(2,1)S(1)}, bf16[64,1536]{1,0:T(8,128)(2,1)S(1)}, u32[]{:S(2)}, u32[]{:S(2)}) collective-permute-start(bf16[64,1536]{1,0:T(8,128)(2,1)S(1)} %get-tuple-element.45), channel_id=1, source_target_pairs={{0,16},{1,17},{2,18},{3,19},{4,20},{5,21},{6,22},{7,23},{8,24},{9,... | collective-permute-start | bytes 589832 | tf_op jit(solution)/shard_map/ppermute | solution.py:53
  246.5 14.8 %collective-permute-start.13 = (bf16[64,1536]{1,0:T(8,128)(2,1)S(1)}, bf16[64,1536]{1,0:T(8,128)(2,1)S(1)}, u32[]{:S(2)}, u32[]{:S(2)}) collective-permute-start(bf16[64,1536]{1,0:T(8,128)(2,1)S(1)} %get-tuple-element.33), channel_id=1, source_target_pairs={{0,96},{1,97},{2,98},{3,99},{4,100},{5,101},{6,102},{7,103},{8,104... | collective-permute-start | bytes 589832 | tf_op jit(solution)/shard_map/ppermute | solution.py:53
  247.4 13.9 %collective-permute-start.14 = (bf16[64,1536]{1,0:T(8,128)(2,1)S(1)}, bf16[64,1536]{1,0:T(8,128)(2,1)S(1)}, u32[]{:S(2)}, u32[]{:S(2)}) collective-permute-start(bf16[64,1536]{1,0:T(8,128)(2,1)S(1)} %get-tuple-element.34), channel_id=1, source_target_pairs={{0,32},{1,33},{2,34},{3,35},{4,36},{5,37},{6,38},{7,39},{8,40},{9,... | collective-permute-start | bytes 589832 | tf_op jit(solution)/shard_map/ppermute | solution.py:53
  248.1 13.3 %collective-permute-start.15 = (bf16[64,1536]{1,0:T(8,128)(2,1)S(1)}, bf16[64,1536]{1,0:T(8,128)(2,1)S(1)}, u32[]{:S(2)}, u32[]{:S(2)}) collective-permute-start(bf16[64,1536]{1,0:T(8,128)(2,1)S(1)} %get-tuple-element.35), channel_id=1, source_target_pairs={{0,64},{1,65},{2,66},{3,67},{4,68},{5,69},{6,70},{7,71},{8,72},{9,... | collective-permute-start | bytes 589832 | tf_op jit(solution)/shard_map/ppermute | solution.py:53
  255.2 10.8 %collective-permute-start.32 = (bf16[64,768]{1,0:T(8,128)(2,1)S(1)}, bf16[64,768]{1,0:T(8,128)(2,1)S(1)}, u32[]{:S(2)}, u32[]{:S(2)}) collective-permute-start(bf16[64,768]{1,0:T(8,128)(2,1)S(1)} %get-tuple-element.48), channel_id=1, source_target_pairs={{0,1},{1,0},{2,3},{3,2},{4,5},{5,4},{6,7},{7,6},{8,9},{9,8},{10,11... | collective-permute-start | bytes 294920 | tf_op jit(solution)/shard_map/ppermute | solution.py:62
  261.4 4.8 %collective-permute-start.31 = (bf16[64,768]{1,0:T(8,128)(2,1)S(1)}, bf16[64,768]{1,0:T(8,128)(2,1)S(1)}, u32[]{:S(2)}, u32[]{:S(2)}) collective-permute-start(bf16[64,768]{1,0:T(8,128)(2,1)S(1)} %get-tuple-element.47), channel_id=1, source_target_pairs={{0,1},{1,0},{2,3},{3,2},{4,5},{5,4},{6,7},{7,6},{8,9},{9,8},{10,11... | collective-permute-start | bytes 294920 | tf_op jit(solution)/shard_map/ppermute | solution.py:62
Sparse Core Ops, SparseCore 0:
  9.0 103.6 all-gather.1

commit v6 on v5

--- a/solution.py
+++ b/solution.py
@@ -66,7 +66,7 @@
     return pltpu.CompilerParams(vmem_limit_bytes=mb * MB)
 
 
-def act_kernel(moved_ref, first_ref, second_ref):
+def act_kernel(cut, moved_ref, first_ref, second_ref):
     cols, _, chans = moved_ref.shape
     half = first_ref.shape[0]
     values = moved_ref[:, : 2 * half, :].astype(F32)
@@ -76,77 +76,112 @@
     scale = 1.0 / jnp.sqrt(square - mean * mean + 1e-05)
     for j in range(cols):
         part = ((values[j] - mean) * scale * gains[j][None, :]).astype(BF)
-        first_ref[:, j * chans : (j + 1) * chans] = part[:half]
-        second_ref[:, j * chans : (j + 1) * chans] = part[half:]
-
-
-def normalize(moved, half):
+        for low, high in ((0, cut), (cut, chans)):
+            at = cols * low + j * (high - low)
+            first_ref[:, at : at + high - low] = part[:half, low:high]
+            second_ref[:, at : at + high - low] = part[half:, low:high]
+
+
+def normalize(moved, half, cut):
     cols, _, chans = moved.shape
     shape = jax.ShapeDtypeStruct((half, cols * chans), BF)
-    return pl.pallas_call(act_kernel, out_shape=(shape, shape), compiler_params=params(16))(moved)
+    return pl.pallas_call(
+        functools.partial(act_kernel, cut), out_shape=(shape, shape), compiler_params=params(16)
+    )(moved)
+
+
+def fill(sources, target, sems):
+    rows = target.shape[0] // len(sources)
+    copies = [
+        pltpu.make_async_copy(source, target.at[pl.ds(i * rows, rows)], sems.at[i])
+        for i, source in enumerate(sources)
+    ]
+
+    @pl.when(pl.program_id(0) == 0)
+    def _():
+        for copy in copies:
+            copy.start()
+        for copy in copies:
+            copy.wait()
 
 
 def mm1_kernel(*refs):
-    pieces, (w_ref, b_ref, o_ref) = refs[:-3], refs[-3:]
-    left = jnp.concatenate([p[...] for p in pieces], axis=0)
-    pre = jnp.dot(left, w_ref[...], preferred_element_type=F32) + b_ref[...]
-    o_ref[...] = (0.5 * pre * (1.0 + lax.erf(pre * math.sqrt(0.5)))).astype(BF)
-
-
-def matmul_in(pieces, w, b):
-    depth, width = w.shape
-    rows = pieces[0].shape[0]
-    tokens = len(pieces) * rows
+    pieces, (wa_ref, wb_ref, b_ref, o1_ref, o2_ref, left, sems) = refs[:-7], refs[-7:]
+    fill(pieces, left, sems)
+    cut = wa_ref.shape[0]
+    pre = jnp.dot(left[:, :cut], wa_ref[...], preferred_element_type=F32)
+    pre = pre + jnp.dot(left[:, cut:], wb_ref[...], preferred_element_type=F32) + b_ref[...]
+    hidden = (0.5 * pre * (1.0 + lax.erf(pre * math.sqrt(0.5)))).astype(BF)
+    half = o1_ref.shape[0]
+    o1_ref[...] = hidden[:half]
+    o2_ref[...] = hidden[half:]
+
+
+def matmul_in(pieces, wa, wb, b):
+    rows, depth = pieces[0].shape
+    width = wa.shape[1]
+    count = len(pieces)
+    tokens = count * rows
     tile = 256
     return pl.pallas_call(
         mm1_kernel,
         grid=(width // tile,),
-        in_specs=[pl.BlockSpec((rows, depth), lambda i: (0, 0)) for _ in pieces]
+        in_specs=[pl.BlockSpec(memory_space=pl.ANY) for _ in pieces]
         + [
-            pl.BlockSpec((depth, tile), lambda i: (0, i)),
+            pl.BlockSpec((wa.shape[0], tile), lambda i: (0, i)),
+            pl.BlockSpec((wb.shape[0], tile), lambda i: (0, i)),
             pl.BlockSpec((1, tile), lambda i: (0, i)),
         ],
-        out_specs=pl.BlockSpec((tokens, tile), lambda i: (0, i)),
-        out_shape=jax.ShapeDtypeStruct((tokens, width), BF),
-        compiler_params=params(58),
+        out_specs=[pl.BlockSpec((tokens // 2, tile), lambda i: (0, i))] * 2,
+        out_shape=[jax.ShapeDtypeStruct((tokens // 2, width), BF)] * 2,
+        scratch_shapes=[pltpu.VMEM((tokens, depth), BF), pltpu.SemaphoreType.DMA((count,))],
+        compiler_params=params(60),
         cost_estimate=pl.CostEstimate(
             flops=2 * tokens * depth * width,
             bytes_accessed=2 * (tokens * depth + depth * width),
             transcendentals=0,
         ),
-    )(*pieces, w, b[None])
+    )(*pieces, wa, wb, b[None])
 
 
 def mm2_kernel(*refs):
-    hiddens, (own_ref, other_ref), outs = refs[:SIDE], refs[SIDE : SIDE + 2], refs[SIDE + 2 :]
-    rows, width = outs[0].shape
-    chans = own_ref.shape[1]
-    for i, h_ref in enumerate(hiddens):
-
-        @pl.when(pl.program_id(0) == i)
-        def _(h_ref=h_ref):
-            for at, w_ref in ((0, own_ref), (chans, other_ref)):
-                out = jnp.dot(h_ref[...], w_ref[...], preferred_element_type=F32)
-                for p, o_ref in enumerate(outs):
-                    o_ref[:, at : at + chans] = out[p * rows : (p + 1) * rows].astype(BF)
+    hiddens, (own_ref, other_ref) = refs[:SIDE], refs[SIDE : SIDE + 2]
+    outs, (left, sems) = refs[SIDE + 2 : -2], refs[-2:]
+    fill(hiddens, left, sems)
+    steps = pl.num_programs(0) // 2
+    rows = outs[0].shape[0] // SIDE
+
+    def part(w_ref):
+        out = jnp.dot(left[...], w_ref[...], preferred_element_type=F32).astype(BF)
+        for x in range(SIDE):
+            for p, o_ref in enumerate(outs):
+                at = (x * len(outs) + p) * rows
+                o_ref[x * rows : (x + 1) * rows, :] = out[at : at + rows]
+
+    pl.when(pl.program_id(0) < steps)(lambda: part(own_ref))
+    pl.when(pl.program_id(0) >= steps)(lambda: part(other_ref))
 
 
 def matmul_out(hiddens, own, other, count):
     depth, chans = own.shape
-    tokens = hiddens[0].shape[0]
-    rows = tokens // count
-    steps = len(hiddens)
-    whole = pl.BlockSpec((depth, chans), lambda i: (0, 0))
+    tokens = SIDE * hiddens[0].shape[0]
+    tile = 256
+    steps = chans // tile
     return pl.pallas_call(
         mm2_kernel,
-        grid=(steps,),
-        in_specs=[pl.BlockSpec((tokens, depth), lambda i: (0, 0))] * steps + [whole] * 2,
-        out_specs=[pl.BlockSpec((rows, 2 * chans), lambda i: (i, 0))] * count,
-        out_shape=[jax.ShapeDtypeStruct((steps * rows, 2 * chans), BF)] * count,
-        compiler_params=params(58),
+        grid=(2 * steps,),
+        in_specs=[pl.BlockSpec(memory_space=pl.ANY)] * SIDE
+        + [
+            pl.BlockSpec((depth, tile), lambda i: (0, jnp.minimum(i, steps - 1))),
+            pl.BlockSpec((depth, tile), lambda i: (0, jnp.maximum(i - steps, 0))),
+        ],
+        out_specs=[pl.BlockSpec((tokens // count, tile), lambda i: (0, i))] * count,
+        out_shape=[jax.ShapeDtypeStruct((tokens // count, 2 * chans), BF)] * count,
+        scratch_shapes=[pltpu.VMEM((tokens, depth), BF), pltpu.SemaphoreType.DMA((SIDE,))],
+        compiler_params=params(32),
         cost_estimate=pl.CostEstimate(
-            flops=4 * steps * tokens * depth * chans,
-            bytes_accessed=2 * (steps * tokens * depth + 2 * depth * chans + 2 * steps * tokens * chans),
+            flops=4 * tokens * depth * chans,
+            bytes_accessed=2 * (tokens * depth + 2 * depth * chans + 2 * tokens * chans),
             transcendentals=0,
         ),
     )(*hiddens, own, other)
@@ -321,7 +356,8 @@
 def on_device(image, filter_bank, gain_first, gain_second, w_in, b_in, w_out, b_out):
     rows_here, width, chans = image.shape
     cols = lax.axis_size("col")
-    w_in_all = lax.all_gather(w_in, "col", axis=0, tiled=True)
+    cut = w_in.shape[0] * 2 // 3
+    w_in_low = lax.all_gather(w_in[:cut], "col", axis=0, tiled=True)
     resid = spectral(image, filter_bank, gain_first)
     tokens = rows_here * width
     own = tokens // cols
@@ -335,10 +371,12 @@
         axis=1,
     )
     moved = exchange(message, "col")
-    first, second = normalize(moved, half)
+    moved, w_rest, w_in_low = tie([moved, w_in[cut:], w_in_low], [])
+    w_in_high = lax.all_gather(w_rest, "col", axis=0, tiled=True)
+    first, second = normalize(moved, half, cut)
     first, second = gather_near(first, "z"), gather_near(second, "y")
-    parts = [gather_far(first, "y"), gather_far(second, "z")]
-    hiddens = [gather_far(matmul_in(part, w_in_all, b_in), "x") for part in parts]
+    pieces = gather_far(first, "y") + gather_far(second, "z")
+    hiddens = [gather_far(hidden, "x") for hidden in matmul_in(pieces, w_in_low, w_in_high, b_in)]
     other = swap_cores(w_out)
     sums = []
     for hidden, (large, small) in zip(hiddens, (("y", "z"), ("z", "y"))):

time: 277 us -> 279 us (level)
  starting transfers between devices: 62.2 us -> 94.8 us
  blocking collectives: 42.6 us -> 13.2 us
  Pallas kernels: 46.6 us -> 36.2 us
  local copies, waits for them, and re-layouts: 5.84 us -> 13.3 us
    all_to_all x1 -> x0, blocking collectives: 29.4 us -> none  [exchange(): return lax.all_to_all(a, axis, split_axis=0, concat_axis=0, tiled=True)]
    all_to_all x2 -> x3, starting transfers between devices: 11.6 us -> 24.3 us  [exchange(): return lax.all_to_all(a, axis, split_axis=0, concat_axis=0, tiled=True)]
    ppermute x30, starting transfers between devices: 36.8 us -> 49.1 us  [hop(): return lax.ppermute(a, ('row', 'col'), pairs)]
    all_to_all x2 -> x3, waiting for transfers between devices: 20 us -> 28.2 us  [exchange(): return lax.all_to_all(a, axis, split_axis=0, concat_axis=0, tiled=True)]
    ppermute x3, starting transfers between devices: 13.8 us -> 21.5 us  [swap_cores(): return lax.ppermute(a, 'col', pairs)]
    pallas_call x2 -> x1, Pallas kernels: 23.7 us -> 17 us  [matmul_in(): pl.pallas_call(mm1_kernel, grid=(width // tile,), in_specs=[pl.BlockSpec(...]
    ppermute x30, waiting for transfers between devices: 74.6 us -> 69.1 us  [hop(): return lax.ppermute(a, ('row', 'col'), pairs)]
    slice x0 -> x2, local copies, waits for them, and re-layouts: none -> 4.74 us  [the longest x1 2.65 us: on_device(): w_in_low = lax.all_gather(w_in[:cut], 'col', axis=0, tiled=True)]
  transfers between devices with their start and end apart: 36 -> 38, of which waited for: 19 -> 18; matrix products, arithmetic and copies ran while one was open for 4% -> 5% of each run, Pallas kernels for 16% -> 13%
where the time goes in v6:
time: 279 us; the launch traced here: 278 us
  waiting for transfers between devices  97.6 us (35%)
  starting transfers between devices  94.8 us (34%)
  Pallas kernels  36.2 us (13%)
  between operations  13.7 us (5%)
  local copies, waits for them, and re-layouts  13.3 us (5%)
  blocking collectives  13.2 us (5%)
  matrix products  7.39 us (3%)
    ppermute x30, waiting for transfers between devices, hop(): return lax.ppermute(a, ('row', 'col'), pairs)  69.1 us
    ppermute x30, starting transfers between devices, hop(): return lax.ppermute(a, ('row', 'col'), pairs)  49.1 us
    all_to_all x3, waiting for transfers between devices, exchange(): return lax.all_to_all(a, axis, split_axis=0, concat_axis=0, tiled=True)  28.2 us
    all_to_all x3, starting transfers between devices, exchange(): return lax.all_to_all(a, axis, split_axis=0, concat_axis=0, tiled=True)  24.3 us
    ppermute x3, starting transfers between devices, swap_cores(): return lax.ppermute(a, 'col', pairs)  21.5 us
    pallas_call x1, Pallas kernels, matmul_in(): pl.pallas_call(mm1_kernel, grid=(width // tile,), in_specs=[pl.BlockSpec(...  17 us
    pallas_call x2, Pallas kernels, matmul_out(): pl.pallas_call(mm2_kernel, grid=(2 * steps,), in_specs=[pl.BlockSpec(memo...  16.3 us
    psum x1, blocking collectives, spectral(): lax.psum((jnp.sum(source, axis=-1), jnp.sum(source * source, axis=-1)), '...  13.2 us
  transfers between devices with their start and end apart: 38, of which 18 were waited for; matrix products, arithmetic and copies ran while one was open for 5% of the time, Pallas kernels for 13%

profile of v6, /device:TPU:1, one launch (start us, length us, event | category | flops | bytes accessed | tf_op | source)
XLA Modules:
  0.0 277.7 jit_solution(82287394242801448)
XLA Ops:
  6.5 2.7 slice.23
  9.2 1.0 copy-done.4
  10.5 13.2 %all-reduce.1 = (f32[256]{0:T(256)S(1)}, f32[256]{0:T(256)S(1)}) all-reduce(f32[256]{0:T(256)S(1)} %reduce_sum.25, f32[256]{0:T(256)S(1)} %reduce_sum.23), channel_id=1, replica_groups=mesh['row'=16,'col'=8] {'col'}, use_global_device_ids=true, to_apply=%region_3.0 | all-reduce | flops 512 | bytes 4096 | tf_op jit(solution)/shard_map/psum | solution.py:294
  23.9 1.7 convolution_convert_fusion
  25.6 7.8 %all-to-all-start = ((bf16[16,32,768]{2,1,0:T(8,128)(2,1)}), bf16[16,32,768]{2,1,0:T(8,128)(2,1)S(1)}, u32[]{:S(2)}, u32[]{:S(2)}) async-start(bf16[16,32,768]{2,1,0:T(8,128)(2,1)} %bitcast.3), calls=%async_computation | async-start | bytes 1572864 | tf_op jit(solution)/shard_map/all_to_all | solution.py:266
  33.5 1.5 fusion.19
  35.6 9.6 %all-to-all-done = bf16[16,32,768]{2,1,0:T(8,128)(2,1)S(1)} async-done(((bf16[16,32,768]{2,1,0:T(8,128)(2,1)}), bf16[16,32,768]{2,1,0:T(8,128)(2,1)S(1)}, u32[]{:S(2)}, u32[]{:S(2)}) %all-to-all-start) | async-done | bytes 786464 | tf_op jit(solution)/shard_map/all_to_all | solution.py:266
  45.2 2.3 fusion.21
  47.5 0.9 fusion.5
  48.6 1.9 add_convert_fusion
  50.4 3.7 %all-to-all-start.1 = ((bf16[16,32,768]{2,1,0:T(8,128)(2,1)}), bf16[16,32,768]{2,1,0:T(8,128)(2,1)S(1)}, u32[]{:S(2)}, u32[]{:S(2)}) async-start(bf16[16,32,768]{2,1,0:T(8,128)(2,1)} %bitcast.6), calls=%async_computation.1 | async-start | bytes 1572864 | tf_op jit(solution)/shard_map/all_to_all | solution.py:266
  54.3 10.5 %all-to-all-done.1 = bf16[16,32,768]{2,1,0:T(8,128)(2,1)S(1)} async-done(((bf16[16,32,768]{2,1,0:T(8,128)(2,1)}), bf16[16,32,768]{2,1,0:T(8,128)(2,1)S(1)}, u32[]{:S(2)}, u32[]{:S(2)}) %all-to-all-start.1) | async-done | bytes 786464 | tf_op jit(solution)/shard_map/all_to_all | solution.py:266
  64.8 0.6 fusion.20
  65.4 0.9 pad_maximum_fusion.2
  66.2 12.7 %all-to-all-start.2 = ((bf16[8,48,768]{2,1,0:T(8,128)(2,1)}), bf16[8,48,768]{2,1,0:T(8,128)(2,1)S(1)}, u32[]{:S(2)}, u32[]{:S(2)}) async-start(bf16[8,48,768]{2,1,0:T(8,128)(2,1)} %pad_maximum_fusion.2), calls=%async_computation.2 | async-start | bytes 1179648 | tf_op jit(solution)/shard_map/all_to_all | solution.py:266
  79.0 2.1 slice.22.refs_1_
  81.0 8.1 %all-to-all-done.2.refs_0_ = bf16[8,48,768]{2,1,0:T(8,128)(2,1)S(1)} async-done(((bf16[8,48,768]{2,1,0:T(8,128)(2,1)}), bf16[8,48,768]{2,1,0:T(8,128)(2,1)S(1)}, u32[]{:S(2)}, u32[]{:S(2)}) %all-to-all-start.2) | async-done | bytes 589856 | tf_op jit(solution)/shard_map/all_to_all | solution.py:266
  89.1 0.8 copy-done
  90.0 1.1 copy-done.1
  91.4 0.4 collective-permute-start.6
  91.8 2.3 collective-permute-start.7
  94.2 2.7 collective-permute-start.1
  96.8 1.4 collective-permute-done.6
  98.2 0.5 collective-permute-start.2
  98.8 1.9 collective-permute-done.8
  100.8 1.5 collective-permute-start.9
  102.4 1.9 collective-permute-done.2
  104.4 0.8 collective-permute-start.3
  105.2 1.5 collective-permute-start.10
  106.7 7.5 %collective-permute-done.9.refs_5_ = bf16[64,6144]{1,0:T(8,128)(2,1)S(1)} collective-permute-done((bf16[64,6144]{1,0:T(8,128)(2,1)S(1)}, bf16[64,6144]{1,0:T(8,128)(2,1)S(1)}, u32[]{:S(2)}, u32[]{:S(2)}) %collective-permute-start.9) | collective-permute-done | bytes 786464 | tf_op jit(solution)/shard_map/ppermute | solution.py:53
  114.3 3.5 %collective-permute-start.11 = (bf16[64,6144]{1,0:T(8,128)(2,1)S(1)}, bf16[64,6144]{1,0:T(8,128)(2,1)S(1)}, u32[]{:S(2)}, u32[]{:S(2)}) collective-permute-start(bf16[64,6144]{1,0:T(8,128)(2,1)S(1)} %collective-permute-done.9.refs_5_), channel_id=1, source_target_pairs={{0,32},{1,97},{2,34},{3,99},{4,36},{5,101},{6,38},{7,103},{8,40},{... | collective-permute-start | bytes 2359304 | tf_op jit(solution)/shard_map/ppermute | solution.py:53
  117.8 1.5 collective-permute-start.5
  119.3 9.3 %collective-permute-start.15 = (bf16[1536,768]{1,0:T(8,128)(2,1)}, bf16[1536,768]{1,0:T(8,128)(2,1)}, u32[]{:S(2)}, u32[]{:S(2)}) collective-permute-start(bf16[1536,768]{1,0:T(8,128)(2,1)} %refs_4_.3), channel_id=1, source_target_pairs={{0,1},{1,0},{2,3},{3,2},{4,5},{5,4},{6,7},{7,6},{8,9},{9,8},{10,11... | collective-permute-start | bytes 7077896 | tf_op jit(solution)/shard_map/ppermute | solution.py:62
  128.6 0.6 broadcast_in_dim.7.refs_10_
  129.2 3.8 %collective-permute-done.11.refs_7_ = bf16[64,6144]{1,0:T(8,128)(2,1)S(1)} collective-permute-done((bf16[64,6144]{1,0:T(8,128)(2,1)S(1)}, bf16[64,6144]{1,0:T(8,128)(2,1)S(1)}, u32[]{:S(2)}, u32[]{:S(2)}) %collective-permute-start.11) | collective-permute-done | bytes 786464 | tf_op jit(solution)/shard_map/ppermute | solution.py:53
  133.0 0.9 copy-done.19
  133.9 1.5 collective-permute-done.5.refs_3_
  135.4 17.0 %shard_map.129 = (bf16[256,1536]{1,0:T(8,128)(2,1)}, bf16[256,1536]{1,0:T(8,128)(2,1)}) custom-call(bf16[64,6144]{1,0:T(8,128)(2,1)} %bitcast.50, bf16[64,6144]{1,0:T(8,128)(2,1)} %copy-done.16, bf16[64,6144]{1,0:T(8,128)(2,1)} %copy-done.18, bf16[64,6144]{1,0:T(8,128)(2,1)} %collective-permute-done.5.refs_3_, bf16[64,6144]{1,0:T(8,128)(2,1)} %bitcast.47, ...), custom_call_target="tpu_custom_call" | custom-call | flops 9663676416 | bytes 25165824 | tf_op jit(solution)/shard_map/pallas_call | solution.py:126
  152.4 1.0 collective-permute-start.22
  153.3 1.9 collective-permute-start.12
  155.2 8.3 %collective-permute-done.22.refs_1_ = bf16[256,1536]{1,0:T(8,128)(2,1)S(1)} collective-permute-done((bf16[256,1536]{1,0:T(8,128)(2,1)}, bf16[256,1536]{1,0:T(8,128)(2,1)S(1)}, u32[]{:S(2)}, u32[]{:S(2)}) %collective-permute-start.22) | collective-permute-done | bytes 786464 | tf_op jit(solution)/shard_map/ppermute | solution.py:53
  163.5 2.1 collective-permute-start.24
  165.6 13.7 %collective-permute-done.12.refs_1_ = bf16[256,1536]{1,0:T(8,128)(2,1)S(1)} collective-permute-done((bf16[256,1536]{1,0:T(8,128)(2,1)}, bf16[256,1536]{1,0:T(8,128)(2,1)S(1)}, u32[]{:S(2)}, u32[]{:S(2)}) %collective-permute-start.12) | collective-permute-done | bytes 786464 | tf_op jit(solution)/shard_map/ppermute | solution.py:53
  179.2 1.7 collective-permute-start.14
  181.0 12.3 %collective-permute-done.24.refs_3_ = bf16[256,1536]{1,0:T(8,128)(2,1)S(1)} collective-permute-done((bf16[256,1536]{1,0:T(8,128)(2,1)S(1)}, bf16[256,1536]{1,0:T(8,128)(2,1)S(1)}, u32[]{:S(2)}, u32[]{:S(2)}) %collective-permute-start.24) | collective-permute-done | bytes 786464 | tf_op jit(solution)/shard_map/ppermute | solution.py:53
  193.3 1.1 copy-done.3
  194.5 8.1 %shard_map.134 = (bf16[256,1536]{1,0:T(8,128)(2,1)S(1)}, bf16[256,1536]{1,0:T(8,128)(2,1)S(1)}, bf16[256,1536]{1,0:T(8,128)(2,1)S(1)}, bf16[256,1536]{1,0:T(8,128)(2,1)S(1)}) custom-call(bf16[256,1536]{1,0:T(8,128)(2,1)S(1)} %copy-done.3, bf16[256,1536]{1,0:T(8,128)(2,1)S(1)} %collective-permute-done.22.refs_1_, ...), custom_call_target="tpu_custom_call" | custom-call | flops 4831838208 | bytes 11010048 | tf_op jit(solution)/shard_map/pallas_call | solution.py:170
  202.6 1.0 collective-permute-start.26
  203.6 2.3 collective-permute-done.14.refs_3_
  205.9 8.1 %shard_map.130 = (bf16[256,1536]{1,0:T(8,128)(2,1)S(1)}, bf16[256,1536]{1,0:T(8,128)(2,1)S(1)}, bf16[256,1536]{1,0:T(8,128)(2,1)S(1)}, bf16[256,1536]{1,0:T(8,128)(2,1)S(1)}) custom-call(bf16[256,1536]{1,0:T(8,128)(2,1)S(1)} %copy-done.2, bf16[256,1536]{1,0:T(8,128)(2,1)S(1)} %collective-permute-done.12.refs_1_, ...), custom_call_target="tpu_custom_call" | custom-call | flops 4831838208 | bytes 11010048 | tf_op jit(solution)/shard_map/pallas_call | solution.py:170
  214.1 1.3 collective-permute-start.25
  216.0 6.7 %collective-permute-start.16 = (bf16[256,1536]{1,0:T(8,128)(2,1)S(1)}, bf16[256,1536]{1,0:T(8,128)(2,1)S(1)}, u32[]{:S(2)}, u32[]{:S(2)}) collective-permute-start(bf16[256,1536]{1,0:T(8,128)(2,1)S(1)} %get-tuple-element.39), channel_id=1, source_target_pairs={{0,8},{1,25},{2,10},{3,27},{4,12},{5,29},{6,14},{7,31},{8,16},{9,1... | collective-permute-start | bytes 2359304 | tf_op jit(solution)/shard_map/ppermute | solution.py:53
  222.7 5.5 %collective-permute-done.17.b = bf16[256,1536]{1,0:T(8,128)(2,1)S(1)} collective-permute-done((bf16[256,1536]{1,0:T(8,128)(2,1)S(1)}, bf16[256,1536]{1,0:T(8,128)(2,1)S(1)}, u32[]{:S(2)}, u32[]{:S(2)}) %collective-permute-start.17) | collective-permute-done | bytes 786464 | tf_op jit(solution)/shard_map/ppermute | solution.py:53
  228.5 2.7 collective-permute-done.25.b
  231.6 11.5 %collective-permute-start.28 = (bf16[64,1536]{1,0:T(8,128)(2,1)S(1)}, bf16[64,1536]{1,0:T(8,128)(2,1)S(1)}, u32[]{:S(2)}, u32[]{:S(2)}) collective-permute-start(bf16[64,1536]{1,0:T(8,128)(2,1)S(1)} %get-tuple-element.53), channel_id=1, source_target_pairs={{0,24},{1,25},{2,26},{3,27},{4,28},{5,29},{6,30},{7,31},{8,0},{9,1... | collective-permute-start | bytes 589832 | tf_op jit(solution)/shard_map/ppermute | solution.py:53
  243.1 1.3 collective-permute-start.30
  244.4 3.4 %collective-permute-done.18.c = bf16[256,1536]{1,0:T(8,128)(2,1)S(1)} collective-permute-done((bf16[256,1536]{1,0:T(8,128)(2,1)S(1)}, bf16[256,1536]{1,0:T(8,128)(2,1)S(1)}, u32[]{:S(2)}, u32[]{:S(2)}) %collective-permute-start.18) | collective-permute-done | bytes 786464 | tf_op jit(solution)/shard_map/ppermute | solution.py:53
  248.1 4.0 %collective-permute-start.19 = (bf16[64,1536]{1,0:T(8,128)(2,1)S(1)}, bf16[64,1536]{1,0:T(8,128)(2,1)S(1)}, u32[]{:S(2)}, u32[]{:S(2)}) collective-permute-start(bf16[64,1536]{1,0:T(8,128)(2,1)S(1)} %get-tuple-element.43), channel_id=1, source_target_pairs={{0,96},{1,97},{2,98},{3,99},{4,100},{5,101},{6,102},{7,103},{8,104... | collective-permute-start | bytes 589832 | tf_op jit(solution)/shard_map/ppermute | solution.py:53
  252.2 1.3 collective-permute-start.21
  253.4 2.7 collective-permute-done.30.d
  256.3 5.1 %collective-permute-start.32 = (bf16[64,768]{1,0:T(8,128)(2,1)S(1)}, bf16[64,768]{1,0:T(8,128)(2,1)S(1)}, u32[]{:S(2)}, u32[]{:S(2)}) collective-permute-start(bf16[64,768]{1,0:T(8,128)(2,1)S(1)} %get-tuple-element.58), channel_id=1, source_target_pairs={{0,1},{1,0},{2,3},{3,2},{4,5},{5,4},{6,7},{7,6},{8,9},{9,8},{10,11... | collective-permute-start | bytes 294920 | tf_op jit(solution)/shard_map/ppermute | solution.py:62
  261.5 7.0 %collective-permute-start.31 = (bf16[64,768]{1,0:T(8,128)(2,1)S(1)}, bf16[64,768]{1,0:T(8,128)(2,1)S(1)}, u32[]{:S(2)}, u32[]{:S(2)}) collective-permute-start(bf16[64,768]{1,0:T(8,128)(2,1)S(1)} %get-tuple-element.57), channel_id=1, source_target_pairs={{0,1},{1,0},{2,3},{3,2},{4,5},{5,4},{6,7},{7,6},{8,9},{9,8},{10,11... | collective-permute-start | bytes 294920 | tf_op jit(solution)/shard_map/ppermute | solution.py:62
  268.5 0.7 dynamic-slice_bitcast_fusion.place_ref
  269.5 1.4 shard_map.138
  (94 shorter events, 3.8 us)
Async XLA Ops:
  6.5 82.6 %all-gather.3.cloned.1.call-start = ((), (), s32[]{:S(2)}) async-start(), calls=%async_computation.3 | async-start | bytes 14155776 | tf_op jit(solution)/shard_map/all_gather | solution.py:360
  9.2 1.0 copy-start.4
  9.2 14.5 %copy-start.12 = (f32[768]{0:T(1024)S(1)}, f32[768]{0:T(1024)}, u32[]{:S(2)}) copy-start(f32[768]{0:T(1024)} %param.15) | copy-start | bytes 9220
  9.2 14.7 %copy-start.10 = (f32[512,256]{1,0:T(8,128)S(1)}, f32[512,256]{1,0:T(8,128)}, u32[]{:S(2)}) copy-start(f32[512,256]{1,0:T(8,128)} %constant.28.clone) | copy-start | bytes 1572868
  25.6 19.6 %all-to-all-start = ((bf16[16,32,768]{2,1,0:T(8,128)(2,1)}), bf16[16,32,768]{2,1,0:T(8,128)(2,1)S(1)}, u32[]{:S(2)}, u32[]{:S(2)}) async-start(bf16[16,32,768]{2,1,0:T(8,128)(2,1)} %bitcast.3), calls=%async_computation | async-start | bytes 1572864 | tf_op jit(solution)/shard_map/all_to_all | solution.py:266
  45.2 2.3 copy-start.8
  47.5 1.0 copy-start.7
  50.4 3.8 %copy-start.14 = (f32[768]{0:T(1024)S(1)}, f32[768]{0:T(1024)}, u32[]{:S(2)}) copy-start(f32[768]{0:T(1024)} %param.16) | copy-start | bytes 9220
  50.4 14.3 %copy-start.9 = (f32[256,512]{1,0:T(8,128)S(1)}, f32[256,512]{1,0:T(8,128)}, u32[]{:S(2)}) copy-start(f32[256,512]{1,0:T(8,128)} %constant.31.clone) | copy-start | bytes 1572868
  50.4 14.3 %all-to-all-start.1 = ((bf16[16,32,768]{2,1,0:T(8,128)(2,1)}), bf16[16,32,768]{2,1,0:T(8,128)(2,1)S(1)}, u32[]{:S(2)}, u32[]{:S(2)}) async-start(bf16[16,32,768]{2,1,0:T(8,128)(2,1)} %bitcast.6), calls=%async_computation.1 | async-start | bytes 1572864 | tf_op jit(solution)/shard_map/all_to_all | solution.py:266
  66.2 22.9 %all-to-all-start.2 = ((bf16[8,48,768]{2,1,0:T(8,128)(2,1)}), bf16[8,48,768]{2,1,0:T(8,128)(2,1)S(1)}, u32[]{:S(2)}, u32[]{:S(2)}) async-start(bf16[8,48,768]{2,1,0:T(8,128)(2,1)} %pad_maximum_fusion.2), calls=%async_computation.2 | async-start | bytes 1179648 | tf_op jit(solution)/shard_map/all_to_all | solution.py:266
  79.0 56.4 %all-gather.5.cloned.1.call-start = ((), (), s32[]{:S(2)}) async-start(), calls=%async_computation.4 | async-start | bytes 7077888 | tf_op jit(solution)/shard_map/all_gather | solution.py:375
  89.1 0.8 copy-start
  90.0 1.1 copy-start.1
  91.4 6.8 %collective-permute-start.6 = (bf16[16,6144]{1,0:T(8,128)(2,1)S(1)}, bf16[16,6144]{1,0:T(8,128)(2,1)S(1)}, u32[]{:S(2)}, u32[]{:S(2)}) collective-permute-start(bf16[16,6144]{1,0:T(8,128)(2,1)S(1)} %get-tuple-element.34), channel_id=1, source_target_pairs={{0,8},{1,9},{2,10},{3,11},{4,12},{5,13},{6,14},{7,15},{8,16},{9,17... | collective-permute-start | bytes 589832 | tf_op jit(solution)/shard_map/ppermute | solution.py:53
  91.8 6.9 %collective-permute-start.7 = (bf16[16,6144]{1,0:T(8,128)(2,1)S(1)}, bf16[16,6144]{1,0:T(8,128)(2,1)S(1)}, u32[]{:S(2)}, u32[]{:S(2)}) collective-permute-start(bf16[16,6144]{1,0:T(8,128)(2,1)S(1)} %get-tuple-element.34), channel_id=1, source_target_pairs={{0,24},{1,25},{2,26},{3,27},{4,28},{5,29},{6,30},{7,31},{8,0},{9,1... | collective-permute-start | bytes 589832 | tf_op jit(solution)/shard_map/ppermute | solution.py:53
  94.1 6.6 %collective-permute-start.8 = (bf16[16,6144]{1,0:T(8,128)(2,1)S(1)}, bf16[16,6144]{1,0:T(8,128)(2,1)S(1)}, u32[]{:S(2)}, u32[]{:S(2)}) collective-permute-start(bf16[16,6144]{1,0:T(8,128)(2,1)S(1)} %get-tuple-element.34), channel_id=1, source_target_pairs={{0,16},{1,17},{2,18},{3,19},{4,20},{5,21},{6,22},{7,23},{8,24},{9,... | collective-permute-start | bytes 589832 | tf_op jit(solution)/shard_map/ppermute | solution.py:53
  94.1 8.2 %collective-permute-start = (bf16[16,6144]{1,0:T(8,128)(2,1)S(1)}, bf16[16,6144]{1,0:T(8,128)(2,1)S(1)}, u32[]{:S(2)}, u32[]{:S(2)}) collective-permute-start(bf16[16,6144]{1,0:T(8,128)(2,1)S(1)} %get-tuple-element.33), channel_id=1, source_target_pairs={{0,32},{1,33},{2,34},{3,35},{4,36},{5,37},{6,38},{7,39},{8,40},{9,... | collective-permute-start | bytes 589832 | tf_op jit(solution)/shard_map/ppermute | solution.py:53
  94.2 8.2 %collective-permute-start.1 = (bf16[16,6144]{1,0:T(8,128)(2,1)S(1)}, bf16[16,6144]{1,0:T(8,128)(2,1)S(1)}, u32[]{:S(2)}, u32[]{:S(2)}) collective-permute-start(bf16[16,6144]{1,0:T(8,128)(2,1)S(1)} %get-tuple-element.33), channel_id=1, source_target_pairs={{0,96},{1,97},{2,98},{3,99},{4,100},{5,101},{6,102},{7,103},{8,104... | collective-permute-start | bytes 589832 | tf_op jit(solution)/shard_map/ppermute | solution.py:53
  98.2 6.1 %collective-permute-start.2 = (bf16[16,6144]{1,0:T(8,128)(2,1)S(1)}, bf16[16,6144]{1,0:T(8,128)(2,1)S(1)}, u32[]{:S(2)}, u32[]{:S(2)}) collective-permute-start(bf16[16,6144]{1,0:T(8,128)(2,1)S(1)} %get-tuple-element.33), channel_id=1, source_target_pairs={{0,64},{1,65},{2,66},{3,67},{4,68},{5,69},{6,70},{7,71},{8,72},{9,... | collective-permute-start | bytes 589832 | tf_op jit(solution)/shard_map/ppermute | solution.py:53
  100.7 27.9 %copy-start.11 = (f32[1536]{0:T(1024)S(1)}, f32[1536]{0:T(1024)}, u32[]{:S(2)}) copy-start(f32[1536]{0:T(1024)} %param.18) | copy-start | bytes 18436
  100.8 34.5 %copy-start.5 = (bf16[4,16,6144]{2,1,0:T(8,128)(2,1)}, bf16[4,16,6144]{2,1,0:T(8,128)(2,1)S(1)}, u32[]{:S(2)}) copy-start(bf16[4,16,6144]{2,1,0:T(8,128)(2,1)S(1)} %pad_maximum_fusion.1) | copy-start | bytes 2359300
  100.8 13.4 %collective-permute-start.9 = (bf16[64,6144]{1,0:T(8,128)(2,1)S(1)}, bf16[64,6144]{1,0:T(8,128)(2,1)S(1)}, u32[]{:S(2)}, u32[]{:S(2)}) collective-permute-start(bf16[64,6144]{1,0:T(8,128)(2,1)S(1)} %bitcast.45), channel_id=1, source_target_pairs={{0,32},{1,97},{2,34},{3,99},{4,36},{5,101},{6,38},{7,103},{8,40},{... | collective-permute-start | bytes 2359304 | tf_op jit(solution)/shard_map/ppermute | solution.py:53
  104.4 31.0 %copy-start.6 = (bf16[4,16,6144]{2,1,0:T(8,128)(2,1)}, bf16[4,16,6144]{2,1,0:T(8,128)(2,1)S(1)}, u32[]{:S(2)}) copy-start(bf16[4,16,6144]{2,1,0:T(8,128)(2,1)S(1)} %pad_maximum_fusion) | copy-start | bytes 2359300
  104.4 13.4 %collective-permute-start.3 = (bf16[64,6144]{1,0:T(8,128)(2,1)S(1)}, bf16[64,6144]{1,0:T(8,128)(2,1)S(1)}, u32[]{:S(2)}, u32[]{:S(2)}) collective-permute-start(bf16[64,6144]{1,0:T(8,128)(2,1)S(1)} %bitcast.48), channel_id=1, source_target_pairs={{0,8},{1,25},{2,10},{3,27},{4,12},{5,29},{6,14},{7,31},{8,16},{9,1... | collective-permute-start | bytes 2359304 | tf_op jit(solution)/shard_map/ppermute | solution.py:53
  105.2 24.0 %collective-permute-start.10 = (bf16[64,6144]{1,0:T(8,128)(2,1)S(1)}, bf16[64,6144]{1,0:T(8,128)(2,1)S(1)}, u32[]{:S(2)}, u32[]{:S(2)}) collective-permute-start(bf16[64,6144]{1,0:T(8,128)(2,1)S(1)} %bitcast.46), channel_id=1, source_target_pairs={{0,96},{1,33},{2,98},{3,35},{4,100},{5,37},{6,102},{7,39},{8,104},... | collective-permute-start | bytes 2359304 | tf_op jit(solution)/shard_map/ppermute | solution.py:53
  106.7 22.5 %collective-permute-start.4 = (bf16[64,6144]{1,0:T(8,128)(2,1)S(1)}, bf16[64,6144]{1,0:T(8,128)(2,1)S(1)}, u32[]{:S(2)}, u32[]{:S(2)}) collective-permute-start(bf16[64,6144]{1,0:T(8,128)(2,1)S(1)} %bitcast.49), channel_id=1, source_target_pairs={{0,24},{1,9},{2,26},{3,11},{4,28},{5,13},{6,30},{7,15},{8,0},{9,17... | collective-permute-start | bytes 2359304 | tf_op jit(solution)/shard_map/ppermute | solution.py:53
  114.3 21.1 %copy-start.15 = (bf16[64,6144]{1,0:T(8,128)(2,1)}, bf16[64,6144]{1,0:T(8,128)(2,1)S(1)}, u32[]{:S(2)}) copy-start(bf16[64,6144]{1,0:T(8,128)(2,1)S(1)} %collective-permute-done.9.refs_5_) | copy-start | bytes 2359300
  114.3 18.7 %collective-permute-start.11 = (bf16[64,6144]{1,0:T(8,128)(2,1)S(1)}, bf16[64,6144]{1,0:T(8,128)(2,1)S(1)}, u32[]{:S(2)}, u32[]{:S(2)}) collective-permute-start(bf16[64,6144]{1,0:T(8,128)(2,1)S(1)} %collective-permute-done.9.refs_5_), channel_id=1, source_target_pairs={{0,32},{1,97},{2,34},{3,99},{4,36},{5,101},{6,38},{7,103},{8,40},{... | collective-permute-start | bytes 2359304 | tf_op jit(solution)/shard_map/ppermute | solution.py:53
  117.8 15.2 %copy-start.16 = (bf16[64,6144]{1,0:T(8,128)(2,1)}, bf16[64,6144]{1,0:T(8,128)(2,1)S(1)}, u32[]{:S(2)}) copy-start(bf16[64,6144]{1,0:T(8,128)(2,1)S(1)} %collective-permute-done.3.refs_1_) | copy-start | bytes 2359300
  117.8 17.6 %collective-permute-start.5 = (bf16[64,6144]{1,0:T(8,128)(2,1)S(1)}, bf16[64,6144]{1,0:T(8,128)(2,1)}, u32[]{:S(2)}, u32[]{:S(2)}) collective-permute-start(bf16[64,6144]{1,0:T(8,128)(2,1)S(1)} %collective-permute-done.3.refs_1_), channel_id=1, source_target_pairs={{0,8},{1,25},{2,10},{3,27},{4,12},{5,29},{6,14},{7,31},{8,16},{9,1... | collective-permute-start | bytes 2359304 | tf_op jit(solution)/shard_map/ppermute | solution.py:53
  119.3 61.7 %collective-permute-start.15 = (bf16[1536,768]{1,0:T(8,128)(2,1)}, bf16[1536,768]{1,0:T(8,128)(2,1)}, u32[]{:S(2)}, u32[]{:S(2)}) collective-permute-start(bf16[1536,768]{1,0:T(8,128)(2,1)} %refs_4_.3), channel_id=1, source_target_pairs={{0,1},{1,0},{2,3},{3,2},{4,5},{5,4},{6,7},{7,6},{8,9},{9,8},{10,11... | collective-permute-start | bytes 7077896 | tf_op jit(solution)/shard_map/ppermute | solution.py:62
  129.2 3.8 %copy-start.17 = (bf16[64,6144]{1,0:T(8,128)(2,1)}, bf16[64,6144]{1,0:T(8,128)(2,1)S(1)}, u32[]{:S(2)}) copy-start(bf16[64,6144]{1,0:T(8,128)(2,1)S(1)} %collective-permute-done.10.refs_6_) | copy-start | bytes 2359300
  129.2 3.8 %copy-start.18 = (bf16[64,6144]{1,0:T(8,128)(2,1)}, bf16[64,6144]{1,0:T(8,128)(2,1)S(1)}, u32[]{:S(2)}) copy-start(bf16[64,6144]{1,0:T(8,128)(2,1)S(1)} %collective-permute-done.4.refs_2_) | copy-start | bytes 2359300
  133.0 0.9 copy-start.19
  152.4 11.1 %collective-permute-start.22 = (bf16[256,1536]{1,0:T(8,128)(2,1)}, bf16[256,1536]{1,0:T(8,128)(2,1)S(1)}, u32[]{:S(2)}, u32[]{:S(2)}) collective-permute-start(bf16[256,1536]{1,0:T(8,128)(2,1)} %get-tuple-element.47.refs_0_), channel_id=1, source_target_pairs={{0,2},{1,7},{2,4},{3,1},{4,6},{5,3},{6,0},{7,5},{8,10},{9,15},{10,... | collective-permute-start | bytes 2359304 | tf_op jit(solution)/shard_map/ppermute | solution.py:53
  153.3 52.6 %copy-start.2 = (bf16[256,1536]{1,0:T(8,128)(2,1)S(1)}, bf16[256,1536]{1,0:T(8,128)(2,1)}, u32[]{:S(2)}) copy-start(bf16[256,1536]{1,0:T(8,128)(2,1)} %get-tuple-element.37.refs_0_) | copy-start | bytes 2359300
  153.3 25.9 %collective-permute-start.12 = (bf16[256,1536]{1,0:T(8,128)(2,1)}, bf16[256,1536]{1,0:T(8,128)(2,1)S(1)}, u32[]{:S(2)}, u32[]{:S(2)}) collective-permute-start(bf16[256,1536]{1,0:T(8,128)(2,1)} %get-tuple-element.37.refs_0_), channel_id=1, source_target_pairs={{0,2},{1,7},{2,4},{3,1},{4,6},{5,3},{6,0},{7,5},{8,10},{9,15},{10,... | collective-permute-start | bytes 2359304 | tf_op jit(solution)/shard_map/ppermute | solution.py:53
  155.2 25.8 %collective-permute-start.23 = (bf16[256,1536]{1,0:T(8,128)(2,1)}, bf16[256,1536]{1,0:T(8,128)(2,1)S(1)}, u32[]{:S(2)}, u32[]{:S(2)}) collective-permute-start(bf16[256,1536]{1,0:T(8,128)(2,1)} %get-tuple-element.47.refs_0_), channel_id=1, source_target_pairs={{0,6},{1,3},{2,0},{3,5},{4,2},{5,7},{6,4},{7,1},{8,14},{9,11},{10,... | collective-permute-start | bytes 2359304 | tf_op jit(solution)/shard_map/ppermute | solution.py:53
  163.5 29.8 %collective-permute-start.24 = (bf16[256,1536]{1,0:T(8,128)(2,1)S(1)}, bf16[256,1536]{1,0:T(8,128)(2,1)S(1)}, u32[]{:S(2)}, u32[]{:S(2)}) collective-permute-start(bf16[256,1536]{1,0:T(8,128)(2,1)S(1)} %collective-permute-done.22.refs_1_), channel_id=1, source_target_pairs={{0,2},{1,7},{2,4},{3,1},{4,6},{5,3},{6,0},{7,5},{8,10},{9,15},{10,... | collective-permute-start | bytes 2359304 | tf_op jit(solution)/shard_map/ppermute | solution.py:53
  165.6 38.1 %collective-permute-start.13 = (bf16[256,1536]{1,0:T(8,128)(2,1)}, bf16[256,1536]{1,0:T(8,128)(2,1)S(1)}, u32[]{:S(2)}, u32[]{:S(2)}) collective-permute-start(bf16[256,1536]{1,0:T(8,128)(2,1)} %get-tuple-element.37.refs_0_), channel_id=1, source_target_pairs={{0,6},{1,3},{2,0},{3,5},{4,2},{5,7},{6,4},{7,1},{8,14},{9,11},{10,... | collective-permute-start | bytes 2359304 | tf_op jit(solution)/shard_map/ppermute | solution.py:53
  179.2 26.7 %collective-permute-start.14 = (bf16[256,1536]{1,0:T(8,128)(2,1)S(1)}, bf16[256,1536]{1,0:T(8,128)(2,1)S(1)}, u32[]{:S(2)}, u32[]{:S(2)}) collective-permute-start(bf16[256,1536]{1,0:T(8,128)(2,1)S(1)} %collective-permute-done.12.refs_1_), channel_id=1, source_target_pairs={{0,2},{1,7},{2,4},{3,1},{4,6},{5,3},{6,0},{7,5},{8,10},{9,15},{10,... | collective-permute-start | bytes 2359304 | tf_op jit(solution)/shard_map/ppermute | solution.py:53
  193.3 1.1 copy-start.3
  202.6 12.9 %collective-permute-start.26 = (bf16[256,1536]{1,0:T(8,128)(2,1)S(1)}, bf16[256,1536]{1,0:T(8,128)(2,1)S(1)}, u32[]{:S(2)}, u32[]{:S(2)}) collective-permute-start(bf16[256,1536]{1,0:T(8,128)(2,1)S(1)} %get-tuple-element.51), channel_id=1, source_target_pairs={{0,96},{1,33},{2,98},{3,35},{4,100},{5,37},{6,102},{7,39},{8,104},... | collective-permute-start | bytes 2359304 | tf_op jit(solution)/shard_map/ppermute | solution.py:53
  214.1 14.1 %collective-permute-start.17 = (bf16[256,1536]{1,0:T(8,128)(2,1)S(1)}, bf16[256,1536]{1,0:T(8,128)(2,1)S(1)}, u32[]{:S(2)}, u32[]{:S(2)}) collective-permute-start(bf16[256,1536]{1,0:T(8,128)(2,1)S(1)} %get-tuple-element.41), channel_id=1, source_target_pairs={{0,24},{1,9},{2,26},{3,11},{4,28},{5,13},{6,30},{7,15},{8,0},{9,17... | collective-permute-start | bytes 2359304 | tf_op jit(solution)/shard_map/ppermute | solution.py:53
  214.1 17.1 %collective-permute-start.25 = (bf16[256,1536]{1,0:T(8,128)(2,1)S(1)}, bf16[256,1536]{1,0:T(8,128)(2,1)S(1)}, u32[]{:S(2)}, u32[]{:S(2)}) collective-permute-start(bf16[256,1536]{1,0:T(8,128)(2,1)S(1)} %get-tuple-element.49), channel_id=1, source_target_pairs={{0,32},{1,97},{2,34},{3,99},{4,36},{5,101},{6,38},{7,103},{8,40},{... | collective-permute-start | bytes 2359304 | tf_op jit(solution)/shard_map/ppermute | solution.py:53
  215.7 15.5 %collective-permute-start.27 = (bf16[256,1536]{1,0:T(8,128)(2,1)S(1)}, bf16[256,1536]{1,0:T(8,128)(2,1)S(1)}, u32[]{:S(2)}, u32[]{:S(2)}) collective-permute-start(bf16[256,1536]{1,0:T(8,128)(2,1)S(1)} %shard_map.135), channel_id=1, source_target_pairs={{0,96},{1,33},{2,98},{3,35},{4,100},{5,37},{6,102},{7,39},{8,104},... | collective-permute-start | bytes 2359304 | tf_op jit(solution)/shard_map/ppermute | solution.py:53
  216.0 28.4 %collective-permute-start.16 = (bf16[256,1536]{1,0:T(8,128)(2,1)S(1)}, bf16[256,1536]{1,0:T(8,128)(2,1)S(1)}, u32[]{:S(2)}, u32[]{:S(2)}) collective-permute-start(bf16[256,1536]{1,0:T(8,128)(2,1)S(1)} %get-tuple-element.39), channel_id=1, source_target_pairs={{0,8},{1,25},{2,10},{3,27},{4,12},{5,29},{6,14},{7,31},{8,16},{9,1... | collective-permute-start | bytes 2359304 | tf_op jit(solution)/shard_map/ppermute | solution.py:53
  228.4 19.4 %collective-permute-start.18 = (bf16[256,1536]{1,0:T(8,128)(2,1)S(1)}, bf16[256,1536]{1,0:T(8,128)(2,1)S(1)}, u32[]{:S(2)}, u32[]{:S(2)}) collective-permute-start(bf16[256,1536]{1,0:T(8,128)(2,1)S(1)} %shard_map.131), channel_id=1, source_target_pairs={{0,24},{1,9},{2,26},{3,11},{4,28},{5,13},{6,30},{7,15},{8,0},{9,17... | collective-permute-start | bytes 2359304 | tf_op jit(solution)/shard_map/ppermute | solution.py:53
  231.6 21.9 %copy-start.13 = (f32[768]{0:T(1024)S(1)}, f32[768]{0:T(1024)}, u32[]{:S(2)}) copy-start(f32[768]{0:T(1024)} %param.20) | copy-start | bytes 9220
  231.6 20.6 %collective-permute-start.28 = (bf16[64,1536]{1,0:T(8,128)(2,1)S(1)}, bf16[64,1536]{1,0:T(8,128)(2,1)S(1)}, u32[]{:S(2)}, u32[]{:S(2)}) collective-permute-start(bf16[64,1536]{1,0:T(8,128)(2,1)S(1)} %get-tuple-element.53), channel_id=1, source_target_pairs={{0,24},{1,25},{2,26},{3,27},{4,28},{5,29},{6,30},{7,31},{8,0},{9,1... | collective-permute-start | bytes 589832 | tf_op jit(solution)/shard_map/ppermute | solution.py:53
  243.1 10.3 %collective-permute-start.29 = (bf16[64,1536]{1,0:T(8,128)(2,1)S(1)}, bf16[64,1536]{1,0:T(8,128)(2,1)S(1)}, u32[]{:S(2)}, u32[]{:S(2)}) collective-permute-start(bf16[64,1536]{1,0:T(8,128)(2,1)S(1)} %get-tuple-element.54), channel_id=1, source_target_pairs={{0,8},{1,9},{2,10},{3,11},{4,12},{5,13},{6,14},{7,15},{8,16},{9,17... | collective-permute-start | bytes 589832 | tf_op jit(solution)/shard_map/ppermute | solution.py:53
  243.1 13.1 %collective-permute-start.30 = (bf16[64,1536]{1,0:T(8,128)(2,1)S(1)}, bf16[64,1536]{1,0:T(8,128)(2,1)S(1)}, u32[]{:S(2)}, u32[]{:S(2)}) collective-permute-start(bf16[64,1536]{1,0:T(8,128)(2,1)S(1)} %get-tuple-element.55), channel_id=1, source_target_pairs={{0,16},{1,17},{2,18},{3,19},{4,20},{5,21},{6,22},{7,23},{8,24},{9,... | collective-permute-start | bytes 589832 | tf_op jit(solution)/shard_map/ppermute | solution.py:53
  248.1 13.3 %collective-permute-start.19 = (bf16[64,1536]{1,0:T(8,128)(2,1)S(1)}, bf16[64,1536]{1,0:T(8,128)(2,1)S(1)}, u32[]{:S(2)}, u32[]{:S(2)}) collective-permute-start(bf16[64,1536]{1,0:T(8,128)(2,1)S(1)} %get-tuple-element.43), channel_id=1, source_target_pairs={{0,96},{1,97},{2,98},{3,99},{4,100},{5,101},{6,102},{7,103},{8,104... | collective-permute-start | bytes 589832 | tf_op jit(solution)/shard_map/ppermute | solution.py:53
  252.2 9.2 %collective-permute-start.20 = (bf16[64,1536]{1,0:T(8,128)(2,1)S(1)}, bf16[64,1536]{1,0:T(8,128)(2,1)S(1)}, u32[]{:S(2)}, u32[]{:S(2)}) collective-permute-start(bf16[64,1536]{1,0:T(8,128)(2,1)S(1)} %get-tuple-element.44), channel_id=1, source_target_pairs={{0,32},{1,33},{2,34},{3,35},{4,36},{5,37},{6,38},{7,39},{8,40},{9,... | collective-permute-start | bytes 589832 | tf_op jit(solution)/shard_map/ppermute | solution.py:53
  252.2 9.2 %collective-permute-start.21 = (bf16[64,1536]{1,0:T(8,128)(2,1)S(1)}, bf16[64,1536]{1,0:T(8,128)(2,1)S(1)}, u32[]{:S(2)}, u32[]{:S(2)}) collective-permute-start(bf16[64,1536]{1,0:T(8,128)(2,1)S(1)} %get-tuple-element.45), channel_id=1, source_target_pairs={{0,64},{1,65},{2,66},{3,67},{4,68},{5,69},{6,70},{7,71},{8,72},{9,... | collective-permute-start | bytes 589832 | tf_op jit(solution)/shard_map/ppermute | solution.py:53
  256.3 12.9 %collective-permute-start.32 = (bf16[64,768]{1,0:T(8,128)(2,1)S(1)}, bf16[64,768]{1,0:T(8,128)(2,1)S(1)}, u32[]{:S(2)}, u32[]{:S(2)}) collective-permute-start(bf16[64,768]{1,0:T(8,128)(2,1)S(1)} %get-tuple-element.58), channel_id=1, source_target_pairs={{0,1},{1,0},{2,3},{3,2},{4,5},{5,4},{6,7},{7,6},{8,9},{9,8},{10,11... | collective-permute-start | bytes 294920 | tf_op jit(solution)/shard_map/ppermute | solution.py:62
  261.5 8.0 %collective-permute-start.31 = (bf16[64,768]{1,0:T(8,128)(2,1)S(1)}, bf16[64,768]{1,0:T(8,128)(2,1)S(1)}, u32[]{:S(2)}, u32[]{:S(2)}) collective-permute-start(bf16[64,768]{1,0:T(8,128)(2,1)S(1)} %get-tuple-element.57), channel_id=1, source_target_pairs={{0,1},{1,0},{2,3},{3,2},{4,5},{5,4},{6,7},{7,6},{8,9},{9,8},{10,11... | collective-permute-start | bytes 294920 | tf_op jit(solution)/shard_map/ppermute | solution.py:62
Sparse Core Ops, SparseCore 0:
  9.3 71.0 all-gather.2
  90.1 37.1 all-gather.4

commit v7 on v6

--- a/solution.py
+++ b/solution.py
@@ -66,7 +66,7 @@
     return pltpu.CompilerParams(vmem_limit_bytes=mb * MB)
 
 
-def act_kernel(cut, moved_ref, first_ref, second_ref):
+def act_kernel(moved_ref, first_ref, second_ref):
     cols, _, chans = moved_ref.shape
     half = first_ref.shape[0]
     values = moved_ref[:, : 2 * half, :].astype(F32)
@@ -76,18 +76,14 @@
     scale = 1.0 / jnp.sqrt(square - mean * mean + 1e-05)
     for j in range(cols):
         part = ((values[j] - mean) * scale * gains[j][None, :]).astype(BF)
-        for low, high in ((0, cut), (cut, chans)):
-            at = cols * low + j * (high - low)
-            first_ref[:, at : at + high - low] = part[:half, low:high]
-            second_ref[:, at : at + high - low] = part[half:, low:high]
-
-
-def normalize(moved, half, cut):
+        first_ref[:, j * chans : (j + 1) * chans] = part[:half]
+        second_ref[:, j * chans : (j + 1) * chans] = part[half:]
+
+
+def normalize(moved, half):
     cols, _, chans = moved.shape
     shape = jax.ShapeDtypeStruct((half, cols * chans), BF)
-    return pl.pallas_call(
-        functools.partial(act_kernel, cut), out_shape=(shape, shape), compiler_params=params(16)
-    )(moved)
+    return pl.pallas_call(act_kernel, out_shape=(shape, shape), compiler_params=params(16))(moved)
 
 
 def fill(sources, target, sems):
@@ -105,55 +101,54 @@
             copy.wait()
 
 
-def mm1_kernel(*refs):
-    pieces, (wa_ref, wb_ref, b_ref, o1_ref, o2_ref, left, sems) = refs[:-7], refs[-7:]
+def mm1_kernel(count, *refs):
+    pieces, (w_ref, b_ref), (o1_ref, o2_ref, left, sems) = refs[:count], refs[count : count + 2], refs[-4:]
     fill(pieces, left, sems)
-    cut = wa_ref.shape[0]
-    pre = jnp.dot(left[:, :cut], wa_ref[...], preferred_element_type=F32)
-    pre = pre + jnp.dot(left[:, cut:], wb_ref[...], preferred_element_type=F32) + b_ref[...]
+    pre = jnp.dot(left[...], w_ref[...], preferred_element_type=F32) + b_ref[...]
     hidden = (0.5 * pre * (1.0 + lax.erf(pre * math.sqrt(0.5)))).astype(BF)
     half = o1_ref.shape[0]
     o1_ref[...] = hidden[:half]
     o2_ref[...] = hidden[half:]
 
 
-def matmul_in(pieces, wa, wb, b):
+def matmul_in(first, second, w, b, total, into=()):
+    pieces = [*first, *second]
     rows, depth = pieces[0].shape
-    width = wa.shape[1]
+    width = w.shape[1]
     count = len(pieces)
-    tokens = count * rows
     tile = 256
-    return pl.pallas_call(
-        mm1_kernel,
+    block = len(first) * rows
+    at = total // block - 1 if into else 0
+    anywhere = pl.BlockSpec(memory_space=pl.ANY)
+    return pl.pallas_call(
+        functools.partial(mm1_kernel, count),
         grid=(width // tile,),
-        in_specs=[pl.BlockSpec(memory_space=pl.ANY) for _ in pieces]
-        + [
-            pl.BlockSpec((wa.shape[0], tile), lambda i: (0, i)),
-            pl.BlockSpec((wb.shape[0], tile), lambda i: (0, i)),
-            pl.BlockSpec((1, tile), lambda i: (0, i)),
-        ],
-        out_specs=[pl.BlockSpec((tokens // 2, tile), lambda i: (0, i))] * 2,
-        out_shape=[jax.ShapeDtypeStruct((tokens // 2, width), BF)] * 2,
-        scratch_shapes=[pltpu.VMEM((tokens, depth), BF), pltpu.SemaphoreType.DMA((count,))],
-        compiler_params=params(60),
+        in_specs=[anywhere] * count
+        + [pl.BlockSpec((depth, tile), lambda i: (0, i)), pl.BlockSpec((1, tile), lambda i: (0, i))]
+        + [anywhere] * len(into),
+        out_specs=[pl.BlockSpec((block, tile), lambda i: (at, i))] * 2,
+        out_shape=[jax.ShapeDtypeStruct((total, width), BF)] * 2,
+        input_output_aliases={count + 2 + i: i for i in range(len(into))},
+        scratch_shapes=[pltpu.VMEM((count * rows, depth), BF), pltpu.SemaphoreType.DMA((count,))],
+        compiler_params=params(58),
         cost_estimate=pl.CostEstimate(
-            flops=2 * tokens * depth * width,
-            bytes_accessed=2 * (tokens * depth + depth * width),
+            flops=2 * count * rows * depth * width,
+            bytes_accessed=2 * (count * rows * depth + depth * width),
             transcendentals=0,
         ),
-    )(*pieces, wa, wb, b[None])
-
-
-def mm2_kernel(*refs):
-    hiddens, (own_ref, other_ref) = refs[:SIDE], refs[SIDE : SIDE + 2]
-    outs, (left, sems) = refs[SIDE + 2 : -2], refs[-2:]
+    )(*pieces, w, b[None], *into)
+
+
+def mm2_kernel(count, *refs):
+    hiddens, (own_ref, other_ref) = refs[:count], refs[count : count + 2]
+    outs, (left, sems) = refs[-2 - SIDE : -2], refs[-2:]
     fill(hiddens, left, sems)
     steps = pl.num_programs(0) // 2
-    rows = outs[0].shape[0] // SIDE
+    rows = outs[0].shape[0] // count
 
     def part(w_ref):
         out = jnp.dot(left[...], w_ref[...], preferred_element_type=F32).astype(BF)
-        for x in range(SIDE):
+        for x in range(count):
             for p, o_ref in enumerate(outs):
                 at = (x * len(outs) + p) * rows
                 o_ref[x * rows : (x + 1) * rows, :] = out[at : at + rows]
@@ -162,29 +157,36 @@
     pl.when(pl.program_id(0) >= steps)(lambda: part(other_ref))
 
 
-def matmul_out(hiddens, own, other, count):
+def matmul_out(hiddens, own, other, into=()):
     depth, chans = own.shape
-    tokens = SIDE * hiddens[0].shape[0]
+    count = len(hiddens)
+    tokens = count * hiddens[0].shape[0]
+    total = hiddens[0].shape[0]
     tile = 256
     steps = chans // tile
-    return pl.pallas_call(
-        mm2_kernel,
+    block = tokens // SIDE
+    at = SIDE - 1 if into else 0
+    anywhere = pl.BlockSpec(memory_space=pl.ANY)
+    return pl.pallas_call(
+        functools.partial(mm2_kernel, count),
         grid=(2 * steps,),
-        in_specs=[pl.BlockSpec(memory_space=pl.ANY)] * SIDE
+        in_specs=[anywhere] * count
         + [
             pl.BlockSpec((depth, tile), lambda i: (0, jnp.minimum(i, steps - 1))),
             pl.BlockSpec((depth, tile), lambda i: (0, jnp.maximum(i - steps, 0))),
-        ],
-        out_specs=[pl.BlockSpec((tokens // count, tile), lambda i: (0, i))] * count,
-        out_shape=[jax.ShapeDtypeStruct((tokens // count, 2 * chans), BF)] * count,
-        scratch_shapes=[pltpu.VMEM((tokens, depth), BF), pltpu.SemaphoreType.DMA((SIDE,))],
-        compiler_params=params(32),
+        ]
+        + [anywhere] * len(into),
+        out_specs=[pl.BlockSpec((block, tile), lambda i: (at, i))] * SIDE,
+        out_shape=[jax.ShapeDtypeStruct((total, 2 * chans), BF)] * SIDE,
+        input_output_aliases={count + 2 + i: i for i in range(len(into))},
+        scratch_shapes=[pltpu.VMEM((tokens, depth), BF), pltpu.SemaphoreType.DMA((count,))],
+        compiler_params=params(58),
         cost_estimate=pl.CostEstimate(
             flops=4 * tokens * depth * chans,
             bytes_accessed=2 * (tokens * depth + 2 * depth * chans + 2 * tokens * chans),
             transcendentals=0,
         ),
-    )(*hiddens, own, other)
+    )(*hiddens, own, other, *into)
 
 
 def pair_kernel(a, b, o):
@@ -356,8 +358,7 @@
 def on_device(image, filter_bank, gain_first, gain_second, w_in, b_in, w_out, b_out):
     rows_here, width, chans = image.shape
     cols = lax.axis_size("col")
-    cut = w_in.shape[0] * 2 // 3
-    w_in_low = lax.all_gather(w_in[:cut], "col", axis=0, tiled=True)
+    w_in_all = lax.all_gather(w_in, "col", axis=0, tiled=True)
     resid = spectral(image, filter_bank, gain_first)
     tokens = rows_here * width
     own = tokens // cols
@@ -371,17 +372,19 @@
         axis=1,
     )
     moved = exchange(message, "col")
-    moved, w_rest, w_in_low = tie([moved, w_in[cut:], w_in_low], [])
-    w_in_high = lax.all_gather(w_rest, "col", axis=0, tiled=True)
-    first, second = normalize(moved, half, cut)
+    first, second = normalize(moved, half)
     first, second = gather_near(first, "z"), gather_near(second, "y")
-    pieces = gather_far(first, "y") + gather_far(second, "z")
-    hiddens = [gather_far(hidden, "x") for hidden in matmul_in(pieces, w_in_low, w_in_high, b_in)]
+    first, second = gather_far(first, "y"), gather_far(second, "z")
+    total = SIDE * SIDE * half
+    hidden = matmul_in(first[:-1], second[:-1], w_in_all, b_in, total)
+    hidden = matmul_in(first[-1:], second[-1:], w_in_all, b_in, total, hidden)
     other = swap_cores(w_out)
+    hiddens = [gather_far(h, "x") for h in hidden]
+    outs = [matmul_out(h[:-1], w_out, other) for h in hiddens]
+    outs = [matmul_out(h[-1:], w_out, other, out) for h, out in zip(hiddens, outs)]
     sums = []
-    for hidden, (large, small) in zip(hiddens, (("y", "z"), ("z", "y"))):
-        outs = matmul_out(hidden, w_out, other, SIDE)
-        sums.append(add_last(reduce_far(outs, large, small, half)))
+    for out, (large, small) in zip(outs, (("y", "z"), ("z", "y"))):
+        sums.append(add_last(reduce_far(out, large, small, half)))
     (own1, give1), (own2, give2) = sums
     got1, got2 = swap_cores(give1), swap_cores(give2)
     resid = resid.reshape(cols, own, chans)

time: 279 us -> 288 us (1.032)
  starting transfers between devices: 94.8 us -> 60.2 us
  blocking collectives: 13.2 us -> 42.6 us
  Pallas kernels: 36.2 us -> 63.3 us
  waiting for transfers between devices: 97.6 us -> 90.9 us
  local copies, waits for them, and re-layouts: 13.3 us -> 6.73 us
    all_to_all x0 -> x1, blocking collectives: none -> 29.4 us  [exchange(): return lax.all_to_all(a, axis, split_axis=0, concat_axis=0, tiled=True)]
    pallas_call x5 -> x7, Pallas kernels: 33.6 us -> 60.7 us  [the longest x4 34.5 us: matmul_out(): pl.pallas_call(functools.partial(mm2_kernel, count), grid=(2 * steps,), i...]
    ppermute x30, starting transfers between devices: 49.1 us -> 27.3 us  [hop(): return lax.ppermute(a, ('row', 'col'), pairs)]
    all_to_all x3 -> x2, starting transfers between devices: 24.3 us -> 11.6 us  [exchange(): return lax.all_to_all(a, axis, split_axis=0, concat_axis=0, tiled=True)]
    all_to_all x3 -> x2, waiting for transfers between devices: 28.2 us -> 20.1 us  [exchange(): return lax.all_to_all(a, axis, split_axis=0, concat_axis=0, tiled=True)]
    slice x2 -> x0, local copies, waits for them, and re-layouts: 4.74 us -> none  [the longest x1 2.65 us: on_device(): w_in_low = lax.all_gather(w_in[:cut], 'col', axis=0, tiled=True)]
  transfers between devices with their start and end apart: 38 -> 36, of which waited for: 18 -> 14; matrix products, arithmetic and copies ran while one was open for 5% -> 4% of each run, Pallas kernels for 13% -> 22%
where the time goes in v7:
time: 288 us; the launch traced here: 286 us
  waiting for transfers between devices  90.9 us (32%)
  Pallas kernels  63.3 us (22%)
  starting transfers between devices  60.2 us (21%)
  blocking collectives  42.6 us (15%)
  between operations  13.9 us (5%)
  matrix products  7.35 us (3%)
  local copies, waits for them, and re-layouts  6.73 us (2%)
    ppermute x30, waiting for transfers between devices, hop(): return lax.ppermute(a, ('row', 'col'), pairs)  69.9 us
    pallas_call x4, Pallas kernels, matmul_out(): pl.pallas_call(functools.partial(mm2_kernel, count), grid=(2 * steps,), i...  34.5 us
    all_to_all x1, blocking collectives, exchange(): return lax.all_to_all(a, axis, split_axis=0, concat_axis=0, tiled=True)  29.4 us
    ppermute x30, starting transfers between devices, hop(): return lax.ppermute(a, ('row', 'col'), pairs)  27.3 us
    pallas_call x2, Pallas kernels, matmul_in(): pl.pallas_call(functools.partial(mm1_kernel, count), grid=(width // tile,...  25.9 us
    ppermute x3, starting transfers between devices, swap_cores(): return lax.ppermute(a, 'col', pairs)  21.3 us
    all_to_all x2, waiting for transfers between devices, exchange(): return lax.all_to_all(a, axis, split_axis=0, concat_axis=0, tiled=True)  20.1 us
    psum x1, blocking collectives, spectral(): lax.psum((jnp.sum(source, axis=-1), jnp.sum(source * source, axis=-1)), '...  13.2 us
  transfers between devices with their start and end apart: 36, of which 14 were waited for; matrix products, arithmetic and copies ran while one was open for 4% of the time, Pallas kernels for 22%

profile of v7, /device:TPU:1, one launch (start us, length us, event | category | flops | bytes accessed | tf_op | source)
XLA Modules:
  0.0 285.6 jit_solution(18016285348034454270)
XLA Ops:
  6.5 0.7 all-gather.2.cloned.1.call-update
  7.3 0.3 copy-done.5
  7.9 13.2 %all-reduce.1 = (f32[256]{0:T(256)S(1)}, f32[256]{0:T(256)S(1)}) all-reduce(f32[256]{0:T(256)S(1)} %reduce_sum.25, f32[256]{0:T(256)S(1)} %reduce_sum.23), channel_id=1, replica_groups=mesh['row'=16,'col'=8] {'col'}, use_global_device_ids=true, to_apply=%region_3.0 | all-reduce | flops 512 | bytes 4096 | tf_op jit(solution)/shard_map/psum | solution.py:296
  21.3 1.7 convolution_convert_fusion
  23.0 7.8 %all-to-all-start = ((bf16[16,32,768]{2,1,0:T(8,128)(2,1)}), bf16[16,32,768]{2,1,0:T(8,128)(2,1)S(1)}, u32[]{:S(2)}, u32[]{:S(2)}) async-start(bf16[16,32,768]{2,1,0:T(8,128)(2,1)} %bitcast.3), calls=%async_computation | async-start | bytes 1572864 | tf_op jit(solution)/shard_map/all_to_all | solution.py:268
  30.9 1.5 fusion.19
  32.3 0.3 reshape_squeeze.6
  32.6 0.3 reshape_squeeze.7
  32.9 9.7 %all-to-all-done = bf16[16,32,768]{2,1,0:T(8,128)(2,1)S(1)} async-done(((bf16[16,32,768]{2,1,0:T(8,128)(2,1)}), bf16[16,32,768]{2,1,0:T(8,128)(2,1)S(1)}, u32[]{:S(2)}, u32[]{:S(2)}) %all-to-all-start) | async-done | bytes 786464 | tf_op jit(solution)/shard_map/all_to_all | solution.py:268
  42.6 2.3 fusion.21
  44.9 0.9 fusion.5
  45.9 1.8 add_convert_fusion
  47.8 3.7 %all-to-all-start.1 = ((bf16[16,32,768]{2,1,0:T(8,128)(2,1)}), bf16[16,32,768]{2,1,0:T(8,128)(2,1)S(1)}, u32[]{:S(2)}, u32[]{:S(2)}) async-start(bf16[16,32,768]{2,1,0:T(8,128)(2,1)} %bitcast.6), calls=%async_computation.1 | async-start | bytes 1572864 | tf_op jit(solution)/shard_map/all_to_all | solution.py:268
  51.6 10.4 %all-to-all-done.1 = bf16[16,32,768]{2,1,0:T(8,128)(2,1)S(1)} async-done(((bf16[16,32,768]{2,1,0:T(8,128)(2,1)}), bf16[16,32,768]{2,1,0:T(8,128)(2,1)S(1)}, u32[]{:S(2)}, u32[]{:S(2)}) %all-to-all-start.1) | async-done | bytes 786464 | tf_op jit(solution)/shard_map/all_to_all | solution.py:268
  62.0 0.6 fusion.20
  62.7 29.4 %all_to_all.15.moved_ref = bf16[8,48,768]{2,1,0:T(8,128)(2,1)S(1)} all-to-all(bf16[8,48,768]{2,1,0:T(8,128)(2,1)S(1)} %pad_maximum_fusion.2), channel_id=1, replica_groups=mesh['row'=16,'col'=8] {'col'}, dimensions={0} | all-to-all | bytes 1179648 | tf_op jit(solution)/shard_map/all_to_all | solution.py:268
  92.1 0.3 shard_map.127
  92.4 0.4 collective-permute-start.5
  92.8 2.3 collective-permute-start.6
  95.1 2.7 collective-permute-start.1
  97.8 1.5 collective-permute-done.5
  99.3 0.5 collective-permute-start.2
  99.8 1.8 collective-permute-done.7
  101.8 1.4 collective-permute-start.8
  103.2 2.2 collective-permute-done.2
  105.5 0.8 collective-permute-start.3
  106.2 1.4 collective-permute-start.11
  107.7 11.1 %collective-permute-start.14 = (bf16[1536,768]{1,0:T(8,128)(2,1)S(1)}, bf16[1536,768]{1,0:T(8,128)(2,1)}, u32[]{:S(2)}, u32[]{:S(2)}) collective-permute-start(bf16[1536,768]{1,0:T(8,128)(2,1)S(1)} %copy-done.4), channel_id=1, source_target_pairs={{0,1},{1,0},{2,3},{3,2},{4,5},{5,4},{6,7},{7,6},{8,9},{9,8},{10,11... | collective-permute-start | bytes 7077896 | tf_op jit(solution)/shard_map/ppermute | solution.py:62
  118.8 1.1 collective-permute-start.4
  119.9 0.6 broadcast_in_dim.7.refs_7_.refs_3_
  120.5 8.4 %collective-permute-done.11.refs_5_ = bf16[64,6144]{1,0:T(8,128)(2,1)S(1)} collective-permute-done((bf16[64,6144]{1,0:T(8,128)(2,1)S(1)}, bf16[64,6144]{1,0:T(8,128)(2,1)S(1)}, u32[]{:S(2)}, u32[]{:S(2)}) %collective-permute-start.11) | collective-permute-done | bytes 786464 | tf_op jit(solution)/shard_map/ppermute | solution.py:53
  128.9 0.9 copy-done.21
  129.9 14.8 %shard_map.128 = (bf16[256,1536]{1,0:T(8,128)(2,1)}, bf16[256,1536]{1,0:T(8,128)(2,1)}) custom-call(bf16[64,6144]{1,0:T(8,128)(2,1)} %bitcast.50, bf16[64,6144]{1,0:T(8,128)(2,1)} %collective-permute-done.3.refs_1_, bf16[64,6144]{1,0:T(8,128)(2,1)} %collective-permute-done.10.refs_2_, bf16[64,6144]{1,0:T(8,128)(2,1)} %bitcast.47, ...), custom_call_target="tpu_custom_call" | custom-call | flops 7247757312 | bytes 23592960 | tf_op jit(solution)/shard_map/pallas_call | solution.py:123
  144.7 11.1 %shard_map.129 = (bf16[256,1536]{1,0:T(8,128)(2,1)}, bf16[256,1536]{1,0:T(8,128)(2,1)}) custom-call(bf16[64,6144]{1,0:T(8,128)(2,1)} %collective-permute-done.4.refs_0_, bf16[64,6144]{1,0:T(8,128)(2,1)} %collective-permute-done.9.refs_1_, ...), custom_call_target="tpu_custom_call", output_to_operand_aliasing={{0}: (4, {}), {1}: (5, {})} | custom-call | flops 2415919104 | bytes 20447232 | tf_op jit(solution)/shard_map/pallas_call | solution.py:123
  155.8 1.0 collective-permute-start.22
  157.0 1.3 collective-permute-start.24
  158.2 10.6 %collective-permute-done.22.refs_1_ = bf16[256,1536]{1,0:T(8,128)(2,1)} collective-permute-done((bf16[256,1536]{1,0:T(8,128)(2,1)}, bf16[256,1536]{1,0:T(8,128)(2,1)}, u32[]{:S(2)}, u32[]{:S(2)}) %collective-permute-start.22) | collective-permute-done | bytes 786464 | tf_op jit(solution)/shard_map/ppermute | solution.py:53
  168.9 0.3 collective-permute-start.23
  169.1 1.2 collective-permute-start.15
  170.3 13.8 %collective-permute-done.12.refs_1_ = bf16[256,1536]{1,0:T(8,128)(2,1)S(1)} collective-permute-done((bf16[256,1536]{1,0:T(8,128)(2,1)}, bf16[256,1536]{1,0:T(8,128)(2,1)S(1)}, u32[]{:S(2)}, u32[]{:S(2)}) %collective-permute-start.12) | collective-permute-done | bytes 786464 | tf_op jit(solution)/shard_map/ppermute | solution.py:53
  184.1 1.7 collective-permute-start.13
  185.8 9.7 %shard_map.135 = (bf16[256,1536]{1,0:T(8,128)(2,1)}, bf16[256,1536]{1,0:T(8,128)(2,1)}, bf16[256,1536]{1,0:T(8,128)(2,1)}, bf16[256,1536]{1,0:T(8,128)(2,1)}) custom-call(bf16[256,1536]{1,0:T(8,128)(2,1)} %get-tuple-element.57.refs_0_, bf16[256,1536]{1,0:T(8,128)(2,1)} %collective-permute-done.22.refs_1_, bf16[256,1536]{1,0:T(8,128)(2,1)} %collective-permute-done.24.refs_2_, ...), custom_call_target="tpu_custom_call" | custom-call | flops 3623878656 | bytes 9437184 | tf_op jit(solution)/shard_map/pallas_call | solution.py:170
  195.6 3.0 %collective-permute-done.23.refs_0_ = bf16[256,1536]{1,0:T(8,128)(2,1)S(1)} collective-permute-done((bf16[256,1536]{1,0:T(8,128)(2,1)}, bf16[256,1536]{1,0:T(8,128)(2,1)S(1)}, u32[]{:S(2)}, u32[]{:S(2)}) %collective-permute-start.23) | collective-permute-done | bytes 786464 | tf_op jit(solution)/shard_map/ppermute | solution.py:53
  198.6 0.9 copy-done.7
  199.5 7.5 %shard_map.136 = (bf16[256,1536]{1,0:T(8,128)(2,1)}, bf16[256,1536]{1,0:T(8,128)(2,1)}, bf16[256,1536]{1,0:T(8,128)(2,1)}, bf16[256,1536]{1,0:T(8,128)(2,1)}) custom-call(bf16[256,1536]{1,0:T(8,128)(2,1)} %copy-done.7, bf16[1536,768]{1,0:T(8,128)(2,1)} %refs_1_.3, ...), custom_call_target="tpu_custom_call", output_to_operand_aliasing={{0}: (3, {}), {1}: (4, {}), {2}: (5, {}), {3}: (6, {})} | custom-call | flops 1207959552 | bytes 6291456 | tf_op jit(solution)/shard_map/pallas_call | solution.py:170
  207.0 9.8 %shard_map.130 = (bf16[256,1536]{1,0:T(8,128)(2,1)}, bf16[256,1536]{1,0:T(8,128)(2,1)}, bf16[256,1536]{1,0:T(8,128)(2,1)}, bf16[256,1536]{1,0:T(8,128)(2,1)}) custom-call(bf16[256,1536]{1,0:T(8,128)(2,1)} %get-tuple-element.43.refs_0_, bf16[256,1536]{1,0:T(8,128)(2,1)} %copy-done.20, bf16[256,1536]{1,0:T(8,128)(2,1)} %collective-permute-done.15.refs_2_, ...), custom_call_target="tpu_custom_call" | custom-call | flops 3623878656 | bytes 9437184 | tf_op jit(solution)/shard_map/pallas_call | solution.py:170
  216.8 0.9 copy-done.6
  217.7 7.6 %shard_map.131 = (bf16[256,1536]{1,0:T(8,128)(2,1)}, bf16[256,1536]{1,0:T(8,128)(2,1)}, bf16[256,1536]{1,0:T(8,128)(2,1)}, bf16[256,1536]{1,0:T(8,128)(2,1)}) custom-call(bf16[256,1536]{1,0:T(8,128)(2,1)} %copy-done.6, bf16[1536,768]{1,0:T(8,128)(2,1)} %refs_1_.3, ...), custom_call_target="tpu_custom_call", output_to_operand_aliasing={{0}: (3, {}), {1}: (4, {}), {2}: (5, {}), {3}: (6, {})} | custom-call | flops 1207959552 | bytes 6291456 | tf_op jit(solution)/shard_map/pallas_call | solution.py:170
  225.4 2.7 collective-permute-start.25
  228.4 2.7 collective-permute-start.16
  231.1 6.8 %collective-permute-done.17.b = bf16[256,1536]{1,0:T(8,128)(2,1)S(1)} collective-permute-done((bf16[256,1536]{1,0:T(8,128)(2,1)}, bf16[256,1536]{1,0:T(8,128)(2,1)S(1)}, u32[]{:S(2)}, u32[]{:S(2)}) %collective-permute-start.17) | collective-permute-done | bytes 786464 | tf_op jit(solution)/shard_map/ppermute | solution.py:53
  238.3 5.4 %collective-permute-done.27.c = bf16[256,1536]{1,0:T(8,128)(2,1)S(1)} collective-permute-done((bf16[256,1536]{1,0:T(8,128)(2,1)S(1)}, bf16[256,1536]{1,0:T(8,128)(2,1)S(1)}, u32[]{:S(2)}, u32[]{:S(2)}) %collective-permute-start.27) | collective-permute-done | bytes 786464 | tf_op jit(solution)/shard_map/ppermute | solution.py:53
  243.6 0.3 shard_map.138
  244.0 2.5 collective-permute-start.28
  246.4 1.3 collective-permute-start.30
  247.7 10.2 %collective-permute-done.18.c = bf16[256,1536]{1,0:T(8,128)(2,1)S(1)} collective-permute-done((bf16[256,1536]{1,0:T(8,128)(2,1)S(1)}, bf16[256,1536]{1,0:T(8,128)(2,1)S(1)}, u32[]{:S(2)}, u32[]{:S(2)}) %collective-permute-start.18) | collective-permute-done | bytes 786464 | tf_op jit(solution)/shard_map/ppermute | solution.py:53
  257.9 0.3 shard_map.133
  258.3 1.5 collective-permute-start.20
  259.8 6.2 %collective-permute-done.29.c = bf16[64,1536]{1,0:T(8,128)(2,1)S(1)} collective-permute-done((bf16[64,1536]{1,0:T(8,128)(2,1)S(1)}, bf16[64,1536]{1,0:T(8,128)(2,1)S(1)}, u32[]{:S(2)}, u32[]{:S(2)}) %collective-permute-start.29) | collective-permute-done | bytes 196640 | tf_op jit(solution)/shard_map/ppermute | solution.py:53
  266.1 4.6 %collective-permute-start.32 = (bf16[64,768]{1,0:T(8,128)(2,1)S(1)}, bf16[64,768]{1,0:T(8,128)(2,1)S(1)}, u32[]{:S(2)}, u32[]{:S(2)}) collective-permute-start(bf16[64,768]{1,0:T(8,128)(2,1)S(1)} %get-tuple-element.72), channel_id=1, source_target_pairs={{0,1},{1,0},{2,3},{3,2},{4,5},{5,4},{6,7},{7,6},{8,9},{9,8},{10,11... | collective-permute-start | bytes 294920 | tf_op jit(solution)/shard_map/ppermute | solution.py:62
  270.8 5.6 %collective-permute-start.31 = (bf16[64,768]{1,0:T(8,128)(2,1)S(1)}, bf16[64,768]{1,0:T(8,128)(2,1)S(1)}, u32[]{:S(2)}, u32[]{:S(2)}) collective-permute-start(bf16[64,768]{1,0:T(8,128)(2,1)S(1)} %get-tuple-element.71), channel_id=1, source_target_pairs={{0,1},{1,0},{2,3},{3,2},{4,5},{5,4},{6,7},{7,6},{8,9},{9,8},{10,11... | collective-permute-start | bytes 294920 | tf_op jit(solution)/shard_map/ppermute | solution.py:62
  276.4 0.7 dynamic-slice_bitcast_fusion.place_ref
  277.1 0.2 collective-permute-done.31.got1
  277.4 1.4 shard_map.140
  (94 shorter events, 2.4 us)
Async XLA Ops:
  6.5 14.8 %copy-start.15 = (f32[512,256]{1,0:T(8,128)S(1)}, f32[512,256]{1,0:T(8,128)}, u32[]{:S(2)}) copy-start(f32[512,256]{1,0:T(8,128)} %constant.28.clone) | copy-start | bytes 1572868
  6.5 1.1 copy-start.5
  6.5 14.6 %copy-start.17 = (f32[768]{0:T(1024)S(1)}, f32[768]{0:T(1024)}, u32[]{:S(2)}) copy-start(f32[768]{0:T(1024)} %param.15) | copy-start | bytes 9220
  6.5 123.3 %all-gather.2.cloned.1.call-start = ((), (), s32[]{:S(2)}) async-start(), calls=%async_computation.3 | async-start | bytes 21233664 | tf_op jit(solution)/shard_map/all_gather | solution.py:361
  23.0 19.6 %all-to-all-start = ((bf16[16,32,768]{2,1,0:T(8,128)(2,1)}), bf16[16,32,768]{2,1,0:T(8,128)(2,1)S(1)}, u32[]{:S(2)}, u32[]{:S(2)}) async-start(bf16[16,32,768]{2,1,0:T(8,128)(2,1)} %bitcast.3), calls=%async_computation | async-start | bytes 1572864 | tf_op jit(solution)/shard_map/all_to_all | solution.py:268
  42.6 2.3 copy-start.13
  44.9 1.0 copy-start.12
  47.8 3.8 %copy-start.19 = (f32[768]{0:T(1024)S(1)}, f32[768]{0:T(1024)}, u32[]{:S(2)}) copy-start(f32[768]{0:T(1024)} %param.16) | copy-start | bytes 9220
  47.8 14.2 %copy-start.14 = (f32[256,512]{1,0:T(8,128)S(1)}, f32[256,512]{1,0:T(8,128)}, u32[]{:S(2)}) copy-start(f32[256,512]{1,0:T(8,128)} %constant.31.clone) | copy-start | bytes 1572868
  47.8 14.2 %all-to-all-start.1 = ((bf16[16,32,768]{2,1,0:T(8,128)(2,1)}), bf16[16,32,768]{2,1,0:T(8,128)(2,1)S(1)}, u32[]{:S(2)}, u32[]{:S(2)}) async-start(bf16[16,32,768]{2,1,0:T(8,128)(2,1)} %bitcast.6), calls=%async_computation.1 | async-start | bytes 1572864 | tf_op jit(solution)/shard_map/all_to_all | solution.py:268
  92.4 6.9 %collective-permute-start.5 = (bf16[16,6144]{1,0:T(8,128)(2,1)S(1)}, bf16[16,6144]{1,0:T(8,128)(2,1)S(1)}, u32[]{:S(2)}, u32[]{:S(2)}) collective-permute-start(bf16[16,6144]{1,0:T(8,128)(2,1)S(1)} %get-tuple-element.40), channel_id=1, source_target_pairs={{0,8},{1,9},{2,10},{3,11},{4,12},{5,13},{6,14},{7,15},{8,16},{9,17... | collective-permute-start | bytes 589832 | tf_op jit(solution)/shard_map/ppermute | solution.py:53
  92.8 7.0 %collective-permute-start.6 = (bf16[16,6144]{1,0:T(8,128)(2,1)S(1)}, bf16[16,6144]{1,0:T(8,128)(2,1)S(1)}, u32[]{:S(2)}, u32[]{:S(2)}) collective-permute-start(bf16[16,6144]{1,0:T(8,128)(2,1)S(1)} %get-tuple-element.40), channel_id=1, source_target_pairs={{0,24},{1,25},{2,26},{3,27},{4,28},{5,29},{6,30},{7,31},{8,0},{9,1... | collective-permute-start | bytes 589832 | tf_op jit(solution)/shard_map/ppermute | solution.py:53
  95.1 6.5 %collective-permute-start.7 = (bf16[16,6144]{1,0:T(8,128)(2,1)S(1)}, bf16[16,6144]{1,0:T(8,128)(2,1)S(1)}, u32[]{:S(2)}, u32[]{:S(2)}) collective-permute-start(bf16[16,6144]{1,0:T(8,128)(2,1)S(1)} %get-tuple-element.40), channel_id=1, source_target_pairs={{0,16},{1,17},{2,18},{3,19},{4,20},{5,21},{6,22},{7,23},{8,24},{9,... | collective-permute-start | bytes 589832 | tf_op jit(solution)/shard_map/ppermute | solution.py:53
  95.1 8.0 %collective-permute-start = (bf16[16,6144]{1,0:T(8,128)(2,1)S(1)}, bf16[16,6144]{1,0:T(8,128)(2,1)S(1)}, u32[]{:S(2)}, u32[]{:S(2)}) collective-permute-start(bf16[16,6144]{1,0:T(8,128)(2,1)S(1)} %get-tuple-element.39), channel_id=1, source_target_pairs={{0,32},{1,33},{2,34},{3,35},{4,36},{5,37},{6,38},{7,39},{8,40},{9,... | collective-permute-start | bytes 589832 | tf_op jit(solution)/shard_map/ppermute | solution.py:53
  95.1 8.0 %collective-permute-start.1 = (bf16[16,6144]{1,0:T(8,128)(2,1)S(1)}, bf16[16,6144]{1,0:T(8,128)(2,1)S(1)}, u32[]{:S(2)}, u32[]{:S(2)}) collective-permute-start(bf16[16,6144]{1,0:T(8,128)(2,1)S(1)} %get-tuple-element.39), channel_id=1, source_target_pairs={{0,96},{1,97},{2,98},{3,99},{4,100},{5,101},{6,102},{7,103},{8,104... | collective-permute-start | bytes 589832 | tf_op jit(solution)/shard_map/ppermute | solution.py:53
  99.3 6.1 %collective-permute-start.2 = (bf16[16,6144]{1,0:T(8,128)(2,1)S(1)}, bf16[16,6144]{1,0:T(8,128)(2,1)S(1)}, u32[]{:S(2)}, u32[]{:S(2)}) collective-permute-start(bf16[16,6144]{1,0:T(8,128)(2,1)S(1)} %get-tuple-element.39), channel_id=1, source_target_pairs={{0,64},{1,65},{2,66},{3,67},{4,68},{5,69},{6,70},{7,71},{8,72},{9,... | collective-permute-start | bytes 589832 | tf_op jit(solution)/shard_map/ppermute | solution.py:53
  101.7 6.1 %copy-start.4 = (bf16[1536,768]{1,0:T(8,128)(2,1)S(1)}, bf16[1536,768]{1,0:T(8,128)(2,1)}, u32[]{:S(2)}) copy-start(bf16[1536,768]{1,0:T(8,128)(2,1)} %refs_1_.3) | copy-start | bytes 7077892
  101.7 18.3 %copy-start.16 = (f32[1536]{0:T(1024)S(1)}, f32[1536]{0:T(1024)}, u32[]{:S(2)}) copy-start(f32[1536]{0:T(1024)} %param.18) | copy-start | bytes 18436
  101.8 17.0 %copy-start.10 = (bf16[4,16,6144]{2,1,0:T(8,128)(2,1)}, bf16[4,16,6144]{2,1,0:T(8,128)(2,1)S(1)}, u32[]{:S(2)}) copy-start(bf16[4,16,6144]{2,1,0:T(8,128)(2,1)S(1)} %pad_maximum_fusion.1) | copy-start | bytes 2359300
  101.8 17.0 %collective-permute-start.8 = (bf16[64,6144]{1,0:T(8,128)(2,1)S(1)}, bf16[64,6144]{1,0:T(8,128)(2,1)}, u32[]{:S(2)}, u32[]{:S(2)}) collective-permute-start(bf16[64,6144]{1,0:T(8,128)(2,1)S(1)} %bitcast.45), channel_id=1, source_target_pairs={{0,32},{1,97},{2,34},{3,99},{4,36},{5,101},{6,38},{7,103},{8,40},{... | collective-permute-start | bytes 2359304 | tf_op jit(solution)/shard_map/ppermute | solution.py:53
  105.4 23.5 %copy-start.11 = (bf16[4,16,6144]{2,1,0:T(8,128)(2,1)}, bf16[4,16,6144]{2,1,0:T(8,128)(2,1)S(1)}, u32[]{:S(2)}) copy-start(bf16[4,16,6144]{2,1,0:T(8,128)(2,1)S(1)} %pad_maximum_fusion) | copy-start | bytes 2359300
  105.5 13.4 %collective-permute-start.3 = (bf16[64,6144]{1,0:T(8,128)(2,1)S(1)}, bf16[64,6144]{1,0:T(8,128)(2,1)}, u32[]{:S(2)}, u32[]{:S(2)}) collective-permute-start(bf16[64,6144]{1,0:T(8,128)(2,1)S(1)} %bitcast.48), channel_id=1, source_target_pairs={{0,8},{1,25},{2,10},{3,27},{4,12},{5,29},{6,14},{7,31},{8,16},{9,1... | collective-permute-start | bytes 2359304 | tf_op jit(solution)/shard_map/ppermute | solution.py:53
  106.2 22.7 %collective-permute-start.11 = (bf16[64,6144]{1,0:T(8,128)(2,1)S(1)}, bf16[64,6144]{1,0:T(8,128)(2,1)S(1)}, u32[]{:S(2)}, u32[]{:S(2)}) collective-permute-start(bf16[64,6144]{1,0:T(8,128)(2,1)S(1)} %bitcast.46), channel_id=1, source_target_pairs={{0,96},{1,33},{2,98},{3,35},{4,100},{5,37},{6,102},{7,39},{8,104},... | collective-permute-start | bytes 2359304 | tf_op jit(solution)/shard_map/ppermute | solution.py:53
  107.6 22.3 %collective-permute-start.10 = (bf16[64,6144]{1,0:T(8,128)(2,1)S(1)}, bf16[64,6144]{1,0:T(8,128)(2,1)}, u32[]{:S(2)}, u32[]{:S(2)}) collective-permute-start(bf16[64,6144]{1,0:T(8,128)(2,1)S(1)} %bitcast.49), channel_id=1, source_target_pairs={{0,24},{1,9},{2,26},{3,11},{4,28},{5,13},{6,30},{7,15},{8,0},{9,17... | collective-permute-start | bytes 2359304 | tf_op jit(solution)/shard_map/ppermute | solution.py:53
  107.7 78.1 %collective-permute-start.14 = (bf16[1536,768]{1,0:T(8,128)(2,1)S(1)}, bf16[1536,768]{1,0:T(8,128)(2,1)}, u32[]{:S(2)}, u32[]{:S(2)}) collective-permute-start(bf16[1536,768]{1,0:T(8,128)(2,1)S(1)} %copy-done.4), channel_id=1, source_target_pairs={{0,1},{1,0},{2,3},{3,2},{4,5},{5,4},{6,7},{7,6},{8,9},{9,8},{10,11... | collective-permute-start | bytes 7077896 | tf_op jit(solution)/shard_map/ppermute | solution.py:62
  118.8 25.9 %collective-permute-start.9 = (bf16[64,6144]{1,0:T(8,128)(2,1)}, bf16[64,6144]{1,0:T(8,128)(2,1)}, u32[]{:S(2)}, u32[]{:S(2)}) collective-permute-start(bf16[64,6144]{1,0:T(8,128)(2,1)} %collective-permute-done.8.refs_4_), channel_id=1, source_target_pairs={{0,32},{1,97},{2,34},{3,99},{4,36},{5,101},{6,38},{7,103},{8,40},{... | collective-permute-start | bytes 2359304 | tf_op jit(solution)/shard_map/ppermute | solution.py:53
  118.8 25.9 %collective-permute-start.4 = (bf16[64,6144]{1,0:T(8,128)(2,1)}, bf16[64,6144]{1,0:T(8,128)(2,1)}, u32[]{:S(2)}, u32[]{:S(2)}) collective-permute-start(bf16[64,6144]{1,0:T(8,128)(2,1)} %collective-permute-done.3.refs_1_), channel_id=1, source_target_pairs={{0,8},{1,25},{2,10},{3,27},{4,12},{5,29},{6,14},{7,31},{8,16},{9,1... | collective-permute-start | bytes 2359304 | tf_op jit(solution)/shard_map/ppermute | solution.py:53
  128.9 0.9 copy-start.21
  155.8 13.0 %collective-permute-start.22 = (bf16[256,1536]{1,0:T(8,128)(2,1)}, bf16[256,1536]{1,0:T(8,128)(2,1)}, u32[]{:S(2)}, u32[]{:S(2)}) collective-permute-start(bf16[256,1536]{1,0:T(8,128)(2,1)} %get-tuple-element.57.refs_0_), channel_id=1, source_target_pairs={{0,2},{1,7},{2,4},{3,1},{4,6},{5,3},{6,0},{7,5},{8,10},{9,15},{10,... | collective-permute-start | bytes 2359304 | tf_op jit(solution)/shard_map/ppermute | solution.py:53
  156.8 27.3 %collective-permute-start.12 = (bf16[256,1536]{1,0:T(8,128)(2,1)}, bf16[256,1536]{1,0:T(8,128)(2,1)S(1)}, u32[]{:S(2)}, u32[]{:S(2)}) collective-permute-start(bf16[256,1536]{1,0:T(8,128)(2,1)} %get-tuple-element.43.refs_0_), channel_id=1, source_target_pairs={{0,2},{1,7},{2,4},{3,1},{4,6},{5,3},{6,0},{7,5},{8,10},{9,15},{10,... | collective-permute-start | bytes 2359304 | tf_op jit(solution)/shard_map/ppermute | solution.py:53
  157.0 28.9 %collective-permute-start.24 = (bf16[256,1536]{1,0:T(8,128)(2,1)}, bf16[256,1536]{1,0:T(8,128)(2,1)}, u32[]{:S(2)}, u32[]{:S(2)}) collective-permute-start(bf16[256,1536]{1,0:T(8,128)(2,1)} %get-tuple-element.57.refs_0_), channel_id=1, source_target_pairs={{0,6},{1,3},{2,0},{3,5},{4,2},{5,7},{6,4},{7,1},{8,14},{9,11},{10,... | collective-permute-start | bytes 2359304 | tf_op jit(solution)/shard_map/ppermute | solution.py:53
  168.9 29.7 %collective-permute-start.23 = (bf16[256,1536]{1,0:T(8,128)(2,1)}, bf16[256,1536]{1,0:T(8,128)(2,1)S(1)}, u32[]{:S(2)}, u32[]{:S(2)}) collective-permute-start(bf16[256,1536]{1,0:T(8,128)(2,1)} %collective-permute-done.22.refs_1_), channel_id=1, source_target_pairs={{0,2},{1,7},{2,4},{3,1},{4,6},{5,3},{6,0},{7,5},{8,10},{9,15},{10,... | collective-permute-start | bytes 2359304 | tf_op jit(solution)/shard_map/ppermute | solution.py:53
  169.1 37.9 %collective-permute-start.15 = (bf16[256,1536]{1,0:T(8,128)(2,1)}, bf16[256,1536]{1,0:T(8,128)(2,1)}, u32[]{:S(2)}, u32[]{:S(2)}) collective-permute-start(bf16[256,1536]{1,0:T(8,128)(2,1)} %get-tuple-element.43.refs_0_), channel_id=1, source_target_pairs={{0,6},{1,3},{2,0},{3,5},{4,2},{5,7},{6,4},{7,1},{8,14},{9,11},{10,... | collective-permute-start | bytes 2359304 | tf_op jit(solution)/shard_map/ppermute | solution.py:53
  184.1 11.5 %copy-start.20 = (bf16[256,1536]{1,0:T(8,128)(2,1)}, bf16[256,1536]{1,0:T(8,128)(2,1)S(1)}, u32[]{:S(2)}) copy-start(bf16[256,1536]{1,0:T(8,128)(2,1)S(1)} %collective-permute-done.12.refs_1_) | copy-start | bytes 2359300
  184.1 32.7 %collective-permute-start.13 = (bf16[256,1536]{1,0:T(8,128)(2,1)S(1)}, bf16[256,1536]{1,0:T(8,128)(2,1)S(1)}, u32[]{:S(2)}, u32[]{:S(2)}) collective-permute-start(bf16[256,1536]{1,0:T(8,128)(2,1)S(1)} %collective-permute-done.12.refs_1_), channel_id=1, source_target_pairs={{0,2},{1,7},{2,4},{3,1},{4,6},{5,3},{6,0},{7,5},{8,10},{9,15},{10,... | collective-permute-start | bytes 2359304 | tf_op jit(solution)/shard_map/ppermute | solution.py:53
  198.6 0.9 copy-start.7
  206.9 21.2 %collective-permute-start.26 = (bf16[256,1536]{1,0:T(8,128)(2,1)}, bf16[256,1536]{1,0:T(8,128)(2,1)S(1)}, u32[]{:S(2)}, u32[]{:S(2)}) collective-permute-start(bf16[256,1536]{1,0:T(8,128)(2,1)} %get-tuple-element.65), channel_id=1, source_target_pairs={{0,96},{1,33},{2,98},{3,35},{4,100},{5,37},{6,102},{7,39},{8,104},... | collective-permute-start | bytes 2359304 | tf_op jit(solution)/shard_map/ppermute | solution.py:53
  216.8 0.9 copy-start.6
  217.7 7.7 %copy-start.9 = (bf16[256,1536]{1,0:T(8,128)(2,1)S(1)}, bf16[256,1536]{1,0:T(8,128)(2,1)}, u32[]{:S(2)}) copy-start(bf16[256,1536]{1,0:T(8,128)(2,1)} %get-tuple-element.63) | copy-start | bytes 2359300
  217.7 10.4 %copy-start.3 = (bf16[256,1536]{1,0:T(8,128)(2,1)S(1)}, bf16[256,1536]{1,0:T(8,128)(2,1)}, u32[]{:S(2)}) copy-start(bf16[256,1536]{1,0:T(8,128)(2,1)} %get-tuple-element.64.a) | copy-start | bytes 2359300
  225.3 3.1 %copy-start.8 = (bf16[256,1536]{1,0:T(8,128)(2,1)S(1)}, bf16[256,1536]{1,0:T(8,128)(2,1)}, u32[]{:S(2)}) copy-start(bf16[256,1536]{1,0:T(8,128)(2,1)} %get-tuple-element.49) | copy-start | bytes 2359300
  225.3 12.6 %copy-start.1 = (bf16[256,1536]{1,0:T(8,128)(2,1)S(1)}, bf16[256,1536]{1,0:T(8,128)(2,1)}, u32[]{:S(2)}) copy-start(bf16[256,1536]{1,0:T(8,128)(2,1)} %get-tuple-element.50.a) | copy-start | bytes 2359300
  225.3 12.6 %collective-permute-start.17 = (bf16[256,1536]{1,0:T(8,128)(2,1)}, bf16[256,1536]{1,0:T(8,128)(2,1)S(1)}, u32[]{:S(2)}, u32[]{:S(2)}) collective-permute-start(bf16[256,1536]{1,0:T(8,128)(2,1)} %get-tuple-element.51), channel_id=1, source_target_pairs={{0,24},{1,9},{2,26},{3,11},{4,28},{5,13},{6,30},{7,15},{8,0},{9,17... | collective-permute-start | bytes 2359304 | tf_op jit(solution)/shard_map/ppermute | solution.py:53
  225.4 12.8 %collective-permute-start.25 = (bf16[256,1536]{1,0:T(8,128)(2,1)S(1)}, bf16[256,1536]{1,0:T(8,128)(2,1)S(1)}, u32[]{:S(2)}, u32[]{:S(2)}) collective-permute-start(bf16[256,1536]{1,0:T(8,128)(2,1)S(1)} %copy-done.9), channel_id=1, source_target_pairs={{0,32},{1,97},{2,34},{3,99},{4,36},{5,101},{6,38},{7,103},{8,40},{... | collective-permute-start | bytes 2359304 | tf_op jit(solution)/shard_map/ppermute | solution.py:53
  228.3 15.3 %copy-start.2 = (bf16[256,1536]{1,0:T(8,128)(2,1)S(1)}, bf16[256,1536]{1,0:T(8,128)(2,1)}, u32[]{:S(2)}) copy-start(bf16[256,1536]{1,0:T(8,128)(2,1)} %get-tuple-element.62.a) | copy-start | bytes 2359300
  228.3 15.3 %collective-permute-start.27 = (bf16[256,1536]{1,0:T(8,128)(2,1)S(1)}, bf16[256,1536]{1,0:T(8,128)(2,1)S(1)}, u32[]{:S(2)}, u32[]{:S(2)}) collective-permute-start(bf16[256,1536]{1,0:T(8,128)(2,1)S(1)} %shard_map.137), channel_id=1, source_target_pairs={{0,96},{1,33},{2,98},{3,35},{4,100},{5,37},{6,102},{7,39},{8,104},... | collective-permute-start | bytes 2359304 | tf_op jit(solution)/shard_map/ppermute | solution.py:53
  228.4 19.3 %collective-permute-start.16 = (bf16[256,1536]{1,0:T(8,128)(2,1)S(1)}, bf16[256,1536]{1,0:T(8,128)(2,1)S(1)}, u32[]{:S(2)}, u32[]{:S(2)}) collective-permute-start(bf16[256,1536]{1,0:T(8,128)(2,1)S(1)} %copy-done.8), channel_id=1, source_target_pairs={{0,8},{1,25},{2,10},{3,27},{4,12},{5,29},{6,14},{7,31},{8,16},{9,1... | collective-permute-start | bytes 2359304 | tf_op jit(solution)/shard_map/ppermute | solution.py:53
  238.2 19.8 %copy-start = (bf16[256,1536]{1,0:T(8,128)(2,1)S(1)}, bf16[256,1536]{1,0:T(8,128)(2,1)}, u32[]{:S(2)}) copy-start(bf16[256,1536]{1,0:T(8,128)(2,1)} %get-tuple-element.48.a) | copy-start | bytes 2359300
  238.2 19.8 %collective-permute-start.18 = (bf16[256,1536]{1,0:T(8,128)(2,1)S(1)}, bf16[256,1536]{1,0:T(8,128)(2,1)S(1)}, u32[]{:S(2)}, u32[]{:S(2)}) collective-permute-start(bf16[256,1536]{1,0:T(8,128)(2,1)S(1)} %shard_map.132), channel_id=1, source_target_pairs={{0,24},{1,9},{2,26},{3,11},{4,28},{5,13},{6,30},{7,15},{8,0},{9,17... | collective-permute-start | bytes 2359304 | tf_op jit(solution)/shard_map/ppermute | solution.py:53
  243.9 15.8 %copy-start.18 = (f32[768]{0:T(1024)S(1)}, f32[768]{0:T(1024)}, u32[]{:S(2)}) copy-start(f32[768]{0:T(1024)} %param.20) | copy-start | bytes 9220
  244.0 15.8 %collective-permute-start.28 = (bf16[64,1536]{1,0:T(8,128)(2,1)S(1)}, bf16[64,1536]{1,0:T(8,128)(2,1)S(1)}, u32[]{:S(2)}, u32[]{:S(2)}) collective-permute-start(bf16[64,1536]{1,0:T(8,128)(2,1)S(1)} %get-tuple-element.67), channel_id=1, source_target_pairs={{0,24},{1,25},{2,26},{3,27},{4,28},{5,29},{6,30},{7,31},{8,0},{9,1... | collective-permute-start | bytes 589832 | tf_op jit(solution)/shard_map/ppermute | solution.py:53
  246.4 19.6 %collective-permute-start.29 = (bf16[64,1536]{1,0:T(8,128)(2,1)S(1)}, bf16[64,1536]{1,0:T(8,128)(2,1)S(1)}, u32[]{:S(2)}, u32[]{:S(2)}) collective-permute-start(bf16[64,1536]{1,0:T(8,128)(2,1)S(1)} %get-tuple-element.68), channel_id=1, source_target_pairs={{0,8},{1,9},{2,10},{3,11},{4,12},{5,13},{6,14},{7,15},{8,16},{9,17... | collective-permute-start | bytes 589832 | tf_op jit(solution)/shard_map/ppermute | solution.py:53
  246.4 19.6 %collective-permute-start.30 = (bf16[64,1536]{1,0:T(8,128)(2,1)S(1)}, bf16[64,1536]{1,0:T(8,128)(2,1)S(1)}, u32[]{:S(2)}, u32[]{:S(2)}) collective-permute-start(bf16[64,1536]{1,0:T(8,128)(2,1)S(1)} %get-tuple-element.69), channel_id=1, source_target_pairs={{0,16},{1,17},{2,18},{3,19},{4,20},{5,21},{6,22},{7,23},{8,24},{9,... | collective-permute-start | bytes 589832 | tf_op jit(solution)/shard_map/ppermute | solution.py:53
  258.2 12.5 %collective-permute-start.19 = (bf16[64,1536]{1,0:T(8,128)(2,1)S(1)}, bf16[64,1536]{1,0:T(8,128)(2,1)S(1)}, u32[]{:S(2)}, u32[]{:S(2)}) collective-permute-start(bf16[64,1536]{1,0:T(8,128)(2,1)S(1)} %get-tuple-element.53), channel_id=1, source_target_pairs={{0,96},{1,97},{2,98},{3,99},{4,100},{5,101},{6,102},{7,103},{8,104... | collective-permute-start | bytes 589832 | tf_op jit(solution)/shard_map/ppermute | solution.py:53
  258.3 12.4 %collective-permute-start.20 = (bf16[64,1536]{1,0:T(8,128)(2,1)S(1)}, bf16[64,1536]{1,0:T(8,128)(2,1)S(1)}, u32[]{:S(2)}, u32[]{:S(2)}) collective-permute-start(bf16[64,1536]{1,0:T(8,128)(2,1)S(1)} %get-tuple-element.54), channel_id=1, source_target_pairs={{0,32},{1,33},{2,34},{3,35},{4,36},{5,37},{6,38},{7,39},{8,40},{9,... | collective-permute-start | bytes 589832 | tf_op jit(solution)/shard_map/ppermute | solution.py:53
  259.8 10.9 %collective-permute-start.21 = (bf16[64,1536]{1,0:T(8,128)(2,1)S(1)}, bf16[64,1536]{1,0:T(8,128)(2,1)S(1)}, u32[]{:S(2)}, u32[]{:S(2)}) collective-permute-start(bf16[64,1536]{1,0:T(8,128)(2,1)S(1)} %get-tuple-element.55), channel_id=1, source_target_pairs={{0,64},{1,65},{2,66},{3,67},{4,68},{5,69},{6,70},{7,71},{8,72},{9,... | collective-permute-start | bytes 589832 | tf_op jit(solution)/shard_map/ppermute | solution.py:53
  266.1 11.0 %collective-permute-start.32 = (bf16[64,768]{1,0:T(8,128)(2,1)S(1)}, bf16[64,768]{1,0:T(8,128)(2,1)S(1)}, u32[]{:S(2)}, u32[]{:S(2)}) collective-permute-start(bf16[64,768]{1,0:T(8,128)(2,1)S(1)} %get-tuple-element.72), channel_id=1, source_target_pairs={{0,1},{1,0},{2,3},{3,2},{4,5},{5,4},{6,7},{7,6},{8,9},{9,8},{10,11... | collective-permute-start | bytes 294920 | tf_op jit(solution)/shard_map/ppermute | solution.py:62
  270.8 6.5 %collective-permute-start.31 = (bf16[64,768]{1,0:T(8,128)(2,1)S(1)}, bf16[64,768]{1,0:T(8,128)(2,1)S(1)}, u32[]{:S(2)}, u32[]{:S(2)}) collective-permute-start(bf16[64,768]{1,0:T(8,128)(2,1)S(1)} %get-tuple-element.71), channel_id=1, source_target_pairs={{0,1},{1,0},{2,3},{3,2},{4,5},{5,4},{6,7},{7,6},{8,9},{9,8},{10,11... | collective-permute-start | bytes 294920 | tf_op jit(solution)/shard_map/ppermute | solution.py:62
Sparse Core Ops, SparseCore 0:
  9.0 103.6 all-gather.1

commit v8 on v5

--- a/solution.py
+++ b/solution.py
@@ -66,24 +66,23 @@
     return pltpu.CompilerParams(vmem_limit_bytes=mb * MB)
 
 
-def act_kernel(moved_ref, first_ref, second_ref):
+def act_kernel(moved_ref, gain_ref, first_ref, second_ref):
     cols, _, chans = moved_ref.shape
     half = first_ref.shape[0]
-    values = moved_ref[:, : 2 * half, :].astype(F32)
-    gains = jnp.sum(moved_ref[:, 2 * half :, :].astype(F32)[:, :3], axis=1)
+    values = moved_ref[...].astype(F32)
     mean = jnp.sum(jnp.sum(values, axis=0), axis=-1, keepdims=True) / (cols * chans)
     square = jnp.sum(jnp.sum(values * values, axis=0), axis=-1, keepdims=True) / (cols * chans)
     scale = 1.0 / jnp.sqrt(square - mean * mean + 1e-05)
     for j in range(cols):
-        part = ((values[j] - mean) * scale * gains[j][None, :]).astype(BF)
+        part = ((values[j] - mean) * scale * gain_ref[j : j + 1, :]).astype(BF)
         first_ref[:, j * chans : (j + 1) * chans] = part[:half]
         second_ref[:, j * chans : (j + 1) * chans] = part[half:]
 
 
-def normalize(moved, half):
+def normalize(moved, gains, half):
     cols, _, chans = moved.shape
     shape = jax.ShapeDtypeStruct((half, cols * chans), BF)
-    return pl.pallas_call(act_kernel, out_shape=(shape, shape), compiler_params=params(16))(moved)
+    return pl.pallas_call(act_kernel, out_shape=(shape, shape), compiler_params=params(16))(moved, gains)
 
 
 def mm1_kernel(*refs):
@@ -117,36 +116,59 @@
     )(*pieces, w, b[None])
 
 
+def fill(sources, target, sems):
+    rows = target.shape[0] // len(sources)
+    copies = [
+        pltpu.make_async_copy(source, target.at[pl.ds(i * rows, rows)], sems.at[i])
+        for i, source in enumerate(sources)
+    ]
+
+    @pl.when(pl.program_id(0) == 0)
+    def _():
+        for copy in copies:
+            copy.start()
+        for copy in copies:
+            copy.wait()
+
+
 def mm2_kernel(*refs):
-    hiddens, (own_ref, other_ref), outs = refs[:SIDE], refs[SIDE : SIDE + 2], refs[SIDE + 2 :]
-    rows, width = outs[0].shape
-    chans = own_ref.shape[1]
-    for i, h_ref in enumerate(hiddens):
-
-        @pl.when(pl.program_id(0) == i)
-        def _(h_ref=h_ref):
-            for at, w_ref in ((0, own_ref), (chans, other_ref)):
-                out = jnp.dot(h_ref[...], w_ref[...], preferred_element_type=F32)
-                for p, o_ref in enumerate(outs):
-                    o_ref[:, at : at + chans] = out[p * rows : (p + 1) * rows].astype(BF)
+    hiddens, (own_ref, other_ref) = refs[:SIDE], refs[SIDE : SIDE + 2]
+    outs, (left, sems) = refs[SIDE + 2 : -2], refs[-2:]
+    fill(hiddens, left, sems)
+    steps = pl.num_programs(0) // 2
+    rows = outs[0].shape[0] // SIDE
+
+    def part(w_ref):
+        out = jnp.dot(left[...], w_ref[...], preferred_element_type=F32).astype(BF)
+        for x in range(SIDE):
+            for p, o_ref in enumerate(outs):
+                at = (x * len(outs) + p) * rows
+                o_ref[x * rows : (x + 1) * rows, :] = out[at : at + rows]
+
+    pl.when(pl.program_id(0) < steps)(lambda: part(own_ref))
+    pl.when(pl.program_id(0) >= steps)(lambda: part(other_ref))
 
 
 def matmul_out(hiddens, own, other, count):
     depth, chans = own.shape
-    tokens = hiddens[0].shape[0]
-    rows = tokens // count
-    steps = len(hiddens)
-    whole = pl.BlockSpec((depth, chans), lambda i: (0, 0))
+    tokens = SIDE * hiddens[0].shape[0]
+    tile = 256
+    steps = chans // tile
     return pl.pallas_call(
         mm2_kernel,
-        grid=(steps,),
-        in_specs=[pl.BlockSpec((tokens, depth), lambda i: (0, 0))] * steps + [whole] * 2,
-        out_specs=[pl.BlockSpec((rows, 2 * chans), lambda i: (i, 0))] * count,
-        out_shape=[jax.ShapeDtypeStruct((steps * rows, 2 * chans), BF)] * count,
-        compiler_params=params(58),
+        grid=(2 * steps,),
+        in_specs=[pl.BlockSpec(memory_space=pl.ANY)] * SIDE
+        + [
+            pl.BlockSpec((depth, tile), lambda i: (0, jnp.minimum(i, steps - 1))),
+            pl.BlockSpec((depth, tile), lambda i: (0, jnp.maximum(i - steps, 0))),
+        ],
+        out_specs=[pl.BlockSpec((tokens // count, tile), lambda i: (0, i))] * count,
+        out_shape=[jax.ShapeDtypeStruct((tokens // count, 2 * chans), BF)] * count,
+        scratch_shapes=[pltpu.VMEM((tokens, depth), BF), pltpu.SemaphoreType.DMA((SIDE,))],
+        compiler_params=params(32),
         cost_estimate=pl.CostEstimate(
-            flops=4 * steps * tokens * depth * chans,
-            bytes_accessed=2 * (steps * tokens * depth + 2 * depth * chans + 2 * steps * tokens * chans),
+            flops=4 * tokens * depth * chans,
+            bytes_accessed=2 * (tokens * depth + 2 * depth * chans + 2 * tokens * chans),
             transcendentals=0,
         ),
     )(*hiddens, own, other)
@@ -248,7 +270,7 @@
     )(*values, *others)
 
 
-def spectral(image, filter_bank, gain_first):
+def spectral(image, filter_bank, gain_first, early):
     rows_here, width, chans = image.shape
     groups = lax.axis_size("row")
     width_all = chans * lax.axis_size("col")
@@ -264,6 +286,7 @@
     normed = (source - mean) / jnp.sqrt(square - mean * mean + 1e-05) * gain_first
     col = jnp.dot(one, normed, precision=high).astype(BF)
     col = exchange(col.reshape(groups, -1, chans), "row").reshape(-1, chans)
+    (col,) = tie([col], early)
     spec = jnp.dot(two, col.astype(F32), precision=high)
     split = spec.shape[0] // 2
     spec_re, spec_im = spec[:split], spec[split:]
@@ -274,12 +297,6 @@
     back = jnp.dot(three, filt, precision=high).astype(BF)
     back = exchange(back.reshape(groups, -1, chans), "row").reshape(-1, chans)
     return source + jnp.dot(four, back.astype(F32), precision=high)
-
-
-def three_parts(gain):
-    top = lax.reduce_precision(gain, 8, 7)
-    mid = lax.reduce_precision(gain - top, 8, 7)
-    return jnp.stack([top, mid, gain - top - mid]).astype(BF)
 
 
 def block_places():
@@ -305,6 +322,20 @@
     return [a, one, two, hop(one, axis, APART)]
 
 
+def gather_gains(gain):
+    pair = jnp.stack([gain, swap_cores(gain)])
+    rows = jnp.concatenate(gather_far(pair, "x"))
+    table = []
+    for x in range(SIDE):
+        for core in range(2):
+            steps = (0, APART[core], OTHER[core], 2)
+            table.append([(x - s) % SIDE * 2 + (core ^ k) for s in steps for k in range(2)])
+    places = jnp.asarray(np.array(table, np.int32))[lax.axis_index("col")]
+    count = rows.shape[0]
+    mine = lax.broadcasted_iota(jnp.int32, (count, count), 0) == places[None, :]
+    return jnp.sum(jnp.where(mine[:, :, None], rows[None], 0.0), axis=1)
+
+
 def reduce_far(outs, large, small, half):
     own, fore, back, far = outs
     far = hop(far, large, OTHER)
@@ -322,20 +353,13 @@
     rows_here, width, chans = image.shape
     cols = lax.axis_size("col")
     w_in_all = lax.all_gather(w_in, "col", axis=0, tiled=True)
-    resid = spectral(image, filter_bank, gain_first)
+    gains = gather_gains(gain_second)
+    resid = spectral(image, filter_bank, gain_first, [gains])
     tokens = rows_here * width
     own = tokens // cols
     half = own // 2
-    extra = jnp.pad(three_parts(gain_second), ((0, half - 3), (0, 0)))
-    message = jnp.concatenate(
-        [
-            resid.astype(BF).reshape(cols, own, chans),
-            jnp.broadcast_to(extra[None], (cols, half, chans)),
-        ],
-        axis=1,
-    )
-    moved = exchange(message, "col")
-    first, second = normalize(moved, half)
+    moved = exchange(resid.astype(BF).reshape(cols, own, chans), "col")
+    first, second = normalize(moved, gains, half)
     first, second = gather_near(first, "z"), gather_near(second, "y")
     parts = [gather_far(first, "y"), gather_far(second, "z")]
     hiddens = [gather_far(matmul_in(part, w_in_all, b_in), "x") for part in parts]

time: 277 us -> 266 us (0.960)
  waiting for transfers between devices: 95.6 us -> 66.8 us
  starting transfers between devices: 62.2 us -> 71.6 us
  blocking collectives: 42.6 us -> 50 us
  local copies, waits for them, and re-layouts: 5.84 us -> 11.1 us
  Pallas kernels: 46.6 us -> 42.5 us
    all_to_all x2 -> x1, waiting for transfers between devices: 20 us -> 0.01 us  [exchange(): return lax.all_to_all(a, axis, split_axis=0, concat_axis=0, tiled=True)]
    ppermute x30 -> x33, waiting for transfers between devices: 74.6 us -> 65.8 us  [hop(): return lax.ppermute(a, ('row', 'col'), pairs)]
    all_to_all x1 -> x2, blocking collectives: 29.4 us -> 38 us  [exchange(): return lax.all_to_all(a, axis, split_axis=0, concat_axis=0, tiled=True)]
    ppermute x30 -> x33, starting transfers between devices: 36.8 us -> 44.2 us  [hop(): return lax.ppermute(a, ('row', 'col'), pairs)]
    ppermute x3 -> x4, starting transfers between devices: 13.8 us -> 19.5 us  [swap_cores(): return lax.ppermute(a, 'col', pairs)]
    pallas_call x2 -> x3, Pallas kernels: 19.9 us -> 15.8 us  [the longest x2 15.8 us: matmul_out(): pl.pallas_call(mm2_kernel, grid=(2 * steps,), in_specs=[pl.BlockSpec(memo...]
    all_to_all x2 -> x1, starting transfers between devices: 11.6 us -> 7.85 us  [exchange(): return lax.all_to_all(a, axis, split_axis=0, concat_axis=0, tiled=True)]
  transfers between devices with their start and end apart: 36 -> 39, of which waited for: 19 -> 17; matrix products, arithmetic and copies ran while one was open for 4% -> 6% of each run, Pallas kernels for 16% -> 16%
where the time goes in v8:
time: 266 us; the launch traced here: 265 us
  starting transfers between devices  71.6 us (27%)
  waiting for transfers between devices  66.8 us (25%)
  blocking collectives  50 us (19%)
  Pallas kernels  42.5 us (16%)
  between operations  13.7 us (5%)
  local copies, waits for them, and re-layouts  11.1 us (4%)
  matrix products  6.72 us (3%)
    ppermute x33, waiting for transfers between devices, hop(): return lax.ppermute(a, ('row', 'col'), pairs)  65.8 us
    ppermute x33, starting transfers between devices, hop(): return lax.ppermute(a, ('row', 'col'), pairs)  44.2 us
    all_to_all x2, blocking collectives, exchange(): return lax.all_to_all(a, axis, split_axis=0, concat_axis=0, tiled=True)  38 us
    pallas_call x2, Pallas kernels, matmul_in(): pl.pallas_call(mm1_kernel, grid=(width // tile,), in_specs=[pl.BlockSpec(...  23.8 us
    ppermute x4, starting transfers between devices, swap_cores(): return lax.ppermute(a, 'col', pairs)  19.5 us
    pallas_call x2, Pallas kernels, matmul_out(): pl.pallas_call(mm2_kernel, grid=(2 * steps,), in_specs=[pl.BlockSpec(memo...  15.8 us
    psum x1, blocking collectives, spectral(): lax.psum((jnp.sum(source, axis=-1), jnp.sum(source * source, axis=-1)), '...  12 us
    all_to_all x1, starting transfers between devices, exchange(): return lax.all_to_all(a, axis, split_axis=0, concat_axis=0, tiled=True)  7.85 us
  transfers between devices with their start and end apart: 39, of which 17 were waited for; matrix products, arithmetic and copies ran while one was open for 6% of the time, Pallas kernels for 16%

profile of v8, /device:TPU:1, one launch (start us, length us, event | category | flops | bytes accessed | tf_op | source)
XLA Modules:
  0.0 264.7 jit_solution(964126658970165566)
XLA Ops:
  6.6 0.7 all-gather.2.cloned.1.call-update
  7.3 1.5 collective-permute-start
  9.1 12.0 %all-reduce = (f32[256]{0:T(256)S(1)}, f32[256]{0:T(256)S(1)}) all-reduce(f32[256]{0:T(256)S(1)} %reduce_sum.34, f32[256]{0:T(256)S(1)} %reduce_sum.32), channel_id=1, replica_groups=mesh['row'=16,'col'=8] {'col'}, use_global_device_ids=true, to_apply=%region_3.4 | all-reduce | flops 512 | bytes 4096 | tf_op jit(solution)/shard_map/psum | solution.py:281
  21.4 1.7 convolution_convert_fusion
  23.0 7.8 %all-to-all-start = ((bf16[16,32,768]{2,1,0:T(8,128)(2,1)}), bf16[16,32,768]{2,1,0:T(8,128)(2,1)S(1)}, u32[]{:S(2)}, u32[]{:S(2)}) async-start(bf16[16,32,768]{2,1,0:T(8,128)(2,1)} %bitcast.3), calls=%async_computation | async-start | bytes 1572864 | tf_op jit(solution)/shard_map/all_to_all | solution.py:253
  30.9 2.4 fusion.13
  33.3 2.4 collective-permute-start.1
  35.7 0.7 dynamic-slice_bitcast_fusion
  36.5 3.4 %collective-permute-start.3 = (f32[2,768]{1,0:T(2,128)S(1)}, f32[2,768]{1,0:T(2,128)S(1)}, u32[]{:S(2)}, u32[]{:S(2)}) collective-permute-start(f32[2,768]{1,0:T(2,128)S(1)} %collective-permute-done.1), channel_id=1, source_target_pairs={{0,2},{1,7},{2,4},{3,1},{4,6},{5,3},{6,0},{7,5},{8,10},{9,15},{10,... | collective-permute-start | bytes 18440 | tf_op jit(solution)/shard_map/ppermute | solution.py:53
  39.9 1.4 reshape_squeeze.6
  41.3 1.2 reshape_squeeze.7
  42.5 0.7 select_reduce_fusion.refs_1_.gain_ref
  43.2 0.9 copy-done.6
  44.1 2.6 fusion.15
  46.7 0.9 fusion.5
  47.7 1.0 add_convert_fusion
  48.7 17.1 %all_to_all.15 = bf16[16,32,768]{2,1,0:T(8,128)(2,1)S(1)} all-to-all(bf16[16,32,768]{2,1,0:T(8,128)(2,1)S(1)} %bitcast.48), channel_id=1, replica_groups=mesh['row'=16,'col'=8] {'row'}, dimensions={0} | all-to-all | bytes 1572864 | tf_op jit(solution)/shard_map/all_to_all | solution.py:253
  66.4 20.9 %all_to_all.16.moved_ref = bf16[8,32,768]{2,1,0:T(8,128)(2,1)S(1)} all-to-all(bf16[8,32,768]{2,1,0:T(8,128)(2,1)S(1)} %bitcast.50), channel_id=1, replica_groups=mesh['row'=16,'col'=8] {'col'}, dimensions={0} | all-to-all | bytes 786432 | tf_op jit(solution)/shard_map/all_to_all | solution.py:253
  87.6 0.7 collective-permute-start.22
  88.3 2.0 collective-permute-start.21
  90.9 1.6 collective-permute-start.5
  92.5 1.9 collective-permute-done.22
  94.4 2.4 collective-permute-done.21
  96.8 2.5 collective-permute-done.20
  99.5 0.6 collective-permute-start.23
  100.1 1.5 collective-permute-done.4
  101.6 1.0 pad_maximum_fusion
  102.6 1.7 collective-permute-start.7
  104.3 1.2 collective-permute-start.24
  105.5 6.0 %collective-permute-done.23.refs_1_ = bf16[64,6144]{1,0:T(8,128)(2,1)S(1)} collective-permute-done((bf16[64,6144]{1,0:T(8,128)(2,1)S(1)}, bf16[64,6144]{1,0:T(8,128)(2,1)S(1)}, u32[]{:S(2)}, u32[]{:S(2)}) %collective-permute-start.23) | collective-permute-done | bytes 786464 | tf_op jit(solution)/shard_map/ppermute | solution.py:53
  111.5 2.6 collective-permute-start.25
  114.1 5.7 %collective-permute-start.13 = (bf16[1536,768]{1,0:T(8,128)(2,1)S(1)}, bf16[1536,768]{1,0:T(8,128)(2,1)}, u32[]{:S(2)}, u32[]{:S(2)}) collective-permute-start(bf16[1536,768]{1,0:T(8,128)(2,1)S(1)} %copy-done.3), channel_id=1, source_target_pairs={{0,1},{1,0},{2,3},{3,2},{4,5},{5,4},{6,7},{7,6},{8,9},{9,8},{10,11... | collective-permute-start | bytes 7077896 | tf_op jit(solution)/shard_map/ppermute | solution.py:62
  119.9 2.7 %collective-permute-start.9 = (bf16[64,6144]{1,0:T(8,128)(2,1)}, bf16[64,6144]{1,0:T(8,128)(2,1)}, u32[]{:S(2)}, u32[]{:S(2)}) collective-permute-start(bf16[64,6144]{1,0:T(8,128)(2,1)} %collective-permute-done.7.refs_1_), channel_id=1, source_target_pairs={{0,8},{1,25},{2,10},{3,27},{4,12},{5,29},{6,14},{7,31},{8,16},{9,1... | collective-permute-start | bytes 2359304 | tf_op jit(solution)/shard_map/ppermute | solution.py:53
  123.2 0.9 copy-done.11
  124.0 3.6 %collective-permute-done.25.refs_3_ = bf16[64,6144]{1,0:T(8,128)(2,1)} collective-permute-done((bf16[64,6144]{1,0:T(8,128)(2,1)S(1)}, bf16[64,6144]{1,0:T(8,128)(2,1)}, u32[]{:S(2)}, u32[]{:S(2)}) %collective-permute-start.25) | collective-permute-done | bytes 786464 | tf_op jit(solution)/shard_map/ppermute | solution.py:53
  127.6 11.8 %shard_map.143.refs_0_ = bf16[256,1536]{1,0:T(8,128)(2,1)} custom-call(bf16[64,6144]{1,0:T(8,128)(2,1)} %bitcast.47, bf16[64,6144]{1,0:T(8,128)(2,1)} %copy-done.10, bf16[64,6144]{1,0:T(8,128)(2,1)} %copy-done.11, bf16[64,6144]{1,0:T(8,128)(2,1)} %collective-permute-done.25.refs_3_, bf16[6144,1536]{1,0:T(8,128)(2,1)} %all-gather.2.cloned.1.call-done.refs_4_, ...), custom_call_target="tpu_custom_call" | custom-call | flops 4831838208 | bytes 22020096 | tf_op jit(solution)/shard_map/pallas_call | solution.py:100
  139.5 0.9 collective-permute-start.26
  140.4 12.0 %shard_map.138.refs_0_ = bf16[256,1536]{1,0:T(8,128)(2,1)} custom-call(bf16[64,6144]{1,0:T(8,128)(2,1)} %bitcast.14.refs_0_, bf16[64,6144]{1,0:T(8,128)(2,1)} %collective-permute-done.7.refs_1_, bf16[64,6144]{1,0:T(8,128)(2,1)} %collective-permute-done.8.refs_2_, bf16[64,6144]{1,0:T(8,128)(2,1)} %collective-permute-done.9.refs_3_, ...), custom_call_target="tpu_custom_call" | custom-call | flops 4831838208 | bytes 22020096 | tf_op jit(solution)/shard_map/pallas_call | solution.py:100
  152.7 1.1 collective-permute-start.27
  153.8 1.6 collective-permute-start.28
  155.4 0.9 copy-done.4
  156.3 10.3 %collective-permute-done.10.refs_1_ = bf16[256,1536]{1,0:T(8,128)(2,1)S(1)} collective-permute-done((bf16[256,1536]{1,0:T(8,128)(2,1)}, bf16[256,1536]{1,0:T(8,128)(2,1)S(1)}, u32[]{:S(2)}, u32[]{:S(2)}) %collective-permute-start.10) | collective-permute-done | bytes 786464 | tf_op jit(solution)/shard_map/ppermute | solution.py:53
  166.7 3.7 %collective-permute-done.27.refs_2_ = bf16[256,1536]{1,0:T(8,128)(2,1)S(1)} collective-permute-done((bf16[256,1536]{1,0:T(8,128)(2,1)S(1)}, bf16[256,1536]{1,0:T(8,128)(2,1)S(1)}, u32[]{:S(2)}, u32[]{:S(2)}) %collective-permute-start.27) | collective-permute-done | bytes 786464 | tf_op jit(solution)/shard_map/ppermute | solution.py:53
  170.3 13.2 %collective-permute-done.28.refs_3_ = bf16[256,1536]{1,0:T(8,128)(2,1)S(1)} collective-permute-done((bf16[256,1536]{1,0:T(8,128)(2,1)S(1)}, bf16[256,1536]{1,0:T(8,128)(2,1)S(1)}, u32[]{:S(2)}, u32[]{:S(2)}) %collective-permute-start.28) | collective-permute-done | bytes 786464 | tf_op jit(solution)/shard_map/ppermute | solution.py:53
  183.5 1.1 copy-done.5
  184.6 7.9 %shard_map.144 = (bf16[256,1536]{1,0:T(8,128)(2,1)S(1)}, bf16[256,1536]{1,0:T(8,128)(2,1)S(1)}, bf16[256,1536]{1,0:T(8,128)(2,1)S(1)}, bf16[256,1536]{1,0:T(8,128)(2,1)S(1)}) custom-call(bf16[256,1536]{1,0:T(8,128)(2,1)S(1)} %copy-done.1, bf16[256,1536]{1,0:T(8,128)(2,1)S(1)} %copy-done.5, bf16[256,1536]{1,0:T(8,128)(2,1)S(1)} %collective-permute-done.27.refs_2_, ...), custom_call_target="tpu_custom_call" | custom-call | flops 4831838208 | bytes 11010048 | tf_op jit(solution)/shard_map/pallas_call | solution.py:157
  192.6 2.5 collective-permute-start.30
  195.1 2.3 collective-permute-done.12.refs_3_
  197.4 7.9 %shard_map.139 = (bf16[256,1536]{1,0:T(8,128)(2,1)S(1)}, bf16[256,1536]{1,0:T(8,128)(2,1)S(1)}, bf16[256,1536]{1,0:T(8,128)(2,1)S(1)}, bf16[256,1536]{1,0:T(8,128)(2,1)S(1)}) custom-call(bf16[256,1536]{1,0:T(8,128)(2,1)S(1)} %copy-done, bf16[256,1536]{1,0:T(8,128)(2,1)S(1)} %collective-permute-done.10.refs_1_, ...), custom_call_target="tpu_custom_call" | custom-call | flops 4831838208 | bytes 11010048 | tf_op jit(solution)/shard_map/pallas_call | solution.py:157
  205.4 2.0 collective-permute-start.29
  207.7 2.7 %collective-permute-start.14 = (bf16[256,1536]{1,0:T(8,128)(2,1)S(1)}, bf16[256,1536]{1,0:T(8,128)(2,1)S(1)}, u32[]{:S(2)}, u32[]{:S(2)}) collective-permute-start(bf16[256,1536]{1,0:T(8,128)(2,1)S(1)} %get-tuple-element.29), channel_id=1, source_target_pairs={{0,8},{1,25},{2,10},{3,27},{4,12},{5,29},{6,14},{7,31},{8,16},{9,1... | collective-permute-start | bytes 2359304 | tf_op jit(solution)/shard_map/ppermute | solution.py:53
  210.4 7.3 %collective-permute-done.15.b = bf16[256,1536]{1,0:T(8,128)(2,1)S(1)} collective-permute-done((bf16[256,1536]{1,0:T(8,128)(2,1)S(1)}, bf16[256,1536]{1,0:T(8,128)(2,1)S(1)}, u32[]{:S(2)}, u32[]{:S(2)}) %collective-permute-start.15) | collective-permute-done | bytes 786464 | tf_op jit(solution)/shard_map/ppermute | solution.py:53
  218.0 3.2 %collective-permute-done.29.b = bf16[256,1536]{1,0:T(8,128)(2,1)S(1)} collective-permute-done((bf16[256,1536]{1,0:T(8,128)(2,1)S(1)}, bf16[256,1536]{1,0:T(8,128)(2,1)S(1)}, u32[]{:S(2)}, u32[]{:S(2)}) %collective-permute-start.29) | collective-permute-done | bytes 786464 | tf_op jit(solution)/shard_map/ppermute | solution.py:53
  221.2 1.5 collective-permute-done.31.c
  223.0 5.1 %collective-permute-start.32 = (bf16[64,1536]{1,0:T(8,128)(2,1)S(1)}, bf16[64,1536]{1,0:T(8,128)(2,1)S(1)}, u32[]{:S(2)}, u32[]{:S(2)}) collective-permute-start(bf16[64,1536]{1,0:T(8,128)(2,1)S(1)} %get-tuple-element.43), channel_id=1, source_target_pairs={{0,24},{1,25},{2,26},{3,27},{4,28},{5,29},{6,30},{7,31},{8,0},{9,1... | collective-permute-start | bytes 589832 | tf_op jit(solution)/shard_map/ppermute | solution.py:53
  228.1 3.0 %collective-permute-start.34 = (bf16[64,1536]{1,0:T(8,128)(2,1)S(1)}, bf16[64,1536]{1,0:T(8,128)(2,1)S(1)}, u32[]{:S(2)}, u32[]{:S(2)}) collective-permute-start(bf16[64,1536]{1,0:T(8,128)(2,1)S(1)} %get-tuple-element.45), channel_id=1, source_target_pairs={{0,16},{1,17},{2,18},{3,19},{4,20},{5,21},{6,22},{7,23},{8,24},{9,... | collective-permute-start | bytes 589832 | tf_op jit(solution)/shard_map/ppermute | solution.py:53
  231.1 5.5 %collective-permute-done.16.c = bf16[256,1536]{1,0:T(8,128)(2,1)S(1)} collective-permute-done((bf16[256,1536]{1,0:T(8,128)(2,1)S(1)}, bf16[256,1536]{1,0:T(8,128)(2,1)S(1)}, u32[]{:S(2)}, u32[]{:S(2)}) %collective-permute-start.16) | collective-permute-done | bytes 786464 | tf_op jit(solution)/shard_map/ppermute | solution.py:53
  237.0 3.5 %collective-permute-start.17 = (bf16[64,1536]{1,0:T(8,128)(2,1)S(1)}, bf16[64,1536]{1,0:T(8,128)(2,1)S(1)}, u32[]{:S(2)}, u32[]{:S(2)}) collective-permute-start(bf16[64,1536]{1,0:T(8,128)(2,1)S(1)} %get-tuple-element.33), channel_id=1, source_target_pairs={{0,96},{1,97},{2,98},{3,99},{4,100},{5,101},{6,102},{7,103},{8,104... | collective-permute-start | bytes 589832 | tf_op jit(solution)/shard_map/ppermute | solution.py:53
  240.4 1.8 collective-permute-start.19
  242.2 0.8 collective-permute-done.33.c
  243.1 6.7 %collective-permute-start.36 = (bf16[64,768]{1,0:T(8,128)(2,1)S(1)}, bf16[64,768]{1,0:T(8,128)(2,1)S(1)}, u32[]{:S(2)}, u32[]{:S(2)}) collective-permute-start(bf16[64,768]{1,0:T(8,128)(2,1)S(1)} %get-tuple-element.48), channel_id=1, source_target_pairs={{0,1},{1,0},{2,3},{3,2},{4,5},{5,4},{6,7},{7,6},{8,9},{9,8},{10,11... | collective-permute-start | bytes 294920 | tf_op jit(solution)/shard_map/ppermute | solution.py:62
  249.9 5.6 %collective-permute-start.35 = (bf16[64,768]{1,0:T(8,128)(2,1)S(1)}, bf16[64,768]{1,0:T(8,128)(2,1)S(1)}, u32[]{:S(2)}, u32[]{:S(2)}) collective-permute-start(bf16[64,768]{1,0:T(8,128)(2,1)S(1)} %get-tuple-element.47), channel_id=1, source_target_pairs={{0,1},{1,0},{2,3},{3,2},{4,5},{5,4},{6,7},{7,6},{8,9},{9,8},{10,11... | collective-permute-start | bytes 294920 | tf_op jit(solution)/shard_map/ppermute | solution.py:62
  255.5 0.7 dynamic-slice_bitcast_fusion.1.place_ref
  256.4 1.4 shard_map.148
  (96 shorter events, 5.2 us)
Async XLA Ops:
  6.5 14.8 %copy-start.15 = (f32[512,256]{1,0:T(8,128)S(1)}, f32[512,256]{1,0:T(8,128)}, u32[]{:S(2)}) copy-start(f32[512,256]{1,0:T(8,128)} %constant.29.clone) | copy-start | bytes 1572868
  6.5 0.7 copy-start.18
  6.5 2.2 copy-start.8
  6.5 14.6 %copy-start.17 = (f32[768]{0:T(1024)S(1)}, f32[768]{0:T(1024)}, u32[]{:S(2)}) copy-start(f32[768]{0:T(1024)} %param.16) | copy-start | bytes 9220
  6.5 121.1 %all-gather.2.cloned.1.call-start = ((), (), s32[]{:S(2)}) async-start(), calls=%async_computation.3 | async-start | bytes 21233664 | tf_op jit(solution)/shard_map/all_gather | solution.py:355
  7.3 26.0 %collective-permute-start = (f32[768]{0:T(1024)S(1)}, f32[768]{0:T(1024)S(1)}, u32[]{:S(2)}, u32[]{:S(2)}) collective-permute-start(f32[768]{0:T(1024)S(1)} %copy-done.18), channel_id=1, source_target_pairs={{0,1},{1,0},{2,3},{3,2},{4,5},{5,4},{6,7},{7,6},{8,9},{9,8},{10,11... | collective-permute-start | bytes 9224 | tf_op jit(solution)/shard_map/ppermute | solution.py:62
  23.0 20.2 %all-to-all-start = ((bf16[16,32,768]{2,1,0:T(8,128)(2,1)}), bf16[16,32,768]{2,1,0:T(8,128)(2,1)S(1)}, u32[]{:S(2)}, u32[]{:S(2)}) async-start(bf16[16,32,768]{2,1,0:T(8,128)(2,1)} %bitcast.3), calls=%async_computation | async-start | bytes 1572864 | tf_op jit(solution)/shard_map/all_to_all | solution.py:253
  33.3 3.2 %collective-permute-start.1 = (f32[2,768]{1,0:T(2,128)S(1)}, f32[2,768]{1,0:T(2,128)S(1)}, u32[]{:S(2)}, u32[]{:S(2)}) collective-permute-start(f32[2,768]{1,0:T(2,128)S(1)} %pad_maximum_fusion.2), channel_id=1, source_target_pairs={{0,2},{1,7},{2,4},{3,1},{4,6},{5,3},{6,0},{7,5},{8,10},{9,15},{10,... | collective-permute-start | bytes 18440 | tf_op jit(solution)/shard_map/ppermute | solution.py:53
  36.4 6.1 %collective-permute-start.2 = (f32[2,768]{1,0:T(2,128)S(1)}, f32[2,768]{1,0:T(2,128)S(1)}, u32[]{:S(2)}, u32[]{:S(2)}) collective-permute-start(f32[2,768]{1,0:T(2,128)S(1)} %pad_maximum_fusion.2), channel_id=1, source_target_pairs={{0,6},{1,3},{2,0},{3,5},{4,2},{5,7},{6,4},{7,1},{8,14},{9,11},{10,... | collective-permute-start | bytes 18440 | tf_op jit(solution)/shard_map/ppermute | solution.py:53
  36.5 6.0 %collective-permute-start.3 = (f32[2,768]{1,0:T(2,128)S(1)}, f32[2,768]{1,0:T(2,128)S(1)}, u32[]{:S(2)}, u32[]{:S(2)}) collective-permute-start(f32[2,768]{1,0:T(2,128)S(1)} %collective-permute-done.1), channel_id=1, source_target_pairs={{0,2},{1,7},{2,4},{3,1},{4,6},{5,3},{6,0},{7,5},{8,10},{9,15},{10,... | collective-permute-start | bytes 18440 | tf_op jit(solution)/shard_map/ppermute | solution.py:53
  43.2 0.9 copy-start.6
  44.1 2.6 copy-start.7
  44.1 2.6 copy-start.13
  46.7 1.0 copy-start.12
  48.7 17.1 %copy-start.14 = (f32[256,512]{1,0:T(8,128)S(1)}, f32[256,512]{1,0:T(8,128)}, u32[]{:S(2)}) copy-start(f32[256,512]{1,0:T(8,128)} %constant.32.clone) | copy-start | bytes 1572868
  65.8 21.5 %copy-start.2 = (f32[8,768]{1,0:T(8,128)S(1)}, f32[8,768]{1,0:T(8,128)}, u32[]{:S(2)}) copy-start(f32[8,768]{1,0:T(8,128)} %select_reduce_fusion.refs_1_.gain_ref) | copy-start | bytes 73732
  87.6 6.8 %collective-permute-start.22 = (bf16[16,6144]{1,0:T(8,128)(2,1)S(1)}, bf16[16,6144]{1,0:T(8,128)(2,1)S(1)}, u32[]{:S(2)}, u32[]{:S(2)}) collective-permute-start(bf16[16,6144]{1,0:T(8,128)(2,1)S(1)} %get-tuple-element.37), channel_id=1, source_target_pairs={{0,16},{1,17},{2,18},{3,19},{4,20},{5,21},{6,22},{7,23},{8,24},{9,... | collective-permute-start | bytes 589832 | tf_op jit(solution)/shard_map/ppermute | solution.py:53
  88.3 8.5 %collective-permute-start.21 = (bf16[16,6144]{1,0:T(8,128)(2,1)S(1)}, bf16[16,6144]{1,0:T(8,128)(2,1)S(1)}, u32[]{:S(2)}, u32[]{:S(2)}) collective-permute-start(bf16[16,6144]{1,0:T(8,128)(2,1)S(1)} %get-tuple-element.37), channel_id=1, source_target_pairs={{0,24},{1,25},{2,26},{3,27},{4,28},{5,29},{6,30},{7,31},{8,0},{9,1... | collective-permute-start | bytes 589832 | tf_op jit(solution)/shard_map/ppermute | solution.py:53
  90.4 9.0 %collective-permute-start.20 = (bf16[16,6144]{1,0:T(8,128)(2,1)S(1)}, bf16[16,6144]{1,0:T(8,128)(2,1)S(1)}, u32[]{:S(2)}, u32[]{:S(2)}) collective-permute-start(bf16[16,6144]{1,0:T(8,128)(2,1)S(1)} %get-tuple-element.37), channel_id=1, source_target_pairs={{0,8},{1,9},{2,10},{3,11},{4,12},{5,13},{6,14},{7,15},{8,16},{9,17... | collective-permute-start | bytes 589832 | tf_op jit(solution)/shard_map/ppermute | solution.py:53
  90.4 9.7 %collective-permute-start.6 = (bf16[16,6144]{1,0:T(8,128)(2,1)S(1)}, bf16[16,6144]{1,0:T(8,128)(2,1)S(1)}, u32[]{:S(2)}, u32[]{:S(2)}) collective-permute-start(bf16[16,6144]{1,0:T(8,128)(2,1)S(1)} %get-tuple-element.27), channel_id=1, source_target_pairs={{0,64},{1,65},{2,66},{3,67},{4,68},{5,69},{6,70},{7,71},{8,72},{9,... | collective-permute-start | bytes 589832 | tf_op jit(solution)/shard_map/ppermute | solution.py:53
  90.9 9.2 %collective-permute-start.5 = (bf16[16,6144]{1,0:T(8,128)(2,1)S(1)}, bf16[16,6144]{1,0:T(8,128)(2,1)S(1)}, u32[]{:S(2)}, u32[]{:S(2)}) collective-permute-start(bf16[16,6144]{1,0:T(8,128)(2,1)S(1)} %get-tuple-element.27), channel_id=1, source_target_pairs={{0,96},{1,97},{2,98},{3,99},{4,100},{5,101},{6,102},{7,103},{8,104... | collective-permute-start | bytes 589832 | tf_op jit(solution)/shard_map/ppermute | solution.py:53
  94.4 7.2 %collective-permute-start.4 = (bf16[16,6144]{1,0:T(8,128)(2,1)S(1)}, bf16[16,6144]{1,0:T(8,128)(2,1)S(1)}, u32[]{:S(2)}, u32[]{:S(2)}) collective-permute-start(bf16[16,6144]{1,0:T(8,128)(2,1)S(1)} %get-tuple-element.27), channel_id=1, source_target_pairs={{0,32},{1,33},{2,34},{3,35},{4,36},{5,37},{6,38},{7,39},{8,40},{9,... | collective-permute-start | bytes 589832 | tf_op jit(solution)/shard_map/ppermute | solution.py:53
  99.3 14.8 %copy-start.3 = (bf16[1536,768]{1,0:T(8,128)(2,1)S(1)}, bf16[1536,768]{1,0:T(8,128)(2,1)}, u32[]{:S(2)}) copy-start(bf16[1536,768]{1,0:T(8,128)(2,1)} %refs_4_.3) | copy-start | bytes 7077892
  99.4 23.2 %copy-start.16 = (f32[1536]{0:T(1024)S(1)}, f32[1536]{0:T(1024)}, u32[]{:S(2)}) copy-start(f32[1536]{0:T(1024)} %param.19) | copy-start | bytes 18436
  99.5 12.1 %copy-start.9 = (bf16[4,16,6144]{2,1,0:T(8,128)(2,1)}, bf16[4,16,6144]{2,1,0:T(8,128)(2,1)S(1)}, u32[]{:S(2)}) copy-start(bf16[4,16,6144]{2,1,0:T(8,128)(2,1)S(1)} %pad_maximum_fusion.1) | copy-start | bytes 2359300
  99.5 12.0 %collective-permute-start.23 = (bf16[64,6144]{1,0:T(8,128)(2,1)S(1)}, bf16[64,6144]{1,0:T(8,128)(2,1)S(1)}, u32[]{:S(2)}, u32[]{:S(2)}) collective-permute-start(bf16[64,6144]{1,0:T(8,128)(2,1)S(1)} %bitcast.45), channel_id=1, source_target_pairs={{0,32},{1,97},{2,34},{3,99},{4,36},{5,101},{6,38},{7,103},{8,40},{... | collective-permute-start | bytes 2359304 | tf_op jit(solution)/shard_map/ppermute | solution.py:53
  102.6 17.2 %collective-permute-start.7 = (bf16[64,6144]{1,0:T(8,128)(2,1)}, bf16[64,6144]{1,0:T(8,128)(2,1)}, u32[]{:S(2)}, u32[]{:S(2)}) collective-permute-start(bf16[64,6144]{1,0:T(8,128)(2,1)} %bitcast.14.refs_0_), channel_id=1, source_target_pairs={{0,8},{1,25},{2,10},{3,27},{4,12},{5,29},{6,14},{7,31},{8,16},{9,1... | collective-permute-start | bytes 2359304 | tf_op jit(solution)/shard_map/ppermute | solution.py:53
  104.3 18.9 %collective-permute-start.24 = (bf16[64,6144]{1,0:T(8,128)(2,1)S(1)}, bf16[64,6144]{1,0:T(8,128)(2,1)S(1)}, u32[]{:S(2)}, u32[]{:S(2)}) collective-permute-start(bf16[64,6144]{1,0:T(8,128)(2,1)S(1)} %bitcast.46), channel_id=1, source_target_pairs={{0,96},{1,33},{2,98},{3,35},{4,100},{5,37},{6,102},{7,39},{8,104},... | collective-permute-start | bytes 2359304 | tf_op jit(solution)/shard_map/ppermute | solution.py:53
  111.5 11.6 %copy-start.10 = (bf16[64,6144]{1,0:T(8,128)(2,1)}, bf16[64,6144]{1,0:T(8,128)(2,1)S(1)}, u32[]{:S(2)}) copy-start(bf16[64,6144]{1,0:T(8,128)(2,1)S(1)} %collective-permute-done.23.refs_1_) | copy-start | bytes 2359300
  111.5 16.1 %collective-permute-start.25 = (bf16[64,6144]{1,0:T(8,128)(2,1)S(1)}, bf16[64,6144]{1,0:T(8,128)(2,1)}, u32[]{:S(2)}, u32[]{:S(2)}) collective-permute-start(bf16[64,6144]{1,0:T(8,128)(2,1)S(1)} %collective-permute-done.23.refs_1_), channel_id=1, source_target_pairs={{0,32},{1,97},{2,34},{3,99},{4,36},{5,101},{6,38},{7,103},{8,40},{... | collective-permute-start | bytes 2359304 | tf_op jit(solution)/shard_map/ppermute | solution.py:53
  114.1 52.5 %collective-permute-start.13 = (bf16[1536,768]{1,0:T(8,128)(2,1)S(1)}, bf16[1536,768]{1,0:T(8,128)(2,1)}, u32[]{:S(2)}, u32[]{:S(2)}) collective-permute-start(bf16[1536,768]{1,0:T(8,128)(2,1)S(1)} %copy-done.3), channel_id=1, source_target_pairs={{0,1},{1,0},{2,3},{3,2},{4,5},{5,4},{6,7},{7,6},{8,9},{9,8},{10,11... | collective-permute-start | bytes 7077896 | tf_op jit(solution)/shard_map/ppermute | solution.py:62
  119.9 20.5 %collective-permute-start.8 = (bf16[64,6144]{1,0:T(8,128)(2,1)}, bf16[64,6144]{1,0:T(8,128)(2,1)}, u32[]{:S(2)}, u32[]{:S(2)}) collective-permute-start(bf16[64,6144]{1,0:T(8,128)(2,1)} %bitcast.14.refs_0_), channel_id=1, source_target_pairs={{0,24},{1,9},{2,26},{3,11},{4,28},{5,13},{6,30},{7,15},{8,0},{9,17... | collective-permute-start | bytes 2359304 | tf_op jit(solution)/shard_map/ppermute | solution.py:53
  119.9 20.5 %collective-permute-start.9 = (bf16[64,6144]{1,0:T(8,128)(2,1)}, bf16[64,6144]{1,0:T(8,128)(2,1)}, u32[]{:S(2)}, u32[]{:S(2)}) collective-permute-start(bf16[64,6144]{1,0:T(8,128)(2,1)} %collective-permute-done.7.refs_1_), channel_id=1, source_target_pairs={{0,8},{1,25},{2,10},{3,27},{4,12},{5,29},{6,14},{7,31},{8,16},{9,1... | collective-permute-start | bytes 2359304 | tf_op jit(solution)/shard_map/ppermute | solution.py:53
  123.2 0.9 copy-start.11
  139.5 13.2 %copy-start.1 = (bf16[256,1536]{1,0:T(8,128)(2,1)S(1)}, bf16[256,1536]{1,0:T(8,128)(2,1)}, u32[]{:S(2)}) copy-start(bf16[256,1536]{1,0:T(8,128)(2,1)} %shard_map.143.refs_0_) | copy-start | bytes 2359300
  139.5 14.3 %collective-permute-start.26 = (bf16[256,1536]{1,0:T(8,128)(2,1)}, bf16[256,1536]{1,0:T(8,128)(2,1)S(1)}, u32[]{:S(2)}, u32[]{:S(2)}) collective-permute-start(bf16[256,1536]{1,0:T(8,128)(2,1)} %shard_map.143.refs_0_), channel_id=1, source_target_pairs={{0,2},{1,7},{2,4},{3,1},{4,6},{5,3},{6,0},{7,5},{8,10},{9,15},{10,... | collective-permute-start | bytes 2359304 | tf_op jit(solution)/shard_map/ppermute | solution.py:53
  152.3 45.1 %copy-start = (bf16[256,1536]{1,0:T(8,128)(2,1)S(1)}, bf16[256,1536]{1,0:T(8,128)(2,1)}, u32[]{:S(2)}) copy-start(bf16[256,1536]{1,0:T(8,128)(2,1)} %shard_map.138.refs_0_) | copy-start | bytes 2359300
  152.3 14.3 %collective-permute-start.10 = (bf16[256,1536]{1,0:T(8,128)(2,1)}, bf16[256,1536]{1,0:T(8,128)(2,1)S(1)}, u32[]{:S(2)}, u32[]{:S(2)}) collective-permute-start(bf16[256,1536]{1,0:T(8,128)(2,1)} %shard_map.138.refs_0_), channel_id=1, source_target_pairs={{0,2},{1,7},{2,4},{3,1},{4,6},{5,3},{6,0},{7,5},{8,10},{9,15},{10,... | collective-permute-start | bytes 2359304 | tf_op jit(solution)/shard_map/ppermute | solution.py:53
  152.7 17.6 %collective-permute-start.27 = (bf16[256,1536]{1,0:T(8,128)(2,1)S(1)}, bf16[256,1536]{1,0:T(8,128)(2,1)S(1)}, u32[]{:S(2)}, u32[]{:S(2)}) collective-permute-start(bf16[256,1536]{1,0:T(8,128)(2,1)S(1)} %copy-done.1), channel_id=1, source_target_pairs={{0,6},{1,3},{2,0},{3,5},{4,2},{5,7},{6,4},{7,1},{8,14},{9,11},{10,... | collective-permute-start | bytes 2359304 | tf_op jit(solution)/shard_map/ppermute | solution.py:53
  153.8 29.7 %collective-permute-start.28 = (bf16[256,1536]{1,0:T(8,128)(2,1)S(1)}, bf16[256,1536]{1,0:T(8,128)(2,1)S(1)}, u32[]{:S(2)}, u32[]{:S(2)}) collective-permute-start(bf16[256,1536]{1,0:T(8,128)(2,1)S(1)} %collective-permute-done.26.refs_1_), channel_id=1, source_target_pairs={{0,2},{1,7},{2,4},{3,1},{4,6},{5,3},{6,0},{7,5},{8,10},{9,15},{10,... | collective-permute-start | bytes 2359304 | tf_op jit(solution)/shard_map/ppermute | solution.py:53
  155.4 0.9 copy-start.4
  156.3 38.7 %collective-permute-start.11 = (bf16[256,1536]{1,0:T(8,128)(2,1)}, bf16[256,1536]{1,0:T(8,128)(2,1)S(1)}, u32[]{:S(2)}, u32[]{:S(2)}) collective-permute-start(bf16[256,1536]{1,0:T(8,128)(2,1)} %shard_map.138.refs_0_), channel_id=1, source_target_pairs={{0,6},{1,3},{2,0},{3,5},{4,2},{5,7},{6,4},{7,1},{8,14},{9,11},{10,... | collective-permute-start | bytes 2359304 | tf_op jit(solution)/shard_map/ppermute | solution.py:53
  166.6 30.7 %collective-permute-start.12 = (bf16[256,1536]{1,0:T(8,128)(2,1)S(1)}, bf16[256,1536]{1,0:T(8,128)(2,1)S(1)}, u32[]{:S(2)}, u32[]{:S(2)}) collective-permute-start(bf16[256,1536]{1,0:T(8,128)(2,1)S(1)} %collective-permute-done.10.refs_1_), channel_id=1, source_target_pairs={{0,2},{1,7},{2,4},{3,1},{4,6},{5,3},{6,0},{7,5},{8,10},{9,15},{10,... | collective-permute-start | bytes 2359304 | tf_op jit(solution)/shard_map/ppermute | solution.py:53
  183.5 1.1 copy-start.5
  192.6 14.9 %collective-permute-start.30 = (bf16[256,1536]{1,0:T(8,128)(2,1)S(1)}, bf16[256,1536]{1,0:T(8,128)(2,1)S(1)}, u32[]{:S(2)}, u32[]{:S(2)}) collective-permute-start(bf16[256,1536]{1,0:T(8,128)(2,1)S(1)} %get-tuple-element.41), channel_id=1, source_target_pairs={{0,96},{1,33},{2,98},{3,35},{4,100},{5,37},{6,102},{7,39},{8,104},... | collective-permute-start | bytes 2359304 | tf_op jit(solution)/shard_map/ppermute | solution.py:53
  205.3 12.4 %collective-permute-start.15 = (bf16[256,1536]{1,0:T(8,128)(2,1)S(1)}, bf16[256,1536]{1,0:T(8,128)(2,1)S(1)}, u32[]{:S(2)}, u32[]{:S(2)}) collective-permute-start(bf16[256,1536]{1,0:T(8,128)(2,1)S(1)} %get-tuple-element.31), channel_id=1, source_target_pairs={{0,24},{1,9},{2,26},{3,11},{4,28},{5,13},{6,30},{7,15},{8,0},{9,17... | collective-permute-start | bytes 2359304 | tf_op jit(solution)/shard_map/ppermute | solution.py:53
  205.4 15.8 %collective-permute-start.29 = (bf16[256,1536]{1,0:T(8,128)(2,1)S(1)}, bf16[256,1536]{1,0:T(8,128)(2,1)S(1)}, u32[]{:S(2)}, u32[]{:S(2)}) collective-permute-start(bf16[256,1536]{1,0:T(8,128)(2,1)S(1)} %get-tuple-element.39), channel_id=1, source_target_pairs={{0,32},{1,97},{2,34},{3,99},{4,36},{5,101},{6,38},{7,103},{8,40},{... | collective-permute-start | bytes 2359304 | tf_op jit(solution)/shard_map/ppermute | solution.py:53
  207.7 15.0 %collective-permute-start.31 = (bf16[256,1536]{1,0:T(8,128)(2,1)S(1)}, bf16[256,1536]{1,0:T(8,128)(2,1)S(1)}, u32[]{:S(2)}, u32[]{:S(2)}) collective-permute-start(bf16[256,1536]{1,0:T(8,128)(2,1)S(1)} %shard_map.145), channel_id=1, source_target_pairs={{0,96},{1,33},{2,98},{3,35},{4,100},{5,37},{6,102},{7,39},{8,104},... | collective-permute-start | bytes 2359304 | tf_op jit(solution)/shard_map/ppermute | solution.py:53
  207.7 23.4 %collective-permute-start.14 = (bf16[256,1536]{1,0:T(8,128)(2,1)S(1)}, bf16[256,1536]{1,0:T(8,128)(2,1)S(1)}, u32[]{:S(2)}, u32[]{:S(2)}) collective-permute-start(bf16[256,1536]{1,0:T(8,128)(2,1)S(1)} %get-tuple-element.29), channel_id=1, source_target_pairs={{0,8},{1,25},{2,10},{3,27},{4,12},{5,29},{6,14},{7,31},{8,16},{9,1... | collective-permute-start | bytes 2359304 | tf_op jit(solution)/shard_map/ppermute | solution.py:53
  217.9 18.7 %collective-permute-start.16 = (bf16[256,1536]{1,0:T(8,128)(2,1)S(1)}, bf16[256,1536]{1,0:T(8,128)(2,1)S(1)}, u32[]{:S(2)}, u32[]{:S(2)}) collective-permute-start(bf16[256,1536]{1,0:T(8,128)(2,1)S(1)} %shard_map.140), channel_id=1, source_target_pairs={{0,24},{1,9},{2,26},{3,11},{4,28},{5,13},{6,30},{7,15},{8,0},{9,17... | collective-permute-start | bytes 2359304 | tf_op jit(solution)/shard_map/ppermute | solution.py:53
  223.0 19.2 %copy-start.19 = (f32[768]{0:T(1024)S(1)}, f32[768]{0:T(1024)}, u32[]{:S(2)}) copy-start(f32[768]{0:T(1024)} %param.21) | copy-start | bytes 9220
  223.0 17.4 %collective-permute-start.32 = (bf16[64,1536]{1,0:T(8,128)(2,1)S(1)}, bf16[64,1536]{1,0:T(8,128)(2,1)S(1)}, u32[]{:S(2)}, u32[]{:S(2)}) collective-permute-start(bf16[64,1536]{1,0:T(8,128)(2,1)S(1)} %get-tuple-element.43), channel_id=1, source_target_pairs={{0,24},{1,25},{2,26},{3,27},{4,28},{5,29},{6,30},{7,31},{8,0},{9,1... | collective-permute-start | bytes 589832 | tf_op jit(solution)/shard_map/ppermute | solution.py:53
  228.1 14.9 %collective-permute-start.33 = (bf16[64,1536]{1,0:T(8,128)(2,1)S(1)}, bf16[64,1536]{1,0:T(8,128)(2,1)S(1)}, u32[]{:S(2)}, u32[]{:S(2)}) collective-permute-start(bf16[64,1536]{1,0:T(8,128)(2,1)S(1)} %get-tuple-element.44), channel_id=1, source_target_pairs={{0,8},{1,9},{2,10},{3,11},{4,12},{5,13},{6,14},{7,15},{8,16},{9,17... | collective-permute-start | bytes 589832 | tf_op jit(solution)/shard_map/ppermute | solution.py:53
  228.1 14.9 %collective-permute-start.34 = (bf16[64,1536]{1,0:T(8,128)(2,1)S(1)}, bf16[64,1536]{1,0:T(8,128)(2,1)S(1)}, u32[]{:S(2)}, u32[]{:S(2)}) collective-permute-start(bf16[64,1536]{1,0:T(8,128)(2,1)S(1)} %get-tuple-element.45), channel_id=1, source_target_pairs={{0,16},{1,17},{2,18},{3,19},{4,20},{5,21},{6,22},{7,23},{8,24},{9,... | collective-permute-start | bytes 589832 | tf_op jit(solution)/shard_map/ppermute | solution.py:53
  237.0 12.8 %collective-permute-start.17 = (bf16[64,1536]{1,0:T(8,128)(2,1)S(1)}, bf16[64,1536]{1,0:T(8,128)(2,1)S(1)}, u32[]{:S(2)}, u32[]{:S(2)}) collective-permute-start(bf16[64,1536]{1,0:T(8,128)(2,1)S(1)} %get-tuple-element.33), channel_id=1, source_target_pairs={{0,96},{1,97},{2,98},{3,99},{4,100},{5,101},{6,102},{7,103},{8,104... | collective-permute-start | bytes 589832 | tf_op jit(solution)/shard_map/ppermute | solution.py:53
  240.4 9.4 %collective-permute-start.18 = (bf16[64,1536]{1,0:T(8,128)(2,1)S(1)}, bf16[64,1536]{1,0:T(8,128)(2,1)S(1)}, u32[]{:S(2)}, u32[]{:S(2)}) collective-permute-start(bf16[64,1536]{1,0:T(8,128)(2,1)S(1)} %get-tuple-element.34), channel_id=1, source_target_pairs={{0,32},{1,33},{2,34},{3,35},{4,36},{5,37},{6,38},{7,39},{8,40},{9,... | collective-permute-start | bytes 589832 | tf_op jit(solution)/shard_map/ppermute | solution.py:53
  240.4 9.4 %collective-permute-start.19 = (bf16[64,1536]{1,0:T(8,128)(2,1)S(1)}, bf16[64,1536]{1,0:T(8,128)(2,1)S(1)}, u32[]{:S(2)}, u32[]{:S(2)}) collective-permute-start(bf16[64,1536]{1,0:T(8,128)(2,1)S(1)} %get-tuple-element.35), channel_id=1, source_target_pairs={{0,64},{1,65},{2,66},{3,67},{4,68},{5,69},{6,70},{7,71},{8,72},{9,... | collective-permute-start | bytes 589832 | tf_op jit(solution)/shard_map/ppermute | solution.py:53
  243.1 13.1 %collective-permute-start.36 = (bf16[64,768]{1,0:T(8,128)(2,1)S(1)}, bf16[64,768]{1,0:T(8,128)(2,1)S(1)}, u32[]{:S(2)}, u32[]{:S(2)}) collective-permute-start(bf16[64,768]{1,0:T(8,128)(2,1)S(1)} %get-tuple-element.48), channel_id=1, source_target_pairs={{0,1},{1,0},{2,3},{3,2},{4,5},{5,4},{6,7},{7,6},{8,9},{9,8},{10,11... | collective-permute-start | bytes 294920 | tf_op jit(solution)/shard_map/ppermute | solution.py:62
  249.9 6.5 %collective-permute-start.35 = (bf16[64,768]{1,0:T(8,128)(2,1)S(1)}, bf16[64,768]{1,0:T(8,128)(2,1)S(1)}, u32[]{:S(2)}, u32[]{:S(2)}) collective-permute-start(bf16[64,768]{1,0:T(8,128)(2,1)S(1)} %get-tuple-element.47), channel_id=1, source_target_pairs={{0,1},{1,0},{2,3},{3,2},{4,5},{5,4},{6,7},{7,6},{8,9},{9,8},{10,11... | collective-permute-start | bytes 294920 | tf_op jit(solution)/shard_map/ppermute | solution.py:62
Sparse Core Ops, SparseCore 0:
  9.1 101.7 all-gather.1

commit v9 on v8

--- a/solution.py
+++ b/solution.py
@@ -165,7 +165,7 @@
         out_specs=[pl.BlockSpec((tokens // count, tile), lambda i: (0, i))] * count,
         out_shape=[jax.ShapeDtypeStruct((tokens // count, 2 * chans), BF)] * count,
         scratch_shapes=[pltpu.VMEM((tokens, depth), BF), pltpu.SemaphoreType.DMA((SIDE,))],
-        compiler_params=params(32),
+        compiler_params=params(58),
         cost_estimate=pl.CostEstimate(
             flops=4 * tokens * depth * chans,
             bytes_accessed=2 * (tokens * depth + 2 * depth * chans + 2 * tokens * chans),
@@ -286,7 +286,6 @@
     normed = (source - mean) / jnp.sqrt(square - mean * mean + 1e-05) * gain_first
     col = jnp.dot(one, normed, precision=high).astype(BF)
     col = exchange(col.reshape(groups, -1, chans), "row").reshape(-1, chans)
-    (col,) = tie([col], early)
     spec = jnp.dot(two, col.astype(F32), precision=high)
     split = spec.shape[0] // 2
     spec_re, spec_im = spec[:split], spec[split:]
@@ -296,6 +295,7 @@
     )
     back = jnp.dot(three, filt, precision=high).astype(BF)
     back = exchange(back.reshape(groups, -1, chans), "row").reshape(-1, chans)
+    (back,) = tie([back], early)
     return source + jnp.dot(four, back.astype(F32), precision=high)
 
 
@@ -319,6 +319,11 @@
 
 def gather_far(a, axis):
     one, two = hop(a, axis, APART), hop(a, axis, OTHER)
+    return [a, one, two, hop(one, axis, APART)]
+
+
+def gather_both(a, axis):
+    one, two = tie([hop(a, axis, APART), hop(a, axis, OTHER)], [])
     return [a, one, two, hop(one, axis, APART)]
 
 
@@ -362,7 +367,7 @@
     first, second = normalize(moved, gains, half)
     first, second = gather_near(first, "z"), gather_near(second, "y")
     parts = [gather_far(first, "y"), gather_far(second, "z")]
-    hiddens = [gather_far(matmul_in(part, w_in_all, b_in), "x") for part in parts]
+    hiddens = [gather_both(matmul_in(part, w_in_all, b_in), "x") for part in parts]
     other = swap_cores(w_out)
     sums = []
     for hidden, (large, small) in zip(hiddens, (("y", "z"), ("z", "y"))):

time: 266 us -> 273 us (1.026)
  blocking collectives: 50 us -> 34.7 us
  starting transfers between devices: 71.6 us -> 81.3 us
  waiting for transfers between devices: 66.8 us -> 76.1 us
  Pallas kernels: 42.5 us -> 48.4 us
  local copies, waits for them, and re-layouts: 11.1 us -> 7.4 us
    all_to_all x2 -> x1, blocking collectives: 38 us -> 21.5 us  [exchange(): return lax.all_to_all(a, axis, split_axis=0, concat_axis=0, tiled=True)]
    all_to_all x1 -> x2, waiting for transfers between devices: 0.01 us -> 9.73 us  [exchange(): return lax.all_to_all(a, axis, split_axis=0, concat_axis=0, tiled=True)]
    pallas_call x2, Pallas kernels: 15.8 us -> 21.9 us  [matmul_out(): pl.pallas_call(mm2_kernel, grid=(2 * steps,), in_specs=[pl.BlockSpec(memo...]
    all_to_all x1 -> x2, starting transfers between devices: 7.85 us -> 11.6 us  [exchange(): return lax.all_to_all(a, axis, split_axis=0, concat_axis=0, tiled=True)]
    ppermute x33, starting transfers between devices: 44.2 us -> 47.5 us  [hop(): return lax.ppermute(a, ('row', 'col'), pairs)]
  transfers between devices with their start and end apart: 39 -> 40, of which waited for: 17 -> 20; matrix products, arithmetic and copies ran while one was open for 6% -> 5% of each run, Pallas kernels for 16% -> 17%
where the time goes in v9:
time: 273 us; the launch traced here: 272 us
  starting transfers between devices  81.3 us (30%)
  waiting for transfers between devices  76.1 us (28%)
  Pallas kernels  48.4 us (18%)
  blocking collectives  34.7 us (13%)
  between operations  13.7 us (5%)
  matrix products  8.86 us (3%)
  local copies, waits for them, and re-layouts  7.4 us (3%)
    ppermute x33, waiting for transfers between devices, hop(): return lax.ppermute(a, ('row', 'col'), pairs)  64.6 us
    ppermute x33, starting transfers between devices, hop(): return lax.ppermute(a, ('row', 'col'), pairs)  47.5 us
    pallas_call x2, Pallas kernels, matmul_in(): pl.pallas_call(mm1_kernel, grid=(width // tile,), in_specs=[pl.BlockSpec(...  23.7 us
    ppermute x4, starting transfers between devices, swap_cores(): return lax.ppermute(a, 'col', pairs)  22.2 us
    pallas_call x2, Pallas kernels, matmul_out(): pl.pallas_call(mm2_kernel, grid=(2 * steps,), in_specs=[pl.BlockSpec(memo...  21.9 us
    all_to_all x1, blocking collectives, exchange(): return lax.all_to_all(a, axis, split_axis=0, concat_axis=0, tiled=True)  21.5 us
    psum x1, blocking collectives, spectral(): lax.psum((jnp.sum(source, axis=-1), jnp.sum(source * source, axis=-1)), '...  13.2 us
    all_to_all x2, starting transfers between devices, exchange(): return lax.all_to_all(a, axis, split_axis=0, concat_axis=0, tiled=True)  11.6 us
  transfers between devices with their start and end apart: 40, of which 20 were waited for; matrix products, arithmetic and copies ran while one was open for 5% of the time, Pallas kernels for 17%

profile of v9, /device:TPU:1, one launch (start us, length us, event | category | flops | bytes accessed | tf_op | source)
XLA Modules:
  0.0 271.9 jit_solution(3055654032129482976)
XLA Ops:
  6.5 0.7 all-gather.2.cloned.1.call-update
  7.9 13.2 %all-reduce = (f32[256]{0:T(256)S(1)}, f32[256]{0:T(256)S(1)}) all-reduce(f32[256]{0:T(256)S(1)} %reduce_sum.34, f32[256]{0:T(256)S(1)} %reduce_sum.32), channel_id=1, replica_groups=mesh['row'=16,'col'=8] {'col'}, use_global_device_ids=true, to_apply=%region_3.4 | all-reduce | flops 512 | bytes 4096 | tf_op jit(solution)/shard_map/psum | solution.py:281
  21.3 1.7 convolution_convert_fusion
  23.0 7.9 %all-to-all-start = ((bf16[16,32,768]{2,1,0:T(8,128)(2,1)}), bf16[16,32,768]{2,1,0:T(8,128)(2,1)}, u32[]{:S(2)}, u32[]{:S(2)}) async-start(bf16[16,32,768]{2,1,0:T(8,128)(2,1)} %bitcast.3), calls=%async_computation | async-start | bytes 1572864 | tf_op jit(solution)/shard_map/all_to_all | solution.py:253
  30.9 1.5 fusion.13
  32.9 9.7 %all-to-all-done = bf16[16,32,768]{2,1,0:T(8,128)(2,1)} async-done(((bf16[16,32,768]{2,1,0:T(8,128)(2,1)}), bf16[16,32,768]{2,1,0:T(8,128)(2,1)}, u32[]{:S(2)}, u32[]{:S(2)}) %all-to-all-start) | async-done | bytes 786464 | tf_op jit(solution)/shard_map/all_to_all | solution.py:253
  42.7 2.5 fusion.15
  45.2 0.9 fusion.5
  46.3 1.8 add_convert_fusion
  48.1 3.7 %all-to-all-start.1 = ((bf16[16,32,768]{2,1,0:T(8,128)(2,1)}), bf16[16,32,768]{2,1,0:T(8,128)(2,1)S(1)}, u32[]{:S(2)}, u32[]{:S(2)}) async-start(bf16[16,32,768]{2,1,0:T(8,128)(2,1)} %bitcast.6), calls=%async_computation.1 | async-start | bytes 1572864 | tf_op jit(solution)/shard_map/all_to_all | solution.py:253
  51.9 3.7 %collective-permute-start = (f32[768]{0:T(1024)S(1)}, f32[768]{0:T(1024)S(1)}, u32[]{:S(2)}, u32[]{:S(2)}) collective-permute-start(f32[768]{0:T(1024)S(1)} %copy-done.19), channel_id=1, source_target_pairs={{0,1},{1,0},{2,3},{3,2},{4,5},{5,4},{6,7},{7,6},{8,9},{9,8},{10,11... | collective-permute-start | bytes 9224 | tf_op jit(solution)/shard_map/ppermute | solution.py:62
  55.6 0.8 collective-permute-done
  56.5 3.5 %collective-permute-start.1 = (f32[2,768]{1,0:T(2,128)S(1)}, f32[2,768]{1,0:T(2,128)S(1)}, u32[]{:S(2)}, u32[]{:S(2)}) collective-permute-start(f32[2,768]{1,0:T(2,128)S(1)} %pad_maximum_fusion.2), channel_id=1, source_target_pairs={{0,2},{1,7},{2,4},{3,1},{4,6},{5,3},{6,0},{7,5},{8,10},{9,15},{10,... | collective-permute-start | bytes 18440 | tf_op jit(solution)/shard_map/ppermute | solution.py:53
  59.9 0.7 dynamic-slice_bitcast_fusion
  60.7 3.4 %collective-permute-start.3 = (f32[2,768]{1,0:T(2,128)S(1)}, f32[2,768]{1,0:T(2,128)S(1)}, u32[]{:S(2)}, u32[]{:S(2)}) collective-permute-start(f32[2,768]{1,0:T(2,128)S(1)} %collective-permute-done.1), channel_id=1, source_target_pairs={{0,2},{1,7},{2,4},{3,1},{4,6},{5,3},{6,0},{7,5},{8,10},{9,15},{10,... | collective-permute-start | bytes 18440 | tf_op jit(solution)/shard_map/ppermute | solution.py:53
  64.1 0.7 collective-permute-done.2
  64.9 0.7 select_reduce_fusion.refs_1_.gain_ref
  65.7 0.9 copy-done.5
  66.6 1.9 fusion.14
  68.4 21.5 %all_to_all.15.moved_ref = bf16[8,32,768]{2,1,0:T(8,128)(2,1)S(1)} all-to-all(bf16[8,32,768]{2,1,0:T(8,128)(2,1)S(1)} %bitcast.51), channel_id=1, replica_groups=mesh['row'=16,'col'=8] {'col'}, dimensions={0} | all-to-all | bytes 786432 | tf_op jit(solution)/shard_map/all_to_all | solution.py:253
  90.3 0.5 collective-permute-start.22
  90.8 2.2 collective-permute-start.21
  93.6 1.7 collective-permute-start.5
  95.2 1.8 collective-permute-done.22
  97.1 2.1 collective-permute-done.21
  99.2 2.8 %collective-permute-done.20 = bf16[16,6144]{1,0:T(8,128)(2,1)S(1)} collective-permute-done((bf16[16,6144]{1,0:T(8,128)(2,1)S(1)}, bf16[16,6144]{1,0:T(8,128)(2,1)S(1)}, u32[]{:S(2)}, u32[]{:S(2)}) %collective-permute-start.20) | collective-permute-done | bytes 196640 | tf_op jit(solution)/shard_map/ppermute | solution.py:53
  102.1 0.6 collective-permute-start.23
  102.7 1.6 collective-permute-done.4
  104.4 2.3 collective-permute-start.7
  106.7 8.2 %collective-permute-done.23.refs_1_ = bf16[64,6144]{1,0:T(8,128)(2,1)S(1)} collective-permute-done((bf16[64,6144]{1,0:T(8,128)(2,1)S(1)}, bf16[64,6144]{1,0:T(8,128)(2,1)S(1)}, u32[]{:S(2)}, u32[]{:S(2)}) %collective-permute-start.23) | collective-permute-done | bytes 786464 | tf_op jit(solution)/shard_map/ppermute | solution.py:53
  114.9 2.5 collective-permute-start.25
  117.4 5.1 %collective-permute-start.13 = (bf16[1536,768]{1,0:T(8,128)(2,1)}, bf16[1536,768]{1,0:T(8,128)(2,1)}, u32[]{:S(2)}, u32[]{:S(2)}) collective-permute-start(bf16[1536,768]{1,0:T(8,128)(2,1)} %refs_4_.3), channel_id=1, source_target_pairs={{0,1},{1,0},{2,3},{3,2},{4,5},{5,4},{6,7},{7,6},{8,9},{9,8},{10,11... | collective-permute-start | bytes 7077896 | tf_op jit(solution)/shard_map/ppermute | solution.py:62
  122.6 2.5 collective-permute-start.9
  125.2 0.6 broadcast_in_dim.35.refs_5_
  125.8 0.9 copy-done.11
  126.7 3.6 %collective-permute-done.25.refs_3_ = bf16[64,6144]{1,0:T(8,128)(2,1)} collective-permute-done((bf16[64,6144]{1,0:T(8,128)(2,1)S(1)}, bf16[64,6144]{1,0:T(8,128)(2,1)}, u32[]{:S(2)}, u32[]{:S(2)}) %collective-permute-start.25) | collective-permute-done | bytes 786464 | tf_op jit(solution)/shard_map/ppermute | solution.py:53
  130.3 11.8 %shard_map.144.refs_0_ = bf16[256,1536]{1,0:T(8,128)(2,1)} custom-call(bf16[64,6144]{1,0:T(8,128)(2,1)} %bitcast.50, bf16[64,6144]{1,0:T(8,128)(2,1)} %copy-done.10, bf16[64,6144]{1,0:T(8,128)(2,1)} %copy-done.11, bf16[64,6144]{1,0:T(8,128)(2,1)} %collective-permute-done.25.refs_3_, bf16[6144,1536]{1,0:T(8,128)(2,1)} %all-gather.2.cloned.1.call-done.refs_4_, ...), custom_call_target="tpu_custom_call" | custom-call | flops 4831838208 | bytes 22020096 | tf_op jit(solution)/shard_map/pallas_call | solution.py:100
  142.3 2.5 collective-permute-start.26
  144.8 11.8 %shard_map.138.refs_0_ = bf16[256,1536]{1,0:T(8,128)(2,1)} custom-call(bf16[64,6144]{1,0:T(8,128)(2,1)} %bitcast.47, bf16[64,6144]{1,0:T(8,128)(2,1)} %copy-done.9, bf16[64,6144]{1,0:T(8,128)(2,1)} %collective-permute-done.8.refs_2_, bf16[64,6144]{1,0:T(8,128)(2,1)} %collective-permute-done.9.refs_3_, ...), custom_call_target="tpu_custom_call" | custom-call | flops 4831838208 | bytes 22020096 | tf_op jit(solution)/shard_map/pallas_call | solution.py:100
  156.7 2.7 collective-permute-start.10
  159.4 2.3 collective-permute-start.28
  161.7 13.0 %collective-permute-done.11.refs_1_ = bf16[256,1536]{1,0:T(8,128)(2,1)S(1)} collective-permute-done((bf16[256,1536]{1,0:T(8,128)(2,1)}, bf16[256,1536]{1,0:T(8,128)(2,1)S(1)}, u32[]{:S(2)}, u32[]{:S(2)}) %collective-permute-start.11) | collective-permute-done | bytes 786464 | tf_op jit(solution)/shard_map/ppermute | solution.py:53
  174.6 2.2 collective-permute-done.10.refs_0_
  176.9 3.3 %collective-permute-start.12 = (bf16[256,1536]{1,0:T(8,128)(2,1)}, bf16[256,1536]{1,0:T(8,128)(2,1)S(1)}, u32[]{:S(2)}, u32[]{:S(2)}) collective-permute-start(bf16[256,1536]{1,0:T(8,128)(2,1)} %get-tuple-element.32.refs_1_), channel_id=1, source_target_pairs={{0,2},{1,7},{2,4},{3,1},{4,6},{5,3},{6,0},{7,5},{8,10},{9,15},{10,... | collective-permute-start | bytes 2359304 | tf_op jit(solution)/shard_map/ppermute | solution.py:53
  180.2 7.6 %collective-permute-done.28.refs_3_ = bf16[256,1536]{1,0:T(8,128)(2,1)} collective-permute-done((bf16[256,1536]{1,0:T(8,128)(2,1)}, bf16[256,1536]{1,0:T(8,128)(2,1)}, u32[]{:S(2)}, u32[]{:S(2)}) %collective-permute-start.28) | collective-permute-done | bytes 786464 | tf_op jit(solution)/shard_map/ppermute | solution.py:53
  187.8 10.8 %shard_map.146 = (bf16[256,1536]{1,0:T(8,128)(2,1)}, bf16[256,1536]{1,0:T(8,128)(2,1)}, bf16[256,1536]{1,0:T(8,128)(2,1)}, bf16[256,1536]{1,0:T(8,128)(2,1)}) custom-call(bf16[256,1536]{1,0:T(8,128)(2,1)} %shard_map.144.refs_0_, bf16[256,1536]{1,0:T(8,128)(2,1)} %get-tuple-element.44.refs_1_, bf16[256,1536]{1,0:T(8,128)(2,1)} %get-tuple-element.45.refs_2_, ...), custom_call_target="tpu_custom_call" | custom-call | flops 4831838208 | bytes 11010048 | tf_op jit(solution)/shard_map/pallas_call | solution.py:157
  198.6 0.6 collective-permute-start.30
  199.2 0.9 copy-done.23
  200.1 11.0 %shard_map.140 = (bf16[256,1536]{1,0:T(8,128)(2,1)}, bf16[256,1536]{1,0:T(8,128)(2,1)}, bf16[256,1536]{1,0:T(8,128)(2,1)}, bf16[256,1536]{1,0:T(8,128)(2,1)}) custom-call(bf16[256,1536]{1,0:T(8,128)(2,1)} %shard_map.138.refs_0_, bf16[256,1536]{1,0:T(8,128)(2,1)} %get-tuple-element.32.refs_1_, bf16[256,1536]{1,0:T(8,128)(2,1)} %get-tuple-element.33.refs_2_, ...), custom_call_target="tpu_custom_call" | custom-call | flops 4831838208 | bytes 11010048 | tf_op jit(solution)/shard_map/pallas_call | solution.py:157
  211.3 2.3 collective-permute-start.29
  213.8 2.7 collective-permute-start.14
  216.5 7.3 %collective-permute-done.15.b = bf16[256,1536]{1,0:T(8,128)(2,1)S(1)} collective-permute-done((bf16[256,1536]{1,0:T(8,128)(2,1)}, bf16[256,1536]{1,0:T(8,128)(2,1)S(1)}, u32[]{:S(2)}, u32[]{:S(2)}) %collective-permute-start.15) | collective-permute-done | bytes 786464 | tf_op jit(solution)/shard_map/ppermute | solution.py:53
  224.1 0.8 collective-permute-done.29.b
  224.9 6.5 %collective-permute-done.31.c = bf16[256,1536]{1,0:T(8,128)(2,1)S(1)} collective-permute-done((bf16[256,1536]{1,0:T(8,128)(2,1)S(1)}, bf16[256,1536]{1,0:T(8,128)(2,1)S(1)}, u32[]{:S(2)}, u32[]{:S(2)}) %collective-permute-start.31) | collective-permute-done | bytes 786464 | tf_op jit(solution)/shard_map/ppermute | solution.py:53
  231.8 5.5 %collective-permute-start.32 = (bf16[64,1536]{1,0:T(8,128)(2,1)S(1)}, bf16[64,1536]{1,0:T(8,128)(2,1)S(1)}, u32[]{:S(2)}, u32[]{:S(2)}) collective-permute-start(bf16[64,1536]{1,0:T(8,128)(2,1)S(1)} %get-tuple-element.51), channel_id=1, source_target_pairs={{0,24},{1,25},{2,26},{3,27},{4,28},{5,29},{6,30},{7,31},{8,0},{9,1... | collective-permute-start | bytes 589832 | tf_op jit(solution)/shard_map/ppermute | solution.py:53
  237.3 1.3 collective-permute-start.34
  238.5 2.3 collective-permute-done.16.c
  241.2 2.4 collective-permute-start.17
  243.7 1.7 collective-permute-start.19
  245.3 3.9 %collective-permute-done.34.d = bf16[64,1536]{1,0:T(8,128)(2,1)S(1)} collective-permute-done((bf16[64,1536]{1,0:T(8,128)(2,1)S(1)}, bf16[64,1536]{1,0:T(8,128)(2,1)S(1)}, u32[]{:S(2)}, u32[]{:S(2)}) %collective-permute-start.34) | collective-permute-done | bytes 196640 | tf_op jit(solution)/shard_map/ppermute | solution.py:53
  249.3 6.3 %collective-permute-start.36 = (bf16[64,768]{1,0:T(8,128)(2,1)S(1)}, bf16[64,768]{1,0:T(8,128)(2,1)S(1)}, u32[]{:S(2)}, u32[]{:S(2)}) collective-permute-start(bf16[64,768]{1,0:T(8,128)(2,1)S(1)} %get-tuple-element.56), channel_id=1, source_target_pairs={{0,1},{1,0},{2,3},{3,2},{4,5},{5,4},{6,7},{7,6},{8,9},{9,8},{10,11... | collective-permute-start | bytes 294920 | tf_op jit(solution)/shard_map/ppermute | solution.py:62
  255.7 7.0 %collective-permute-start.35 = (bf16[64,768]{1,0:T(8,128)(2,1)S(1)}, bf16[64,768]{1,0:T(8,128)(2,1)S(1)}, u32[]{:S(2)}, u32[]{:S(2)}) collective-permute-start(bf16[64,768]{1,0:T(8,128)(2,1)S(1)} %get-tuple-element.55), channel_id=1, source_target_pairs={{0,1},{1,0},{2,3},{3,2},{4,5},{5,4},{6,7},{7,6},{8,9},{9,8},{10,11... | collective-permute-start | bytes 294920 | tf_op jit(solution)/shard_map/ppermute | solution.py:62
  262.7 0.7 dynamic-slice_bitcast_fusion.1.place_ref
  263.7 1.4 shard_map.150
  (107 shorter events, 5.0 us)
Async XLA Ops:
  6.5 14.8 %copy-start.16 = (f32[512,256]{1,0:T(8,128)S(1)}, f32[512,256]{1,0:T(8,128)}, u32[]{:S(2)}) copy-start(f32[512,256]{1,0:T(8,128)} %constant.29.clone) | copy-start | bytes 1572868
  6.5 1.1 copy-start.6
  6.5 14.6 %copy-start.18 = (f32[768]{0:T(1024)S(1)}, f32[768]{0:T(1024)}, u32[]{:S(2)}) copy-start(f32[768]{0:T(1024)} %param.16) | copy-start | bytes 9220
  6.5 123.7 %all-gather.2.cloned.1.call-start = ((), (), s32[]{:S(2)}) async-start(), calls=%async_computation.3 | async-start | bytes 21233664 | tf_op jit(solution)/shard_map/all_gather | solution.py:360
  23.0 19.7 %all-to-all-start = ((bf16[16,32,768]{2,1,0:T(8,128)(2,1)}), bf16[16,32,768]{2,1,0:T(8,128)(2,1)}, u32[]{:S(2)}, u32[]{:S(2)}) async-start(bf16[16,32,768]{2,1,0:T(8,128)(2,1)} %bitcast.3), calls=%async_computation | async-start | bytes 1572864 | tf_op jit(solution)/shard_map/all_to_all | solution.py:253
  42.7 2.5 copy-start.14
  45.2 1.0 copy-start.13
  48.1 3.8 %copy-start.19 = (f32[768]{0:T(1024)S(1)}, f32[768]{0:T(1024)}, u32[]{:S(2)}) copy-start(f32[768]{0:T(1024)} %param.17) | copy-start | bytes 9220
  48.1 18.4 %copy-start.15 = (f32[256,512]{1,0:T(8,128)S(1)}, f32[256,512]{1,0:T(8,128)}, u32[]{:S(2)}) copy-start(f32[256,512]{1,0:T(8,128)} %constant.32.clone) | copy-start | bytes 1572868
  48.1 17.6 %all-to-all-start.1 = ((bf16[16,32,768]{2,1,0:T(8,128)(2,1)}), bf16[16,32,768]{2,1,0:T(8,128)(2,1)S(1)}, u32[]{:S(2)}, u32[]{:S(2)}) async-start(bf16[16,32,768]{2,1,0:T(8,128)(2,1)} %bitcast.6), calls=%async_computation.1 | async-start | bytes 1572864 | tf_op jit(solution)/shard_map/all_to_all | solution.py:253
  51.9 4.6 %collective-permute-start = (f32[768]{0:T(1024)S(1)}, f32[768]{0:T(1024)S(1)}, u32[]{:S(2)}, u32[]{:S(2)}) collective-permute-start(f32[768]{0:T(1024)S(1)} %copy-done.19), channel_id=1, source_target_pairs={{0,1},{1,0},{2,3},{3,2},{4,5},{5,4},{6,7},{7,6},{8,9},{9,8},{10,11... | collective-permute-start | bytes 9224 | tf_op jit(solution)/shard_map/ppermute | solution.py:62
  56.5 4.2 %collective-permute-start.1 = (f32[2,768]{1,0:T(2,128)S(1)}, f32[2,768]{1,0:T(2,128)S(1)}, u32[]{:S(2)}, u32[]{:S(2)}) collective-permute-start(f32[2,768]{1,0:T(2,128)S(1)} %pad_maximum_fusion.2), channel_id=1, source_target_pairs={{0,2},{1,7},{2,4},{3,1},{4,6},{5,3},{6,0},{7,5},{8,10},{9,15},{10,... | collective-permute-start | bytes 18440 | tf_op jit(solution)/shard_map/ppermute | solution.py:53
  60.6 4.2 %collective-permute-start.2 = (f32[2,768]{1,0:T(2,128)S(1)}, f32[2,768]{1,0:T(2,128)S(1)}, u32[]{:S(2)}, u32[]{:S(2)}) collective-permute-start(f32[2,768]{1,0:T(2,128)S(1)} %pad_maximum_fusion.2), channel_id=1, source_target_pairs={{0,6},{1,3},{2,0},{3,5},{4,2},{5,7},{6,4},{7,1},{8,14},{9,11},{10,... | collective-permute-start | bytes 18440 | tf_op jit(solution)/shard_map/ppermute | solution.py:53
  60.7 4.2 %collective-permute-start.3 = (f32[2,768]{1,0:T(2,128)S(1)}, f32[2,768]{1,0:T(2,128)S(1)}, u32[]{:S(2)}, u32[]{:S(2)}) collective-permute-start(f32[2,768]{1,0:T(2,128)S(1)} %collective-permute-done.1), channel_id=1, source_target_pairs={{0,2},{1,7},{2,4},{3,1},{4,6},{5,3},{6,0},{7,5},{8,10},{9,15},{10,... | collective-permute-start | bytes 18440 | tf_op jit(solution)/shard_map/ppermute | solution.py:53
  65.7 0.9 copy-start.5
  66.6 23.4 %copy-start.4 = (f32[8,768]{1,0:T(8,128)S(1)}, f32[8,768]{1,0:T(8,128)}, u32[]{:S(2)}) copy-start(f32[8,768]{1,0:T(8,128)} %select_reduce_fusion.refs_1_.gain_ref) | copy-start | bytes 73732
  90.3 6.8 %collective-permute-start.22 = (bf16[16,6144]{1,0:T(8,128)(2,1)S(1)}, bf16[16,6144]{1,0:T(8,128)(2,1)S(1)}, u32[]{:S(2)}, u32[]{:S(2)}) collective-permute-start(bf16[16,6144]{1,0:T(8,128)(2,1)S(1)} %get-tuple-element.43), channel_id=1, source_target_pairs={{0,16},{1,17},{2,18},{3,19},{4,20},{5,21},{6,22},{7,23},{8,24},{9,... | collective-permute-start | bytes 589832 | tf_op jit(solution)/shard_map/ppermute | solution.py:53
  90.8 8.4 %collective-permute-start.21 = (bf16[16,6144]{1,0:T(8,128)(2,1)S(1)}, bf16[16,6144]{1,0:T(8,128)(2,1)S(1)}, u32[]{:S(2)}, u32[]{:S(2)}) collective-permute-start(bf16[16,6144]{1,0:T(8,128)(2,1)S(1)} %get-tuple-element.43), channel_id=1, source_target_pairs={{0,24},{1,25},{2,26},{3,27},{4,28},{5,29},{6,30},{7,31},{8,0},{9,1... | collective-permute-start | bytes 589832 | tf_op jit(solution)/shard_map/ppermute | solution.py:53
  93.0 8.9 %collective-permute-start.20 = (bf16[16,6144]{1,0:T(8,128)(2,1)S(1)}, bf16[16,6144]{1,0:T(8,128)(2,1)S(1)}, u32[]{:S(2)}, u32[]{:S(2)}) collective-permute-start(bf16[16,6144]{1,0:T(8,128)(2,1)S(1)} %get-tuple-element.43), channel_id=1, source_target_pairs={{0,8},{1,9},{2,10},{3,11},{4,12},{5,13},{6,14},{7,15},{8,16},{9,17... | collective-permute-start | bytes 589832 | tf_op jit(solution)/shard_map/ppermute | solution.py:53
  93.0 9.6 %collective-permute-start.6 = (bf16[16,6144]{1,0:T(8,128)(2,1)S(1)}, bf16[16,6144]{1,0:T(8,128)(2,1)S(1)}, u32[]{:S(2)}, u32[]{:S(2)}) collective-permute-start(bf16[16,6144]{1,0:T(8,128)(2,1)S(1)} %get-tuple-element.31), channel_id=1, source_target_pairs={{0,64},{1,65},{2,66},{3,67},{4,68},{5,69},{6,70},{7,71},{8,72},{9,... | collective-permute-start | bytes 589832 | tf_op jit(solution)/shard_map/ppermute | solution.py:53
  93.6 9.1 %collective-permute-start.5 = (bf16[16,6144]{1,0:T(8,128)(2,1)S(1)}, bf16[16,6144]{1,0:T(8,128)(2,1)S(1)}, u32[]{:S(2)}, u32[]{:S(2)}) collective-permute-start(bf16[16,6144]{1,0:T(8,128)(2,1)S(1)} %get-tuple-element.31), channel_id=1, source_target_pairs={{0,96},{1,97},{2,98},{3,99},{4,100},{5,101},{6,102},{7,103},{8,104... | collective-permute-start | bytes 589832 | tf_op jit(solution)/shard_map/ppermute | solution.py:53
  97.1 7.2 %collective-permute-start.4 = (bf16[16,6144]{1,0:T(8,128)(2,1)S(1)}, bf16[16,6144]{1,0:T(8,128)(2,1)S(1)}, u32[]{:S(2)}, u32[]{:S(2)}) collective-permute-start(bf16[16,6144]{1,0:T(8,128)(2,1)S(1)} %get-tuple-element.31), channel_id=1, source_target_pairs={{0,32},{1,33},{2,34},{3,35},{4,36},{5,37},{6,38},{7,39},{8,40},{9,... | collective-permute-start | bytes 589832 | tf_op jit(solution)/shard_map/ppermute | solution.py:53
  102.0 23.2 %copy-start.17 = (f32[1536]{0:T(1024)S(1)}, f32[1536]{0:T(1024)}, u32[]{:S(2)}) copy-start(f32[1536]{0:T(1024)} %param.19) | copy-start | bytes 18436
  102.1 28.2 %copy-start.8 = (bf16[4,16,6144]{2,1,0:T(8,128)(2,1)}, bf16[4,16,6144]{2,1,0:T(8,128)(2,1)S(1)}, u32[]{:S(2)}) copy-start(bf16[4,16,6144]{2,1,0:T(8,128)(2,1)S(1)} %pad_maximum_fusion.1) | copy-start | bytes 2359300
  102.1 12.8 %collective-permute-start.23 = (bf16[64,6144]{1,0:T(8,128)(2,1)S(1)}, bf16[64,6144]{1,0:T(8,128)(2,1)S(1)}, u32[]{:S(2)}, u32[]{:S(2)}) collective-permute-start(bf16[64,6144]{1,0:T(8,128)(2,1)S(1)} %bitcast.48), channel_id=1, source_target_pairs={{0,32},{1,97},{2,34},{3,99},{4,36},{5,101},{6,38},{7,103},{8,40},{... | collective-permute-start | bytes 2359304 | tf_op jit(solution)/shard_map/ppermute | solution.py:53
  104.4 37.7 %copy-start.7 = (bf16[4,16,6144]{2,1,0:T(8,128)(2,1)}, bf16[4,16,6144]{2,1,0:T(8,128)(2,1)S(1)}, u32[]{:S(2)}) copy-start(bf16[4,16,6144]{2,1,0:T(8,128)(2,1)S(1)} %pad_maximum_fusion) | copy-start | bytes 2359300
  104.4 18.2 %collective-permute-start.7 = (bf16[64,6144]{1,0:T(8,128)(2,1)S(1)}, bf16[64,6144]{1,0:T(8,128)(2,1)S(1)}, u32[]{:S(2)}, u32[]{:S(2)}) collective-permute-start(bf16[64,6144]{1,0:T(8,128)(2,1)S(1)} %bitcast.45), channel_id=1, source_target_pairs={{0,8},{1,25},{2,10},{3,27},{4,12},{5,29},{6,14},{7,31},{8,16},{9,1... | collective-permute-start | bytes 2359304 | tf_op jit(solution)/shard_map/ppermute | solution.py:53
  106.7 19.1 %collective-permute-start.24 = (bf16[64,6144]{1,0:T(8,128)(2,1)S(1)}, bf16[64,6144]{1,0:T(8,128)(2,1)S(1)}, u32[]{:S(2)}, u32[]{:S(2)}) collective-permute-start(bf16[64,6144]{1,0:T(8,128)(2,1)S(1)} %bitcast.49), channel_id=1, source_target_pairs={{0,96},{1,33},{2,98},{3,35},{4,100},{5,37},{6,102},{7,39},{8,104},... | collective-permute-start | bytes 2359304 | tf_op jit(solution)/shard_map/ppermute | solution.py:53
  114.9 10.9 %copy-start.10 = (bf16[64,6144]{1,0:T(8,128)(2,1)}, bf16[64,6144]{1,0:T(8,128)(2,1)S(1)}, u32[]{:S(2)}) copy-start(bf16[64,6144]{1,0:T(8,128)(2,1)S(1)} %collective-permute-done.23.refs_1_) | copy-start | bytes 2359300
  114.9 15.4 %collective-permute-start.25 = (bf16[64,6144]{1,0:T(8,128)(2,1)S(1)}, bf16[64,6144]{1,0:T(8,128)(2,1)}, u32[]{:S(2)}, u32[]{:S(2)}) collective-permute-start(bf16[64,6144]{1,0:T(8,128)(2,1)S(1)} %collective-permute-done.23.refs_1_), channel_id=1, source_target_pairs={{0,32},{1,97},{2,34},{3,99},{4,36},{5,101},{6,38},{7,103},{8,40},{... | collective-permute-start | bytes 2359304 | tf_op jit(solution)/shard_map/ppermute | solution.py:53
  117.4 62.8 %collective-permute-start.13 = (bf16[1536,768]{1,0:T(8,128)(2,1)}, bf16[1536,768]{1,0:T(8,128)(2,1)}, u32[]{:S(2)}, u32[]{:S(2)}) collective-permute-start(bf16[1536,768]{1,0:T(8,128)(2,1)} %refs_4_.3), channel_id=1, source_target_pairs={{0,1},{1,0},{2,3},{3,2},{4,5},{5,4},{6,7},{7,6},{8,9},{9,8},{10,11... | collective-permute-start | bytes 7077896 | tf_op jit(solution)/shard_map/ppermute | solution.py:62
  122.5 22.4 %collective-permute-start.8 = (bf16[64,6144]{1,0:T(8,128)(2,1)S(1)}, bf16[64,6144]{1,0:T(8,128)(2,1)}, u32[]{:S(2)}, u32[]{:S(2)}) collective-permute-start(bf16[64,6144]{1,0:T(8,128)(2,1)S(1)} %bitcast.46), channel_id=1, source_target_pairs={{0,24},{1,9},{2,26},{3,11},{4,28},{5,13},{6,30},{7,15},{8,0},{9,17... | collective-permute-start | bytes 2359304 | tf_op jit(solution)/shard_map/ppermute | solution.py:53
  122.6 19.5 %copy-start.9 = (bf16[64,6144]{1,0:T(8,128)(2,1)}, bf16[64,6144]{1,0:T(8,128)(2,1)S(1)}, u32[]{:S(2)}) copy-start(bf16[64,6144]{1,0:T(8,128)(2,1)S(1)} %collective-permute-done.7.refs_1_) | copy-start | bytes 2359300
  122.6 22.2 %collective-permute-start.9 = (bf16[64,6144]{1,0:T(8,128)(2,1)S(1)}, bf16[64,6144]{1,0:T(8,128)(2,1)}, u32[]{:S(2)}, u32[]{:S(2)}) collective-permute-start(bf16[64,6144]{1,0:T(8,128)(2,1)S(1)} %collective-permute-done.7.refs_1_), channel_id=1, source_target_pairs={{0,8},{1,25},{2,10},{3,27},{4,12},{5,29},{6,14},{7,31},{8,16},{9,1... | collective-permute-start | bytes 2359304 | tf_op jit(solution)/shard_map/ppermute | solution.py:53
  125.8 0.9 copy-start.11
  142.1 17.3 %collective-permute-start.27 = (bf16[256,1536]{1,0:T(8,128)(2,1)}, bf16[256,1536]{1,0:T(8,128)(2,1)}, u32[]{:S(2)}, u32[]{:S(2)}) collective-permute-start(bf16[256,1536]{1,0:T(8,128)(2,1)} %shard_map.144.refs_0_), channel_id=1, source_target_pairs={{0,6},{1,3},{2,0},{3,5},{4,2},{5,7},{6,4},{7,1},{8,14},{9,11},{10,... | collective-permute-start | bytes 2359304 | tf_op jit(solution)/shard_map/ppermute | solution.py:53
  142.3 17.0 %collective-permute-start.26 = (bf16[256,1536]{1,0:T(8,128)(2,1)}, bf16[256,1536]{1,0:T(8,128)(2,1)}, u32[]{:S(2)}, u32[]{:S(2)}) collective-permute-start(bf16[256,1536]{1,0:T(8,128)(2,1)} %shard_map.144.refs_0_), channel_id=1, source_target_pairs={{0,2},{1,7},{2,4},{3,1},{4,6},{5,3},{6,0},{7,5},{8,10},{9,15},{10,... | collective-permute-start | bytes 2359304 | tf_op jit(solution)/shard_map/ppermute | solution.py:53
  156.7 18.0 %collective-permute-start.11 = (bf16[256,1536]{1,0:T(8,128)(2,1)}, bf16[256,1536]{1,0:T(8,128)(2,1)S(1)}, u32[]{:S(2)}, u32[]{:S(2)}) collective-permute-start(bf16[256,1536]{1,0:T(8,128)(2,1)} %shard_map.138.refs_0_), channel_id=1, source_target_pairs={{0,6},{1,3},{2,0},{3,5},{4,2},{5,7},{6,4},{7,1},{8,14},{9,11},{10,... | collective-permute-start | bytes 2359304 | tf_op jit(solution)/shard_map/ppermute | solution.py:53
  156.7 20.2 %collective-permute-start.10 = (bf16[256,1536]{1,0:T(8,128)(2,1)}, bf16[256,1536]{1,0:T(8,128)(2,1)}, u32[]{:S(2)}, u32[]{:S(2)}) collective-permute-start(bf16[256,1536]{1,0:T(8,128)(2,1)} %shard_map.138.refs_0_), channel_id=1, source_target_pairs={{0,2},{1,7},{2,4},{3,1},{4,6},{5,3},{6,0},{7,5},{8,10},{9,15},{10,... | collective-permute-start | bytes 2359304 | tf_op jit(solution)/shard_map/ppermute | solution.py:53
  159.4 28.4 %collective-permute-start.28 = (bf16[256,1536]{1,0:T(8,128)(2,1)}, bf16[256,1536]{1,0:T(8,128)(2,1)}, u32[]{:S(2)}, u32[]{:S(2)}) collective-permute-start(bf16[256,1536]{1,0:T(8,128)(2,1)} %get-tuple-element.44.refs_1_), channel_id=1, source_target_pairs={{0,2},{1,7},{2,4},{3,1},{4,6},{5,3},{6,0},{7,5},{8,10},{9,15},{10,... | collective-permute-start | bytes 2359304 | tf_op jit(solution)/shard_map/ppermute | solution.py:53
  174.6 2.2 copy-start.12
  176.9 22.3 %collective-permute-start.12 = (bf16[256,1536]{1,0:T(8,128)(2,1)}, bf16[256,1536]{1,0:T(8,128)(2,1)S(1)}, u32[]{:S(2)}, u32[]{:S(2)}) collective-permute-start(bf16[256,1536]{1,0:T(8,128)(2,1)} %get-tuple-element.32.refs_1_), channel_id=1, source_target_pairs={{0,2},{1,7},{2,4},{3,1},{4,6},{5,3},{6,0},{7,5},{8,10},{9,15},{10,... | collective-permute-start | bytes 2359304 | tf_op jit(solution)/shard_map/ppermute | solution.py:53
  198.6 14.9 %collective-permute-start.30 = (bf16[256,1536]{1,0:T(8,128)(2,1)}, bf16[256,1536]{1,0:T(8,128)(2,1)S(1)}, u32[]{:S(2)}, u32[]{:S(2)}) collective-permute-start(bf16[256,1536]{1,0:T(8,128)(2,1)} %get-tuple-element.49), channel_id=1, source_target_pairs={{0,96},{1,33},{2,98},{3,35},{4,100},{5,37},{6,102},{7,39},{8,104},... | collective-permute-start | bytes 2359304 | tf_op jit(solution)/shard_map/ppermute | solution.py:53
  199.2 0.9 copy-start.23
  200.1 11.2 %copy-start.22 = (bf16[256,1536]{1,0:T(8,128)(2,1)S(1)}, bf16[256,1536]{1,0:T(8,128)(2,1)}, u32[]{:S(2)}) copy-start(bf16[256,1536]{1,0:T(8,128)(2,1)} %get-tuple-element.47) | copy-start | bytes 2359300
  200.1 13.4 %copy-start.2 = (bf16[256,1536]{1,0:T(8,128)(2,1)S(1)}, bf16[256,1536]{1,0:T(8,128)(2,1)}, u32[]{:S(2)}) copy-start(bf16[256,1536]{1,0:T(8,128)(2,1)} %get-tuple-element.48.a) | copy-start | bytes 2359300
  211.1 2.7 copy-start.21
  211.1 12.6 %copy-start.3 = (bf16[256,1536]{1,0:T(8,128)(2,1)S(1)}, bf16[256,1536]{1,0:T(8,128)(2,1)}, u32[]{:S(2)}) copy-start(bf16[256,1536]{1,0:T(8,128)(2,1)} %get-tuple-element.36.a) | copy-start | bytes 2359300
  211.2 12.6 %collective-permute-start.15 = (bf16[256,1536]{1,0:T(8,128)(2,1)}, bf16[256,1536]{1,0:T(8,128)(2,1)S(1)}, u32[]{:S(2)}, u32[]{:S(2)}) collective-permute-start(bf16[256,1536]{1,0:T(8,128)(2,1)} %get-tuple-element.37), channel_id=1, source_target_pairs={{0,24},{1,9},{2,26},{3,11},{4,28},{5,13},{6,30},{7,15},{8,0},{9,17... | collective-permute-start | bytes 2359304 | tf_op jit(solution)/shard_map/ppermute | solution.py:53
  211.3 13.7 %collective-permute-start.29 = (bf16[256,1536]{1,0:T(8,128)(2,1)S(1)}, bf16[256,1536]{1,0:T(8,128)(2,1)S(1)}, u32[]{:S(2)}, u32[]{:S(2)}) collective-permute-start(bf16[256,1536]{1,0:T(8,128)(2,1)S(1)} %copy-done.22), channel_id=1, source_target_pairs={{0,32},{1,97},{2,34},{3,99},{4,36},{5,101},{6,38},{7,103},{8,40},{... | collective-permute-start | bytes 2359304 | tf_op jit(solution)/shard_map/ppermute | solution.py:53
  213.7 17.7 %copy-start.1 = (bf16[256,1536]{1,0:T(8,128)(2,1)S(1)}, bf16[256,1536]{1,0:T(8,128)(2,1)}, u32[]{:S(2)}) copy-start(bf16[256,1536]{1,0:T(8,128)(2,1)} %get-tuple-element.46.a) | copy-start | bytes 2359300
  213.7 17.7 %collective-permute-start.31 = (bf16[256,1536]{1,0:T(8,128)(2,1)S(1)}, bf16[256,1536]{1,0:T(8,128)(2,1)S(1)}, u32[]{:S(2)}, u32[]{:S(2)}) collective-permute-start(bf16[256,1536]{1,0:T(8,128)(2,1)S(1)} %shard_map.147), channel_id=1, source_target_pairs={{0,96},{1,33},{2,98},{3,35},{4,100},{5,37},{6,102},{7,39},{8,104},... | collective-permute-start | bytes 2359304 | tf_op jit(solution)/shard_map/ppermute | solution.py:53
  213.8 24.7 %collective-permute-start.14 = (bf16[256,1536]{1,0:T(8,128)(2,1)S(1)}, bf16[256,1536]{1,0:T(8,128)(2,1)S(1)}, u32[]{:S(2)}, u32[]{:S(2)}) collective-permute-start(bf16[256,1536]{1,0:T(8,128)(2,1)S(1)} %copy-done.21), channel_id=1, source_target_pairs={{0,8},{1,25},{2,10},{3,27},{4,12},{5,29},{6,14},{7,31},{8,16},{9,1... | collective-permute-start | bytes 2359304 | tf_op jit(solution)/shard_map/ppermute | solution.py:53
  224.0 16.9 %copy-start = (bf16[256,1536]{1,0:T(8,128)(2,1)S(1)}, bf16[256,1536]{1,0:T(8,128)(2,1)}, u32[]{:S(2)}) copy-start(bf16[256,1536]{1,0:T(8,128)(2,1)} %get-tuple-element.34.a) | copy-start | bytes 2359300
  224.0 16.9 %collective-permute-start.16 = (bf16[256,1536]{1,0:T(8,128)(2,1)S(1)}, bf16[256,1536]{1,0:T(8,128)(2,1)S(1)}, u32[]{:S(2)}, u32[]{:S(2)}) collective-permute-start(bf16[256,1536]{1,0:T(8,128)(2,1)S(1)} %shard_map.141), channel_id=1, source_target_pairs={{0,24},{1,9},{2,26},{3,11},{4,28},{5,13},{6,30},{7,15},{8,0},{9,17... | collective-permute-start | bytes 2359304 | tf_op jit(solution)/shard_map/ppermute | solution.py:53
  231.8 13.5 %copy-start.20 = (f32[768]{0:T(1024)S(1)}, f32[768]{0:T(1024)}, u32[]{:S(2)}) copy-start(f32[768]{0:T(1024)} %param.21) | copy-start | bytes 9220
  231.8 11.9 %collective-permute-start.32 = (bf16[64,1536]{1,0:T(8,128)(2,1)S(1)}, bf16[64,1536]{1,0:T(8,128)(2,1)S(1)}, u32[]{:S(2)}, u32[]{:S(2)}) collective-permute-start(bf16[64,1536]{1,0:T(8,128)(2,1)S(1)} %get-tuple-element.51), channel_id=1, source_target_pairs={{0,24},{1,25},{2,26},{3,27},{4,28},{5,29},{6,30},{7,31},{8,0},{9,1... | collective-permute-start | bytes 589832 | tf_op jit(solution)/shard_map/ppermute | solution.py:53
  237.3 8.0 %collective-permute-start.33 = (bf16[64,1536]{1,0:T(8,128)(2,1)S(1)}, bf16[64,1536]{1,0:T(8,128)(2,1)S(1)}, u32[]{:S(2)}, u32[]{:S(2)}) collective-permute-start(bf16[64,1536]{1,0:T(8,128)(2,1)S(1)} %get-tuple-element.52), channel_id=1, source_target_pairs={{0,8},{1,9},{2,10},{3,11},{4,12},{5,13},{6,14},{7,15},{8,16},{9,17... | collective-permute-start | bytes 589832 | tf_op jit(solution)/shard_map/ppermute | solution.py:53
  237.3 11.9 %collective-permute-start.34 = (bf16[64,1536]{1,0:T(8,128)(2,1)S(1)}, bf16[64,1536]{1,0:T(8,128)(2,1)S(1)}, u32[]{:S(2)}, u32[]{:S(2)}) collective-permute-start(bf16[64,1536]{1,0:T(8,128)(2,1)S(1)} %get-tuple-element.53), channel_id=1, source_target_pairs={{0,16},{1,17},{2,18},{3,19},{4,20},{5,21},{6,22},{7,23},{8,24},{9,... | collective-permute-start | bytes 589832 | tf_op jit(solution)/shard_map/ppermute | solution.py:53
  241.2 14.4 %collective-permute-start.17 = (bf16[64,1536]{1,0:T(8,128)(2,1)S(1)}, bf16[64,1536]{1,0:T(8,128)(2,1)S(1)}, u32[]{:S(2)}, u32[]{:S(2)}) collective-permute-start(bf16[64,1536]{1,0:T(8,128)(2,1)S(1)} %get-tuple-element.39), channel_id=1, source_target_pairs={{0,96},{1,97},{2,98},{3,99},{4,100},{5,101},{6,102},{7,103},{8,104... | collective-permute-start | bytes 589832 | tf_op jit(solution)/shard_map/ppermute | solution.py:53
  243.6 12.0 %collective-permute-start.18 = (bf16[64,1536]{1,0:T(8,128)(2,1)S(1)}, bf16[64,1536]{1,0:T(8,128)(2,1)S(1)}, u32[]{:S(2)}, u32[]{:S(2)}) collective-permute-start(bf16[64,1536]{1,0:T(8,128)(2,1)S(1)} %get-tuple-element.40), channel_id=1, source_target_pairs={{0,32},{1,33},{2,34},{3,35},{4,36},{5,37},{6,38},{7,39},{8,40},{9,... | collective-permute-start | bytes 589832 | tf_op jit(solution)/shard_map/ppermute | solution.py:53
  243.7 12.0 %collective-permute-start.19 = (bf16[64,1536]{1,0:T(8,128)(2,1)S(1)}, bf16[64,1536]{1,0:T(8,128)(2,1)S(1)}, u32[]{:S(2)}, u32[]{:S(2)}) collective-permute-start(bf16[64,1536]{1,0:T(8,128)(2,1)S(1)} %get-tuple-element.41), channel_id=1, source_target_pairs={{0,64},{1,65},{2,66},{3,67},{4,68},{5,69},{6,70},{7,71},{8,72},{9,... | collective-permute-start | bytes 589832 | tf_op jit(solution)/shard_map/ppermute | solution.py:53
  249.3 14.2 %collective-permute-start.36 = (bf16[64,768]{1,0:T(8,128)(2,1)S(1)}, bf16[64,768]{1,0:T(8,128)(2,1)S(1)}, u32[]{:S(2)}, u32[]{:S(2)}) collective-permute-start(bf16[64,768]{1,0:T(8,128)(2,1)S(1)} %get-tuple-element.56), channel_id=1, source_target_pairs={{0,1},{1,0},{2,3},{3,2},{4,5},{5,4},{6,7},{7,6},{8,9},{9,8},{10,11... | collective-permute-start | bytes 294920 | tf_op jit(solution)/shard_map/ppermute | solution.py:62
  255.7 8.0 %collective-permute-start.35 = (bf16[64,768]{1,0:T(8,128)(2,1)S(1)}, bf16[64,768]{1,0:T(8,128)(2,1)S(1)}, u32[]{:S(2)}, u32[]{:S(2)}) collective-permute-start(bf16[64,768]{1,0:T(8,128)(2,1)S(1)} %get-tuple-element.55), channel_id=1, source_target_pairs={{0,1},{1,0},{2,3},{3,2},{4,5},{5,4},{6,7},{7,6},{8,9},{9,8},{10,11... | collective-permute-start | bytes 294920 | tf_op jit(solution)/shard_map/ppermute | solution.py:62
Sparse Core Ops, SparseCore 0:
  9.0 101.7 all-gather.1

commit v10 on v9

--- a/solution.py
+++ b/solution.py
@@ -165,7 +165,7 @@
         out_specs=[pl.BlockSpec((tokens // count, tile), lambda i: (0, i))] * count,
         out_shape=[jax.ShapeDtypeStruct((tokens // count, 2 * chans), BF)] * count,
         scratch_shapes=[pltpu.VMEM((tokens, depth), BF), pltpu.SemaphoreType.DMA((SIDE,))],
-        compiler_params=params(58),
+        compiler_params=params(32),
         cost_estimate=pl.CostEstimate(
             flops=4 * tokens * depth * chans,
             bytes_accessed=2 * (tokens * depth + 2 * depth * chans + 2 * tokens * chans),
@@ -286,6 +286,7 @@
     normed = (source - mean) / jnp.sqrt(square - mean * mean + 1e-05) * gain_first
     col = jnp.dot(one, normed, precision=high).astype(BF)
     col = exchange(col.reshape(groups, -1, chans), "row").reshape(-1, chans)
+    (col,) = tie([col], early)
     spec = jnp.dot(two, col.astype(F32), precision=high)
     split = spec.shape[0] // 2
     spec_re, spec_im = spec[:split], spec[split:]
@@ -295,7 +296,6 @@
     )
     back = jnp.dot(three, filt, precision=high).astype(BF)
     back = exchange(back.reshape(groups, -1, chans), "row").reshape(-1, chans)
-    (back,) = tie([back], early)
     return source + jnp.dot(four, back.astype(F32), precision=high)
 
 

time: 273 us -> 266 us (0.974)
  blocking collectives: 34.7 us -> 50 us
  waiting for transfers between devices: 76.1 us -> 65.1 us
  starting transfers between devices: 81.3 us -> 74 us
    all_to_all x1 -> x2, blocking collectives: 21.5 us -> 38 us  [exchange(): return lax.all_to_all(a, axis, split_axis=0, concat_axis=0, tiled=True)]
    all_to_all x2 -> x1, waiting for transfers between devices: 9.73 us -> 0.01 us  [exchange(): return lax.all_to_all(a, axis, split_axis=0, concat_axis=0, tiled=True)]
    all_to_all x2 -> x1, starting transfers between devices: 11.6 us -> 7.85 us  [exchange(): return lax.all_to_all(a, axis, split_axis=0, concat_axis=0, tiled=True)]
    pallas_call x2, Pallas kernels: 21.9 us -> 19.1 us  [matmul_out(): pl.pallas_call(mm2_kernel, grid=(2 * steps,), in_specs=[pl.BlockSpec(memo...]
  transfers between devices with their start and end apart: 40 -> 39, of which waited for: 20 -> 16; matrix products, arithmetic and copies ran while one was open for 5% -> 6% of each run, Pallas kernels for 17% -> 17%
where the time goes in v10:
time: 266 us
  starting transfers between devices  74 us (28%)
  waiting for transfers between devices  65.1 us (24%)
  blocking collectives  50 us (19%)
  Pallas kernels  45.7 us (17%)
  between operations  13.7 us (5%)
  local copies, waits for them, and re-layouts  9.03 us (3%)
  matrix products  6.72 us (3%)
    ppermute x33, waiting for transfers between devices, hop(): return lax.ppermute(a, ('row', 'col'), pairs)  64.1 us
    ppermute x33, starting transfers between devices, hop(): return lax.ppermute(a, ('row', 'col'), pairs)  46.3 us
    all_to_all x2, blocking collectives, exchange(): return lax.all_to_all(a, axis, split_axis=0, concat_axis=0, tiled=True)  38 us
    pallas_call x2, Pallas kernels, matmul_in(): pl.pallas_call(mm1_kernel, grid=(width // tile,), in_specs=[pl.BlockSpec(...  23.7 us
    ppermute x4, starting transfers between devices, swap_cores(): return lax.ppermute(a, 'col', pairs)  19.8 us
    pallas_call x2, Pallas kernels, matmul_out(): pl.pallas_call(mm2_kernel, grid=(2 * steps,), in_specs=[pl.BlockSpec(memo...  19.1 us
    psum x1, blocking collectives, spectral(): lax.psum((jnp.sum(source, axis=-1), jnp.sum(source * source, axis=-1)), '...  12 us
    all_to_all x1, starting transfers between devices, exchange(): return lax.all_to_all(a, axis, split_axis=0, concat_axis=0, tiled=True)  7.85 us
  transfers between devices with their start and end apart: 39, of which 16 were waited for; matrix products, arithmetic and copies ran while one was open for 6% of the time, Pallas kernels for 17%

profile of v10, /device:TPU:1, one launch (start us, length us, event | category | flops | bytes accessed | tf_op | source)
XLA Modules:
  0.0 265.6 jit_solution(16242560887597592493)
XLA Ops:
  6.6 0.7 all-gather.2.cloned.1.call-update
  7.3 1.5 collective-permute-start
  9.1 12.0 %all-reduce = (f32[256]{0:T(256)S(1)}, f32[256]{0:T(256)S(1)}) all-reduce(f32[256]{0:T(256)S(1)} %reduce_sum.34, f32[256]{0:T(256)S(1)} %reduce_sum.32), channel_id=1, replica_groups=mesh['row'=16,'col'=8] {'col'}, use_global_device_ids=true, to_apply=%region_3.4 | all-reduce | flops 512 | bytes 4096 | tf_op jit(solution)/shard_map/psum | solution.py:281
  21.4 1.7 convolution_convert_fusion
  23.0 7.8 %all-to-all-start = ((bf16[16,32,768]{2,1,0:T(8,128)(2,1)}), bf16[16,32,768]{2,1,0:T(8,128)(2,1)S(1)}, u32[]{:S(2)}, u32[]{:S(2)}) async-start(bf16[16,32,768]{2,1,0:T(8,128)(2,1)} %bitcast.3), calls=%async_computation | async-start | bytes 1572864 | tf_op jit(solution)/shard_map/all_to_all | solution.py:253
  30.9 2.4 fusion.13
  33.3 2.4 collective-permute-start.1
  35.7 0.7 dynamic-slice_bitcast_fusion
  36.4 3.4 %collective-permute-start.3 = (f32[2,768]{1,0:T(2,128)S(1)}, f32[2,768]{1,0:T(2,128)S(1)}, u32[]{:S(2)}, u32[]{:S(2)}) collective-permute-start(f32[2,768]{1,0:T(2,128)S(1)} %collective-permute-done.1), channel_id=1, source_target_pairs={{0,2},{1,7},{2,4},{3,1},{4,6},{5,3},{6,0},{7,5},{8,10},{9,15},{10,... | collective-permute-start | bytes 18440 | tf_op jit(solution)/shard_map/ppermute | solution.py:53
  39.9 1.4 reshape_squeeze.6
  41.3 1.2 reshape_squeeze.7
  42.5 0.7 select_reduce_fusion.refs_1_.gain_ref
  43.2 0.9 copy-done.3
  44.1 2.6 fusion.15
  46.7 0.9 fusion.5
  47.7 1.0 add_convert_fusion
  48.7 17.1 %all_to_all.15 = bf16[16,32,768]{2,1,0:T(8,128)(2,1)S(1)} all-to-all(bf16[16,32,768]{2,1,0:T(8,128)(2,1)S(1)} %bitcast.51), channel_id=1, replica_groups=mesh['row'=16,'col'=8] {'row'}, dimensions={0} | all-to-all | bytes 1572864 | tf_op jit(solution)/shard_map/all_to_all | solution.py:253
  65.8 0.6 fusion.14
  66.4 20.9 %all_to_all.16.moved_ref = bf16[8,32,768]{2,1,0:T(8,128)(2,1)S(1)} all-to-all(bf16[8,32,768]{2,1,0:T(8,128)(2,1)S(1)} %bitcast.53), channel_id=1, replica_groups=mesh['row'=16,'col'=8] {'col'}, dimensions={0} | all-to-all | bytes 786432 | tf_op jit(solution)/shard_map/all_to_all | solution.py:253
  87.6 0.7 collective-permute-start.22
  88.3 2.0 collective-permute-start.21
  90.4 0.6 collective-permute-start.6
  90.9 1.6 collective-permute-start.5
  92.5 1.9 collective-permute-done.22
  94.4 2.4 collective-permute-done.21
  96.8 2.5 collective-permute-done.20
  99.5 0.6 collective-permute-start.23
  100.1 1.5 collective-permute-done.4
  101.7 1.7 collective-permute-start.7
  103.4 1.2 collective-permute-start.24
  104.7 7.6 %collective-permute-done.23.refs_1_ = bf16[64,6144]{1,0:T(8,128)(2,1)S(1)} collective-permute-done((bf16[64,6144]{1,0:T(8,128)(2,1)S(1)}, bf16[64,6144]{1,0:T(8,128)(2,1)S(1)}, u32[]{:S(2)}, u32[]{:S(2)}) %collective-permute-start.23) | collective-permute-done | bytes 786464 | tf_op jit(solution)/shard_map/ppermute | solution.py:53
  112.2 2.6 collective-permute-start.25
  114.9 5.5 %collective-permute-start.13 = (bf16[1536,768]{1,0:T(8,128)(2,1)}, bf16[1536,768]{1,0:T(8,128)(2,1)}, u32[]{:S(2)}, u32[]{:S(2)}) collective-permute-start(bf16[1536,768]{1,0:T(8,128)(2,1)} %refs_4_.3), channel_id=1, source_target_pairs={{0,1},{1,0},{2,3},{3,2},{4,5},{5,4},{6,7},{7,6},{8,9},{9,8},{10,11... | collective-permute-start | bytes 7077896 | tf_op jit(solution)/shard_map/ppermute | solution.py:62
  120.4 2.7 %collective-permute-start.9 = (bf16[64,6144]{1,0:T(8,128)(2,1)S(1)}, bf16[64,6144]{1,0:T(8,128)(2,1)}, u32[]{:S(2)}, u32[]{:S(2)}) collective-permute-start(bf16[64,6144]{1,0:T(8,128)(2,1)S(1)} %collective-permute-done.7.refs_1_), channel_id=1, source_target_pairs={{0,8},{1,25},{2,10},{3,27},{4,12},{5,29},{6,14},{7,31},{8,16},{9,1... | collective-permute-start | bytes 2359304 | tf_op jit(solution)/shard_map/ppermute | solution.py:53
  123.1 0.6 broadcast_in_dim.35.refs_5_
  123.7 0.9 copy-done.10
  124.6 3.0 %collective-permute-done.25.refs_3_ = bf16[64,6144]{1,0:T(8,128)(2,1)} collective-permute-done((bf16[64,6144]{1,0:T(8,128)(2,1)S(1)}, bf16[64,6144]{1,0:T(8,128)(2,1)}, u32[]{:S(2)}, u32[]{:S(2)}) %collective-permute-start.25) | collective-permute-done | bytes 786464 | tf_op jit(solution)/shard_map/ppermute | solution.py:53
  127.6 11.9 %shard_map.144.refs_0_ = bf16[256,1536]{1,0:T(8,128)(2,1)} custom-call(bf16[64,6144]{1,0:T(8,128)(2,1)} %bitcast.50, bf16[64,6144]{1,0:T(8,128)(2,1)} %copy-done.9, bf16[64,6144]{1,0:T(8,128)(2,1)} %copy-done.10, bf16[64,6144]{1,0:T(8,128)(2,1)} %collective-permute-done.25.refs_3_, bf16[6144,1536]{1,0:T(8,128)(2,1)} %all-gather.2.cloned.1.call-done.refs_4_, ...), custom_call_target="tpu_custom_call" | custom-call | flops 4831838208 | bytes 22020096 | tf_op jit(solution)/shard_map/pallas_call | solution.py:100
  139.8 2.5 collective-permute-start.26
  142.3 11.8 %shard_map.138.refs_0_ = bf16[256,1536]{1,0:T(8,128)(2,1)} custom-call(bf16[64,6144]{1,0:T(8,128)(2,1)} %bitcast.47, bf16[64,6144]{1,0:T(8,128)(2,1)} %copy-done.8, bf16[64,6144]{1,0:T(8,128)(2,1)} %collective-permute-done.8.refs_2_, bf16[64,6144]{1,0:T(8,128)(2,1)} %collective-permute-done.9.refs_3_, ...), custom_call_target="tpu_custom_call" | custom-call | flops 4831838208 | bytes 22020096 | tf_op jit(solution)/shard_map/pallas_call | solution.py:100
  154.1 2.7 %collective-permute-start.10 = (bf16[256,1536]{1,0:T(8,128)(2,1)}, bf16[256,1536]{1,0:T(8,128)(2,1)}, u32[]{:S(2)}, u32[]{:S(2)}) collective-permute-start(bf16[256,1536]{1,0:T(8,128)(2,1)} %shard_map.138.refs_0_), channel_id=1, source_target_pairs={{0,2},{1,7},{2,4},{3,1},{4,6},{5,3},{6,0},{7,5},{8,10},{9,15},{10,... | collective-permute-start | bytes 2359304 | tf_op jit(solution)/shard_map/ppermute | solution.py:53
  156.8 1.7 collective-permute-start.28
  158.5 13.0 %collective-permute-done.11.refs_1_ = bf16[256,1536]{1,0:T(8,128)(2,1)} collective-permute-done((bf16[256,1536]{1,0:T(8,128)(2,1)}, bf16[256,1536]{1,0:T(8,128)(2,1)}, u32[]{:S(2)}, u32[]{:S(2)}) %collective-permute-start.11) | collective-permute-done | bytes 786464 | tf_op jit(solution)/shard_map/ppermute | solution.py:53
  171.5 2.2 collective-permute-done.10.refs_0_
  173.7 3.4 %collective-permute-start.12 = (bf16[256,1536]{1,0:T(8,128)(2,1)}, bf16[256,1536]{1,0:T(8,128)(2,1)S(1)}, u32[]{:S(2)}, u32[]{:S(2)}) collective-permute-start(bf16[256,1536]{1,0:T(8,128)(2,1)} %get-tuple-element.32.refs_1_), channel_id=1, source_target_pairs={{0,2},{1,7},{2,4},{3,1},{4,6},{5,3},{6,0},{7,5},{8,10},{9,15},{10,... | collective-permute-start | bytes 2359304 | tf_op jit(solution)/shard_map/ppermute | solution.py:53
  177.1 8.1 %collective-permute-done.28.refs_3_ = bf16[256,1536]{1,0:T(8,128)(2,1)} collective-permute-done((bf16[256,1536]{1,0:T(8,128)(2,1)}, bf16[256,1536]{1,0:T(8,128)(2,1)}, u32[]{:S(2)}, u32[]{:S(2)}) %collective-permute-start.28) | collective-permute-done | bytes 786464 | tf_op jit(solution)/shard_map/ppermute | solution.py:53
  185.2 9.7 %shard_map.146 = (bf16[256,1536]{1,0:T(8,128)(2,1)S(1)}, bf16[256,1536]{1,0:T(8,128)(2,1)S(1)}, bf16[256,1536]{1,0:T(8,128)(2,1)S(1)}, bf16[256,1536]{1,0:T(8,128)(2,1)S(1)}) custom-call(bf16[256,1536]{1,0:T(8,128)(2,1)S(1)} %copy-done, bf16[256,1536]{1,0:T(8,128)(2,1)} %get-tuple-element.44.refs_1_, bf16[256,1536]{1,0:T(8,128)(2,1)} %get-tuple-element.45.refs_2_, ...), custom_call_target="tpu_custom_call" | custom-call | flops 4831838208 | bytes 11010048 | tf_op jit(solution)/shard_map/pallas_call | solution.py:157
  194.9 0.5 collective-permute-start.30
  195.5 9.4 %shard_map.140 = (bf16[256,1536]{1,0:T(8,128)(2,1)S(1)}, bf16[256,1536]{1,0:T(8,128)(2,1)S(1)}, bf16[256,1536]{1,0:T(8,128)(2,1)S(1)}, bf16[256,1536]{1,0:T(8,128)(2,1)S(1)}) custom-call(bf16[256,1536]{1,0:T(8,128)(2,1)S(1)} %copy-done.1, bf16[256,1536]{1,0:T(8,128)(2,1)} %get-tuple-element.32.refs_1_, bf16[256,1536]{1,0:T(8,128)(2,1)} %get-tuple-element.33.refs_2_, ...), custom_call_target="tpu_custom_call" | custom-call | flops 4831838208 | bytes 11010048 | tf_op jit(solution)/shard_map/pallas_call | solution.py:157
  205.2 2.1 collective-permute-start.29
  207.5 2.7 %collective-permute-start.14 = (bf16[256,1536]{1,0:T(8,128)(2,1)S(1)}, bf16[256,1536]{1,0:T(8,128)(2,1)S(1)}, u32[]{:S(2)}, u32[]{:S(2)}) collective-permute-start(bf16[256,1536]{1,0:T(8,128)(2,1)S(1)} %get-tuple-element.35), channel_id=1, source_target_pairs={{0,8},{1,25},{2,10},{3,27},{4,12},{5,29},{6,14},{7,31},{8,16},{9,1... | collective-permute-start | bytes 2359304 | tf_op jit(solution)/shard_map/ppermute | solution.py:53
  210.2 7.1 %collective-permute-done.15.b = bf16[256,1536]{1,0:T(8,128)(2,1)S(1)} collective-permute-done((bf16[256,1536]{1,0:T(8,128)(2,1)S(1)}, bf16[256,1536]{1,0:T(8,128)(2,1)S(1)}, u32[]{:S(2)}, u32[]{:S(2)}) %collective-permute-start.15) | collective-permute-done | bytes 786464 | tf_op jit(solution)/shard_map/ppermute | solution.py:53
  217.6 1.3 collective-permute-done.29.b
  218.9 6.2 %collective-permute-done.31.c = bf16[256,1536]{1,0:T(8,128)(2,1)S(1)} collective-permute-done((bf16[256,1536]{1,0:T(8,128)(2,1)S(1)}, bf16[256,1536]{1,0:T(8,128)(2,1)S(1)}, u32[]{:S(2)}, u32[]{:S(2)}) %collective-permute-start.31) | collective-permute-done | bytes 786464 | tf_op jit(solution)/shard_map/ppermute | solution.py:53
  225.4 5.5 %collective-permute-start.32 = (bf16[64,1536]{1,0:T(8,128)(2,1)S(1)}, bf16[64,1536]{1,0:T(8,128)(2,1)S(1)}, u32[]{:S(2)}, u32[]{:S(2)}) collective-permute-start(bf16[64,1536]{1,0:T(8,128)(2,1)S(1)} %get-tuple-element.51), channel_id=1, source_target_pairs={{0,24},{1,25},{2,26},{3,27},{4,28},{5,29},{6,30},{7,31},{8,0},{9,1... | collective-permute-start | bytes 589832 | tf_op jit(solution)/shard_map/ppermute | solution.py:53
  231.0 1.6 collective-permute-start.34
  232.6 2.1 collective-permute-done.16.c
  235.0 2.0 collective-permute-start.17
  237.0 1.3 collective-permute-start.19
  238.3 5.1 %collective-permute-done.34.d = bf16[64,1536]{1,0:T(8,128)(2,1)S(1)} collective-permute-done((bf16[64,1536]{1,0:T(8,128)(2,1)S(1)}, bf16[64,1536]{1,0:T(8,128)(2,1)S(1)}, u32[]{:S(2)}, u32[]{:S(2)}) %collective-permute-start.34) | collective-permute-done | bytes 196640 | tf_op jit(solution)/shard_map/ppermute | solution.py:53
  243.5 5.8 %collective-permute-start.36 = (bf16[64,768]{1,0:T(8,128)(2,1)S(1)}, bf16[64,768]{1,0:T(8,128)(2,1)S(1)}, u32[]{:S(2)}, u32[]{:S(2)}) collective-permute-start(bf16[64,768]{1,0:T(8,128)(2,1)S(1)} %get-tuple-element.56), channel_id=1, source_target_pairs={{0,1},{1,0},{2,3},{3,2},{4,5},{5,4},{6,7},{7,6},{8,9},{9,8},{10,11... | collective-permute-start | bytes 294920 | tf_op jit(solution)/shard_map/ppermute | solution.py:62
  249.4 7.0 %collective-permute-start.35 = (bf16[64,768]{1,0:T(8,128)(2,1)S(1)}, bf16[64,768]{1,0:T(8,128)(2,1)S(1)}, u32[]{:S(2)}, u32[]{:S(2)}) collective-permute-start(bf16[64,768]{1,0:T(8,128)(2,1)S(1)} %get-tuple-element.55), channel_id=1, source_target_pairs={{0,1},{1,0},{2,3},{3,2},{4,5},{5,4},{6,7},{7,6},{8,9},{9,8},{10,11... | collective-permute-start | bytes 294920 | tf_op jit(solution)/shard_map/ppermute | solution.py:62
  256.4 0.7 dynamic-slice_bitcast_fusion.1.place_ref
  257.4 1.4 shard_map.150
  (96 shorter events, 3.6 us)
Async XLA Ops:
  6.5 14.8 %copy-start.14 = (f32[512,256]{1,0:T(8,128)S(1)}, f32[512,256]{1,0:T(8,128)}, u32[]{:S(2)}) copy-start(f32[512,256]{1,0:T(8,128)} %constant.29.clone) | copy-start | bytes 1572868
  6.5 0.7 copy-start.17
  6.5 2.2 copy-start.5
  6.5 14.6 %copy-start.16 = (f32[768]{0:T(1024)S(1)}, f32[768]{0:T(1024)}, u32[]{:S(2)}) copy-start(f32[768]{0:T(1024)} %param.16) | copy-start | bytes 9220
  6.5 121.1 %all-gather.2.cloned.1.call-start = ((), (), s32[]{:S(2)}) async-start(), calls=%async_computation.3 | async-start | bytes 21233664 | tf_op jit(solution)/shard_map/all_gather | solution.py:360
  7.3 26.0 %collective-permute-start = (f32[768]{0:T(1024)S(1)}, f32[768]{0:T(1024)S(1)}, u32[]{:S(2)}, u32[]{:S(2)}) collective-permute-start(f32[768]{0:T(1024)S(1)} %copy-done.17), channel_id=1, source_target_pairs={{0,1},{1,0},{2,3},{3,2},{4,5},{5,4},{6,7},{7,6},{8,9},{9,8},{10,11... | collective-permute-start | bytes 9224 | tf_op jit(solution)/shard_map/ppermute | solution.py:62
  23.0 20.2 %all-to-all-start = ((bf16[16,32,768]{2,1,0:T(8,128)(2,1)}), bf16[16,32,768]{2,1,0:T(8,128)(2,1)S(1)}, u32[]{:S(2)}, u32[]{:S(2)}) async-start(bf16[16,32,768]{2,1,0:T(8,128)(2,1)} %bitcast.3), calls=%async_computation | async-start | bytes 1572864 | tf_op jit(solution)/shard_map/all_to_all | solution.py:253
  33.3 3.2 %collective-permute-start.1 = (f32[2,768]{1,0:T(2,128)S(1)}, f32[2,768]{1,0:T(2,128)S(1)}, u32[]{:S(2)}, u32[]{:S(2)}) collective-permute-start(f32[2,768]{1,0:T(2,128)S(1)} %pad_maximum_fusion.2), channel_id=1, source_target_pairs={{0,2},{1,7},{2,4},{3,1},{4,6},{5,3},{6,0},{7,5},{8,10},{9,15},{10,... | collective-permute-start | bytes 18440 | tf_op jit(solution)/shard_map/ppermute | solution.py:53
  36.4 6.1 %collective-permute-start.2 = (f32[2,768]{1,0:T(2,128)S(1)}, f32[2,768]{1,0:T(2,128)S(1)}, u32[]{:S(2)}, u32[]{:S(2)}) collective-permute-start(f32[2,768]{1,0:T(2,128)S(1)} %pad_maximum_fusion.2), channel_id=1, source_target_pairs={{0,6},{1,3},{2,0},{3,5},{4,2},{5,7},{6,4},{7,1},{8,14},{9,11},{10,... | collective-permute-start | bytes 18440 | tf_op jit(solution)/shard_map/ppermute | solution.py:53
  36.4 6.0 %collective-permute-start.3 = (f32[2,768]{1,0:T(2,128)S(1)}, f32[2,768]{1,0:T(2,128)S(1)}, u32[]{:S(2)}, u32[]{:S(2)}) collective-permute-start(f32[2,768]{1,0:T(2,128)S(1)} %collective-permute-done.1), channel_id=1, source_target_pairs={{0,2},{1,7},{2,4},{3,1},{4,6},{5,3},{6,0},{7,5},{8,10},{9,15},{10,... | collective-permute-start | bytes 18440 | tf_op jit(solution)/shard_map/ppermute | solution.py:53
  43.2 0.9 copy-start.3
  44.1 2.6 copy-start.4
  44.1 2.6 copy-start.12
  46.7 1.0 copy-start.11
  48.7 17.1 %copy-start.13 = (f32[256,512]{1,0:T(8,128)S(1)}, f32[256,512]{1,0:T(8,128)}, u32[]{:S(2)}) copy-start(f32[256,512]{1,0:T(8,128)} %constant.32.clone) | copy-start | bytes 1572868
  65.8 21.5 %copy-start.2 = (f32[8,768]{1,0:T(8,128)S(1)}, f32[8,768]{1,0:T(8,128)}, u32[]{:S(2)}) copy-start(f32[8,768]{1,0:T(8,128)} %select_reduce_fusion.refs_1_.gain_ref) | copy-start | bytes 73732
  87.6 6.8 %collective-permute-start.22 = (bf16[16,6144]{1,0:T(8,128)(2,1)S(1)}, bf16[16,6144]{1,0:T(8,128)(2,1)S(1)}, u32[]{:S(2)}, u32[]{:S(2)}) collective-permute-start(bf16[16,6144]{1,0:T(8,128)(2,1)S(1)} %get-tuple-element.43), channel_id=1, source_target_pairs={{0,16},{1,17},{2,18},{3,19},{4,20},{5,21},{6,22},{7,23},{8,24},{9,... | collective-permute-start | bytes 589832 | tf_op jit(solution)/shard_map/ppermute | solution.py:53
  88.3 8.5 %collective-permute-start.21 = (bf16[16,6144]{1,0:T(8,128)(2,1)S(1)}, bf16[16,6144]{1,0:T(8,128)(2,1)S(1)}, u32[]{:S(2)}, u32[]{:S(2)}) collective-permute-start(bf16[16,6144]{1,0:T(8,128)(2,1)S(1)} %get-tuple-element.43), channel_id=1, source_target_pairs={{0,24},{1,25},{2,26},{3,27},{4,28},{5,29},{6,30},{7,31},{8,0},{9,1... | collective-permute-start | bytes 589832 | tf_op jit(solution)/shard_map/ppermute | solution.py:53
  90.4 9.0 %collective-permute-start.20 = (bf16[16,6144]{1,0:T(8,128)(2,1)S(1)}, bf16[16,6144]{1,0:T(8,128)(2,1)S(1)}, u32[]{:S(2)}, u32[]{:S(2)}) collective-permute-start(bf16[16,6144]{1,0:T(8,128)(2,1)S(1)} %get-tuple-element.43), channel_id=1, source_target_pairs={{0,8},{1,9},{2,10},{3,11},{4,12},{5,13},{6,14},{7,15},{8,16},{9,17... | collective-permute-start | bytes 589832 | tf_op jit(solution)/shard_map/ppermute | solution.py:53
  90.4 9.7 %collective-permute-start.6 = (bf16[16,6144]{1,0:T(8,128)(2,1)S(1)}, bf16[16,6144]{1,0:T(8,128)(2,1)S(1)}, u32[]{:S(2)}, u32[]{:S(2)}) collective-permute-start(bf16[16,6144]{1,0:T(8,128)(2,1)S(1)} %get-tuple-element.31), channel_id=1, source_target_pairs={{0,64},{1,65},{2,66},{3,67},{4,68},{5,69},{6,70},{7,71},{8,72},{9,... | collective-permute-start | bytes 589832 | tf_op jit(solution)/shard_map/ppermute | solution.py:53
  90.9 9.2 %collective-permute-start.5 = (bf16[16,6144]{1,0:T(8,128)(2,1)S(1)}, bf16[16,6144]{1,0:T(8,128)(2,1)S(1)}, u32[]{:S(2)}, u32[]{:S(2)}) collective-permute-start(bf16[16,6144]{1,0:T(8,128)(2,1)S(1)} %get-tuple-element.31), channel_id=1, source_target_pairs={{0,96},{1,97},{2,98},{3,99},{4,100},{5,101},{6,102},{7,103},{8,104... | collective-permute-start | bytes 589832 | tf_op jit(solution)/shard_map/ppermute | solution.py:53
  94.4 7.2 %collective-permute-start.4 = (bf16[16,6144]{1,0:T(8,128)(2,1)S(1)}, bf16[16,6144]{1,0:T(8,128)(2,1)S(1)}, u32[]{:S(2)}, u32[]{:S(2)}) collective-permute-start(bf16[16,6144]{1,0:T(8,128)(2,1)S(1)} %get-tuple-element.31), channel_id=1, source_target_pairs={{0,32},{1,33},{2,34},{3,35},{4,36},{5,37},{6,38},{7,39},{8,40},{9,... | collective-permute-start | bytes 589832 | tf_op jit(solution)/shard_map/ppermute | solution.py:53
  99.3 23.8 %copy-start.15 = (f32[1536]{0:T(1024)S(1)}, f32[1536]{0:T(1024)}, u32[]{:S(2)}) copy-start(f32[1536]{0:T(1024)} %param.19) | copy-start | bytes 18436
  99.4 28.2 %copy-start.7 = (bf16[4,16,6144]{2,1,0:T(8,128)(2,1)}, bf16[4,16,6144]{2,1,0:T(8,128)(2,1)S(1)}, u32[]{:S(2)}) copy-start(bf16[4,16,6144]{2,1,0:T(8,128)(2,1)S(1)} %pad_maximum_fusion.1) | copy-start | bytes 2359300
  99.5 12.8 %collective-permute-start.23 = (bf16[64,6144]{1,0:T(8,128)(2,1)S(1)}, bf16[64,6144]{1,0:T(8,128)(2,1)S(1)}, u32[]{:S(2)}, u32[]{:S(2)}) collective-permute-start(bf16[64,6144]{1,0:T(8,128)(2,1)S(1)} %bitcast.48), channel_id=1, source_target_pairs={{0,32},{1,97},{2,34},{3,99},{4,36},{5,101},{6,38},{7,103},{8,40},{... | collective-permute-start | bytes 2359304 | tf_op jit(solution)/shard_map/ppermute | solution.py:53
  101.7 37.8 %copy-start.6 = (bf16[4,16,6144]{2,1,0:T(8,128)(2,1)}, bf16[4,16,6144]{2,1,0:T(8,128)(2,1)S(1)}, u32[]{:S(2)}) copy-start(bf16[4,16,6144]{2,1,0:T(8,128)(2,1)S(1)} %pad_maximum_fusion) | copy-start | bytes 2359300
  101.7 18.7 %collective-permute-start.7 = (bf16[64,6144]{1,0:T(8,128)(2,1)S(1)}, bf16[64,6144]{1,0:T(8,128)(2,1)S(1)}, u32[]{:S(2)}, u32[]{:S(2)}) collective-permute-start(bf16[64,6144]{1,0:T(8,128)(2,1)S(1)} %bitcast.45), channel_id=1, source_target_pairs={{0,8},{1,25},{2,10},{3,27},{4,12},{5,29},{6,14},{7,31},{8,16},{9,1... | collective-permute-start | bytes 2359304 | tf_op jit(solution)/shard_map/ppermute | solution.py:53
  103.4 20.3 %collective-permute-start.24 = (bf16[64,6144]{1,0:T(8,128)(2,1)S(1)}, bf16[64,6144]{1,0:T(8,128)(2,1)S(1)}, u32[]{:S(2)}, u32[]{:S(2)}) collective-permute-start(bf16[64,6144]{1,0:T(8,128)(2,1)S(1)} %bitcast.49), channel_id=1, source_target_pairs={{0,96},{1,33},{2,98},{3,35},{4,100},{5,37},{6,102},{7,39},{8,104},... | collective-permute-start | bytes 2359304 | tf_op jit(solution)/shard_map/ppermute | solution.py:53
  112.2 11.5 %copy-start.9 = (bf16[64,6144]{1,0:T(8,128)(2,1)}, bf16[64,6144]{1,0:T(8,128)(2,1)S(1)}, u32[]{:S(2)}) copy-start(bf16[64,6144]{1,0:T(8,128)(2,1)S(1)} %collective-permute-done.23.refs_1_) | copy-start | bytes 2359300
  112.2 15.4 %collective-permute-start.25 = (bf16[64,6144]{1,0:T(8,128)(2,1)S(1)}, bf16[64,6144]{1,0:T(8,128)(2,1)}, u32[]{:S(2)}, u32[]{:S(2)}) collective-permute-start(bf16[64,6144]{1,0:T(8,128)(2,1)S(1)} %collective-permute-done.23.refs_1_), channel_id=1, source_target_pairs={{0,32},{1,97},{2,34},{3,99},{4,36},{5,101},{6,38},{7,103},{8,40},{... | collective-permute-start | bytes 2359304 | tf_op jit(solution)/shard_map/ppermute | solution.py:53
  114.9 62.2 %collective-permute-start.13 = (bf16[1536,768]{1,0:T(8,128)(2,1)}, bf16[1536,768]{1,0:T(8,128)(2,1)}, u32[]{:S(2)}, u32[]{:S(2)}) collective-permute-start(bf16[1536,768]{1,0:T(8,128)(2,1)} %refs_4_.3), channel_id=1, source_target_pairs={{0,1},{1,0},{2,3},{3,2},{4,5},{5,4},{6,7},{7,6},{8,9},{9,8},{10,11... | collective-permute-start | bytes 7077896 | tf_op jit(solution)/shard_map/ppermute | solution.py:62
  120.4 21.8 %collective-permute-start.8 = (bf16[64,6144]{1,0:T(8,128)(2,1)S(1)}, bf16[64,6144]{1,0:T(8,128)(2,1)}, u32[]{:S(2)}, u32[]{:S(2)}) collective-permute-start(bf16[64,6144]{1,0:T(8,128)(2,1)S(1)} %bitcast.46), channel_id=1, source_target_pairs={{0,24},{1,9},{2,26},{3,11},{4,28},{5,13},{6,30},{7,15},{8,0},{9,17... | collective-permute-start | bytes 2359304 | tf_op jit(solution)/shard_map/ppermute | solution.py:53
  120.4 19.1 %copy-start.8 = (bf16[64,6144]{1,0:T(8,128)(2,1)}, bf16[64,6144]{1,0:T(8,128)(2,1)S(1)}, u32[]{:S(2)}) copy-start(bf16[64,6144]{1,0:T(8,128)(2,1)S(1)} %collective-permute-done.7.refs_1_) | copy-start | bytes 2359300
  120.4 21.8 %collective-permute-start.9 = (bf16[64,6144]{1,0:T(8,128)(2,1)S(1)}, bf16[64,6144]{1,0:T(8,128)(2,1)}, u32[]{:S(2)}, u32[]{:S(2)}) collective-permute-start(bf16[64,6144]{1,0:T(8,128)(2,1)S(1)} %collective-permute-done.7.refs_1_), channel_id=1, source_target_pairs={{0,8},{1,25},{2,10},{3,27},{4,12},{5,29},{6,14},{7,31},{8,16},{9,1... | collective-permute-start | bytes 2359304 | tf_op jit(solution)/shard_map/ppermute | solution.py:53
  123.7 0.9 copy-start.10
  139.5 17.3 %collective-permute-start.27 = (bf16[256,1536]{1,0:T(8,128)(2,1)}, bf16[256,1536]{1,0:T(8,128)(2,1)}, u32[]{:S(2)}, u32[]{:S(2)}) collective-permute-start(bf16[256,1536]{1,0:T(8,128)(2,1)} %shard_map.144.refs_0_), channel_id=1, source_target_pairs={{0,6},{1,3},{2,0},{3,5},{4,2},{5,7},{6,4},{7,1},{8,14},{9,11},{10,... | collective-permute-start | bytes 2359304 | tf_op jit(solution)/shard_map/ppermute | solution.py:53
  139.8 17.0 %collective-permute-start.26 = (bf16[256,1536]{1,0:T(8,128)(2,1)}, bf16[256,1536]{1,0:T(8,128)(2,1)}, u32[]{:S(2)}, u32[]{:S(2)}) collective-permute-start(bf16[256,1536]{1,0:T(8,128)(2,1)} %shard_map.144.refs_0_), channel_id=1, source_target_pairs={{0,2},{1,7},{2,4},{3,1},{4,6},{5,3},{6,0},{7,5},{8,10},{9,15},{10,... | collective-permute-start | bytes 2359304 | tf_op jit(solution)/shard_map/ppermute | solution.py:53
  154.1 31.1 %copy-start = (bf16[256,1536]{1,0:T(8,128)(2,1)S(1)}, bf16[256,1536]{1,0:T(8,128)(2,1)}, u32[]{:S(2)}) copy-start(bf16[256,1536]{1,0:T(8,128)(2,1)} %shard_map.144.refs_0_) | copy-start | bytes 2359300
  154.1 17.4 %collective-permute-start.11 = (bf16[256,1536]{1,0:T(8,128)(2,1)}, bf16[256,1536]{1,0:T(8,128)(2,1)}, u32[]{:S(2)}, u32[]{:S(2)}) collective-permute-start(bf16[256,1536]{1,0:T(8,128)(2,1)} %shard_map.138.refs_0_), channel_id=1, source_target_pairs={{0,6},{1,3},{2,0},{3,5},{4,2},{5,7},{6,4},{7,1},{8,14},{9,11},{10,... | collective-permute-start | bytes 2359304 | tf_op jit(solution)/shard_map/ppermute | solution.py:53
  154.1 19.6 %collective-permute-start.10 = (bf16[256,1536]{1,0:T(8,128)(2,1)}, bf16[256,1536]{1,0:T(8,128)(2,1)}, u32[]{:S(2)}, u32[]{:S(2)}) collective-permute-start(bf16[256,1536]{1,0:T(8,128)(2,1)} %shard_map.138.refs_0_), channel_id=1, source_target_pairs={{0,2},{1,7},{2,4},{3,1},{4,6},{5,3},{6,0},{7,5},{8,10},{9,15},{10,... | collective-permute-start | bytes 2359304 | tf_op jit(solution)/shard_map/ppermute | solution.py:53
  156.8 28.4 %collective-permute-start.28 = (bf16[256,1536]{1,0:T(8,128)(2,1)}, bf16[256,1536]{1,0:T(8,128)(2,1)}, u32[]{:S(2)}, u32[]{:S(2)}) collective-permute-start(bf16[256,1536]{1,0:T(8,128)(2,1)} %get-tuple-element.44.refs_1_), channel_id=1, source_target_pairs={{0,2},{1,7},{2,4},{3,1},{4,6},{5,3},{6,0},{7,5},{8,10},{9,15},{10,... | collective-permute-start | bytes 2359304 | tf_op jit(solution)/shard_map/ppermute | solution.py:53
  173.7 21.8 %collective-permute-start.12 = (bf16[256,1536]{1,0:T(8,128)(2,1)}, bf16[256,1536]{1,0:T(8,128)(2,1)S(1)}, u32[]{:S(2)}, u32[]{:S(2)}) collective-permute-start(bf16[256,1536]{1,0:T(8,128)(2,1)} %get-tuple-element.32.refs_1_), channel_id=1, source_target_pairs={{0,2},{1,7},{2,4},{3,1},{4,6},{5,3},{6,0},{7,5},{8,10},{9,15},{10,... | collective-permute-start | bytes 2359304 | tf_op jit(solution)/shard_map/ppermute | solution.py:53
  185.2 10.3 %copy-start.1 = (bf16[256,1536]{1,0:T(8,128)(2,1)S(1)}, bf16[256,1536]{1,0:T(8,128)(2,1)}, u32[]{:S(2)}) copy-start(bf16[256,1536]{1,0:T(8,128)(2,1)} %shard_map.138.refs_0_) | copy-start | bytes 2359300
  194.9 12.3 %collective-permute-start.30 = (bf16[256,1536]{1,0:T(8,128)(2,1)S(1)}, bf16[256,1536]{1,0:T(8,128)(2,1)S(1)}, u32[]{:S(2)}, u32[]{:S(2)}) collective-permute-start(bf16[256,1536]{1,0:T(8,128)(2,1)S(1)} %get-tuple-element.49), channel_id=1, source_target_pairs={{0,96},{1,33},{2,98},{3,35},{4,100},{5,37},{6,102},{7,39},{8,104},... | collective-permute-start | bytes 2359304 | tf_op jit(solution)/shard_map/ppermute | solution.py:53
  204.9 12.4 %collective-permute-start.15 = (bf16[256,1536]{1,0:T(8,128)(2,1)S(1)}, bf16[256,1536]{1,0:T(8,128)(2,1)S(1)}, u32[]{:S(2)}, u32[]{:S(2)}) collective-permute-start(bf16[256,1536]{1,0:T(8,128)(2,1)S(1)} %get-tuple-element.37), channel_id=1, source_target_pairs={{0,24},{1,9},{2,26},{3,11},{4,28},{5,13},{6,30},{7,15},{8,0},{9,17... | collective-permute-start | bytes 2359304 | tf_op jit(solution)/shard_map/ppermute | solution.py:53
  205.2 13.7 %collective-permute-start.29 = (bf16[256,1536]{1,0:T(8,128)(2,1)S(1)}, bf16[256,1536]{1,0:T(8,128)(2,1)S(1)}, u32[]{:S(2)}, u32[]{:S(2)}) collective-permute-start(bf16[256,1536]{1,0:T(8,128)(2,1)S(1)} %get-tuple-element.47), channel_id=1, source_target_pairs={{0,32},{1,97},{2,34},{3,99},{4,36},{5,101},{6,38},{7,103},{8,40},{... | collective-permute-start | bytes 2359304 | tf_op jit(solution)/shard_map/ppermute | solution.py:53
  207.5 17.6 %collective-permute-start.31 = (bf16[256,1536]{1,0:T(8,128)(2,1)S(1)}, bf16[256,1536]{1,0:T(8,128)(2,1)S(1)}, u32[]{:S(2)}, u32[]{:S(2)}) collective-permute-start(bf16[256,1536]{1,0:T(8,128)(2,1)S(1)} %shard_map.147), channel_id=1, source_target_pairs={{0,96},{1,33},{2,98},{3,35},{4,100},{5,37},{6,102},{7,39},{8,104},... | collective-permute-start | bytes 2359304 | tf_op jit(solution)/shard_map/ppermute | solution.py:53
  207.5 25.1 %collective-permute-start.14 = (bf16[256,1536]{1,0:T(8,128)(2,1)S(1)}, bf16[256,1536]{1,0:T(8,128)(2,1)S(1)}, u32[]{:S(2)}, u32[]{:S(2)}) collective-permute-start(bf16[256,1536]{1,0:T(8,128)(2,1)S(1)} %get-tuple-element.35), channel_id=1, source_target_pairs={{0,8},{1,25},{2,10},{3,27},{4,12},{5,29},{6,14},{7,31},{8,16},{9,1... | collective-permute-start | bytes 2359304 | tf_op jit(solution)/shard_map/ppermute | solution.py:53
  217.5 17.1 %collective-permute-start.16 = (bf16[256,1536]{1,0:T(8,128)(2,1)S(1)}, bf16[256,1536]{1,0:T(8,128)(2,1)S(1)}, u32[]{:S(2)}, u32[]{:S(2)}) collective-permute-start(bf16[256,1536]{1,0:T(8,128)(2,1)S(1)} %shard_map.141), channel_id=1, source_target_pairs={{0,24},{1,9},{2,26},{3,11},{4,28},{5,13},{6,30},{7,15},{8,0},{9,17... | collective-permute-start | bytes 2359304 | tf_op jit(solution)/shard_map/ppermute | solution.py:53
  225.4 12.8 %copy-start.18 = (f32[768]{0:T(1024)S(1)}, f32[768]{0:T(1024)}, u32[]{:S(2)}) copy-start(f32[768]{0:T(1024)} %param.21) | copy-start | bytes 9220
  225.4 11.5 %collective-permute-start.32 = (bf16[64,1536]{1,0:T(8,128)(2,1)S(1)}, bf16[64,1536]{1,0:T(8,128)(2,1)S(1)}, u32[]{:S(2)}, u32[]{:S(2)}) collective-permute-start(bf16[64,1536]{1,0:T(8,128)(2,1)S(1)} %get-tuple-element.51), channel_id=1, source_target_pairs={{0,24},{1,25},{2,26},{3,27},{4,28},{5,29},{6,30},{7,31},{8,0},{9,1... | collective-permute-start | bytes 589832 | tf_op jit(solution)/shard_map/ppermute | solution.py:53
  231.0 7.3 %collective-permute-start.33 = (bf16[64,1536]{1,0:T(8,128)(2,1)S(1)}, bf16[64,1536]{1,0:T(8,128)(2,1)S(1)}, u32[]{:S(2)}, u32[]{:S(2)}) collective-permute-start(bf16[64,1536]{1,0:T(8,128)(2,1)S(1)} %get-tuple-element.52), channel_id=1, source_target_pairs={{0,8},{1,9},{2,10},{3,11},{4,12},{5,13},{6,14},{7,15},{8,16},{9,17... | collective-permute-start | bytes 589832 | tf_op jit(solution)/shard_map/ppermute | solution.py:53
  231.0 12.4 %collective-permute-start.34 = (bf16[64,1536]{1,0:T(8,128)(2,1)S(1)}, bf16[64,1536]{1,0:T(8,128)(2,1)S(1)}, u32[]{:S(2)}, u32[]{:S(2)}) collective-permute-start(bf16[64,1536]{1,0:T(8,128)(2,1)S(1)} %get-tuple-element.53), channel_id=1, source_target_pairs={{0,16},{1,17},{2,18},{3,19},{4,20},{5,21},{6,22},{7,23},{8,24},{9,... | collective-permute-start | bytes 589832 | tf_op jit(solution)/shard_map/ppermute | solution.py:53
  235.0 14.3 %collective-permute-start.17 = (bf16[64,1536]{1,0:T(8,128)(2,1)S(1)}, bf16[64,1536]{1,0:T(8,128)(2,1)S(1)}, u32[]{:S(2)}, u32[]{:S(2)}) collective-permute-start(bf16[64,1536]{1,0:T(8,128)(2,1)S(1)} %get-tuple-element.39), channel_id=1, source_target_pairs={{0,96},{1,97},{2,98},{3,99},{4,100},{5,101},{6,102},{7,103},{8,104... | collective-permute-start | bytes 589832 | tf_op jit(solution)/shard_map/ppermute | solution.py:53
  237.0 12.3 %collective-permute-start.18 = (bf16[64,1536]{1,0:T(8,128)(2,1)S(1)}, bf16[64,1536]{1,0:T(8,128)(2,1)S(1)}, u32[]{:S(2)}, u32[]{:S(2)}) collective-permute-start(bf16[64,1536]{1,0:T(8,128)(2,1)S(1)} %get-tuple-element.40), channel_id=1, source_target_pairs={{0,32},{1,33},{2,34},{3,35},{4,36},{5,37},{6,38},{7,39},{8,40},{9,... | collective-permute-start | bytes 589832 | tf_op jit(solution)/shard_map/ppermute | solution.py:53
  237.0 12.3 %collective-permute-start.19 = (bf16[64,1536]{1,0:T(8,128)(2,1)S(1)}, bf16[64,1536]{1,0:T(8,128)(2,1)S(1)}, u32[]{:S(2)}, u32[]{:S(2)}) collective-permute-start(bf16[64,1536]{1,0:T(8,128)(2,1)S(1)} %get-tuple-element.41), channel_id=1, source_target_pairs={{0,64},{1,65},{2,66},{3,67},{4,68},{5,69},{6,70},{7,71},{8,72},{9,... | collective-permute-start | bytes 589832 | tf_op jit(solution)/shard_map/ppermute | solution.py:53
  243.5 13.6 %collective-permute-start.36 = (bf16[64,768]{1,0:T(8,128)(2,1)S(1)}, bf16[64,768]{1,0:T(8,128)(2,1)S(1)}, u32[]{:S(2)}, u32[]{:S(2)}) collective-permute-start(bf16[64,768]{1,0:T(8,128)(2,1)S(1)} %get-tuple-element.56), channel_id=1, source_target_pairs={{0,1},{1,0},{2,3},{3,2},{4,5},{5,4},{6,7},{7,6},{8,9},{9,8},{10,11... | collective-permute-start | bytes 294920 | tf_op jit(solution)/shard_map/ppermute | solution.py:62
  249.4 8.0 %collective-permute-start.35 = (bf16[64,768]{1,0:T(8,128)(2,1)S(1)}, bf16[64,768]{1,0:T(8,128)(2,1)S(1)}, u32[]{:S(2)}, u32[]{:S(2)}) collective-permute-start(bf16[64,768]{1,0:T(8,128)(2,1)S(1)} %get-tuple-element.55), channel_id=1, source_target_pairs={{0,1},{1,0},{2,3},{3,2},{4,5},{5,4},{6,7},{7,6},{8,9},{9,8},{10,11... | collective-permute-start | bytes 294920 | tf_op jit(solution)/shard_map/ppermute | solution.py:62
Sparse Core Ops, SparseCore 0:
  9.1 101.7 all-gather.1

commit v11 on v8

--- a/solution.py
+++ b/solution.py
@@ -96,7 +96,7 @@
     depth, width = w.shape
     rows = pieces[0].shape[0]
     tokens = len(pieces) * rows
-    tile = 256
+    tile = 512
     return pl.pallas_call(
         mm1_kernel,
         grid=(width // tile,),
@@ -286,7 +286,6 @@
     normed = (source - mean) / jnp.sqrt(square - mean * mean + 1e-05) * gain_first
     col = jnp.dot(one, normed, precision=high).astype(BF)
     col = exchange(col.reshape(groups, -1, chans), "row").reshape(-1, chans)
-    (col,) = tie([col], early)
     spec = jnp.dot(two, col.astype(F32), precision=high)
     split = spec.shape[0] // 2
     spec_re, spec_im = spec[:split], spec[split:]
@@ -296,7 +295,8 @@
     )
     back = jnp.dot(three, filt, precision=high).astype(BF)
     back = exchange(back.reshape(groups, -1, chans), "row").reshape(-1, chans)
-    return source + jnp.dot(four, back.astype(F32), precision=high)
+    back, *early = tie([back, *early], [])
+    return source + jnp.dot(four, back.astype(F32), precision=high), early
 
 
 def block_places():
@@ -323,8 +323,11 @@
 
 
 def gather_gains(gain):
-    pair = jnp.stack([gain, swap_cores(gain)])
-    rows = jnp.concatenate(gather_far(pair, "x"))
+    return gather_far(jnp.stack([gain, swap_cores(gain)]), "x")
+
+
+def place_gains(parts):
+    rows = jnp.concatenate(parts)
     table = []
     for x in range(SIDE):
         for core in range(2):
@@ -354,12 +357,12 @@
     cols = lax.axis_size("col")
     w_in_all = lax.all_gather(w_in, "col", axis=0, tiled=True)
     gains = gather_gains(gain_second)
-    resid = spectral(image, filter_bank, gain_first, [gains])
+    resid, gains = spectral(image, filter_bank, gain_first, gains)
     tokens = rows_here * width
     own = tokens // cols
     half = own // 2
     moved = exchange(resid.astype(BF).reshape(cols, own, chans), "col")
-    first, second = normalize(moved, gains, half)
+    first, second = normalize(moved, place_gains(gains), half)
     first, second = gather_near(first, "z"), gather_near(second, "y")
     parts = [gather_far(first, "y"), gather_far(second, "z")]
     hiddens = [gather_far(matmul_in(part, w_in_all, b_in), "x") for part in parts]

time: 266 us -> 268 us (level)
  waiting for transfers between devices: 66.8 us -> 105 us
  blocking collectives: 50 us -> 13.2 us
  starting transfers between devices: 71.6 us -> 77.3 us
  local copies, waits for them, and re-layouts: 11.1 us -> 6.42 us
  matrix products: 6.72 us -> 9.5 us
    all_to_all x2 -> x0, blocking collectives: 38 us -> none  [exchange(): return lax.all_to_all(a, axis, split_axis=0, concat_axis=0, tiled=True)]
    all_to_all x1 -> x3, waiting for transfers between devices: 0.01 us -> 22.1 us  [exchange(): return lax.all_to_all(a, axis, split_axis=0, concat_axis=0, tiled=True)]
    ppermute x33, waiting for transfers between devices: 65.8 us -> 80.7 us  [hop(): return lax.ppermute(a, ('row', 'col'), pairs)]
    all_to_all x1 -> x3, starting transfers between devices: 7.85 us -> 21.9 us  [exchange(): return lax.all_to_all(a, axis, split_axis=0, concat_axis=0, tiled=True)]
    ppermute x33, starting transfers between devices: 44.2 us -> 39.2 us  [hop(): return lax.ppermute(a, ('row', 'col'), pairs)]
    ppermute x4, starting transfers between devices: 19.5 us -> 16.2 us  [swap_cores(): return lax.ppermute(a, 'col', pairs)]
  transfers between devices with their start and end apart: 39 -> 41, of which waited for: 17 -> 21; matrix products, arithmetic and copies ran while one was open for 6% -> 6% of each run, Pallas kernels for 16% -> 15%
where the time goes in v11:
time: 268 us; the launch traced here: 267 us
  waiting for transfers between devices  105 us (39%)
  starting transfers between devices  77.3 us (29%)
  Pallas kernels  40.9 us (15%)
  between operations  13.7 us (5%)
  blocking collectives  13.2 us (5%)
  matrix products  9.5 us (4%)
  local copies, waits for them, and re-layouts  6.42 us (2%)
    ppermute x33, waiting for transfers between devices, hop(): return lax.ppermute(a, ('row', 'col'), pairs)  80.7 us
    ppermute x33, starting transfers between devices, hop(): return lax.ppermute(a, ('row', 'col'), pairs)  39.2 us
    pallas_call x2, Pallas kernels, matmul_in(): pl.pallas_call(mm1_kernel, grid=(width // tile,), in_specs=[pl.BlockSpec(...  22.2 us
    all_to_all x3, waiting for transfers between devices, exchange(): return lax.all_to_all(a, axis, split_axis=0, concat_axis=0, tiled=True)  22.1 us
    all_to_all x3, starting transfers between devices, exchange(): return lax.all_to_all(a, axis, split_axis=0, concat_axis=0, tiled=True)  21.9 us
    ppermute x4, starting transfers between devices, swap_cores(): return lax.ppermute(a, 'col', pairs)  16.2 us
    pallas_call x2, Pallas kernels, matmul_out(): pl.pallas_call(mm2_kernel, grid=(2 * steps,), in_specs=[pl.BlockSpec(memo...  15.8 us
    psum x1, blocking collectives, spectral(): lax.psum((jnp.sum(source, axis=-1), jnp.sum(source * source, axis=-1)), '...  13.2 us
  transfers between devices with their start and end apart: 41, of which 21 were waited for; matrix products, arithmetic and copies ran while one was open for 6% of the time, Pallas kernels for 15%

profile of v11, /device:TPU:1, one launch (start us, length us, event | category | flops | bytes accessed | tf_op | source)
XLA Modules:
  0.0 267.2 jit_solution(11237760666389279867)
XLA Ops:
  6.5 0.7 all-gather.2.cloned.1.call-update
  7.9 13.2 %all-reduce = (f32[256]{0:T(256)S(1)}, f32[256]{0:T(256)S(1)}) all-reduce(f32[256]{0:T(256)S(1)} %reduce_sum.34, f32[256]{0:T(256)S(1)} %reduce_sum.32), channel_id=1, replica_groups=mesh['row'=16,'col'=8] {'col'}, use_global_device_ids=true, to_apply=%region_3.0 | all-reduce | flops 512 | bytes 4096 | tf_op jit(solution)/shard_map/psum | solution.py:281
  21.3 1.7 convolution_convert_fusion
  23.0 7.9 %all-to-all-start = ((bf16[16,32,768]{2,1,0:T(8,128)(2,1)}), bf16[16,32,768]{2,1,0:T(8,128)(2,1)}, u32[]{:S(2)}, u32[]{:S(2)}) async-start(bf16[16,32,768]{2,1,0:T(8,128)(2,1)} %bitcast.3), calls=%async_computation | async-start | bytes 1572864 | tf_op jit(solution)/shard_map/all_to_all | solution.py:253
  30.9 1.5 fusion.13
  33.0 9.7 %all-to-all-done = bf16[16,32,768]{2,1,0:T(8,128)(2,1)} async-done(((bf16[16,32,768]{2,1,0:T(8,128)(2,1)}), bf16[16,32,768]{2,1,0:T(8,128)(2,1)}, u32[]{:S(2)}, u32[]{:S(2)}) %all-to-all-start) | async-done | bytes 786464 | tf_op jit(solution)/shard_map/all_to_all | solution.py:253
  42.7 2.5 fusion.15
  45.2 0.9 fusion.5
  46.3 1.8 add_convert_fusion
  48.1 3.7 %all-to-all-start.1 = ((bf16[16,32,768]{2,1,0:T(8,128)(2,1)}), bf16[16,32,768]{2,1,0:T(8,128)(2,1)S(1)}, u32[]{:S(2)}, u32[]{:S(2)}) async-start(bf16[16,32,768]{2,1,0:T(8,128)(2,1)} %bitcast.6), calls=%async_computation.1 | async-start | bytes 1572864 | tf_op jit(solution)/shard_map/all_to_all | solution.py:253
  51.9 3.7 %collective-permute-start = (f32[768]{0:T(1024)S(1)}, f32[768]{0:T(1024)S(1)}, u32[]{:S(2)}, u32[]{:S(2)}) collective-permute-start(f32[768]{0:T(1024)S(1)} %copy-done.22), channel_id=1, source_target_pairs={{0,1},{1,0},{2,3},{3,2},{4,5},{5,4},{6,7},{7,6},{8,9},{9,8},{10,11... | collective-permute-start | bytes 9224 | tf_op jit(solution)/shard_map/ppermute | solution.py:62
  55.6 0.8 collective-permute-done
  56.5 3.5 %collective-permute-start.1 = (f32[2,768]{1,0:T(2,128)S(1)}, f32[2,768]{1,0:T(2,128)S(1)}, u32[]{:S(2)}, u32[]{:S(2)}) collective-permute-start(f32[2,768]{1,0:T(2,128)S(1)} %pad_maximum_fusion.3.refs_1_), channel_id=1, source_target_pairs={{0,2},{1,7},{2,4},{3,1},{4,6},{5,3},{6,0},{7,5},{8,10},{9,15},{10,... | collective-permute-start | bytes 18440 | tf_op jit(solution)/shard_map/ppermute | solution.py:53
  60.0 0.8 collective-permute-done.1.refs_2_
  60.7 3.4 %collective-permute-start.3 = (f32[2,768]{1,0:T(2,128)S(1)}, f32[2,768]{1,0:T(2,128)S(1)}, u32[]{:S(2)}, u32[]{:S(2)}) collective-permute-start(f32[2,768]{1,0:T(2,128)S(1)} %collective-permute-done.1.refs_2_), channel_id=1, source_target_pairs={{0,2},{1,7},{2,4},{3,1},{4,6},{5,3},{6,0},{7,5},{8,10},{9,15},{10,... | collective-permute-start | bytes 18440 | tf_op jit(solution)/shard_map/ppermute | solution.py:53
  64.1 0.7 dynamic-slice_bitcast_fusion
  65.8 2.5 fusion.14
  68.3 10.3 %all-to-all-start.2 = ((bf16[8,32,768]{2,1,0:T(8,128)(2,1)}), bf16[8,32,768]{2,1,0:T(8,128)(2,1)S(1)}, u32[]{:S(2)}, u32[]{:S(2)}) async-start(bf16[8,32,768]{2,1,0:T(8,128)(2,1)} %bitcast.8), calls=%async_computation.2 | async-start | bytes 786432 | tf_op jit(solution)/shard_map/all_to_all | solution.py:253
  78.8 12.3 %all-to-all-done.2.moved_ref = bf16[8,32,768]{2,1,0:T(8,128)(2,1)S(1)} async-done(((bf16[8,32,768]{2,1,0:T(8,128)(2,1)}), bf16[8,32,768]{2,1,0:T(8,128)(2,1)S(1)}, u32[]{:S(2)}, u32[]{:S(2)}) %all-to-all-start.2) | async-done | bytes 393248 | tf_op jit(solution)/shard_map/all_to_all | solution.py:253
  91.5 0.5 collective-permute-start.22
  92.0 2.2 collective-permute-start.21
  94.8 1.7 collective-permute-start.5
  96.5 2.1 collective-permute-done.22
  98.5 2.1 collective-permute-done.21
  100.6 2.8 %collective-permute-done.20 = bf16[16,6144]{1,0:T(8,128)(2,1)S(1)} collective-permute-done((bf16[16,6144]{1,0:T(8,128)(2,1)S(1)}, bf16[16,6144]{1,0:T(8,128)(2,1)S(1)}, u32[]{:S(2)}, u32[]{:S(2)}) %collective-permute-start.20) | collective-permute-done | bytes 196640 | tf_op jit(solution)/shard_map/ppermute | solution.py:53
  103.6 0.6 collective-permute-start.23
  104.2 1.2 collective-permute-done.4
  105.4 1.0 pad_maximum_fusion
  106.4 2.6 collective-permute-start.7
  108.9 7.2 %collective-permute-done.23.refs_1_ = bf16[64,6144]{1,0:T(8,128)(2,1)S(1)} collective-permute-done((bf16[64,6144]{1,0:T(8,128)(2,1)S(1)}, bf16[64,6144]{1,0:T(8,128)(2,1)S(1)}, u32[]{:S(2)}, u32[]{:S(2)}) %collective-permute-start.23) | collective-permute-done | bytes 786464 | tf_op jit(solution)/shard_map/ppermute | solution.py:53
  116.1 2.5 collective-permute-start.25
  118.6 4.3 %collective-permute-start.13 = (bf16[1536,768]{1,0:T(8,128)(2,1)S(1)}, bf16[1536,768]{1,0:T(8,128)(2,1)}, u32[]{:S(2)}, u32[]{:S(2)}) collective-permute-start(bf16[1536,768]{1,0:T(8,128)(2,1)S(1)} %copy-done.2), channel_id=1, source_target_pairs={{0,1},{1,0},{2,3},{3,2},{4,5},{5,4},{6,7},{7,6},{8,9},{9,8},{10,11... | collective-permute-start | bytes 7077896 | tf_op jit(solution)/shard_map/ppermute | solution.py:62
  123.4 2.2 collective-permute-start.9
  125.6 0.6 broadcast_in_dim.35.refs_5_
  126.2 0.9 copy-done.7
  127.1 4.6 %collective-permute-done.25.refs_3_ = bf16[64,6144]{1,0:T(8,128)(2,1)} collective-permute-done((bf16[64,6144]{1,0:T(8,128)(2,1)S(1)}, bf16[64,6144]{1,0:T(8,128)(2,1)}, u32[]{:S(2)}, u32[]{:S(2)}) %collective-permute-start.25) | collective-permute-done | bytes 786464 | tf_op jit(solution)/shard_map/ppermute | solution.py:53
  131.7 11.1 %shard_map.143.refs_0_ = bf16[256,1536]{1,0:T(8,128)(2,1)} custom-call(bf16[64,6144]{1,0:T(8,128)(2,1)} %bitcast.47, bf16[64,6144]{1,0:T(8,128)(2,1)} %copy-done.6, bf16[64,6144]{1,0:T(8,128)(2,1)} %copy-done.7, bf16[64,6144]{1,0:T(8,128)(2,1)} %collective-permute-done.25.refs_3_, bf16[6144,1536]{1,0:T(8,128)(2,1)} %all-gather.2.cloned.1.call-done.refs_4_, ...), custom_call_target="tpu_custom_call" | custom-call | flops 4831838208 | bytes 22020096 | tf_op jit(solution)/shard_map/pallas_call | solution.py:100
  142.8 0.9 collective-permute-start.26
  143.7 11.1 %shard_map.138.refs_0_ = bf16[256,1536]{1,0:T(8,128)(2,1)} custom-call(bf16[64,6144]{1,0:T(8,128)(2,1)} %bitcast.14.refs_0_, bf16[64,6144]{1,0:T(8,128)(2,1)} %collective-permute-done.7.refs_1_, bf16[64,6144]{1,0:T(8,128)(2,1)} %collective-permute-done.8.refs_2_, bf16[64,6144]{1,0:T(8,128)(2,1)} %collective-permute-done.9.refs_3_, ...), custom_call_target="tpu_custom_call" | custom-call | flops 4831838208 | bytes 22020096 | tf_op jit(solution)/shard_map/pallas_call | solution.py:100
  154.8 0.5 collective-permute-start.10
  155.4 0.9 collective-permute-start.27
  156.3 1.8 collective-permute-start.28
  158.0 12.1 %collective-permute-done.10.refs_1_ = bf16[256,1536]{1,0:T(8,128)(2,1)S(1)} collective-permute-done((bf16[256,1536]{1,0:T(8,128)(2,1)}, bf16[256,1536]{1,0:T(8,128)(2,1)S(1)}, u32[]{:S(2)}, u32[]{:S(2)}) %collective-permute-start.10) | collective-permute-done | bytes 786464 | tf_op jit(solution)/shard_map/ppermute | solution.py:53
  170.2 3.3 %collective-permute-done.27.refs_2_ = bf16[256,1536]{1,0:T(8,128)(2,1)S(1)} collective-permute-done((bf16[256,1536]{1,0:T(8,128)(2,1)S(1)}, bf16[256,1536]{1,0:T(8,128)(2,1)S(1)}, u32[]{:S(2)}, u32[]{:S(2)}) %collective-permute-start.27) | collective-permute-done | bytes 786464 | tf_op jit(solution)/shard_map/ppermute | solution.py:53
  173.4 13.6 %collective-permute-done.28.refs_3_ = bf16[256,1536]{1,0:T(8,128)(2,1)S(1)} collective-permute-done((bf16[256,1536]{1,0:T(8,128)(2,1)S(1)}, bf16[256,1536]{1,0:T(8,128)(2,1)S(1)}, u32[]{:S(2)}, u32[]{:S(2)}) %collective-permute-start.28) | collective-permute-done | bytes 786464 | tf_op jit(solution)/shard_map/ppermute | solution.py:53
  187.0 7.9 %shard_map.144 = (bf16[256,1536]{1,0:T(8,128)(2,1)S(1)}, bf16[256,1536]{1,0:T(8,128)(2,1)S(1)}, bf16[256,1536]{1,0:T(8,128)(2,1)S(1)}, bf16[256,1536]{1,0:T(8,128)(2,1)S(1)}) custom-call(bf16[256,1536]{1,0:T(8,128)(2,1)S(1)} %copy-done.1, bf16[256,1536]{1,0:T(8,128)(2,1)S(1)} %collective-permute-done.26.refs_1_, ...), custom_call_target="tpu_custom_call" | custom-call | flops 4831838208 | bytes 11010048 | tf_op jit(solution)/shard_map/pallas_call | solution.py:157
  194.9 2.0 collective-permute-start.30
  197.0 2.9 %collective-permute-done.12.refs_3_ = bf16[256,1536]{1,0:T(8,128)(2,1)S(1)} collective-permute-done((bf16[256,1536]{1,0:T(8,128)(2,1)S(1)}, bf16[256,1536]{1,0:T(8,128)(2,1)S(1)}, u32[]{:S(2)}, u32[]{:S(2)}) %collective-permute-start.12) | collective-permute-done | bytes 786464 | tf_op jit(solution)/shard_map/ppermute | solution.py:53
  199.9 7.9 %shard_map.139 = (bf16[256,1536]{1,0:T(8,128)(2,1)S(1)}, bf16[256,1536]{1,0:T(8,128)(2,1)S(1)}, bf16[256,1536]{1,0:T(8,128)(2,1)S(1)}, bf16[256,1536]{1,0:T(8,128)(2,1)S(1)}) custom-call(bf16[256,1536]{1,0:T(8,128)(2,1)S(1)} %copy-done, bf16[256,1536]{1,0:T(8,128)(2,1)S(1)} %collective-permute-done.10.refs_1_, ...), custom_call_target="tpu_custom_call" | custom-call | flops 4831838208 | bytes 11010048 | tf_op jit(solution)/shard_map/pallas_call | solution.py:157
  207.9 2.6 collective-permute-start.29
  210.8 2.4 collective-permute-start.14
  213.2 7.0 %collective-permute-done.15.b = bf16[256,1536]{1,0:T(8,128)(2,1)S(1)} collective-permute-done((bf16[256,1536]{1,0:T(8,128)(2,1)S(1)}, bf16[256,1536]{1,0:T(8,128)(2,1)S(1)}, u32[]{:S(2)}, u32[]{:S(2)}) %collective-permute-start.15) | collective-permute-done | bytes 786464 | tf_op jit(solution)/shard_map/ppermute | solution.py:53
  220.5 3.2 %collective-permute-done.29.b = bf16[256,1536]{1,0:T(8,128)(2,1)S(1)} collective-permute-done((bf16[256,1536]{1,0:T(8,128)(2,1)S(1)}, bf16[256,1536]{1,0:T(8,128)(2,1)S(1)}, u32[]{:S(2)}, u32[]{:S(2)}) %collective-permute-start.29) | collective-permute-done | bytes 786464 | tf_op jit(solution)/shard_map/ppermute | solution.py:53
  223.7 4.2 %collective-permute-done.31.c = bf16[256,1536]{1,0:T(8,128)(2,1)S(1)} collective-permute-done((bf16[256,1536]{1,0:T(8,128)(2,1)S(1)}, bf16[256,1536]{1,0:T(8,128)(2,1)S(1)}, u32[]{:S(2)}, u32[]{:S(2)}) %collective-permute-start.31) | collective-permute-done | bytes 786464 | tf_op jit(solution)/shard_map/ppermute | solution.py:53
  228.2 3.9 %collective-permute-start.32 = (bf16[64,1536]{1,0:T(8,128)(2,1)S(1)}, bf16[64,1536]{1,0:T(8,128)(2,1)S(1)}, u32[]{:S(2)}, u32[]{:S(2)}) collective-permute-start(bf16[64,1536]{1,0:T(8,128)(2,1)S(1)} %get-tuple-element.53), channel_id=1, source_target_pairs={{0,24},{1,25},{2,26},{3,27},{4,28},{5,29},{6,30},{7,31},{8,0},{9,1... | collective-permute-start | bytes 589832 | tf_op jit(solution)/shard_map/ppermute | solution.py:53
  232.1 2.0 collective-permute-start.34
  234.1 7.2 %collective-permute-done.16.c = bf16[256,1536]{1,0:T(8,128)(2,1)S(1)} collective-permute-done((bf16[256,1536]{1,0:T(8,128)(2,1)S(1)}, bf16[256,1536]{1,0:T(8,128)(2,1)S(1)}, u32[]{:S(2)}, u32[]{:S(2)}) %collective-permute-start.16) | collective-permute-done | bytes 786464 | tf_op jit(solution)/shard_map/ppermute | solution.py:53
  241.6 0.5 collective-permute-start.17
  242.1 1.0 collective-permute-start.18
  243.4 6.3 %collective-permute-done.33.c = bf16[64,1536]{1,0:T(8,128)(2,1)S(1)} collective-permute-done((bf16[64,1536]{1,0:T(8,128)(2,1)S(1)}, bf16[64,1536]{1,0:T(8,128)(2,1)S(1)}, u32[]{:S(2)}, u32[]{:S(2)}) %collective-permute-start.33) | collective-permute-done | bytes 196640 | tf_op jit(solution)/shard_map/ppermute | solution.py:53
  249.8 1.3 collective-permute-start.36
  251.2 6.9 %collective-permute-start.35 = (bf16[64,768]{1,0:T(8,128)(2,1)S(1)}, bf16[64,768]{1,0:T(8,128)(2,1)S(1)}, u32[]{:S(2)}, u32[]{:S(2)}) collective-permute-start(bf16[64,768]{1,0:T(8,128)(2,1)S(1)} %get-tuple-element.57), channel_id=1, source_target_pairs={{0,1},{1,0},{2,3},{3,2},{4,5},{5,4},{6,7},{7,6},{8,9},{9,8},{10,11... | collective-permute-start | bytes 294920 | tf_op jit(solution)/shard_map/ppermute | solution.py:62
  258.1 0.7 dynamic-slice_bitcast_fusion.1.place_ref
  259.0 1.4 shard_map.148
  (106 shorter events, 6.1 us)
Async XLA Ops:
  6.5 14.8 %copy-start.11 = (f32[512,256]{1,0:T(8,128)S(1)}, f32[512,256]{1,0:T(8,128)}, u32[]{:S(2)}) copy-start(f32[512,256]{1,0:T(8,128)} %constant.28.clone) | copy-start | bytes 1572868
  6.5 1.1 copy-start.4
  6.5 14.6 %copy-start.21 = (f32[768]{0:T(1024)S(1)}, f32[768]{0:T(1024)}, u32[]{:S(2)}) copy-start(f32[768]{0:T(1024)} %param.16) | copy-start | bytes 9220
  6.5 125.2 %all-gather.2.cloned.1.call-start = ((), (), s32[]{:S(2)}) async-start(), calls=%async_computation.3 | async-start | bytes 21233664 | tf_op jit(solution)/shard_map/all_gather | solution.py:358
  23.0 19.7 %all-to-all-start = ((bf16[16,32,768]{2,1,0:T(8,128)(2,1)}), bf16[16,32,768]{2,1,0:T(8,128)(2,1)}, u32[]{:S(2)}, u32[]{:S(2)}) async-start(bf16[16,32,768]{2,1,0:T(8,128)(2,1)} %bitcast.3), calls=%async_computation | async-start | bytes 1572864 | tf_op jit(solution)/shard_map/all_to_all | solution.py:253
  42.7 2.5 copy-start.9
  45.2 1.0 copy-start.8
  48.1 3.8 %copy-start.22 = (f32[768]{0:T(1024)S(1)}, f32[768]{0:T(1024)}, u32[]{:S(2)}) copy-start(f32[768]{0:T(1024)} %param.17) | copy-start | bytes 9220
  48.1 17.7 %copy-start.10 = (f32[256,512]{1,0:T(8,128)S(1)}, f32[256,512]{1,0:T(8,128)}, u32[]{:S(2)}) copy-start(f32[256,512]{1,0:T(8,128)} %constant.31.clone) | copy-start | bytes 1572868
  48.1 16.8 %all-to-all-start.1 = ((bf16[16,32,768]{2,1,0:T(8,128)(2,1)}), bf16[16,32,768]{2,1,0:T(8,128)(2,1)S(1)}, u32[]{:S(2)}, u32[]{:S(2)}) async-start(bf16[16,32,768]{2,1,0:T(8,128)(2,1)} %bitcast.6), calls=%async_computation.1 | async-start | bytes 1572864 | tf_op jit(solution)/shard_map/all_to_all | solution.py:253
  51.9 4.6 %collective-permute-start = (f32[768]{0:T(1024)S(1)}, f32[768]{0:T(1024)S(1)}, u32[]{:S(2)}, u32[]{:S(2)}) collective-permute-start(f32[768]{0:T(1024)S(1)} %copy-done.22), channel_id=1, source_target_pairs={{0,1},{1,0},{2,3},{3,2},{4,5},{5,4},{6,7},{7,6},{8,9},{9,8},{10,11... | collective-permute-start | bytes 9224 | tf_op jit(solution)/shard_map/ppermute | solution.py:62
  56.5 8.5 %copy-start.12 = (f32[2,768]{1,0:T(2,128)}, f32[2,768]{1,0:T(2,128)S(1)}, u32[]{:S(2)}) copy-start(f32[2,768]{1,0:T(2,128)S(1)} %pad_maximum_fusion.3.refs_1_) | copy-start | bytes 18436
  56.5 4.3 %collective-permute-start.1 = (f32[2,768]{1,0:T(2,128)S(1)}, f32[2,768]{1,0:T(2,128)S(1)}, u32[]{:S(2)}, u32[]{:S(2)}) collective-permute-start(f32[2,768]{1,0:T(2,128)S(1)} %pad_maximum_fusion.3.refs_1_), channel_id=1, source_target_pairs={{0,2},{1,7},{2,4},{3,1},{4,6},{5,3},{6,0},{7,5},{8,10},{9,15},{10,... | collective-permute-start | bytes 18440 | tf_op jit(solution)/shard_map/ppermute | solution.py:53
  60.0 4.9 %collective-permute-start.2 = (f32[2,768]{1,0:T(2,128)S(1)}, f32[2,768]{1,0:T(2,128)S(1)}, u32[]{:S(2)}, u32[]{:S(2)}) collective-permute-start(f32[2,768]{1,0:T(2,128)S(1)} %pad_maximum_fusion.3.refs_1_), channel_id=1, source_target_pairs={{0,6},{1,3},{2,0},{3,5},{4,2},{5,7},{6,4},{7,1},{8,14},{9,11},{10,... | collective-permute-start | bytes 18440 | tf_op jit(solution)/shard_map/ppermute | solution.py:53
  60.7 4.2 %copy-start.14 = (f32[2,768]{1,0:T(2,128)}, f32[2,768]{1,0:T(2,128)S(1)}, u32[]{:S(2)}) copy-start(f32[2,768]{1,0:T(2,128)S(1)} %collective-permute-done.1.refs_2_) | copy-start | bytes 18436
  60.7 4.2 %collective-permute-start.3 = (f32[2,768]{1,0:T(2,128)S(1)}, f32[2,768]{1,0:T(2,128)S(1)}, u32[]{:S(2)}, u32[]{:S(2)}) collective-permute-start(f32[2,768]{1,0:T(2,128)S(1)} %collective-permute-done.1.refs_2_), channel_id=1, source_target_pairs={{0,2},{1,7},{2,4},{3,1},{4,6},{5,3},{6,0},{7,5},{8,10},{9,15},{10,... | collective-permute-start | bytes 18440 | tf_op jit(solution)/shard_map/ppermute | solution.py:53
  64.8 0.6 copy-start.16
  64.9 0.9 copy-start.3
  65.8 12.8 %copy-start.13 = (f32[2,768]{1,0:T(2,128)S(1)}, f32[2,768]{1,0:T(2,128)}, u32[]{:S(2)}) copy-start(f32[2,768]{1,0:T(2,128)} %get-tuple-element.33) | copy-start | bytes 18436
  65.8 12.8 %copy-start.15 = (f32[2,768]{1,0:T(2,128)S(1)}, f32[2,768]{1,0:T(2,128)}, u32[]{:S(2)}) copy-start(f32[2,768]{1,0:T(2,128)} %get-tuple-element.34) | copy-start | bytes 18436
  65.8 12.8 %copy-start.17 = (f32[2,768]{1,0:T(2,128)S(1)}, f32[2,768]{1,0:T(2,128)}, u32[]{:S(2)}) copy-start(f32[2,768]{1,0:T(2,128)} %get-tuple-element.35) | copy-start | bytes 18436
  65.8 12.8 %copy-start.19 = (f32[2,768]{1,0:T(2,128)S(1)}, f32[2,768]{1,0:T(2,128)}, u32[]{:S(2)}) copy-start(f32[2,768]{1,0:T(2,128)} %get-tuple-element.36) | copy-start | bytes 18436
  68.3 22.8 %all-to-all-start.2 = ((bf16[8,32,768]{2,1,0:T(8,128)(2,1)}), bf16[8,32,768]{2,1,0:T(8,128)(2,1)S(1)}, u32[]{:S(2)}, u32[]{:S(2)}) async-start(bf16[8,32,768]{2,1,0:T(8,128)(2,1)} %bitcast.8), calls=%async_computation.2 | async-start | bytes 786432 | tf_op jit(solution)/shard_map/all_to_all | solution.py:253
  91.5 7.1 %collective-permute-start.22 = (bf16[16,6144]{1,0:T(8,128)(2,1)S(1)}, bf16[16,6144]{1,0:T(8,128)(2,1)S(1)}, u32[]{:S(2)}, u32[]{:S(2)}) collective-permute-start(bf16[16,6144]{1,0:T(8,128)(2,1)S(1)} %get-tuple-element.47), channel_id=1, source_target_pairs={{0,16},{1,17},{2,18},{3,19},{4,20},{5,21},{6,22},{7,23},{8,24},{9,... | collective-permute-start | bytes 589832 | tf_op jit(solution)/shard_map/ppermute | solution.py:53
  92.0 8.6 %collective-permute-start.21 = (bf16[16,6144]{1,0:T(8,128)(2,1)S(1)}, bf16[16,6144]{1,0:T(8,128)(2,1)S(1)}, u32[]{:S(2)}, u32[]{:S(2)}) collective-permute-start(bf16[16,6144]{1,0:T(8,128)(2,1)S(1)} %get-tuple-element.47), channel_id=1, source_target_pairs={{0,24},{1,25},{2,26},{3,27},{4,28},{5,29},{6,30},{7,31},{8,0},{9,1... | collective-permute-start | bytes 589832 | tf_op jit(solution)/shard_map/ppermute | solution.py:53
  94.3 9.2 %collective-permute-start.20 = (bf16[16,6144]{1,0:T(8,128)(2,1)S(1)}, bf16[16,6144]{1,0:T(8,128)(2,1)S(1)}, u32[]{:S(2)}, u32[]{:S(2)}) collective-permute-start(bf16[16,6144]{1,0:T(8,128)(2,1)S(1)} %get-tuple-element.47), channel_id=1, source_target_pairs={{0,8},{1,9},{2,10},{3,11},{4,12},{5,13},{6,14},{7,15},{8,16},{9,17... | collective-permute-start | bytes 589832 | tf_op jit(solution)/shard_map/ppermute | solution.py:53
  94.3 9.9 %collective-permute-start.6 = (bf16[16,6144]{1,0:T(8,128)(2,1)S(1)}, bf16[16,6144]{1,0:T(8,128)(2,1)S(1)}, u32[]{:S(2)}, u32[]{:S(2)}) collective-permute-start(bf16[16,6144]{1,0:T(8,128)(2,1)S(1)} %get-tuple-element.37), channel_id=1, source_target_pairs={{0,64},{1,65},{2,66},{3,67},{4,68},{5,69},{6,70},{7,71},{8,72},{9,... | collective-permute-start | bytes 589832 | tf_op jit(solution)/shard_map/ppermute | solution.py:53
  94.8 9.4 %collective-permute-start.5 = (bf16[16,6144]{1,0:T(8,128)(2,1)S(1)}, bf16[16,6144]{1,0:T(8,128)(2,1)S(1)}, u32[]{:S(2)}, u32[]{:S(2)}) collective-permute-start(bf16[16,6144]{1,0:T(8,128)(2,1)S(1)} %get-tuple-element.37), channel_id=1, source_target_pairs={{0,96},{1,97},{2,98},{3,99},{4,100},{5,101},{6,102},{7,103},{8,104... | collective-permute-start | bytes 589832 | tf_op jit(solution)/shard_map/ppermute | solution.py:53
  98.5 6.8 %collective-permute-start.4 = (bf16[16,6144]{1,0:T(8,128)(2,1)S(1)}, bf16[16,6144]{1,0:T(8,128)(2,1)S(1)}, u32[]{:S(2)}, u32[]{:S(2)}) collective-permute-start(bf16[16,6144]{1,0:T(8,128)(2,1)S(1)} %get-tuple-element.37), channel_id=1, source_target_pairs={{0,32},{1,33},{2,34},{3,35},{4,36},{5,37},{6,38},{7,39},{8,40},{9,... | collective-permute-start | bytes 589832 | tf_op jit(solution)/shard_map/ppermute | solution.py:53
  103.5 15.2 %copy-start.2 = (bf16[1536,768]{1,0:T(8,128)(2,1)S(1)}, bf16[1536,768]{1,0:T(8,128)(2,1)}, u32[]{:S(2)}) copy-start(bf16[1536,768]{1,0:T(8,128)(2,1)} %refs_4_.3) | copy-start | bytes 7077892
  103.5 22.2 %copy-start.20 = (f32[1536]{0:T(1024)S(1)}, f32[1536]{0:T(1024)}, u32[]{:S(2)}) copy-start(f32[1536]{0:T(1024)} %param.19) | copy-start | bytes 18436
  103.6 12.6 %copy-start.5 = (bf16[4,16,6144]{2,1,0:T(8,128)(2,1)}, bf16[4,16,6144]{2,1,0:T(8,128)(2,1)S(1)}, u32[]{:S(2)}) copy-start(bf16[4,16,6144]{2,1,0:T(8,128)(2,1)S(1)} %pad_maximum_fusion.1) | copy-start | bytes 2359300
  103.6 12.6 %collective-permute-start.23 = (bf16[64,6144]{1,0:T(8,128)(2,1)S(1)}, bf16[64,6144]{1,0:T(8,128)(2,1)S(1)}, u32[]{:S(2)}, u32[]{:S(2)}) collective-permute-start(bf16[64,6144]{1,0:T(8,128)(2,1)S(1)} %bitcast.45), channel_id=1, source_target_pairs={{0,32},{1,97},{2,34},{3,99},{4,36},{5,101},{6,38},{7,103},{8,40},{... | collective-permute-start | bytes 2359304 | tf_op jit(solution)/shard_map/ppermute | solution.py:53
  106.4 17.0 %collective-permute-start.7 = (bf16[64,6144]{1,0:T(8,128)(2,1)}, bf16[64,6144]{1,0:T(8,128)(2,1)}, u32[]{:S(2)}, u32[]{:S(2)}) collective-permute-start(bf16[64,6144]{1,0:T(8,128)(2,1)} %bitcast.14.refs_0_), channel_id=1, source_target_pairs={{0,8},{1,25},{2,10},{3,27},{4,12},{5,29},{6,14},{7,31},{8,16},{9,1... | collective-permute-start | bytes 2359304 | tf_op jit(solution)/shard_map/ppermute | solution.py:53
  108.9 17.3 %collective-permute-start.24 = (bf16[64,6144]{1,0:T(8,128)(2,1)S(1)}, bf16[64,6144]{1,0:T(8,128)(2,1)S(1)}, u32[]{:S(2)}, u32[]{:S(2)}) collective-permute-start(bf16[64,6144]{1,0:T(8,128)(2,1)S(1)} %bitcast.46), channel_id=1, source_target_pairs={{0,96},{1,33},{2,98},{3,35},{4,100},{5,37},{6,102},{7,39},{8,104},... | collective-permute-start | bytes 2359304 | tf_op jit(solution)/shard_map/ppermute | solution.py:53
  116.1 10.1 %copy-start.6 = (bf16[64,6144]{1,0:T(8,128)(2,1)}, bf16[64,6144]{1,0:T(8,128)(2,1)S(1)}, u32[]{:S(2)}) copy-start(bf16[64,6144]{1,0:T(8,128)(2,1)S(1)} %collective-permute-done.23.refs_1_) | copy-start | bytes 2359300
  116.1 15.6 %collective-permute-start.25 = (bf16[64,6144]{1,0:T(8,128)(2,1)S(1)}, bf16[64,6144]{1,0:T(8,128)(2,1)}, u32[]{:S(2)}, u32[]{:S(2)}) collective-permute-start(bf16[64,6144]{1,0:T(8,128)(2,1)S(1)} %collective-permute-done.23.refs_1_), channel_id=1, source_target_pairs={{0,32},{1,97},{2,34},{3,99},{4,36},{5,101},{6,38},{7,103},{8,40},{... | collective-permute-start | bytes 2359304 | tf_op jit(solution)/shard_map/ppermute | solution.py:53
  118.6 51.5 %collective-permute-start.13 = (bf16[1536,768]{1,0:T(8,128)(2,1)S(1)}, bf16[1536,768]{1,0:T(8,128)(2,1)}, u32[]{:S(2)}, u32[]{:S(2)}) collective-permute-start(bf16[1536,768]{1,0:T(8,128)(2,1)S(1)} %copy-done.2), channel_id=1, source_target_pairs={{0,1},{1,0},{2,3},{3,2},{4,5},{5,4},{6,7},{7,6},{8,9},{9,8},{10,11... | collective-permute-start | bytes 7077896 | tf_op jit(solution)/shard_map/ppermute | solution.py:62
  122.9 20.8 %collective-permute-start.8 = (bf16[64,6144]{1,0:T(8,128)(2,1)}, bf16[64,6144]{1,0:T(8,128)(2,1)}, u32[]{:S(2)}, u32[]{:S(2)}) collective-permute-start(bf16[64,6144]{1,0:T(8,128)(2,1)} %bitcast.14.refs_0_), channel_id=1, source_target_pairs={{0,24},{1,9},{2,26},{3,11},{4,28},{5,13},{6,30},{7,15},{8,0},{9,17... | collective-permute-start | bytes 2359304 | tf_op jit(solution)/shard_map/ppermute | solution.py:53
  123.4 20.3 %collective-permute-start.9 = (bf16[64,6144]{1,0:T(8,128)(2,1)}, bf16[64,6144]{1,0:T(8,128)(2,1)}, u32[]{:S(2)}, u32[]{:S(2)}) collective-permute-start(bf16[64,6144]{1,0:T(8,128)(2,1)} %collective-permute-done.7.refs_1_), channel_id=1, source_target_pairs={{0,8},{1,25},{2,10},{3,27},{4,12},{5,29},{6,14},{7,31},{8,16},{9,1... | collective-permute-start | bytes 2359304 | tf_op jit(solution)/shard_map/ppermute | solution.py:53
  126.2 0.9 copy-start.7
  142.8 12.6 %copy-start.1 = (bf16[256,1536]{1,0:T(8,128)(2,1)S(1)}, bf16[256,1536]{1,0:T(8,128)(2,1)}, u32[]{:S(2)}) copy-start(bf16[256,1536]{1,0:T(8,128)(2,1)} %shard_map.143.refs_0_) | copy-start | bytes 2359300
  142.8 13.5 %collective-permute-start.26 = (bf16[256,1536]{1,0:T(8,128)(2,1)}, bf16[256,1536]{1,0:T(8,128)(2,1)S(1)}, u32[]{:S(2)}, u32[]{:S(2)}) collective-permute-start(bf16[256,1536]{1,0:T(8,128)(2,1)} %shard_map.143.refs_0_), channel_id=1, source_target_pairs={{0,2},{1,7},{2,4},{3,1},{4,6},{5,3},{6,0},{7,5},{8,10},{9,15},{10,... | collective-permute-start | bytes 2359304 | tf_op jit(solution)/shard_map/ppermute | solution.py:53
  154.8 45.1 %copy-start = (bf16[256,1536]{1,0:T(8,128)(2,1)S(1)}, bf16[256,1536]{1,0:T(8,128)(2,1)}, u32[]{:S(2)}) copy-start(bf16[256,1536]{1,0:T(8,128)(2,1)} %shard_map.138.refs_0_) | copy-start | bytes 2359300
  154.8 15.3 %collective-permute-start.10 = (bf16[256,1536]{1,0:T(8,128)(2,1)}, bf16[256,1536]{1,0:T(8,128)(2,1)S(1)}, u32[]{:S(2)}, u32[]{:S(2)}) collective-permute-start(bf16[256,1536]{1,0:T(8,128)(2,1)} %shard_map.138.refs_0_), channel_id=1, source_target_pairs={{0,2},{1,7},{2,4},{3,1},{4,6},{5,3},{6,0},{7,5},{8,10},{9,15},{10,... | collective-permute-start | bytes 2359304 | tf_op jit(solution)/shard_map/ppermute | solution.py:53
  155.4 18.1 %collective-permute-start.27 = (bf16[256,1536]{1,0:T(8,128)(2,1)S(1)}, bf16[256,1536]{1,0:T(8,128)(2,1)S(1)}, u32[]{:S(2)}, u32[]{:S(2)}) collective-permute-start(bf16[256,1536]{1,0:T(8,128)(2,1)S(1)} %copy-done.1), channel_id=1, source_target_pairs={{0,6},{1,3},{2,0},{3,5},{4,2},{5,7},{6,4},{7,1},{8,14},{9,11},{10,... | collective-permute-start | bytes 2359304 | tf_op jit(solution)/shard_map/ppermute | solution.py:53
  156.3 30.7 %collective-permute-start.28 = (bf16[256,1536]{1,0:T(8,128)(2,1)S(1)}, bf16[256,1536]{1,0:T(8,128)(2,1)S(1)}, u32[]{:S(2)}, u32[]{:S(2)}) collective-permute-start(bf16[256,1536]{1,0:T(8,128)(2,1)S(1)} %collective-permute-done.26.refs_1_), channel_id=1, source_target_pairs={{0,2},{1,7},{2,4},{3,1},{4,6},{5,3},{6,0},{7,5},{8,10},{9,15},{10,... | collective-permute-start | bytes 2359304 | tf_op jit(solution)/shard_map/ppermute | solution.py:53
  158.0 38.9 %collective-permute-start.11 = (bf16[256,1536]{1,0:T(8,128)(2,1)}, bf16[256,1536]{1,0:T(8,128)(2,1)S(1)}, u32[]{:S(2)}, u32[]{:S(2)}) collective-permute-start(bf16[256,1536]{1,0:T(8,128)(2,1)} %shard_map.138.refs_0_), channel_id=1, source_target_pairs={{0,6},{1,3},{2,0},{3,5},{4,2},{5,7},{6,4},{7,1},{8,14},{9,11},{10,... | collective-permute-start | bytes 2359304 | tf_op jit(solution)/shard_map/ppermute | solution.py:53
  170.2 29.7 %collective-permute-start.12 = (bf16[256,1536]{1,0:T(8,128)(2,1)S(1)}, bf16[256,1536]{1,0:T(8,128)(2,1)S(1)}, u32[]{:S(2)}, u32[]{:S(2)}) collective-permute-start(bf16[256,1536]{1,0:T(8,128)(2,1)S(1)} %collective-permute-done.10.refs_1_), channel_id=1, source_target_pairs={{0,2},{1,7},{2,4},{3,1},{4,6},{5,3},{6,0},{7,5},{8,10},{9,15},{10,... | collective-permute-start | bytes 2359304 | tf_op jit(solution)/shard_map/ppermute | solution.py:53
  194.9 15.6 %collective-permute-start.30 = (bf16[256,1536]{1,0:T(8,128)(2,1)S(1)}, bf16[256,1536]{1,0:T(8,128)(2,1)S(1)}, u32[]{:S(2)}, u32[]{:S(2)}) collective-permute-start(bf16[256,1536]{1,0:T(8,128)(2,1)S(1)} %get-tuple-element.51), channel_id=1, source_target_pairs={{0,96},{1,33},{2,98},{3,35},{4,100},{5,37},{6,102},{7,39},{8,104},... | collective-permute-start | bytes 2359304 | tf_op jit(solution)/shard_map/ppermute | solution.py:53
  207.8 12.4 %collective-permute-start.15 = (bf16[256,1536]{1,0:T(8,128)(2,1)S(1)}, bf16[256,1536]{1,0:T(8,128)(2,1)S(1)}, u32[]{:S(2)}, u32[]{:S(2)}) collective-permute-start(bf16[256,1536]{1,0:T(8,128)(2,1)S(1)} %get-tuple-element.41), channel_id=1, source_target_pairs={{0,24},{1,9},{2,26},{3,11},{4,28},{5,13},{6,30},{7,15},{8,0},{9,17... | collective-permute-start | bytes 2359304 | tf_op jit(solution)/shard_map/ppermute | solution.py:53
  207.9 15.8 %collective-permute-start.29 = (bf16[256,1536]{1,0:T(8,128)(2,1)S(1)}, bf16[256,1536]{1,0:T(8,128)(2,1)S(1)}, u32[]{:S(2)}, u32[]{:S(2)}) collective-permute-start(bf16[256,1536]{1,0:T(8,128)(2,1)S(1)} %get-tuple-element.49), channel_id=1, source_target_pairs={{0,32},{1,97},{2,34},{3,99},{4,36},{5,101},{6,38},{7,103},{8,40},{... | collective-permute-start | bytes 2359304 | tf_op jit(solution)/shard_map/ppermute | solution.py:53
  210.7 17.2 %collective-permute-start.31 = (bf16[256,1536]{1,0:T(8,128)(2,1)S(1)}, bf16[256,1536]{1,0:T(8,128)(2,1)S(1)}, u32[]{:S(2)}, u32[]{:S(2)}) collective-permute-start(bf16[256,1536]{1,0:T(8,128)(2,1)S(1)} %shard_map.145), channel_id=1, source_target_pairs={{0,96},{1,33},{2,98},{3,35},{4,100},{5,37},{6,102},{7,39},{8,104},... | collective-permute-start | bytes 2359304 | tf_op jit(solution)/shard_map/ppermute | solution.py:53
  210.8 23.3 %collective-permute-start.14 = (bf16[256,1536]{1,0:T(8,128)(2,1)S(1)}, bf16[256,1536]{1,0:T(8,128)(2,1)S(1)}, u32[]{:S(2)}, u32[]{:S(2)}) collective-permute-start(bf16[256,1536]{1,0:T(8,128)(2,1)S(1)} %get-tuple-element.39), channel_id=1, source_target_pairs={{0,8},{1,25},{2,10},{3,27},{4,12},{5,29},{6,14},{7,31},{8,16},{9,1... | collective-permute-start | bytes 2359304 | tf_op jit(solution)/shard_map/ppermute | solution.py:53
  220.4 20.8 %collective-permute-start.16 = (bf16[256,1536]{1,0:T(8,128)(2,1)S(1)}, bf16[256,1536]{1,0:T(8,128)(2,1)S(1)}, u32[]{:S(2)}, u32[]{:S(2)}) collective-permute-start(bf16[256,1536]{1,0:T(8,128)(2,1)S(1)} %shard_map.140), channel_id=1, source_target_pairs={{0,24},{1,9},{2,26},{3,11},{4,28},{5,13},{6,30},{7,15},{8,0},{9,17... | collective-permute-start | bytes 2359304 | tf_op jit(solution)/shard_map/ppermute | solution.py:53
  228.2 15.2 %copy-start.23 = (f32[768]{0:T(1024)S(1)}, f32[768]{0:T(1024)}, u32[]{:S(2)}) copy-start(f32[768]{0:T(1024)} %param.21) | copy-start | bytes 9220
  228.2 14.9 %collective-permute-start.32 = (bf16[64,1536]{1,0:T(8,128)(2,1)S(1)}, bf16[64,1536]{1,0:T(8,128)(2,1)S(1)}, u32[]{:S(2)}, u32[]{:S(2)}) collective-permute-start(bf16[64,1536]{1,0:T(8,128)(2,1)S(1)} %get-tuple-element.53), channel_id=1, source_target_pairs={{0,24},{1,25},{2,26},{3,27},{4,28},{5,29},{6,30},{7,31},{8,0},{9,1... | collective-permute-start | bytes 589832 | tf_op jit(solution)/shard_map/ppermute | solution.py:53
  232.1 17.6 %collective-permute-start.33 = (bf16[64,1536]{1,0:T(8,128)(2,1)S(1)}, bf16[64,1536]{1,0:T(8,128)(2,1)S(1)}, u32[]{:S(2)}, u32[]{:S(2)}) collective-permute-start(bf16[64,1536]{1,0:T(8,128)(2,1)S(1)} %get-tuple-element.54), channel_id=1, source_target_pairs={{0,8},{1,9},{2,10},{3,11},{4,12},{5,13},{6,14},{7,15},{8,16},{9,17... | collective-permute-start | bytes 589832 | tf_op jit(solution)/shard_map/ppermute | solution.py:53
  232.1 17.6 %collective-permute-start.34 = (bf16[64,1536]{1,0:T(8,128)(2,1)S(1)}, bf16[64,1536]{1,0:T(8,128)(2,1)S(1)}, u32[]{:S(2)}, u32[]{:S(2)}) collective-permute-start(bf16[64,1536]{1,0:T(8,128)(2,1)S(1)} %get-tuple-element.55), channel_id=1, source_target_pairs={{0,16},{1,17},{2,18},{3,19},{4,20},{5,21},{6,22},{7,23},{8,24},{9,... | collective-permute-start | bytes 589832 | tf_op jit(solution)/shard_map/ppermute | solution.py:53
  241.6 9.5 %collective-permute-start.17 = (bf16[64,1536]{1,0:T(8,128)(2,1)S(1)}, bf16[64,1536]{1,0:T(8,128)(2,1)S(1)}, u32[]{:S(2)}, u32[]{:S(2)}) collective-permute-start(bf16[64,1536]{1,0:T(8,128)(2,1)S(1)} %get-tuple-element.43), channel_id=1, source_target_pairs={{0,96},{1,97},{2,98},{3,99},{4,100},{5,101},{6,102},{7,103},{8,104... | collective-permute-start | bytes 589832 | tf_op jit(solution)/shard_map/ppermute | solution.py:53
  242.1 9.0 %collective-permute-start.18 = (bf16[64,1536]{1,0:T(8,128)(2,1)S(1)}, bf16[64,1536]{1,0:T(8,128)(2,1)S(1)}, u32[]{:S(2)}, u32[]{:S(2)}) collective-permute-start(bf16[64,1536]{1,0:T(8,128)(2,1)S(1)} %get-tuple-element.44), channel_id=1, source_target_pairs={{0,32},{1,33},{2,34},{3,35},{4,36},{5,37},{6,38},{7,39},{8,40},{9,... | collective-permute-start | bytes 589832 | tf_op jit(solution)/shard_map/ppermute | solution.py:53
  243.1 8.0 %collective-permute-start.19 = (bf16[64,1536]{1,0:T(8,128)(2,1)S(1)}, bf16[64,1536]{1,0:T(8,128)(2,1)S(1)}, u32[]{:S(2)}, u32[]{:S(2)}) collective-permute-start(bf16[64,1536]{1,0:T(8,128)(2,1)S(1)} %get-tuple-element.45), channel_id=1, source_target_pairs={{0,64},{1,65},{2,66},{3,67},{4,68},{5,69},{6,70},{7,71},{8,72},{9,... | collective-permute-start | bytes 589832 | tf_op jit(solution)/shard_map/ppermute | solution.py:53
  249.8 9.0 %collective-permute-start.36 = (bf16[64,768]{1,0:T(8,128)(2,1)S(1)}, bf16[64,768]{1,0:T(8,128)(2,1)S(1)}, u32[]{:S(2)}, u32[]{:S(2)}) collective-permute-start(bf16[64,768]{1,0:T(8,128)(2,1)S(1)} %get-tuple-element.58), channel_id=1, source_target_pairs={{0,1},{1,0},{2,3},{3,2},{4,5},{5,4},{6,7},{7,6},{8,9},{9,8},{10,11... | collective-permute-start | bytes 294920 | tf_op jit(solution)/shard_map/ppermute | solution.py:62
  251.2 7.8 %collective-permute-start.35 = (bf16[64,768]{1,0:T(8,128)(2,1)S(1)}, bf16[64,768]{1,0:T(8,128)(2,1)S(1)}, u32[]{:S(2)}, u32[]{:S(2)}) collective-permute-start(bf16[64,768]{1,0:T(8,128)(2,1)S(1)} %get-tuple-element.57), channel_id=1, source_target_pairs={{0,1},{1,0},{2,3},{3,2},{4,5},{5,4},{6,7},{7,6},{8,9},{9,8},{10,11... | collective-permute-start | bytes 294920 | tf_op jit(solution)/shard_map/ppermute | solution.py:62
  (1 other events, 0.6 us)
Sparse Core Ops, SparseCore 0:
  9.0 101.7 all-gather.1

commit v12 on v8

--- a/solution.py
+++ b/solution.py
@@ -96,7 +96,7 @@
     depth, width = w.shape
     rows = pieces[0].shape[0]
     tokens = len(pieces) * rows
-    tile = 256
+    tile = 512
     return pl.pallas_call(
         mm1_kernel,
         grid=(width // tile,),

time: 266 us -> 265 us (level)
  starting transfers between devices: 71.6 us -> 77.4 us
  waiting for transfers between devices: 66.8 us -> 62.3 us
    ppermute x33, starting transfers between devices: 44.2 us -> 50 us  [hop(): return lax.ppermute(a, ('row', 'col'), pairs)]
    ppermute x33, waiting for transfers between devices: 65.8 us -> 61.3 us  [hop(): return lax.ppermute(a, ('row', 'col'), pairs)]
  transfers between devices with their start and end apart: 39 -> 39, of which waited for: 17 -> 16; matrix products, arithmetic and copies ran while one was open for 6% -> 6% of each run, Pallas kernels for 16% -> 15%
where the time goes in v12:
time: 265 us; the launch traced here: 264 us
  starting transfers between devices  77.4 us (29%)
  waiting for transfers between devices  62.3 us (24%)
  blocking collectives  50 us (19%)
  Pallas kernels  40.9 us (15%)
  between operations  13.7 us (5%)
  local copies, waits for them, and re-layouts  11.1 us (4%)
  matrix products  6.72 us (3%)
    ppermute x33, waiting for transfers between devices, hop(): return lax.ppermute(a, ('row', 'col'), pairs)  61.3 us
    ppermute x33, starting transfers between devices, hop(): return lax.ppermute(a, ('row', 'col'), pairs)  50 us
    all_to_all x2, blocking collectives, exchange(): return lax.all_to_all(a, axis, split_axis=0, concat_axis=0, tiled=True)  38 us
    pallas_call x2, Pallas kernels, matmul_in(): pl.pallas_call(mm1_kernel, grid=(width // tile,), in_specs=[pl.BlockSpec(...  22.1 us
    ppermute x4, starting transfers between devices, swap_cores(): return lax.ppermute(a, 'col', pairs)  19.5 us
    pallas_call x2, Pallas kernels, matmul_out(): pl.pallas_call(mm2_kernel, grid=(2 * steps,), in_specs=[pl.BlockSpec(memo...  15.8 us
    psum x1, blocking collectives, spectral(): lax.psum((jnp.sum(source, axis=-1), jnp.sum(source * source, axis=-1)), '...  12 us
    all_to_all x1, starting transfers between devices, exchange(): return lax.all_to_all(a, axis, split_axis=0, concat_axis=0, tiled=True)  7.85 us
  transfers between devices with their start and end apart: 39, of which 16 were waited for; matrix products, arithmetic and copies ran while one was open for 6% of the time, Pallas kernels for 15%

profile of v12, /device:TPU:1, one launch (start us, length us, event | category | flops | bytes accessed | tf_op | source)
XLA Modules:
  0.0 264.3 jit_solution(15440110044433035662)
XLA Ops:
  6.6 0.7 all-gather.2.cloned.1.call-update
  7.3 1.5 collective-permute-start
  9.1 12.0 %all-reduce = (f32[256]{0:T(256)S(1)}, f32[256]{0:T(256)S(1)}) all-reduce(f32[256]{0:T(256)S(1)} %reduce_sum.34, f32[256]{0:T(256)S(1)} %reduce_sum.32), channel_id=1, replica_groups=mesh['row'=16,'col'=8] {'col'}, use_global_device_ids=true, to_apply=%region_3.4 | all-reduce | flops 512 | bytes 4096 | tf_op jit(solution)/shard_map/psum | solution.py:281
  21.4 1.7 convolution_convert_fusion
  23.0 7.8 %all-to-all-start = ((bf16[16,32,768]{2,1,0:T(8,128)(2,1)}), bf16[16,32,768]{2,1,0:T(8,128)(2,1)S(1)}, u32[]{:S(2)}, u32[]{:S(2)}) async-start(bf16[16,32,768]{2,1,0:T(8,128)(2,1)} %bitcast.3), calls=%async_computation | async-start | bytes 1572864 | tf_op jit(solution)/shard_map/all_to_all | solution.py:253
  30.9 2.4 fusion.13
  33.3 2.4 collective-permute-start.1
  35.7 0.7 dynamic-slice_bitcast_fusion
  36.5 3.4 %collective-permute-start.3 = (f32[2,768]{1,0:T(2,128)S(1)}, f32[2,768]{1,0:T(2,128)S(1)}, u32[]{:S(2)}, u32[]{:S(2)}) collective-permute-start(f32[2,768]{1,0:T(2,128)S(1)} %collective-permute-done.1), channel_id=1, source_target_pairs={{0,2},{1,7},{2,4},{3,1},{4,6},{5,3},{6,0},{7,5},{8,10},{9,15},{10,... | collective-permute-start | bytes 18440 | tf_op jit(solution)/shard_map/ppermute | solution.py:53
  39.9 1.4 reshape_squeeze.6
  41.3 1.2 reshape_squeeze.7
  42.5 0.7 select_reduce_fusion.refs_1_.gain_ref
  43.2 0.9 copy-done.6
  44.1 2.6 fusion.15
  46.7 0.9 fusion.5
  47.7 1.0 add_convert_fusion
  48.7 17.1 %all_to_all.15 = bf16[16,32,768]{2,1,0:T(8,128)(2,1)S(1)} all-to-all(bf16[16,32,768]{2,1,0:T(8,128)(2,1)S(1)} %bitcast.48), channel_id=1, replica_groups=mesh['row'=16,'col'=8] {'row'}, dimensions={0} | all-to-all | bytes 1572864 | tf_op jit(solution)/shard_map/all_to_all | solution.py:253
  66.4 20.9 %all_to_all.16.moved_ref = bf16[8,32,768]{2,1,0:T(8,128)(2,1)S(1)} all-to-all(bf16[8,32,768]{2,1,0:T(8,128)(2,1)S(1)} %bitcast.50), channel_id=1, replica_groups=mesh['row'=16,'col'=8] {'col'}, dimensions={0} | all-to-all | bytes 786432 | tf_op jit(solution)/shard_map/all_to_all | solution.py:253
  87.6 0.7 collective-permute-start.22
  88.3 2.0 collective-permute-start.21
  90.9 1.6 collective-permute-start.5
  92.5 1.9 collective-permute-done.22
  94.4 2.4 collective-permute-done.21
  96.8 2.5 collective-permute-done.20
  99.5 0.6 collective-permute-start.23
  100.1 1.5 collective-permute-done.4
  101.6 1.0 pad_maximum_fusion
  102.6 1.7 collective-permute-start.7
  104.3 1.2 collective-permute-start.24
  105.5 6.0 %collective-permute-done.23.refs_1_ = bf16[64,6144]{1,0:T(8,128)(2,1)S(1)} collective-permute-done((bf16[64,6144]{1,0:T(8,128)(2,1)S(1)}, bf16[64,6144]{1,0:T(8,128)(2,1)S(1)}, u32[]{:S(2)}, u32[]{:S(2)}) %collective-permute-start.23) | collective-permute-done | bytes 786464 | tf_op jit(solution)/shard_map/ppermute | solution.py:53
  111.5 2.6 collective-permute-start.25
  114.1 5.7 %collective-permute-start.13 = (bf16[1536,768]{1,0:T(8,128)(2,1)S(1)}, bf16[1536,768]{1,0:T(8,128)(2,1)}, u32[]{:S(2)}, u32[]{:S(2)}) collective-permute-start(bf16[1536,768]{1,0:T(8,128)(2,1)S(1)} %copy-done.3), channel_id=1, source_target_pairs={{0,1},{1,0},{2,3},{3,2},{4,5},{5,4},{6,7},{7,6},{8,9},{9,8},{10,11... | collective-permute-start | bytes 7077896 | tf_op jit(solution)/shard_map/ppermute | solution.py:62
  119.9 2.7 %collective-permute-start.9 = (bf16[64,6144]{1,0:T(8,128)(2,1)}, bf16[64,6144]{1,0:T(8,128)(2,1)}, u32[]{:S(2)}, u32[]{:S(2)}) collective-permute-start(bf16[64,6144]{1,0:T(8,128)(2,1)} %collective-permute-done.7.refs_1_), channel_id=1, source_target_pairs={{0,8},{1,25},{2,10},{3,27},{4,12},{5,29},{6,14},{7,31},{8,16},{9,1... | collective-permute-start | bytes 2359304 | tf_op jit(solution)/shard_map/ppermute | solution.py:53
  123.2 0.9 copy-done.11
  124.0 3.6 %collective-permute-done.25.refs_3_ = bf16[64,6144]{1,0:T(8,128)(2,1)} collective-permute-done((bf16[64,6144]{1,0:T(8,128)(2,1)S(1)}, bf16[64,6144]{1,0:T(8,128)(2,1)}, u32[]{:S(2)}, u32[]{:S(2)}) %collective-permute-start.25) | collective-permute-done | bytes 786464 | tf_op jit(solution)/shard_map/ppermute | solution.py:53
  127.6 11.1 %shard_map.143.refs_0_ = bf16[256,1536]{1,0:T(8,128)(2,1)} custom-call(bf16[64,6144]{1,0:T(8,128)(2,1)} %bitcast.47, bf16[64,6144]{1,0:T(8,128)(2,1)} %copy-done.10, bf16[64,6144]{1,0:T(8,128)(2,1)} %copy-done.11, bf16[64,6144]{1,0:T(8,128)(2,1)} %collective-permute-done.25.refs_3_, bf16[6144,1536]{1,0:T(8,128)(2,1)} %all-gather.2.cloned.1.call-done.refs_4_, ...), custom_call_target="tpu_custom_call" | custom-call | flops 4831838208 | bytes 22020096 | tf_op jit(solution)/shard_map/pallas_call | solution.py:100
  138.7 0.9 collective-permute-start.26
  139.6 11.0 %shard_map.138.refs_0_ = bf16[256,1536]{1,0:T(8,128)(2,1)} custom-call(bf16[64,6144]{1,0:T(8,128)(2,1)} %bitcast.14.refs_0_, bf16[64,6144]{1,0:T(8,128)(2,1)} %collective-permute-done.7.refs_1_, bf16[64,6144]{1,0:T(8,128)(2,1)} %collective-permute-done.8.refs_2_, bf16[64,6144]{1,0:T(8,128)(2,1)} %collective-permute-done.9.refs_3_, ...), custom_call_target="tpu_custom_call" | custom-call | flops 4831838208 | bytes 22020096 | tf_op jit(solution)/shard_map/pallas_call | solution.py:100
  150.6 0.8 collective-permute-start.10
  151.4 0.7 collective-permute-start.27
  152.1 2.0 collective-permute-start.28
  154.1 0.9 copy-done.4
  155.0 9.9 %collective-permute-done.10.refs_1_ = bf16[256,1536]{1,0:T(8,128)(2,1)S(1)} collective-permute-done((bf16[256,1536]{1,0:T(8,128)(2,1)}, bf16[256,1536]{1,0:T(8,128)(2,1)S(1)}, u32[]{:S(2)}, u32[]{:S(2)}) %collective-permute-start.10) | collective-permute-done | bytes 786464 | tf_op jit(solution)/shard_map/ppermute | solution.py:53
  165.0 5.5 %collective-permute-done.27.refs_2_ = bf16[256,1536]{1,0:T(8,128)(2,1)S(1)} collective-permute-done((bf16[256,1536]{1,0:T(8,128)(2,1)S(1)}, bf16[256,1536]{1,0:T(8,128)(2,1)S(1)}, u32[]{:S(2)}, u32[]{:S(2)}) %collective-permute-start.27) | collective-permute-done | bytes 786464 | tf_op jit(solution)/shard_map/ppermute | solution.py:53
  170.5 11.3 %collective-permute-done.28.refs_3_ = bf16[256,1536]{1,0:T(8,128)(2,1)S(1)} collective-permute-done((bf16[256,1536]{1,0:T(8,128)(2,1)S(1)}, bf16[256,1536]{1,0:T(8,128)(2,1)S(1)}, u32[]{:S(2)}, u32[]{:S(2)}) %collective-permute-start.28) | collective-permute-done | bytes 786464 | tf_op jit(solution)/shard_map/ppermute | solution.py:53
  181.8 1.1 copy-done.5
  182.9 7.9 %shard_map.144 = (bf16[256,1536]{1,0:T(8,128)(2,1)S(1)}, bf16[256,1536]{1,0:T(8,128)(2,1)S(1)}, bf16[256,1536]{1,0:T(8,128)(2,1)S(1)}, bf16[256,1536]{1,0:T(8,128)(2,1)S(1)}) custom-call(bf16[256,1536]{1,0:T(8,128)(2,1)S(1)} %copy-done.1, bf16[256,1536]{1,0:T(8,128)(2,1)S(1)} %copy-done.5, bf16[256,1536]{1,0:T(8,128)(2,1)S(1)} %collective-permute-done.27.refs_2_, ...), custom_call_target="tpu_custom_call" | custom-call | flops 4831838208 | bytes 11010048 | tf_op jit(solution)/shard_map/pallas_call | solution.py:157
  190.9 2.4 collective-permute-start.30
  193.3 2.4 collective-permute-done.12.refs_3_
  195.7 7.9 %shard_map.139 = (bf16[256,1536]{1,0:T(8,128)(2,1)S(1)}, bf16[256,1536]{1,0:T(8,128)(2,1)S(1)}, bf16[256,1536]{1,0:T(8,128)(2,1)S(1)}, bf16[256,1536]{1,0:T(8,128)(2,1)S(1)}) custom-call(bf16[256,1536]{1,0:T(8,128)(2,1)S(1)} %copy-done, bf16[256,1536]{1,0:T(8,128)(2,1)S(1)} %collective-permute-done.10.refs_1_, ...), custom_call_target="tpu_custom_call" | custom-call | flops 4831838208 | bytes 11010048 | tf_op jit(solution)/shard_map/pallas_call | solution.py:157
  203.9 2.7 %collective-permute-start.29 = (bf16[256,1536]{1,0:T(8,128)(2,1)S(1)}, bf16[256,1536]{1,0:T(8,128)(2,1)S(1)}, u32[]{:S(2)}, u32[]{:S(2)}) collective-permute-start(bf16[256,1536]{1,0:T(8,128)(2,1)S(1)} %get-tuple-element.39), channel_id=1, source_target_pairs={{0,32},{1,97},{2,34},{3,99},{4,36},{5,101},{6,38},{7,103},{8,40},{... | collective-permute-start | bytes 2359304 | tf_op jit(solution)/shard_map/ppermute | solution.py:53
  206.8 3.5 %collective-permute-start.14 = (bf16[256,1536]{1,0:T(8,128)(2,1)S(1)}, bf16[256,1536]{1,0:T(8,128)(2,1)S(1)}, u32[]{:S(2)}, u32[]{:S(2)}) collective-permute-start(bf16[256,1536]{1,0:T(8,128)(2,1)S(1)} %get-tuple-element.29), channel_id=1, source_target_pairs={{0,8},{1,25},{2,10},{3,27},{4,12},{5,29},{6,14},{7,31},{8,16},{9,1... | collective-permute-start | bytes 2359304 | tf_op jit(solution)/shard_map/ppermute | solution.py:53
  210.4 5.4 %collective-permute-done.15.b = bf16[256,1536]{1,0:T(8,128)(2,1)S(1)} collective-permute-done((bf16[256,1536]{1,0:T(8,128)(2,1)S(1)}, bf16[256,1536]{1,0:T(8,128)(2,1)S(1)}, u32[]{:S(2)}, u32[]{:S(2)}) %collective-permute-start.15) | collective-permute-done | bytes 786464 | tf_op jit(solution)/shard_map/ppermute | solution.py:53
  216.1 4.2 %collective-permute-done.29.b = bf16[256,1536]{1,0:T(8,128)(2,1)S(1)} collective-permute-done((bf16[256,1536]{1,0:T(8,128)(2,1)S(1)}, bf16[256,1536]{1,0:T(8,128)(2,1)S(1)}, u32[]{:S(2)}, u32[]{:S(2)}) %collective-permute-start.29) | collective-permute-done | bytes 786464 | tf_op jit(solution)/shard_map/ppermute | solution.py:53
  220.2 1.5 collective-permute-done.31.c
  222.1 6.8 %collective-permute-start.32 = (bf16[64,1536]{1,0:T(8,128)(2,1)S(1)}, bf16[64,1536]{1,0:T(8,128)(2,1)S(1)}, u32[]{:S(2)}, u32[]{:S(2)}) collective-permute-start(bf16[64,1536]{1,0:T(8,128)(2,1)S(1)} %get-tuple-element.43), channel_id=1, source_target_pairs={{0,24},{1,25},{2,26},{3,27},{4,28},{5,29},{6,30},{7,31},{8,0},{9,1... | collective-permute-start | bytes 589832 | tf_op jit(solution)/shard_map/ppermute | solution.py:53
  228.9 1.6 collective-permute-start.34
  230.6 3.0 %collective-permute-done.16.c = bf16[256,1536]{1,0:T(8,128)(2,1)S(1)} collective-permute-done((bf16[256,1536]{1,0:T(8,128)(2,1)S(1)}, bf16[256,1536]{1,0:T(8,128)(2,1)S(1)}, u32[]{:S(2)}, u32[]{:S(2)}) %collective-permute-start.16) | collective-permute-done | bytes 786464 | tf_op jit(solution)/shard_map/ppermute | solution.py:53
  233.9 5.6 %collective-permute-start.17 = (bf16[64,1536]{1,0:T(8,128)(2,1)S(1)}, bf16[64,1536]{1,0:T(8,128)(2,1)S(1)}, u32[]{:S(2)}, u32[]{:S(2)}) collective-permute-start(bf16[64,1536]{1,0:T(8,128)(2,1)S(1)} %get-tuple-element.33), channel_id=1, source_target_pairs={{0,96},{1,97},{2,98},{3,99},{4,100},{5,101},{6,102},{7,103},{8,104... | collective-permute-start | bytes 589832 | tf_op jit(solution)/shard_map/ppermute | solution.py:53
  239.5 3.1 %collective-permute-start.19 = (bf16[64,1536]{1,0:T(8,128)(2,1)S(1)}, bf16[64,1536]{1,0:T(8,128)(2,1)S(1)}, u32[]{:S(2)}, u32[]{:S(2)}) collective-permute-start(bf16[64,1536]{1,0:T(8,128)(2,1)S(1)} %get-tuple-element.35), channel_id=1, source_target_pairs={{0,64},{1,65},{2,66},{3,67},{4,68},{5,69},{6,70},{7,71},{8,72},{9,... | collective-permute-start | bytes 589832 | tf_op jit(solution)/shard_map/ppermute | solution.py:53
  242.7 6.1 %collective-permute-start.36 = (bf16[64,768]{1,0:T(8,128)(2,1)S(1)}, bf16[64,768]{1,0:T(8,128)(2,1)S(1)}, u32[]{:S(2)}, u32[]{:S(2)}) collective-permute-start(bf16[64,768]{1,0:T(8,128)(2,1)S(1)} %get-tuple-element.48), channel_id=1, source_target_pairs={{0,1},{1,0},{2,3},{3,2},{4,5},{5,4},{6,7},{7,6},{8,9},{9,8},{10,11... | collective-permute-start | bytes 294920 | tf_op jit(solution)/shard_map/ppermute | solution.py:62
  249.0 6.2 %collective-permute-start.35 = (bf16[64,768]{1,0:T(8,128)(2,1)S(1)}, bf16[64,768]{1,0:T(8,128)(2,1)S(1)}, u32[]{:S(2)}, u32[]{:S(2)}) collective-permute-start(bf16[64,768]{1,0:T(8,128)(2,1)S(1)} %get-tuple-element.47), channel_id=1, source_target_pairs={{0,1},{1,0},{2,3},{3,2},{4,5},{5,4},{6,7},{7,6},{8,9},{9,8},{10,11... | collective-permute-start | bytes 294920 | tf_op jit(solution)/shard_map/ppermute | solution.py:62
  255.1 0.7 dynamic-slice_bitcast_fusion.1.place_ref
  256.1 1.4 shard_map.148
  (96 shorter events, 5.0 us)
Async XLA Ops:
  6.5 14.8 %copy-start.15 = (f32[512,256]{1,0:T(8,128)S(1)}, f32[512,256]{1,0:T(8,128)}, u32[]{:S(2)}) copy-start(f32[512,256]{1,0:T(8,128)} %constant.29.clone) | copy-start | bytes 1572868
  6.5 0.7 copy-start.18
  6.5 2.2 copy-start.8
  6.5 14.6 %copy-start.17 = (f32[768]{0:T(1024)S(1)}, f32[768]{0:T(1024)}, u32[]{:S(2)}) copy-start(f32[768]{0:T(1024)} %param.16) | copy-start | bytes 9220
  6.5 121.1 %all-gather.2.cloned.1.call-start = ((), (), s32[]{:S(2)}) async-start(), calls=%async_computation.3 | async-start | bytes 21233664 | tf_op jit(solution)/shard_map/all_gather | solution.py:355
  7.3 26.0 %collective-permute-start = (f32[768]{0:T(1024)S(1)}, f32[768]{0:T(1024)S(1)}, u32[]{:S(2)}, u32[]{:S(2)}) collective-permute-start(f32[768]{0:T(1024)S(1)} %copy-done.18), channel_id=1, source_target_pairs={{0,1},{1,0},{2,3},{3,2},{4,5},{5,4},{6,7},{7,6},{8,9},{9,8},{10,11... | collective-permute-start | bytes 9224 | tf_op jit(solution)/shard_map/ppermute | solution.py:62
  23.0 20.2 %all-to-all-start = ((bf16[16,32,768]{2,1,0:T(8,128)(2,1)}), bf16[16,32,768]{2,1,0:T(8,128)(2,1)S(1)}, u32[]{:S(2)}, u32[]{:S(2)}) async-start(bf16[16,32,768]{2,1,0:T(8,128)(2,1)} %bitcast.3), calls=%async_computation | async-start | bytes 1572864 | tf_op jit(solution)/shard_map/all_to_all | solution.py:253
  33.3 3.2 %collective-permute-start.1 = (f32[2,768]{1,0:T(2,128)S(1)}, f32[2,768]{1,0:T(2,128)S(1)}, u32[]{:S(2)}, u32[]{:S(2)}) collective-permute-start(f32[2,768]{1,0:T(2,128)S(1)} %pad_maximum_fusion.2), channel_id=1, source_target_pairs={{0,2},{1,7},{2,4},{3,1},{4,6},{5,3},{6,0},{7,5},{8,10},{9,15},{10,... | collective-permute-start | bytes 18440 | tf_op jit(solution)/shard_map/ppermute | solution.py:53
  36.4 6.1 %collective-permute-start.2 = (f32[2,768]{1,0:T(2,128)S(1)}, f32[2,768]{1,0:T(2,128)S(1)}, u32[]{:S(2)}, u32[]{:S(2)}) collective-permute-start(f32[2,768]{1,0:T(2,128)S(1)} %pad_maximum_fusion.2), channel_id=1, source_target_pairs={{0,6},{1,3},{2,0},{3,5},{4,2},{5,7},{6,4},{7,1},{8,14},{9,11},{10,... | collective-permute-start | bytes 18440 | tf_op jit(solution)/shard_map/ppermute | solution.py:53
  36.5 6.0 %collective-permute-start.3 = (f32[2,768]{1,0:T(2,128)S(1)}, f32[2,768]{1,0:T(2,128)S(1)}, u32[]{:S(2)}, u32[]{:S(2)}) collective-permute-start(f32[2,768]{1,0:T(2,128)S(1)} %collective-permute-done.1), channel_id=1, source_target_pairs={{0,2},{1,7},{2,4},{3,1},{4,6},{5,3},{6,0},{7,5},{8,10},{9,15},{10,... | collective-permute-start | bytes 18440 | tf_op jit(solution)/shard_map/ppermute | solution.py:53
  43.2 0.9 copy-start.6
  44.1 2.6 copy-start.7
  44.1 2.6 copy-start.13
  46.7 1.0 copy-start.12
  48.7 17.1 %copy-start.14 = (f32[256,512]{1,0:T(8,128)S(1)}, f32[256,512]{1,0:T(8,128)}, u32[]{:S(2)}) copy-start(f32[256,512]{1,0:T(8,128)} %constant.32.clone) | copy-start | bytes 1572868
  65.8 21.5 %copy-start.2 = (f32[8,768]{1,0:T(8,128)S(1)}, f32[8,768]{1,0:T(8,128)}, u32[]{:S(2)}) copy-start(f32[8,768]{1,0:T(8,128)} %select_reduce_fusion.refs_1_.gain_ref) | copy-start | bytes 73732
  87.6 6.8 %collective-permute-start.22 = (bf16[16,6144]{1,0:T(8,128)(2,1)S(1)}, bf16[16,6144]{1,0:T(8,128)(2,1)S(1)}, u32[]{:S(2)}, u32[]{:S(2)}) collective-permute-start(bf16[16,6144]{1,0:T(8,128)(2,1)S(1)} %get-tuple-element.37), channel_id=1, source_target_pairs={{0,16},{1,17},{2,18},{3,19},{4,20},{5,21},{6,22},{7,23},{8,24},{9,... | collective-permute-start | bytes 589832 | tf_op jit(solution)/shard_map/ppermute | solution.py:53
  88.3 8.5 %collective-permute-start.21 = (bf16[16,6144]{1,0:T(8,128)(2,1)S(1)}, bf16[16,6144]{1,0:T(8,128)(2,1)S(1)}, u32[]{:S(2)}, u32[]{:S(2)}) collective-permute-start(bf16[16,6144]{1,0:T(8,128)(2,1)S(1)} %get-tuple-element.37), channel_id=1, source_target_pairs={{0,24},{1,25},{2,26},{3,27},{4,28},{5,29},{6,30},{7,31},{8,0},{9,1... | collective-permute-start | bytes 589832 | tf_op jit(solution)/shard_map/ppermute | solution.py:53
  90.4 9.0 %collective-permute-start.20 = (bf16[16,6144]{1,0:T(8,128)(2,1)S(1)}, bf16[16,6144]{1,0:T(8,128)(2,1)S(1)}, u32[]{:S(2)}, u32[]{:S(2)}) collective-permute-start(bf16[16,6144]{1,0:T(8,128)(2,1)S(1)} %get-tuple-element.37), channel_id=1, source_target_pairs={{0,8},{1,9},{2,10},{3,11},{4,12},{5,13},{6,14},{7,15},{8,16},{9,17... | collective-permute-start | bytes 589832 | tf_op jit(solution)/shard_map/ppermute | solution.py:53
  90.4 9.7 %collective-permute-start.6 = (bf16[16,6144]{1,0:T(8,128)(2,1)S(1)}, bf16[16,6144]{1,0:T(8,128)(2,1)S(1)}, u32[]{:S(2)}, u32[]{:S(2)}) collective-permute-start(bf16[16,6144]{1,0:T(8,128)(2,1)S(1)} %get-tuple-element.27), channel_id=1, source_target_pairs={{0,64},{1,65},{2,66},{3,67},{4,68},{5,69},{6,70},{7,71},{8,72},{9,... | collective-permute-start | bytes 589832 | tf_op jit(solution)/shard_map/ppermute | solution.py:53
  90.9 9.2 %collective-permute-start.5 = (bf16[16,6144]{1,0:T(8,128)(2,1)S(1)}, bf16[16,6144]{1,0:T(8,128)(2,1)S(1)}, u32[]{:S(2)}, u32[]{:S(2)}) collective-permute-start(bf16[16,6144]{1,0:T(8,128)(2,1)S(1)} %get-tuple-element.27), channel_id=1, source_target_pairs={{0,96},{1,97},{2,98},{3,99},{4,100},{5,101},{6,102},{7,103},{8,104... | collective-permute-start | bytes 589832 | tf_op jit(solution)/shard_map/ppermute | solution.py:53
  94.4 7.2 %collective-permute-start.4 = (bf16[16,6144]{1,0:T(8,128)(2,1)S(1)}, bf16[16,6144]{1,0:T(8,128)(2,1)S(1)}, u32[]{:S(2)}, u32[]{:S(2)}) collective-permute-start(bf16[16,6144]{1,0:T(8,128)(2,1)S(1)} %get-tuple-element.27), channel_id=1, source_target_pairs={{0,32},{1,33},{2,34},{3,35},{4,36},{5,37},{6,38},{7,39},{8,40},{9,... | collective-permute-start | bytes 589832 | tf_op jit(solution)/shard_map/ppermute | solution.py:53
  99.3 14.8 %copy-start.3 = (bf16[1536,768]{1,0:T(8,128)(2,1)S(1)}, bf16[1536,768]{1,0:T(8,128)(2,1)}, u32[]{:S(2)}) copy-start(bf16[1536,768]{1,0:T(8,128)(2,1)} %refs_4_.3) | copy-start | bytes 7077892
  99.4 23.2 %copy-start.16 = (f32[1536]{0:T(1024)S(1)}, f32[1536]{0:T(1024)}, u32[]{:S(2)}) copy-start(f32[1536]{0:T(1024)} %param.19) | copy-start | bytes 18436
  99.5 12.1 %copy-start.9 = (bf16[4,16,6144]{2,1,0:T(8,128)(2,1)}, bf16[4,16,6144]{2,1,0:T(8,128)(2,1)S(1)}, u32[]{:S(2)}) copy-start(bf16[4,16,6144]{2,1,0:T(8,128)(2,1)S(1)} %pad_maximum_fusion.1) | copy-start | bytes 2359300
  99.5 12.0 %collective-permute-start.23 = (bf16[64,6144]{1,0:T(8,128)(2,1)S(1)}, bf16[64,6144]{1,0:T(8,128)(2,1)S(1)}, u32[]{:S(2)}, u32[]{:S(2)}) collective-permute-start(bf16[64,6144]{1,0:T(8,128)(2,1)S(1)} %bitcast.45), channel_id=1, source_target_pairs={{0,32},{1,97},{2,34},{3,99},{4,36},{5,101},{6,38},{7,103},{8,40},{... | collective-permute-start | bytes 2359304 | tf_op jit(solution)/shard_map/ppermute | solution.py:53
  102.6 17.2 %collective-permute-start.7 = (bf16[64,6144]{1,0:T(8,128)(2,1)}, bf16[64,6144]{1,0:T(8,128)(2,1)}, u32[]{:S(2)}, u32[]{:S(2)}) collective-permute-start(bf16[64,6144]{1,0:T(8,128)(2,1)} %bitcast.14.refs_0_), channel_id=1, source_target_pairs={{0,8},{1,25},{2,10},{3,27},{4,12},{5,29},{6,14},{7,31},{8,16},{9,1... | collective-permute-start | bytes 2359304 | tf_op jit(solution)/shard_map/ppermute | solution.py:53
  104.3 18.9 %collective-permute-start.24 = (bf16[64,6144]{1,0:T(8,128)(2,1)S(1)}, bf16[64,6144]{1,0:T(8,128)(2,1)S(1)}, u32[]{:S(2)}, u32[]{:S(2)}) collective-permute-start(bf16[64,6144]{1,0:T(8,128)(2,1)S(1)} %bitcast.46), channel_id=1, source_target_pairs={{0,96},{1,33},{2,98},{3,35},{4,100},{5,37},{6,102},{7,39},{8,104},... | collective-permute-start | bytes 2359304 | tf_op jit(solution)/shard_map/ppermute | solution.py:53
  111.5 11.6 %copy-start.10 = (bf16[64,6144]{1,0:T(8,128)(2,1)}, bf16[64,6144]{1,0:T(8,128)(2,1)S(1)}, u32[]{:S(2)}) copy-start(bf16[64,6144]{1,0:T(8,128)(2,1)S(1)} %collective-permute-done.23.refs_1_) | copy-start | bytes 2359300
  111.5 16.1 %collective-permute-start.25 = (bf16[64,6144]{1,0:T(8,128)(2,1)S(1)}, bf16[64,6144]{1,0:T(8,128)(2,1)}, u32[]{:S(2)}, u32[]{:S(2)}) collective-permute-start(bf16[64,6144]{1,0:T(8,128)(2,1)S(1)} %collective-permute-done.23.refs_1_), channel_id=1, source_target_pairs={{0,32},{1,97},{2,34},{3,99},{4,36},{5,101},{6,38},{7,103},{8,40},{... | collective-permute-start | bytes 2359304 | tf_op jit(solution)/shard_map/ppermute | solution.py:53
  114.1 50.8 %collective-permute-start.13 = (bf16[1536,768]{1,0:T(8,128)(2,1)S(1)}, bf16[1536,768]{1,0:T(8,128)(2,1)}, u32[]{:S(2)}, u32[]{:S(2)}) collective-permute-start(bf16[1536,768]{1,0:T(8,128)(2,1)S(1)} %copy-done.3), channel_id=1, source_target_pairs={{0,1},{1,0},{2,3},{3,2},{4,5},{5,4},{6,7},{7,6},{8,9},{9,8},{10,11... | collective-permute-start | bytes 7077896 | tf_op jit(solution)/shard_map/ppermute | solution.py:62
  119.9 19.7 %collective-permute-start.8 = (bf16[64,6144]{1,0:T(8,128)(2,1)}, bf16[64,6144]{1,0:T(8,128)(2,1)}, u32[]{:S(2)}, u32[]{:S(2)}) collective-permute-start(bf16[64,6144]{1,0:T(8,128)(2,1)} %bitcast.14.refs_0_), channel_id=1, source_target_pairs={{0,24},{1,9},{2,26},{3,11},{4,28},{5,13},{6,30},{7,15},{8,0},{9,17... | collective-permute-start | bytes 2359304 | tf_op jit(solution)/shard_map/ppermute | solution.py:53
  119.9 19.7 %collective-permute-start.9 = (bf16[64,6144]{1,0:T(8,128)(2,1)}, bf16[64,6144]{1,0:T(8,128)(2,1)}, u32[]{:S(2)}, u32[]{:S(2)}) collective-permute-start(bf16[64,6144]{1,0:T(8,128)(2,1)} %collective-permute-done.7.refs_1_), channel_id=1, source_target_pairs={{0,8},{1,25},{2,10},{3,27},{4,12},{5,29},{6,14},{7,31},{8,16},{9,1... | collective-permute-start | bytes 2359304 | tf_op jit(solution)/shard_map/ppermute | solution.py:53
  123.2 0.9 copy-start.11
  138.7 12.7 %copy-start.1 = (bf16[256,1536]{1,0:T(8,128)(2,1)S(1)}, bf16[256,1536]{1,0:T(8,128)(2,1)}, u32[]{:S(2)}) copy-start(bf16[256,1536]{1,0:T(8,128)(2,1)} %shard_map.143.refs_0_) | copy-start | bytes 2359300
  138.7 13.4 %collective-permute-start.26 = (bf16[256,1536]{1,0:T(8,128)(2,1)}, bf16[256,1536]{1,0:T(8,128)(2,1)S(1)}, u32[]{:S(2)}, u32[]{:S(2)}) collective-permute-start(bf16[256,1536]{1,0:T(8,128)(2,1)} %shard_map.143.refs_0_), channel_id=1, source_target_pairs={{0,2},{1,7},{2,4},{3,1},{4,6},{5,3},{6,0},{7,5},{8,10},{9,15},{10,... | collective-permute-start | bytes 2359304 | tf_op jit(solution)/shard_map/ppermute | solution.py:53
  150.6 45.1 %copy-start = (bf16[256,1536]{1,0:T(8,128)(2,1)S(1)}, bf16[256,1536]{1,0:T(8,128)(2,1)}, u32[]{:S(2)}) copy-start(bf16[256,1536]{1,0:T(8,128)(2,1)} %shard_map.138.refs_0_) | copy-start | bytes 2359300
  150.6 14.3 %collective-permute-start.10 = (bf16[256,1536]{1,0:T(8,128)(2,1)}, bf16[256,1536]{1,0:T(8,128)(2,1)S(1)}, u32[]{:S(2)}, u32[]{:S(2)}) collective-permute-start(bf16[256,1536]{1,0:T(8,128)(2,1)} %shard_map.138.refs_0_), channel_id=1, source_target_pairs={{0,2},{1,7},{2,4},{3,1},{4,6},{5,3},{6,0},{7,5},{8,10},{9,15},{10,... | collective-permute-start | bytes 2359304 | tf_op jit(solution)/shard_map/ppermute | solution.py:53
  151.4 19.0 %collective-permute-start.27 = (bf16[256,1536]{1,0:T(8,128)(2,1)S(1)}, bf16[256,1536]{1,0:T(8,128)(2,1)S(1)}, u32[]{:S(2)}, u32[]{:S(2)}) collective-permute-start(bf16[256,1536]{1,0:T(8,128)(2,1)S(1)} %copy-done.1), channel_id=1, source_target_pairs={{0,6},{1,3},{2,0},{3,5},{4,2},{5,7},{6,4},{7,1},{8,14},{9,11},{10,... | collective-permute-start | bytes 2359304 | tf_op jit(solution)/shard_map/ppermute | solution.py:53
  152.1 29.7 %collective-permute-start.28 = (bf16[256,1536]{1,0:T(8,128)(2,1)S(1)}, bf16[256,1536]{1,0:T(8,128)(2,1)S(1)}, u32[]{:S(2)}, u32[]{:S(2)}) collective-permute-start(bf16[256,1536]{1,0:T(8,128)(2,1)S(1)} %collective-permute-done.26.refs_1_), channel_id=1, source_target_pairs={{0,2},{1,7},{2,4},{3,1},{4,6},{5,3},{6,0},{7,5},{8,10},{9,15},{10,... | collective-permute-start | bytes 2359304 | tf_op jit(solution)/shard_map/ppermute | solution.py:53
  154.1 0.9 copy-start.4
  155.0 38.3 %collective-permute-start.11 = (bf16[256,1536]{1,0:T(8,128)(2,1)}, bf16[256,1536]{1,0:T(8,128)(2,1)S(1)}, u32[]{:S(2)}, u32[]{:S(2)}) collective-permute-start(bf16[256,1536]{1,0:T(8,128)(2,1)} %shard_map.138.refs_0_), channel_id=1, source_target_pairs={{0,6},{1,3},{2,0},{3,5},{4,2},{5,7},{6,4},{7,1},{8,14},{9,11},{10,... | collective-permute-start | bytes 2359304 | tf_op jit(solution)/shard_map/ppermute | solution.py:53
  165.0 30.7 %collective-permute-start.12 = (bf16[256,1536]{1,0:T(8,128)(2,1)S(1)}, bf16[256,1536]{1,0:T(8,128)(2,1)S(1)}, u32[]{:S(2)}, u32[]{:S(2)}) collective-permute-start(bf16[256,1536]{1,0:T(8,128)(2,1)S(1)} %collective-permute-done.10.refs_1_), channel_id=1, source_target_pairs={{0,2},{1,7},{2,4},{3,1},{4,6},{5,3},{6,0},{7,5},{8,10},{9,15},{10,... | collective-permute-start | bytes 2359304 | tf_op jit(solution)/shard_map/ppermute | solution.py:53
  181.8 1.1 copy-start.5
  190.9 15.7 %collective-permute-start.30 = (bf16[256,1536]{1,0:T(8,128)(2,1)S(1)}, bf16[256,1536]{1,0:T(8,128)(2,1)S(1)}, u32[]{:S(2)}, u32[]{:S(2)}) collective-permute-start(bf16[256,1536]{1,0:T(8,128)(2,1)S(1)} %get-tuple-element.41), channel_id=1, source_target_pairs={{0,96},{1,33},{2,98},{3,35},{4,100},{5,37},{6,102},{7,39},{8,104},... | collective-permute-start | bytes 2359304 | tf_op jit(solution)/shard_map/ppermute | solution.py:53
  203.6 12.1 %collective-permute-start.15 = (bf16[256,1536]{1,0:T(8,128)(2,1)S(1)}, bf16[256,1536]{1,0:T(8,128)(2,1)S(1)}, u32[]{:S(2)}, u32[]{:S(2)}) collective-permute-start(bf16[256,1536]{1,0:T(8,128)(2,1)S(1)} %get-tuple-element.31), channel_id=1, source_target_pairs={{0,24},{1,9},{2,26},{3,11},{4,28},{5,13},{6,30},{7,15},{8,0},{9,17... | collective-permute-start | bytes 2359304 | tf_op jit(solution)/shard_map/ppermute | solution.py:53
  203.9 16.4 %collective-permute-start.29 = (bf16[256,1536]{1,0:T(8,128)(2,1)S(1)}, bf16[256,1536]{1,0:T(8,128)(2,1)S(1)}, u32[]{:S(2)}, u32[]{:S(2)}) collective-permute-start(bf16[256,1536]{1,0:T(8,128)(2,1)S(1)} %get-tuple-element.39), channel_id=1, source_target_pairs={{0,32},{1,97},{2,34},{3,99},{4,36},{5,101},{6,38},{7,103},{8,40},{... | collective-permute-start | bytes 2359304 | tf_op jit(solution)/shard_map/ppermute | solution.py:53
  206.8 15.0 %collective-permute-start.31 = (bf16[256,1536]{1,0:T(8,128)(2,1)S(1)}, bf16[256,1536]{1,0:T(8,128)(2,1)S(1)}, u32[]{:S(2)}, u32[]{:S(2)}) collective-permute-start(bf16[256,1536]{1,0:T(8,128)(2,1)S(1)} %shard_map.145), channel_id=1, source_target_pairs={{0,96},{1,33},{2,98},{3,35},{4,100},{5,37},{6,102},{7,39},{8,104},... | collective-permute-start | bytes 2359304 | tf_op jit(solution)/shard_map/ppermute | solution.py:53
  206.8 23.7 %collective-permute-start.14 = (bf16[256,1536]{1,0:T(8,128)(2,1)S(1)}, bf16[256,1536]{1,0:T(8,128)(2,1)S(1)}, u32[]{:S(2)}, u32[]{:S(2)}) collective-permute-start(bf16[256,1536]{1,0:T(8,128)(2,1)S(1)} %get-tuple-element.29), channel_id=1, source_target_pairs={{0,8},{1,25},{2,10},{3,27},{4,12},{5,29},{6,14},{7,31},{8,16},{9,1... | collective-permute-start | bytes 2359304 | tf_op jit(solution)/shard_map/ppermute | solution.py:53
  216.0 17.6 %collective-permute-start.16 = (bf16[256,1536]{1,0:T(8,128)(2,1)S(1)}, bf16[256,1536]{1,0:T(8,128)(2,1)S(1)}, u32[]{:S(2)}, u32[]{:S(2)}) collective-permute-start(bf16[256,1536]{1,0:T(8,128)(2,1)S(1)} %shard_map.140), channel_id=1, source_target_pairs={{0,24},{1,9},{2,26},{3,11},{4,28},{5,13},{6,30},{7,15},{8,0},{9,17... | collective-permute-start | bytes 2359304 | tf_op jit(solution)/shard_map/ppermute | solution.py:53
  222.1 20.5 %copy-start.19 = (f32[768]{0:T(1024)S(1)}, f32[768]{0:T(1024)}, u32[]{:S(2)}) copy-start(f32[768]{0:T(1024)} %param.21) | copy-start | bytes 9220
  222.1 17.4 %collective-permute-start.32 = (bf16[64,1536]{1,0:T(8,128)(2,1)S(1)}, bf16[64,1536]{1,0:T(8,128)(2,1)S(1)}, u32[]{:S(2)}, u32[]{:S(2)}) collective-permute-start(bf16[64,1536]{1,0:T(8,128)(2,1)S(1)} %get-tuple-element.43), channel_id=1, source_target_pairs={{0,24},{1,25},{2,26},{3,27},{4,28},{5,29},{6,30},{7,31},{8,0},{9,1... | collective-permute-start | bytes 589832 | tf_op jit(solution)/shard_map/ppermute | solution.py:53
  228.9 13.7 %collective-permute-start.33 = (bf16[64,1536]{1,0:T(8,128)(2,1)S(1)}, bf16[64,1536]{1,0:T(8,128)(2,1)S(1)}, u32[]{:S(2)}, u32[]{:S(2)}) collective-permute-start(bf16[64,1536]{1,0:T(8,128)(2,1)S(1)} %get-tuple-element.44), channel_id=1, source_target_pairs={{0,8},{1,9},{2,10},{3,11},{4,12},{5,13},{6,14},{7,15},{8,16},{9,17... | collective-permute-start | bytes 589832 | tf_op jit(solution)/shard_map/ppermute | solution.py:53
  228.9 13.7 %collective-permute-start.34 = (bf16[64,1536]{1,0:T(8,128)(2,1)S(1)}, bf16[64,1536]{1,0:T(8,128)(2,1)S(1)}, u32[]{:S(2)}, u32[]{:S(2)}) collective-permute-start(bf16[64,1536]{1,0:T(8,128)(2,1)S(1)} %get-tuple-element.45), channel_id=1, source_target_pairs={{0,16},{1,17},{2,18},{3,19},{4,20},{5,21},{6,22},{7,23},{8,24},{9,... | collective-permute-start | bytes 589832 | tf_op jit(solution)/shard_map/ppermute | solution.py:53
  233.9 14.9 %collective-permute-start.17 = (bf16[64,1536]{1,0:T(8,128)(2,1)S(1)}, bf16[64,1536]{1,0:T(8,128)(2,1)S(1)}, u32[]{:S(2)}, u32[]{:S(2)}) collective-permute-start(bf16[64,1536]{1,0:T(8,128)(2,1)S(1)} %get-tuple-element.33), channel_id=1, source_target_pairs={{0,96},{1,97},{2,98},{3,99},{4,100},{5,101},{6,102},{7,103},{8,104... | collective-permute-start | bytes 589832 | tf_op jit(solution)/shard_map/ppermute | solution.py:53
  239.5 9.3 %collective-permute-start.18 = (bf16[64,1536]{1,0:T(8,128)(2,1)S(1)}, bf16[64,1536]{1,0:T(8,128)(2,1)S(1)}, u32[]{:S(2)}, u32[]{:S(2)}) collective-permute-start(bf16[64,1536]{1,0:T(8,128)(2,1)S(1)} %get-tuple-element.34), channel_id=1, source_target_pairs={{0,32},{1,33},{2,34},{3,35},{4,36},{5,37},{6,38},{7,39},{8,40},{9,... | collective-permute-start | bytes 589832 | tf_op jit(solution)/shard_map/ppermute | solution.py:53
  239.5 9.3 %collective-permute-start.19 = (bf16[64,1536]{1,0:T(8,128)(2,1)S(1)}, bf16[64,1536]{1,0:T(8,128)(2,1)S(1)}, u32[]{:S(2)}, u32[]{:S(2)}) collective-permute-start(bf16[64,1536]{1,0:T(8,128)(2,1)S(1)} %get-tuple-element.35), channel_id=1, source_target_pairs={{0,64},{1,65},{2,66},{3,67},{4,68},{5,69},{6,70},{7,71},{8,72},{9,... | collective-permute-start | bytes 589832 | tf_op jit(solution)/shard_map/ppermute | solution.py:53
  242.7 13.1 %collective-permute-start.36 = (bf16[64,768]{1,0:T(8,128)(2,1)S(1)}, bf16[64,768]{1,0:T(8,128)(2,1)S(1)}, u32[]{:S(2)}, u32[]{:S(2)}) collective-permute-start(bf16[64,768]{1,0:T(8,128)(2,1)S(1)} %get-tuple-element.48), channel_id=1, source_target_pairs={{0,1},{1,0},{2,3},{3,2},{4,5},{5,4},{6,7},{7,6},{8,9},{9,8},{10,11... | collective-permute-start | bytes 294920 | tf_op jit(solution)/shard_map/ppermute | solution.py:62
  249.0 7.1 %collective-permute-start.35 = (bf16[64,768]{1,0:T(8,128)(2,1)S(1)}, bf16[64,768]{1,0:T(8,128)(2,1)S(1)}, u32[]{:S(2)}, u32[]{:S(2)}) collective-permute-start(bf16[64,768]{1,0:T(8,128)(2,1)S(1)} %get-tuple-element.47), channel_id=1, source_target_pairs={{0,1},{1,0},{2,3},{3,2},{4,5},{5,4},{6,7},{7,6},{8,9},{9,8},{10,11... | collective-permute-start | bytes 294920 | tf_op jit(solution)/shard_map/ppermute | solution.py:62
Sparse Core Ops, SparseCore 0:
  9.1 101.7 all-gather.1
